TPU v7x, 32 devices: a whole 2x2x4 slice. The times are simulated.
32 devices in a mesh: ctx: 8 (over z, core), fsdp: 4 (over y, x).
Axes of the slice: x: 2, y: 2, z: 4, core: 2. Of those that a mesh axis runs over, the one named last changes fastest.
Arguments:
- streams: bfloat16 [4, 4, 1024, 2048], P('fsdp', None, 'ctx'), may hold values from -6 to 6
- w_attn: bfloat16 [2048, 4, 2048], P('fsdp'), may hold values from -2 to 2
- w_ffn: bfloat16 [8192, 3, 2048], P('fsdp'), may hold values from -2 to 2
- hc_dynamic: float32 [2, 6, 2048], replicated, may hold values from -0.125 to 0.125
- hc_static: float32 [2, 4, 6], replicated, may hold values from -3 to 3
- cotangent: bfloat16 [4, 4, 1024, 2048], P('fsdp', None, 'ctx'), may hold values from -6 to 6
- pair_order: int32 [8], replicated, may hold values from 0 to 7, each once
Outputs:
- streams_out: bfloat16 [4, 4, 1024, 2048], P('fsdp', None, 'ctx')
- streams_grad: float32 [4, 4, 1024, 2048], P('fsdp', None, 'ctx')
- w_attn_grad: float32 [2048, 4, 2048], P('fsdp', None, 'ctx')
- w_ffn_grad: float32 [8192, 3, 2048], P('fsdp', None, 'ctx')
- hc_dynamic_grad: float32 [2, 6, 2048], replicated
- hc_static_grad: float32 [2, 4, 6], replicated
Inputs may be any that keep to these rules, and one draw needn't show every extreme that they name: `pair_order`: every pair index appears once.
All inputs are finite; a program needn't handle non-finite values.
Results may differ from a plain program's by a relative error of at most 0.019.
The roundings to bfloat16 on the way count: a program that leaves them out, or rounds other values in their place, can miss the bound.
Values may be sent and summed in bfloat16 or wider, within the bound.
A program may use at most 256 MiB of HBM per device.

v0:
```python
import jax
import jax.numpy as jnp
from jax import lax
from jax.sharding import PartitionSpec as P

HEADS = 16
HEAD_DIM = 128


EPS = 1e-05
THETA = 10000.0
HIGH = lax.Precision.HIGHEST
MASKED = -1e30
CONTRACT_LAST = (((1,), (1,)), ((), ()))
CONTRACT_FIRST = (((0,), (0,)), ((), ()))


def normalize(values):
    centered = values - jnp.mean(values, axis=-1, keepdims=True)
    inverse = lax.rsqrt(jnp.mean(centered * centered, axis=-1, keepdims=True) + EPS)
    return (centered * inverse, inverse)


def normalize_back(normed, inverse, gradient):
    inner = jnp.mean(gradient * normed, axis=-1, keepdims=True)
    return inverse * (gradient - jnp.mean(gradient, axis=-1, keepdims=True) - normed * inner)


def block_positions(pair_order, length):
    half_size = length // 2
    offsets = jnp.arange(half_size, dtype=jnp.int32)
    mirror = 2 * pair_order.shape[0] - 1 - pair_order
    first_half = pair_order[:, None] * half_size + offsets[None, :]
    second_half = mirror[:, None] * half_size + offsets[None, :]
    return jnp.concatenate([first_half, second_half], axis=1).reshape(-1)


def rope_tables(positions, head_size):
    frequency = THETA ** (-(jnp.arange(head_size // 2, dtype=jnp.float32) * 2.0) / head_size)
    angles = positions.astype(jnp.float32)[:, None] * frequency[None, :]
    return (jnp.cos(angles), jnp.sin(angles))


def rotate(values, cosine_table, sine_table):
    half_size = values.shape[-1] // 2
    first_half = values[..., :half_size]
    second_half = values[..., half_size:]
    cosine_part = cosine_table[:, None, :]
    sine_part = sine_table[:, None, :]
    return jnp.concatenate(
        [
            first_half * cosine_part - second_half * sine_part,
            second_half * cosine_part + first_half * sine_part,
        ],
        axis=-1,
    )


def rotate_back(values, cosine_table, sine_table):
    half_size = values.shape[-1] // 2
    first_half = values[..., :half_size]
    second_half = values[..., half_size:]
    cosine_part = cosine_table[:, None, :]
    sine_part = sine_table[:, None, :]
    return jnp.concatenate(
        [
            first_half * cosine_part + second_half * sine_part,
            second_half * cosine_part - first_half * sine_part,
        ],
        axis=-1,
    )


def mixing(streams, dynamic, static):
    normed, inverse = normalize(streams)
    dynamic_part = jnp.tanh(jnp.einsum("std,kd->stk", normed, dynamic, precision=HIGH))
    return (normed, inverse, dynamic_part, dynamic_part + static[:, None, :])


def branch_input(streams, coefficients):
    return sum((coefficients[i, :, 1:2] * streams[i] for i in range(streams.shape[0])))


def mix_output(streams, coefficients, branch_out):
    number = streams.shape[0]
    return jnp.stack(
        [
            sum((coefficients[i, :, 2 + j : 3 + j] * streams[i] for i in range(number)))
            + coefficients[j, :, 0:1] * branch_out
            for j in range(number)
        ]
    )


def mixing_back(
    streams, normed, inverse, dynamic_part, coefficients, dynamic, branch_out, grad_out, branch_back
):
    number = streams.shape[0]
    grad_branch = sum((coefficients[j, :, 0:1] * grad_out[j] for j in range(number)))
    grad_mixed, branch_grads = branch_back(grad_branch)
    coef_rows = []
    stream_grads = []
    for i in range(number):
        route_grads = [jnp.sum(grad_out[j] * streams[i], axis=-1) for j in range(number)]
        coef_rows.append(
            jnp.stack(
                [
                    jnp.sum(grad_out[i] * branch_out, axis=-1),
                    jnp.sum(grad_mixed * streams[i], axis=-1),
                ]
                + route_grads,
                axis=-1,
            )
        )
        stream_grads.append(
            sum((coefficients[i, :, 2 + j : 3 + j] * grad_out[j] for j in range(number)))
            + coefficients[i, :, 1:2] * grad_mixed
        )
    coef_grad = jnp.stack(coef_rows)
    pre_grad = coef_grad * (1.0 - dynamic_part * dynamic_part)
    dynamic_grad = jnp.einsum("stk,std->kd", pre_grad, normed, precision=HIGH)
    normed_grad = jnp.einsum("stk,kd->std", pre_grad, dynamic, precision=HIGH)
    stream_grads = jnp.stack(stream_grads) + normalize_back(normed, inverse, normed_grad)
    return (stream_grads, dynamic_grad, jnp.sum(coef_grad, axis=1), branch_grads)


def gather_attention(w_attn):
    return lax.all_gather(w_attn, "fsdp", axis=0, tiled=True)


def gather_keys(key_low, value_low):
    return (
        lax.all_gather(key_low, "ctx", axis=0, tiled=True),
        lax.all_gather(value_low, "ctx", axis=0, tiled=True),
    )


def share_rows(values):
    return lax.all_gather(values, "fsdp", axis=0, tiled=True)


def sum_rows(values):
    return lax.psum_scatter(values, "fsdp", scatter_dimension=0, tiled=True)


def local(streams, w_attn, w_ffn, hc_dynamic, hc_static, cotangent, pair_order):
    length = streams.shape[2]
    features = streams.shape[3]
    head_count = HEADS
    head_size = HEAD_DIM
    score_scale = head_size ** (-0.5)
    key_positions = block_positions(pair_order, length)
    query_positions = lax.dynamic_slice_in_dim(
        key_positions, lax.axis_index("ctx") * length, length
    )
    cosine_table, sine_table = rope_tables(query_positions, head_size)
    causal_mask = query_positions[:, None] >= key_positions[None, :]
    inputs = streams[0].astype(jnp.float32)
    normed_one, inverse_one, dynamic_one, coef_one = mixing(inputs, hc_dynamic[0], hc_static[0])
    mixed_one = branch_input(inputs, coef_one)
    attn_normed, attn_inverse = normalize(mixed_one)
    attn_low = attn_normed.astype(jnp.bfloat16)
    w_full = gather_attention(w_attn)
    qkv = jnp.einsum("td,dce->tce", attn_low, w_full[:, 0:3], preferred_element_type=jnp.float32)
    query_low = (
        rotate(qkv[:, 0].reshape(length, head_count, head_size), cosine_table, sine_table)
        .reshape(length, features)
        .astype(jnp.bfloat16)
    )
    key_low = (
        rotate(qkv[:, 1].reshape(length, head_count, head_size), cosine_table, sine_table)
        .reshape(length, features)
        .astype(jnp.bfloat16)
    )
    value_low = qkv[:, 2].astype(jnp.bfloat16)
    all_keys, all_values = gather_keys(key_low, value_low)

    def head_forward(head_index, running):
        attended, log_totals = running
        offset = head_index * head_size
        query_head = lax.dynamic_slice_in_dim(query_low, offset, head_size, 1)
        key_head = lax.dynamic_slice_in_dim(all_keys, offset, head_size, 1)
        value_head = lax.dynamic_slice_in_dim(all_values, offset, head_size, 1)
        scores = (
            lax.dot_general(query_head, key_head, CONTRACT_LAST, preferred_element_type=jnp.float32)
            * score_scale
        )
        scores = jnp.where(causal_mask, scores, MASKED)
        highest = jnp.max(scores, axis=-1, keepdims=True)
        exponent = jnp.exp(scores - highest)
        denominator = jnp.sum(exponent, axis=-1, keepdims=True)
        probs_low = (exponent / denominator).astype(jnp.bfloat16)
        head_out = jnp.dot(probs_low, value_head, preferred_element_type=jnp.float32)
        attended = lax.dynamic_update_slice_in_dim(attended, head_out, offset, 1)
        log_totals = lax.dynamic_update_slice_in_dim(
            log_totals, highest + jnp.log(denominator), head_index, 1
        )
        return (attended, log_totals)

    attended, log_totals = lax.fori_loop(
        0,
        head_count,
        head_forward,
        (jnp.zeros((length, features), jnp.float32), jnp.zeros((length, head_count), jnp.float32)),
    )
    attended_low = attended.astype(jnp.bfloat16)
    attn_branch = jnp.dot(attended_low, w_full[:, 3], preferred_element_type=jnp.float32)
    first_out = mix_output(inputs, coef_one, attn_branch)
    normed_two, inverse_two, dynamic_two, coef_two = mixing(first_out, hc_dynamic[1], hc_static[1])
    mixed_two = branch_input(first_out, coef_two)
    ffn_normed, ffn_inverse = normalize(mixed_two)
    ffn_low = ffn_normed.astype(jnp.bfloat16)
    ffn_rows = share_rows(ffn_low)
    gate_up = jnp.einsum("td,ncd->tcn", ffn_rows, w_ffn[:, 0:2], preferred_element_type=jnp.float32)
    gate = gate_up[:, 0]
    up_part = gate_up[:, 1]
    sigmoid_gate = jax.nn.sigmoid(gate)
    activated = gate * sigmoid_gate
    hidden_low = (activated * up_part).astype(jnp.bfloat16)
    ffn_branch = sum_rows(jnp.dot(hidden_low, w_ffn[:, 2], preferred_element_type=jnp.float32))
    second_out = mix_output(first_out, coef_two, ffn_branch)
    streams_out = second_out.astype(jnp.bfloat16)[None]

    def ffn_back(grad_branch):
        grad_low = grad_branch.astype(jnp.bfloat16)
        grad_rows = share_rows(grad_low)
        grad_hidden = lax.dot_general(
            grad_rows, w_ffn[:, 2], CONTRACT_LAST, preferred_element_type=jnp.float32
        )
        grad_gate = grad_hidden * up_part * sigmoid_gate * (1.0 + gate * (1.0 - sigmoid_gate))
        grad_up = grad_hidden * activated
        grad_gate_up = jnp.stack([grad_gate, grad_up], axis=1).astype(jnp.bfloat16)
        grad_normed = sum_rows(
            jnp.einsum(
                "tcn,ncd->td", grad_gate_up, w_ffn[:, 0:2], preferred_element_type=jnp.float32
            )
        )
        inner_grad = jnp.einsum(
            "tcn,td->ncd", grad_gate_up, ffn_rows, preferred_element_type=jnp.float32
        )
        down_grad = lax.dot_general(
            hidden_low, grad_rows, CONTRACT_FIRST, preferred_element_type=jnp.float32
        )
        weight_grad = jnp.concatenate([inner_grad, down_grad[:, None]], axis=1)
        return (normalize_back(ffn_normed, ffn_inverse, grad_normed), weight_grad)

    def attention_back(grad_branch):
        weights_back = gather_attention(w_attn)
        keys_back, values_back = gather_keys(key_low, value_low)
        grad_low = grad_branch.astype(jnp.bfloat16)
        grad_attended = lax.dot_general(
            grad_low, weights_back[:, 3], CONTRACT_LAST, preferred_element_type=jnp.float32
        )
        attended_grad_low = grad_attended.astype(jnp.bfloat16)

        def head_back(head_index, running):
            query_grad, key_grad, value_grad = running
            offset = head_index * head_size
            query_head = lax.dynamic_slice_in_dim(query_low, offset, head_size, 1)
            key_head = lax.dynamic_slice_in_dim(keys_back, offset, head_size, 1)
            value_head = lax.dynamic_slice_in_dim(values_back, offset, head_size, 1)
            out_grad_head = lax.dynamic_slice_in_dim(attended_grad_low, offset, head_size, 1)
            log_head = lax.dynamic_slice_in_dim(log_totals, head_index, 1, 1)
            scores = (
                lax.dot_general(
                    query_head, key_head, CONTRACT_LAST, preferred_element_type=jnp.float32
                )
                * score_scale
            )
            scores = jnp.where(causal_mask, scores, MASKED)
            probs = jnp.exp(scores - log_head)
            probs_grad = lax.dot_general(
                out_grad_head, value_head, CONTRACT_LAST, preferred_element_type=jnp.float32
            )
            centre = jnp.sum(probs * probs_grad, axis=-1, keepdims=True)
            scores_grad = (probs * (probs_grad - centre)).astype(jnp.bfloat16)
            query_part = (
                jnp.dot(scores_grad, key_head, preferred_element_type=jnp.float32) * score_scale
            )
            key_part = (
                lax.dot_general(
                    scores_grad, query_head, CONTRACT_FIRST, preferred_element_type=jnp.float32
                )
                * score_scale
            )
            value_part = lax.dot_general(
                probs.astype(jnp.bfloat16),
                out_grad_head,
                CONTRACT_FIRST,
                preferred_element_type=jnp.float32,
            )
            query_grad = lax.dynamic_update_slice_in_dim(query_grad, query_part, offset, 1)
            key_grad = lax.dynamic_update_slice_in_dim(key_grad, key_part, offset, 1)
            value_grad = lax.dynamic_update_slice_in_dim(value_grad, value_part, offset, 1)
            return (query_grad, key_grad, value_grad)

        total_rows = keys_back.shape[0]
        query_grad, key_grad, value_grad = lax.fori_loop(
            0,
            head_count,
            head_back,
            (
                jnp.zeros((length, features), jnp.float32),
                jnp.zeros((total_rows, features), jnp.float32),
                jnp.zeros((total_rows, features), jnp.float32),
            ),
        )
        key_own, value_own = (
            lax.psum_scatter(key_grad, "ctx", scatter_dimension=0, tiled=True),
            lax.psum_scatter(value_grad, "ctx", scatter_dimension=0, tiled=True),
        )
        query_back = rotate_back(
            query_grad.reshape(length, head_count, head_size), cosine_table, sine_table
        ).reshape(length, features)
        key_back = rotate_back(
            key_own.reshape(length, head_count, head_size), cosine_table, sine_table
        ).reshape(length, features)
        qkv_grad_low = jnp.stack([query_back, key_back, value_own], axis=1).astype(jnp.bfloat16)
        grad_normed = jnp.einsum(
            "tce,dce->td", qkv_grad_low, weights_back[:, 0:3], preferred_element_type=jnp.float32
        )
        own_rows = w_attn.shape[0]
        inputs_all, outputs_all, grads_all, qkv_grads_all = (
            lax.all_gather(attn_low, "fsdp", axis=0, tiled=True),
            lax.all_gather(attended_low, "fsdp", axis=0, tiled=True),
            lax.all_gather(grad_low, "fsdp", axis=0, tiled=True),
            lax.all_gather(qkv_grad_low, "fsdp", axis=0, tiled=True),
        )
        row_start = lax.axis_index("fsdp") * own_rows
        input_rows = lax.dynamic_slice_in_dim(inputs_all, row_start, own_rows, 1)
        output_rows = lax.dynamic_slice_in_dim(outputs_all, row_start, own_rows, 1)
        inner_grad = jnp.einsum(
            "tr,tce->rce", input_rows, qkv_grads_all, preferred_element_type=jnp.float32
        )
        outer_grad = lax.dot_general(
            output_rows, grads_all, CONTRACT_FIRST, preferred_element_type=jnp.float32
        )
        weight_grad = jnp.concatenate([inner_grad, outer_grad[:, None]], axis=1)
        return (normalize_back(attn_normed, attn_inverse, grad_normed), weight_grad)

    grad_final = cotangent[0].astype(jnp.float32)
    grad_first, dynamic_grad_two, static_grad_two, ffn_grad = mixing_back(
        first_out,
        normed_two,
        inverse_two,
        dynamic_two,
        coef_two,
        hc_dynamic[1],
        ffn_branch,
        grad_final,
        ffn_back,
    )
    grad_inputs, dynamic_grad_one, static_grad_one, attn_grad = mixing_back(
        inputs,
        normed_one,
        inverse_one,
        dynamic_one,
        coef_one,
        hc_dynamic[0],
        attn_branch,
        grad_first,
        attention_back,
    )
    attn_grad, ffn_grad = (
        lax.psum_scatter(
            attn_grad.astype(jnp.bfloat16), "ctx", scatter_dimension=2, tiled=True
        ).astype(jnp.float32),
        lax.psum_scatter(
            ffn_grad.astype(jnp.bfloat16), "ctx", scatter_dimension=2, tiled=True
        ).astype(jnp.float32),
    )
    dynamic_total, static_total = lax.psum(
        (
            jnp.stack([dynamic_grad_one, dynamic_grad_two]),
            jnp.stack([static_grad_one, static_grad_two]),
        ),
        ("ctx", "fsdp"),
    )
    return (streams_out, grad_inputs[None], attn_grad, ffn_grad, dynamic_total, static_total)


def solution(mesh):
    return jax.shard_map(
        local,
        mesh=mesh,
        in_specs=(
            P("fsdp", None, "ctx", None),
            P("fsdp", None, None),
            P("fsdp", None, None),
            P(),
            P(),
            P("fsdp", None, "ctx", None),
            P(),
        ),
        out_specs=(
            P("fsdp", None, "ctx", None),
            P("fsdp", None, "ctx", None),
            P("fsdp", None, "ctx"),
            P("fsdp", None, "ctx"),
            P(),
            P(),
        ),
        check_vma=False,
    )
```

profile of v0, /device:TPU:0, one launch (start us, length us, event | category | flops | bytes accessed | tf_op | source)
XLA Modules:
  0.0 1730.5 jit_solution(3345121138281409791)
XLA Ops:
  7.2 11.2 copy.14
  21.8 4.7 broadcast_add_fusion.1
  29.6 288.9 %all-gather.11.cloned.1.call-done = bf16[2048,4,2048]{2,0,1:T(8,128)(2,1)} async-done(((bf16[512,4,2048]{2,0,1:T(8,128)(2,1)}), bf16[2048,4,2048]{2,0,1:T(8,128)(2,1)}) %all-gather.11.cloned.1.call-update) | async-done | bytes 33554448 | tf_op jit(solution)/shard_map/all_gather | solution.py:128
  318.5 10.1 fusion.35
  336.5 40.3 %all-gather.27.cloned.1.call-done = bf16[1024,1,2048]{2,0,1:T(8,128)(2,1)} async-done(((bf16[128,1,2048]{2,0,1:T(8,128)(2,1)}), bf16[1024,1,2048]{2,0,1:T(8,128)(2,1)}) %all-gather.27.cloned.1.call-update) | async-done | bytes 4194320 | tf_op jit(solution)/shard_map/all_gather | solution.py:134
  376.9 48.1 %all-gather.13.cloned.1.call-done = bf16[1024,2048]{1,0:T(8,128)(2,1)} async-done(((bf16[128,2048]{1,0:T(8,128)(2,1)}), bf16[1024,2048]{1,0:T(8,128)(2,1)}) %all-gather.13.cloned.1.call-update) | async-done | bytes 4194320 | tf_op jit(solution)/shard_map/all_gather | solution.py:133
  424.9 65.2 %while.34 = (s32[]{:T(128)}, bf16[128,2048]{1,0:T(8,128)(2,1)S(1)}, f32[128,16]{0,1:T(8,128)}, bf16[128,2048]{1,0:T(8,128)(2,1)S(1)}, bf16[1024,2048]{1,0:T(8,12...) while((s32[]{:T(128)}, bf16[128,2048]{1,0:T(8,128)(2,1)S(1)}, ...), condition=%wide.region_7.8_spmd.clone, body=%wide.region_4.7_spmd.clone.sunk | while | flops 68288384 | bytes 2207407 | solution.py:200
  490.2 6.6 multiply_add_fusion.1
  501.2 4.6 broadcast_add_fusion
  508.3 3.3 add_convert_fusion.3
  511.9 30.5 %all-gather.15.cloned.1.call-done = bf16[512,2048]{1,0:T(8,128)(2,1)} async-done(((bf16[128,2048]{1,0:T(8,128)(2,1)}), bf16[512,2048]{1,0:T(8,128)(2,1)}) %all-gather.15.cloned.1.call-update) | async-done | bytes 2097168 | tf_op jit(solution)/shard_map/all_gather | solution.py:139
  542.4 15.0 fusion.49
  557.5 22.6 %all-gather.17.cloned.1.call-done = bf16[512,2048]{1,0:T(8,128)(2,1)} async-done(((bf16[128,2048]{1,0:T(8,128)(2,1)}), bf16[512,2048]{1,0:T(8,128)(2,1)}) %all-gather.17.cloned.1.call-update) | async-done | bytes 2097168 | tf_op jit(solution)/shard_map/all_gather | solution.py:139
  580.0 10.5 fusion.96
  592.6 13.8 fusion.69
  606.6 12.3 fusion.43
  619.0 40.2 %reduce-scatter.9.cloned.1.call-done = f32[128,2048]{1,0:T(8,128)} async-done(((f32[512,2048]{1,0:T(8,128)}), f32[128,2048]{1,0:T(8,128)}) %reduce-scatter.9.cloned.1.call-update) | async-done | bytes 1048592 | tf_op jit(solution)/shard_map/reduce_scatter | solution.py:143
  661.0 54.1 %reduce-scatter.7.cloned.1.call-done = f32[128,2048]{1,0:T(8,128)} async-done(((f32[512,2048]{1,0:T(8,128)}), f32[128,2048]{1,0:T(8,128)}) %reduce-scatter.7.cloned.1.call-update) | async-done | bytes 1048592 | tf_op jit(solution)/shard_map/reduce_scatter | solution.py:143
  715.2 5.5 multiply_reduce_fusion.33
  720.8 5.9 fusion.177
  731.2 8.6 fusion.78
  740.9 4.3 broadcast.251.clone
  745.2 4.2 broadcast.251
  749.4 142.2 %while.35 = (s32[]{:T(128)}, f32[128,2048]{1,0:T(8,128)}, f32[1024,2048]{1,0:T(8,128)}, f32[1024,2048]{1,0:T(8,128)}, bf16[128,2048]{1,0:T(8,128)(2,1)}, /*index...) while((s32[]{:T(128)}, f32[128,2048]{1,0:T(8,128)}, ...), condition=%wide.region_44.0_spmd.clone, body=%wide.region_42.0_spmd.clone.sunk | while | flops 169230208 | bytes 5976263 | solution.py:298
  893.0 3.4 fusion.119
  897.0 2.7 copy.33
  899.7 81.7 %reduce-scatter.11.cloned.1.call-done = f32[128,2048]{1,0:T(8,128)} async-done(((f32[1024,2048]{1,0:T(8,128)}), f32[128,2048]{1,0:T(8,128)}) %reduce-scatter.11.cloned.1.call-update) | async-done | bytes 1048592 | tf_op jit(solution)/shard_map/reduce_scatter | solution.py:309
  982.8 3.3 add_convert_fusion.1
  993.8 77.9 %reduce-scatter.13.cloned.1.call-done = f32[128,2048]{1,0:T(8,128)} async-done(((f32[1024,2048]{1,0:T(8,128)}), f32[128,2048]{1,0:T(8,128)}) %reduce-scatter.13.cloned.1.call-update) | async-done | bytes 1048592 | tf_op jit(solution)/shard_map/reduce_scatter | solution.py:310
  1076.4 12.6 convert_bitcast_fusion.1
  1089.0 12.6 convert_bitcast_fusion
  1107.1 14.7 fusion.178
  1121.9 4.2 multiply_reduce_fusion.8
  1126.3 4.1 fusion.79
  1131.1 20.7 %pad_maximum_fusion = bf16[2048,3,2048]{0,2,1:T(8,128)(2,1)} fusion(bf16[2048,1,2048]{0,2,1:T(8,128)(2,1)} %convert_bitcast_fusion.1, bf16[2048,2,2048]{0,2,1:T(8,128)(2,1)} %convert_bitcast_fusion), kind=kLoop, calls=%fused_computation.43 | loop fusion | flops 12582912 | bytes 50331648 | tf_op jit(solution)/shard_map/concatenate | solution.py:244
  1152.0 4.6 fusion.72
  1156.5 24.8 %all-gather.19.cloned.1.call-done = bf16[512,2048]{1,0:T(8,128)(2,1)} async-done(((bf16[128,2048]{1,0:T(8,128)(2,1)}), bf16[512,2048]{1,0:T(8,128)(2,1)}) %all-gather.19.cloned.1.call-update) | async-done | bytes 2097168 | tf_op jit(solution)/shard_map/all_gather | solution.py:324
  1181.3 72.6 %all-gather.21.cloned.1.call-done = bf16[512,3,2048]{2,0,1:T(8,128)(2,1)} async-done(((bf16[128,3,2048]{2,0,1:T(8,128)(2,1)}), bf16[512,3,2048]{2,0,1:T(8,128)(2,1)}) %all-gather.21.cloned.1.call-update) | async-done | bytes 6291472 | tf_op jit(solution)/shard_map/all_gather | solution.py:327
  1253.9 9.3 convolution_convert_fusion
  1263.2 6.7 pad_maximum_fusion.1
  1275.7 39.6 %psum.15 = f32[2,4,6]{2,1,0:T(4,128)} all-reduce(f32[2,4,6]{2,1,0:T(4,128)S(1)} %pad_maximum_fusion.15), channel_id=1, replica_groups=mesh['ctx'=8,'fsdp'=4] {'ctx','fsdp'}, use_global_device_ids=true, to_apply=%region_80.81 | all-reduce | flops 48 | bytes 384 | tf_op jit(solution)/shard_map/psum | solution.py:372
  1315.3 4.6 fusion.176
  1321.9 2.8 fusion.52
  1324.7 57.1 %all-reduce.2.cloned.1.call-done = f32[2,6,2048]{2,1,0:T(8,128)} async-done(((f32[2,6,2048]{2,1,0:T(8,128)}), f32[2,6,2048]{2,1,0:T(8,128)}) %all-reduce.2.cloned.1.call-update) | async-done | bytes 98320 | tf_op jit(solution)/shard_map/psum | solution.py:372
  1383.4 246.8 %reduce-scatter.17.cloned.1.call-done = bf16[2048,3,256]{0,2,1:T(8,128)(2,1)} async-done(((bf16[2048,3,2048]{0,2,1:T(8,128)(2,1)}), bf16[2048,3,256]{0,2,1:T(8,128)(2,1)}) %reduce-scatter.17.cloned.1.call-update) | async-done | bytes 3145744 | tf_op jit(solution)/shard_map/reduce_scatter | solution.py:368
  1630.2 5.4 copy.20
  1635.6 84.8 %reduce-scatter.15.cloned.1.call-done = bf16[512,4,256]{2,0,1:T(8,128)(2,1)} async-done(((bf16[512,4,2048]{2,0,1:T(8,128)(2,1)}), bf16[512,4,256]{2,0,1:T(8,128)(2,1)}) %reduce-scatter.15.cloned.1.call-update) | async-done | bytes 1048592 | tf_op jit(solution)/shard_map/reduce_scatter | solution.py:365
  1720.4 3.4 copy.19
  (498 shorter events, 268.7 us)
Async XLA Ops:
  7.2 311.4 %all-gather.11.cloned.1.call-start = ((), (), s32[]{:S(2)}) async-start(), calls=%async_computation.6 | async-start | bytes 41943040 | tf_op jit(solution)/shard_map/all_gather | solution.py:128
  18.5 358.4 %all-gather.27.cloned.1.call-start = ((), (), s32[]{:S(2)}) async-start(), calls=%async_computation.21 | async-start | bytes 4718592 | tf_op jit(solution)/shard_map/all_gather | solution.py:134
  26.5 463.7 %copy-start.79 = (f32[128]{0:T(128)}, f32[128]{0:T(128)S(1)}, u32[]{:S(2)}) copy-start(f32[128]{0:T(128)S(1)} %get-tuple-element.551) | copy-start | bytes 1540
  26.5 463.7 %copy-start.81 = (f32[128]{0:T(128)}, f32[128]{0:T(128)S(1)}, u32[]{:S(2)}) copy-start(f32[128]{0:T(128)S(1)} %get-tuple-element.554) | copy-start | bytes 1540
  26.5 463.7 %copy-start.83 = (f32[128]{0:T(128)}, f32[128]{0:T(128)S(1)}, u32[]{:S(2)}) copy-start(f32[128]{0:T(128)S(1)} %get-tuple-element.552) | copy-start | bytes 1540
  26.5 463.7 %copy-start.85 = (f32[128]{0:T(128)}, f32[128]{0:T(128)S(1)}, u32[]{:S(2)}) copy-start(f32[128]{0:T(128)S(1)} %get-tuple-element.553) | copy-start | bytes 1540
  26.5 470.3 %copy-start.36 = (f32[128]{0:T(128)}, f32[128]{0:T(128)S(1)}, u32[]{:S(2)}) copy-start(f32[128]{0:T(128)S(1)} %get-tuple-element.549) | copy-start | bytes 1540
  26.5 470.3 %copy-start.38 = (f32[128]{0:T(128)}, f32[128]{0:T(128)S(1)}, u32[]{:S(2)}) copy-start(f32[128]{0:T(128)S(1)} %get-tuple-element.556) | copy-start | bytes 1540
  26.5 470.3 %copy-start.40 = (f32[128]{0:T(128)}, f32[128]{0:T(128)S(1)}, u32[]{:S(2)}) copy-start(f32[128]{0:T(128)S(1)} %get-tuple-element.560) | copy-start | bytes 1540
  26.5 470.3 %copy-start.42 = (f32[128]{0:T(128)}, f32[128]{0:T(128)S(1)}, u32[]{:S(2)}) copy-start(f32[128]{0:T(128)S(1)} %get-tuple-element.563) | copy-start | bytes 1540
  26.5 470.3 %copy-start.48 = (f32[128]{0:T(128)}, f32[128]{0:T(128)S(1)}, u32[]{:S(2)}) copy-start(f32[128]{0:T(128)S(1)} %get-tuple-element.557) | copy-start | bytes 1540
  26.6 470.3 %copy-start.50 = (f32[128]{0:T(128)}, f32[128]{0:T(128)S(1)}, u32[]{:S(2)}) copy-start(f32[128]{0:T(128)S(1)} %get-tuple-element.558) | copy-start | bytes 1540
  26.6 470.3 %copy-start.52 = (f32[128]{0:T(128)}, f32[128]{0:T(128)S(1)}, u32[]{:S(2)}) copy-start(f32[128]{0:T(128)S(1)} %get-tuple-element.561) | copy-start | bytes 1540
  26.6 470.3 %copy-start.54 = (f32[128]{0:T(128)}, f32[128]{0:T(128)S(1)}, u32[]{:S(2)}) copy-start(f32[128]{0:T(128)S(1)} %get-tuple-element.562) | copy-start | bytes 1540
  29.6 300.0 %copy-start.88 = (s32[8]{0:T(128)S(1)}, s32[8]{0:T(128)}, u32[]{:S(2)}) copy-start(s32[8]{0:T(128)} %param.17) | copy-start | bytes 100
  329.6 95.4 %all-gather.13.cloned.1.call-start = ((), (), s32[]{:S(2)}) async-start(), calls=%async_computation.7 | async-start | bytes 4718592 | tf_op jit(solution)/shard_map/all_gather | solution.py:133
  332.9 209.6 %all-gather.15.cloned.1.call-start = ((), (), s32[]{:S(2)}) async-start(), calls=%async_computation.8 | async-start | bytes 2621440 | tf_op jit(solution)/shard_map/all_gather | solution.py:139
  336.0 160.8 %copy-start.60 = (f32[128]{0:T(128)}, f32[128]{0:T(128)S(1)}, u32[]{:S(2)}) copy-start(f32[128]{0:T(128)S(1)} %get-tuple-element.568) | copy-start | bytes 1540
  336.0 160.8 %copy-start.62 = (f32[128]{0:T(128)}, f32[128]{0:T(128)S(1)}, u32[]{:S(2)}) copy-start(f32[128]{0:T(128)S(1)} %get-tuple-element.570) | copy-start | bytes 1540
  336.0 160.9 %copy-start.64 = (f32[128]{0:T(128)}, f32[128]{0:T(128)S(1)}, u32[]{:S(2)}) copy-start(f32[128]{0:T(128)S(1)} %get-tuple-element.571) | copy-start | bytes 1540
  336.0 160.9 %copy-start.66 = (f32[128]{0:T(128)}, f32[128]{0:T(128)S(1)}, u32[]{:S(2)}) copy-start(f32[128]{0:T(128)S(1)} %get-tuple-element.572) | copy-start | bytes 1540
  508.3 71.8 %all-gather.17.cloned.1.call-start = ((), (), s32[]{:S(2)}) async-start(), calls=%async_computation.10 | async-start | bytes 2621440 | tf_op jit(solution)/shard_map/all_gather | solution.py:139
  511.7 147.5 %reduce-scatter.9.cloned.1.call-start = ((), (), s32[]{:S(2)}) async-start(), calls=%async_computation.11 | async-start | bytes 5242880 | tf_op jit(solution)/shard_map/reduce_scatter | solution.py:143
  606.4 108.8 %reduce-scatter.7.cloned.1.call-start = ((), (), s32[]{:S(2)}) async-start(), calls=%async_computation.9 | async-start | bytes 5242880 | tf_op jit(solution)/shard_map/reduce_scatter | solution.py:143
  619.0 362.4 %reduce-scatter.11.cloned.1.call-start = ((), (), s32[]{:S(2)}) async-start(), calls=%async_computation.12 | async-start | bytes 9437184 | tf_op jit(solution)/shard_map/reduce_scatter | solution.py:309
  891.6 180.1 %reduce-scatter.13.cloned.1.call-start = ((), (), s32[]{:S(2)}) async-start(), calls=%async_computation.13 | async-start | bytes 9437184 | tf_op jit(solution)/shard_map/reduce_scatter | solution.py:310
  892.4 259.6 %all-gather.23.cloned.1.call-start = ((), (), s32[]{:S(2)}) async-start(), calls=%async_computation.16 | async-start | bytes 2621440 | tf_op jit(solution)/shard_map/all_gather | solution.py:325
  892.9 259.0 %all-gather.25.cloned.1.call-start = ((), (), s32[]{:S(2)}) async-start(), calls=%async_computation.17 | async-start | bytes 2621440 | tf_op jit(solution)/shard_map/all_gather | solution.py:326
  896.4 284.9 %all-gather.19.cloned.1.call-start = ((), (), s32[]{:S(2)}) async-start(), calls=%async_computation.14 | async-start | bytes 2621440 | tf_op jit(solution)/shard_map/all_gather | solution.py:324
  896.9 356.9 %all-gather.21.cloned.1.call-start = ((), (), s32[]{:S(2)}) async-start(), calls=%async_computation.15 | async-start | bytes 7864320 | tf_op jit(solution)/shard_map/all_gather | solution.py:327
  1076.3 305.5 %all-reduce.2.cloned.1.call-start = ((), (), s32[]{:S(2)}) async-start(), calls=%async_computation.20 | async-start | bytes 262144 | tf_op jit(solution)/shard_map/psum | solution.py:372
  1089.0 12.6 copy-start.12
  1089.0 15.1 copy-start.20
  1131.1 499.2 %reduce-scatter.17.cloned.1.call-start = ((), (), s32[]{:S(2)}) async-start(), calls=%async_computation.19 | async-start | bytes 28311552 | tf_op jit(solution)/shard_map/reduce_scatter | solution.py:368
  1151.8 568.5 %reduce-scatter.15.cloned.1.call-start = ((), (), s32[]{:S(2)}) async-start(), calls=%async_computation.18 | async-start | bytes 9437184 | tf_op jit(solution)/shard_map/reduce_scatter | solution.py:365
  1273.0 42.3 %copy-start.27 = (f32[1,6,2048]{2,0,1:T(1,128)S(1)}, f32[1,6,2048]{2,0,1:T(1,128)}, u32[]{:S(2)}) copy-start(f32[1,6,2048]{2,0,1:T(1,128)} %copy-done.26) | copy-start | bytes 147460
  1273.9 41.4 %copy-start.9 = (bf16[1,4,128,2048]{3,2,1,0:T(8,128)(2,1)S(1)}, bf16[1,4,128,2048]{3,2,1,0:T(8,128)(2,1)}, u32[]{:S(2)}) copy-start(bf16[1,4,128,2048]{3,2,1,0:T(8,128)(2,1)} %param.11) | copy-start | bytes 6291460
  1275.5 44.5 %copy-start.16 = (f32[128,2048]{1,0:T(8,128)S(1)}, f32[128,2048]{1,0:T(8,128)}, u32[]{:S(2)}) copy-start(f32[128,2048]{1,0:T(8,128)} %get-tuple-element.469) | copy-start | bytes 3145732
  1275.5 44.5 %copy-start.49 = (f32[128]{0:T(128)S(1)}, f32[128]{0:T(128)}, u32[]{:S(2)}) copy-start(f32[128]{0:T(128)} %copy-done.48) | copy-start | bytes 1540
  1275.5 44.5 %copy-start.51 = (f32[128]{0:T(128)S(1)}, f32[128]{0:T(128)}, u32[]{:S(2)}) copy-start(f32[128]{0:T(128)} %copy-done.50) | copy-start | bytes 1540
  1275.5 44.5 %copy-start.53 = (f32[128]{0:T(128)S(1)}, f32[128]{0:T(128)}, u32[]{:S(2)}) copy-start(f32[128]{0:T(128)} %copy-done.52) | copy-start | bytes 1540
  1275.5 44.6 %copy-start.55 = (f32[128]{0:T(128)S(1)}, f32[128]{0:T(128)}, u32[]{:S(2)}) copy-start(f32[128]{0:T(128)} %copy-done.54) | copy-start | bytes 1540
  1275.5 44.6 %copy-start.57 = (f32[128]{0:T(128)S(1)}, f32[128]{0:T(128)}, u32[]{:S(2)}) copy-start(f32[128]{0:T(128)} %copy-done.56) | copy-start | bytes 1540
  1275.6 44.6 %copy-start.59 = (f32[128]{0:T(128)S(1)}, f32[128]{0:T(128)}, u32[]{:S(2)}) copy-start(f32[128]{0:T(128)} %copy-done.58) | copy-start | bytes 1540
  1275.6 44.6 %copy-start.65 = (f32[128]{0:T(128)S(1)}, f32[128]{0:T(128)}, u32[]{:S(2)}) copy-start(f32[128]{0:T(128)} %copy-done.64) | copy-start | bytes 1540
  1275.6 44.6 %copy-start.67 = (f32[128]{0:T(128)S(1)}, f32[128]{0:T(128)}, u32[]{:S(2)}) copy-start(f32[128]{0:T(128)} %copy-done.66) | copy-start | bytes 1540
  1275.6 44.6 %copy-start.84 = (f32[128]{0:T(128)S(1)}, f32[128]{0:T(128)}, u32[]{:S(2)}) copy-start(f32[128]{0:T(128)} %copy-done.83) | copy-start | bytes 1540
  1275.6 44.6 %copy-start.86 = (f32[128]{0:T(128)S(1)}, f32[128]{0:T(128)}, u32[]{:S(2)}) copy-start(f32[128]{0:T(128)} %copy-done.85) | copy-start | bytes 1540
  (62 other events, 227.8 us)
Sparse Core Ops, SparseCore 0:
  18.6 299.9 all-gather.10
  329.7 47.1 all-gather.26
  379.0 45.8 all-gather.12
  508.4 34.0 all-gather.14
  544.7 35.2 all-gather.16
  606.5 52.6 reduce-scatter.8
  662.4 52.6 reduce-scatter.6
  891.7 89.5 reduce-scatter.10
  983.7 87.9 reduce-scatter.12
  1073.4 33.6 all-gather.22
  1108.9 35.3 all-gather.24
  1146.0 35.2 all-gather.18
  1183.7 70.1 all-gather.20
  1259.3 122.4 all-reduce.1
  1384.0 246.1 reduce-scatter.16
  1632.4 87.9 reduce-scatter.14
where the time goes:
time: 1740 us; the launch traced here: 1730 us
  waiting for transfers between devices  1170 us (67%)
  matrix products  326 us (19%)
  other arithmetic  91.2 us (5%)
  local copies, waits for them, and re-layouts  83 us (5%)
  blocking collectives  39.6 us (2%)
    all_gather x1, waiting for transfers between devices, gather_attention(): return lax.all_gather(w_attn, 'fsdp', axis=0, tiled=True)  289 us
    reduce_scatter x1, waiting for transfers between devices, local(): lax.psum_scatter(ffn_grad.astype(jnp.bfloat16), 'ctx', scatter_dimension=...  247 us
    reduce_scatter x2, waiting for transfers between devices, sum_rows(): return lax.psum_scatter(values, 'fsdp', scatter_dimension=0, tiled=True)  94.3 us
    reduce_scatter x1, waiting for transfers between devices, local(): lax.psum_scatter(attn_grad.astype(jnp.bfloat16), 'ctx', scatter_dimension...  84.8 us
    reduce_scatter x1, waiting for transfers between devices, attention_back(): lax.psum_scatter(key_grad, 'ctx', scatter_dimension=0, tiled=True)  81.7 us
    reduce_scatter x1, waiting for transfers between devices, attention_back(): lax.psum_scatter(value_grad, 'ctx', scatter_dimension=0, tiled=True)  77.9 us
    all_gather x1, waiting for transfers between devices, attention_back(): lax.all_gather(qkv_grad_low, 'fsdp', axis=0, tiled=True)  72.6 us
    psum x1, waiting for transfers between devices, local(): lax.psum((jnp.stack([dynamic_grad_one, dynamic_grad_two]), jnp.stack([sta...  57.1 us
  transfers between devices with their start and end apart: 16, of which 14 were waited for; matrix products, arithmetic and copies ran while one was open for 11% of the time, Pallas kernels for 0%

commit v1 on v0

v1 whole, which is shorter than its diff:
```python
import functools

import jax
import jax.numpy as jnp
from jax import lax
from jax.sharding import PartitionSpec as P

HEADS = 16
HEAD_DIM = 128


EPS = 1e-05
THETA = 10000.0
HIGH = lax.Precision.HIGHEST
MASKED = -1e30
CONTRACT_LAST = (((1,), (1,)), ((), ()))
CONTRACT_FIRST = (((0,), (0,)), ((), ()))


def normalize(values):
    centered = values - jnp.mean(values, axis=-1, keepdims=True)
    inverse = lax.rsqrt(jnp.mean(centered * centered, axis=-1, keepdims=True) + EPS)
    return (centered * inverse, inverse)


def normalize_back(normed, inverse, gradient):
    inner = jnp.mean(gradient * normed, axis=-1, keepdims=True)
    return inverse * (gradient - jnp.mean(gradient, axis=-1, keepdims=True) - normed * inner)


def block_positions(pair_order, length):
    half_size = length // 2
    offsets = jnp.arange(half_size, dtype=jnp.int32)
    mirror = 2 * pair_order.shape[0] - 1 - pair_order
    first_half = pair_order[:, None] * half_size + offsets[None, :]
    second_half = mirror[:, None] * half_size + offsets[None, :]
    return jnp.concatenate([first_half, second_half], axis=1).reshape(-1)


def rope_tables(positions, head_size):
    frequency = THETA ** (-(jnp.arange(head_size // 2, dtype=jnp.float32) * 2.0) / head_size)
    angles = positions.astype(jnp.float32)[:, None] * frequency[None, :]
    return (jnp.cos(angles), jnp.sin(angles))


def rotate(values, cosine_table, sine_table):
    half_size = values.shape[-1] // 2
    first_half = values[..., :half_size]
    second_half = values[..., half_size:]
    cosine_part = cosine_table[:, None, :]
    sine_part = sine_table[:, None, :]
    return jnp.concatenate(
        [
            first_half * cosine_part - second_half * sine_part,
            second_half * cosine_part + first_half * sine_part,
        ],
        axis=-1,
    )


def rotate_back(values, cosine_table, sine_table):
    half_size = values.shape[-1] // 2
    first_half = values[..., :half_size]
    second_half = values[..., half_size:]
    cosine_part = cosine_table[:, None, :]
    sine_part = sine_table[:, None, :]
    return jnp.concatenate(
        [
            first_half * cosine_part + second_half * sine_part,
            second_half * cosine_part - first_half * sine_part,
        ],
        axis=-1,
    )


def mixing(streams, dynamic, static):
    normed, inverse = normalize(streams)
    dynamic_part = jnp.tanh(jnp.einsum("std,kd->stk", normed, dynamic, precision=HIGH))
    return (normed, inverse, dynamic_part, dynamic_part + static[:, None, :])


def branch_input(streams, coefficients):
    return sum((coefficients[i, :, 1:2] * streams[i] for i in range(streams.shape[0])))


def mix_output(streams, coefficients, branch_out):
    number = streams.shape[0]
    return jnp.stack(
        [
            sum((coefficients[i, :, 2 + j : 3 + j] * streams[i] for i in range(number)))
            + coefficients[j, :, 0:1] * branch_out
            for j in range(number)
        ]
    )


def low(values):
    return values.astype(jnp.bfloat16)


def mm(a, b, dims=None):
    if dims is None:
        return jnp.dot(a, b, preferred_element_type=jnp.float32)
    return lax.dot_general(a, b, dims, preferred_element_type=jnp.float32)


def gather(values, axis, dim=0):
    return lax.all_gather(values, axis, axis=dim, tiled=True)


def scatter(values, axis, dim=0):
    return lax.psum_scatter(values, axis, scatter_dimension=dim, tiled=True)


def attend(query, key, value, allowed):
    scores = mm(query, key, CONTRACT_LAST) * HEAD_DIM ** (-0.5)
    scores = jnp.where(allowed, scores, MASKED)
    highest = jnp.max(scores, axis=-1, keepdims=True)
    exponent = jnp.exp(scores - highest)
    total = jnp.sum(exponent, axis=-1, keepdims=True)
    return (mm(low(exponent / total), value), highest + jnp.log(total))


def attend_back(query, key, value, grad_out, log_total, allowed):
    scale = HEAD_DIM ** (-0.5)
    scores = jnp.where(allowed, mm(query, key, CONTRACT_LAST) * scale, MASKED)
    probs = jnp.exp(scores - log_total)
    probs_grad = mm(grad_out, value, CONTRACT_LAST)
    centre = jnp.sum(probs * probs_grad, axis=-1, keepdims=True)
    scores_grad = low(probs * (probs_grad - centre))
    return (
        mm(scores_grad, key) * scale,
        mm(scores_grad, query, CONTRACT_FIRST) * scale,
        mm(low(probs), grad_out, CONTRACT_FIRST),
    )


def local(n_ctx, n_fsdp, streams, w_attn, w_ffn, hc_dynamic, hc_static, cotangent, pair_order):
    number = streams.shape[1]
    length = streams.shape[2]
    features = streams.shape[3]
    size = HEAD_DIM
    own = features // n_ctx
    heads = own // size
    rows = length * n_ctx
    own_rows = w_attn.shape[0]
    ctx = lax.axis_index("ctx")
    fsdp = lax.axis_index("fsdp")
    both = ("ctx", "fsdp")

    w_planes = jnp.moveaxis(w_attn, 1, 0)
    w_own = lax.dynamic_slice_in_dim(w_planes[0:3], ctx * own, own, 2)
    w_qkv = gather(jnp.moveaxis(w_own, 0, 1).reshape(own_rows, 3 * own), "fsdp")
    w_out = gather(w_planes[3], "fsdp")

    positions = block_positions(pair_order, length)
    cosine_table, sine_table = rope_tables(positions, size)
    allowed = positions[:, None] >= positions[None, :]

    inputs = streams[0].astype(jnp.float32)
    normed_one, inverse_one, dynamic_one, coef_one = mixing(inputs, hc_dynamic[0], hc_static[0])
    mixed_one = branch_input(inputs, coef_one)
    attn_normed, attn_inverse = normalize(mixed_one)
    attn_low = low(attn_normed)
    attn_all = gather(attn_low, "ctx")
    qkv = mm(attn_all, w_qkv).reshape(rows, 3, heads, size)
    query = low(rotate(qkv[:, 0], cosine_table, sine_table))
    key = low(rotate(qkv[:, 1], cosine_table, sine_table))
    value = low(qkv[:, 2])
    outs, logs = [], []
    for h in range(heads):
        out, log_total = attend(query[:, h], key[:, h], value[:, h], allowed)
        outs.append(out)
        logs.append(log_total)
    attended = low(jnp.concatenate(outs, axis=1))
    attended_rows = lax.all_to_all(attended, "ctx", 0, 1, tiled=True)
    attn_branch = mm(attended_rows, w_out)
    attended_cols = lax.all_to_all(attended_rows, "fsdp", 1, 0, tiled=True)

    first_out = mix_output(inputs, coef_one, attn_branch)
    normed_two, inverse_two, dynamic_two, coef_two = mixing(first_out, hc_dynamic[1], hc_static[1])
    mixed_two = branch_input(first_out, coef_two)
    ffn_normed, ffn_inverse = normalize(mixed_two)
    ffn_low = low(ffn_normed)
    grad_final = cotangent[0].astype(jnp.float32)
    grad_ffn = low(sum((coef_two[j, :, 0:1] * grad_final[j] for j in range(number))))

    ffn_rows = gather(ffn_low, "fsdp")
    grad_rows = gather(grad_ffn, "fsdp")
    gate = mm(ffn_rows, w_ffn[:, 0], CONTRACT_LAST)
    up_part = mm(ffn_rows, w_ffn[:, 1], CONTRACT_LAST)
    grad_hidden = mm(grad_rows, w_ffn[:, 2], CONTRACT_LAST)
    sigmoid_gate = jax.nn.sigmoid(gate)
    activated = gate * sigmoid_gate
    hidden_low = low(activated * up_part)
    grad_gate = low(grad_hidden * up_part * sigmoid_gate * (1.0 + gate * (1.0 - sigmoid_gate)))
    grad_up = low(grad_hidden * activated)
    ffn_branch = scatter(low(mm(hidden_low, w_ffn[:, 2])), "fsdp").astype(jnp.float32)
    grad_ffn_normed = scatter(
        low(mm(grad_gate, w_ffn[:, 0]) + mm(grad_up, w_ffn[:, 1])), "fsdp"
    ).astype(jnp.float32)

    def weight_part(left, right):
        blocks = right.reshape(right.shape[0], n_ctx, own)
        return scatter(low(jnp.einsum("tn,tke->kne", left, blocks, preferred_element_type=jnp.float32)), "ctx")[0]

    down_grad = weight_part(hidden_low, grad_rows)
    gate_grad = weight_part(grad_gate, ffn_rows)
    up_grad = weight_part(grad_up, ffn_rows)
    ffn_grad = jnp.stack([gate_grad, up_grad, down_grad], axis=1).astype(jnp.float32)

    second_out = mix_output(first_out, coef_two, ffn_branch)
    streams_out = low(second_out)[None]

    def connect_back(
        values, normed, inverse, dynamic_part, coefficients, dynamic, branch_out, grad_out, grad_mixed
    ):
        coef_rows = []
        grads = []
        for i in range(number):
            coef_rows.append(
                jnp.stack(
                    [
                        jnp.sum(grad_out[i] * branch_out, axis=-1),
                        jnp.sum(grad_mixed * values[i], axis=-1),
                    ]
                    + [jnp.sum(grad_out[j] * values[i], axis=-1) for j in range(number)],
                    axis=-1,
                )
            )
            grads.append(
                sum((coefficients[i, :, 2 + j : 3 + j] * grad_out[j] for j in range(number)))
                + coefficients[i, :, 1:2] * grad_mixed
            )
        coef_grad = jnp.stack(coef_rows)
        pre_grad = coef_grad * (1.0 - dynamic_part * dynamic_part)
        dynamic_grad = jnp.einsum("stk,std->kd", pre_grad, normed, precision=HIGH)
        normed_grad = jnp.einsum("stk,kd->std", pre_grad, dynamic, precision=HIGH)
        grads = jnp.stack(grads) + normalize_back(normed, inverse, normed_grad)
        return (grads, dynamic_grad, jnp.sum(coef_grad, axis=1))

    grad_mixed_two = normalize_back(ffn_normed, ffn_inverse, grad_ffn_normed)
    grad_first, dynamic_grad_two, static_grad_two = connect_back(
        first_out, normed_two, inverse_two, dynamic_two, coef_two, hc_dynamic[1], ffn_branch, grad_final, grad_mixed_two
    )

    grad_attn = low(sum((coef_one[j, :, 0:1] * grad_first[j] for j in range(number))))
    grad_attended = low(mm(grad_attn, w_out, CONTRACT_LAST))
    grad_heads = lax.all_to_all(grad_attended, "ctx", 1, 0, tiled=True)
    grad_attn_rows = gather(grad_attn, "fsdp")
    out_grad = weight_part(attended_cols, grad_attn_rows)
    parts = []
    for h in range(heads):
        parts.append(
            attend_back(
                query[:, h], key[:, h], value[:, h], grad_heads[:, h * size : (h + 1) * size], logs[h], allowed
            )
        )
    query_grad, key_grad, value_grad = (jnp.stack([p[i] for p in parts], axis=1) for i in range(3))
    qkv_grad = low(
        jnp.stack(
            [
                rotate_back(query_grad, cosine_table, sine_table),
                rotate_back(key_grad, cosine_table, sine_table),
                value_grad,
            ],
            axis=1,
        ).reshape(rows, 3 * own)
    )
    grad_attn_normed = scatter(low(mm(qkv_grad, w_qkv, CONTRACT_LAST)), "ctx").astype(jnp.float32)
    inner_grad = scatter(low(mm(attn_all, qkv_grad, CONTRACT_FIRST)), "fsdp").reshape(own_rows, 3, own)
    attn_grad = jnp.concatenate([inner_grad, out_grad[:, None]], axis=1).astype(jnp.float32)

    grad_mixed_one = normalize_back(attn_normed, attn_inverse, grad_attn_normed)
    grad_inputs, dynamic_grad_one, static_grad_one = connect_back(
        inputs, normed_one, inverse_one, dynamic_one, coef_one, hc_dynamic[0], attn_branch, grad_first, grad_mixed_one
    )
    dynamic_total, static_total = lax.psum(
        (
            jnp.stack([dynamic_grad_one, dynamic_grad_two]),
            jnp.stack([static_grad_one, static_grad_two]),
        ),
        both,
    )
    return (streams_out, grad_inputs[None], attn_grad, ffn_grad, dynamic_total, static_total)


def solution(mesh):
    return jax.shard_map(
        functools.partial(local, mesh.shape["ctx"], mesh.shape["fsdp"]),
        mesh=mesh,
        in_specs=(
            P("fsdp", None, "ctx", None),
            P("fsdp", None, None),
            P("fsdp", None, None),
            P(),
            P(),
            P("fsdp", None, "ctx", None),
            P(),
        ),
        out_specs=(
            P("fsdp", None, "ctx", None),
            P("fsdp", None, "ctx", None),
            P("fsdp", None, "ctx"),
            P("fsdp", None, "ctx"),
            P(),
            P(),
        ),
        check_vma=False,
    )
```

time: 1740 us -> 1050 us (0.60)
  waiting for transfers between devices: 1170 us -> 669 us
  matrix products: 326 us -> 164 us
  other arithmetic: 91.2 us -> 66.1 us
  local copies, waits for them, and re-layouts: 83 us -> 63.8 us
    all_gather x9 -> x6, waiting for transfers between devices: 528 us -> 195 us  [gather(): return lax.all_gather(values, axis, axis=dim, tiled=True)]
    reduce_scatter x6 -> x8, waiting for transfers between devices: 585 us -> 374 us  [scatter(): return lax.psum_scatter(values, axis, scatter_dimension=dim, tiled=True)]
    dot_general x128 -> x31, matrix products: 317 us -> 155 us  [the longest x14 58 us: mm(): return lax.dot_general(a, b, dims, preferred_element_type=jnp.float32)]
    concatenate x6 -> x1, other arithmetic: 31.5 us -> 0.83 us  [local(): attended = low(jnp.concatenate(outs, axis=1))]
    all_to_all x0 -> x2, waiting for transfers between devices: none -> 25.2 us  [the longest x1 14.7 us: local(): grad_heads = lax.all_to_all(grad_attended, 'ctx', 1, 0, tiled=True)]
    dynamic_update_slice x16 -> x0, local copies, waits for them, and re-layouts: 20.7 us -> none  [head_forward(): lax.dynamic_update_slice_in_dim(log_totals, highest + jnp.log(denominator...]
    unnamed x199 -> x254, local copies, waits for them, and re-layouts: 36.2 us -> 31.8 us
  transfers between devices with their start and end apart: 16 -> 17, of which waited for: 14 -> 15; matrix products, arithmetic and copies ran while one was open for 11% -> 17% of each run, Pallas kernels for 0% -> 0%
where the time goes in v1:
time: 1050 us; the launch traced here: 1040 us
  waiting for transfers between devices  669 us (64%)
  matrix products  164 us (16%)
  other arithmetic  66.1 us (6%)
  local copies, waits for them, and re-layouts  63.8 us (6%)
  blocking collectives  50.9 us (5%)
  between operations  16 us (2%)
  starting transfers between devices  10.5 us (1%)
    reduce_scatter x8, waiting for transfers between devices, scatter(): return lax.psum_scatter(values, axis, scatter_dimension=dim, tiled=True)  374 us
    all_gather x6, waiting for transfers between devices, gather(): return lax.all_gather(values, axis, axis=dim, tiled=True)  195 us
    psum x1, waiting for transfers between devices, local(): lax.psum((jnp.stack([dynamic_grad_one, dynamic_grad_two]), jnp.stack([sta...  73.7 us
    dot_general x14, matrix products, mm(): return lax.dot_general(a, b, dims, preferred_element_type=jnp.float32)  58 us
    dot_general x9, matrix products, mm(): return jnp.dot(a, b, preferred_element_type=jnp.float32)  44.6 us
    psum x1, blocking collectives, local(): lax.psum((jnp.stack([dynamic_grad_one, dynamic_grad_two]), jnp.stack([sta...  38 us
    dot_general x4, matrix products, weight_part(): jnp.einsum('tn,tke->kne', left, blocks, preferred_element_type=jnp.float32)  34.3 us
    unnamed x254, local copies, waits for them, and re-layouts  31.8 us
  transfers between devices with their start and end apart: 17, of which 15 were waited for; matrix products, arithmetic and copies ran while one was open for 17% of the time, Pallas kernels for 0%

profile of v1, /device:TPU:0, one launch (start us, length us, event | category | flops | bytes accessed | tf_op | source)
XLA Modules:
  0.0 1040.3 jit_solution(2712914209576050663)
XLA Ops:
  7.2 13.7 %copy.28 = bf16[512,4,2048]{0,2,1:T(8,128)(2,1)} copy(bf16[512,4,2048]{2,1,0:T(4,128)(2,1)} %param.8) | data formatting | bytes 16777216 | tf_op args[1]
  20.9 6.0 slice.541
  30.8 4.7 broadcast_add_fusion.1
  43.4 32.3 %all-gather.10.cloned.1.call-done = bf16[2048,768]{0,1:T(8,128)(2,1)} async-done(((bf16[512,768]{0,1:T(8,128)(2,1)}), bf16[2048,768]{0,1:T(8,128)(2,1)}) %all-gather.10.cloned.1.call-update) | async-done | bytes 3145744 | tf_op jit(solution)/shard_map/all_gather | solution.py:108
  75.7 49.4 %all-gather.8.cloned.1.call-done = bf16[1024,2048]{1,0:T(8,128)(2,1)} async-done(((bf16[128,2048]{1,0:T(8,128)(2,1)}), bf16[1024,2048]{1,0:T(8,128)(2,1)}) %all-gather.8.cloned.1.call-update) | async-done | bytes 4194320 | tf_op jit(solution)/shard_map/all_gather | solution.py:108
  125.1 6.2 fusion.160
  144.6 4.1 convert_element_type.142
  148.8 10.5 %all-to-all-done = bf16[8,128,256]{1,2,0:T(8,128)(2,1)S(1)} async-done(((bf16[8,128,256]{1,2,0:T(8,128)(2,1)}), bf16[8,128,256]{1,2,0:T(8,128)(2,1)S(1)}, u32[]{:S(2)}, u32[]{:S(2)}) %all-to-all-start) | async-done | bytes 524320 | tf_op jit(solution)/shard_map/all_to_all | solution.py:176
  159.3 54.4 %all-gather.18.cloned.1.call-done = bf16[1,2048,2048]{1,2,0:T(8,128)(2,1)} async-done(((bf16[1,512,2048]{1,2,0:T(8,128)(2,1)}), bf16[1,2048,2048]{1,2,0:T(8,128)(2,1)}) %all-gather.18.cloned.1.call-update) | async-done | bytes 8388624 | tf_op jit(solution)/shard_map/all_gather | solution.py:108
  213.7 7.8 multiply_add_fusion.1
  226.5 4.6 broadcast_add_fusion
  237.9 31.8 %all-gather.12.cloned.1.call-done = bf16[512,2048]{1,0:T(8,128)(2,1)} async-done(((bf16[128,2048]{1,0:T(8,128)(2,1)}), bf16[512,2048]{1,0:T(8,128)(2,1)}) %all-gather.12.cloned.1.call-update) | async-done | bytes 2097168 | tf_op jit(solution)/shard_map/all_gather | solution.py:108
  269.7 10.5 %fusion.10 = f32[512,2048]{1,0:T(8,128)} fusion(bf16[512,2048]{1,0:T(8,128)(2,1)} %all-gather.12.cloned.1.call-done, bf16[2048,3,2048]{2,0,1:T(8,128)(2,1)} %param.9), kind=kOutput, calls=%fused_computation.10 | convolution fusion | flops 4294967296 | bytes 14680064 | tf_op jit(solution)/shard_map/dot_general | solution.py:104
  280.2 27.1 %all-gather.14.cloned.1.call-done = bf16[512,2048]{1,0:T(8,128)(2,1)} async-done(((bf16[128,2048]{1,0:T(8,128)(2,1)}), bf16[512,2048]{1,0:T(8,128)(2,1)}) %all-gather.14.cloned.1.call-update) | async-done | bytes 2097168 | tf_op jit(solution)/shard_map/all_gather | solution.py:108
  307.3 7.8 fusion.4
  315.1 9.8 multiply_convert_fusion.3
  324.8 8.4 fusion.8
  333.3 9.1 add_convert_fusion
  342.7 9.8 fusion.38
  352.6 25.2 %reduce-scatter.11.cloned.1.call-done = bf16[128,2048]{1,0:T(8,128)(2,1)} async-done(((bf16[512,2048]{1,0:T(8,128)(2,1)}), bf16[128,2048]{1,0:T(8,128)(2,1)}) %reduce-scatter.11.cloned.1.call-update) | async-done | bytes 524304 | tf_op jit(solution)/shard_map/reduce_scatter | solution.py:112
  380.6 36.2 %reduce-scatter.9.cloned.1.call-done = bf16[128,2048]{1,0:T(8,128)(2,1)} async-done(((bf16[512,2048]{1,0:T(8,128)(2,1)}), bf16[128,2048]{1,0:T(8,128)(2,1)}) %reduce-scatter.9.cloned.1.call-update) | async-done | bytes 524304 | tf_op jit(solution)/shard_map/reduce_scatter | solution.py:112
  416.8 5.9 fusion.101
  425.6 5.7 fusion.151
  439.5 4.8 fusion.43
  445.2 4.6 all-to-all-start.1
  450.6 14.7 %all-to-all-done.1 = bf16[128,8,256]{2,0,1:T(8,128)(2,1)} async-done(((bf16[128,8,256]{2,0,1:T(8,128)(2,1)}), bf16[128,8,256]{2,0,1:T(8,128)(2,1)}, u32[]{:S(2)}, u32[]{:S(2)}) %all-to-all-start.1) | async-done | bytes 524320 | tf_op jit(solution)/shard_map/all_to_all | solution.py:249
  481.5 5.0 convolution_convert_fusion
  486.8 7.9 convolution_convert_fusion.1
  494.8 12.8 %all_to_all.54 = bf16[128,4,512]{0,2,1:T(8,128)(2,1)} all-to-all(bf16[128,4,512]{0,2,1:T(8,128)(2,1)} %bitcast.712), channel_id=1, replica_groups=mesh['ctx'=8,'fsdp'=4] {'fsdp'}, dimensions={1} | all-to-all | bytes 1048576 | tf_op jit(solution)/shard_map/all_to_all | solution.py:178
  509.6 3.9 copy.47
  513.6 4.3 convert_bitcast_fusion.3
  518.0 4.0 copy.49
  528.9 12.2 %reduce-scatter.13.cloned.1.call-done = bf16[128,2048]{1,0:T(8,128)(2,1)} async-done(((bf16[1024,2048]{1,0:T(8,128)(2,1)}), bf16[128,2048]{1,0:T(8,128)(2,1)}) %reduce-scatter.13.cloned.1.call-update) | async-done | bytes 524304 | tf_op jit(solution)/shard_map/reduce_scatter | solution.py:112
  542.9 4.0 multiply_reduce_fusion.28
  547.1 4.1 fusion.46
  551.9 10.0 convert_bitcast_fusion.2
  562.4 10.0 convert_bitcast_fusion.1
  572.4 4.0 copy.48
  576.4 10.0 convert_bitcast_fusion
  593.5 30.7 %reduce-scatter.17.cloned.1.call-done = bf16[1,512,256]{1,2,0:T(8,128)(2,1)} async-done(((bf16[8,512,256]{1,2,0:T(8,128)(2,1)}), bf16[1,512,256]{1,2,0:T(8,128)(2,1)}) %reduce-scatter.17.cloned.1.call-update) | async-done | bytes 262160 | tf_op jit(solution)/shard_map/reduce_scatter | solution.py:112
  629.7 38.0 %psum.15 = f32[2,4,6]{2,1,0:T(4,128)} all-reduce(f32[2,4,6]{2,1,0:T(4,128)S(1)} %pad_maximum_fusion.11), channel_id=1, replica_groups=mesh['ctx'=8,'fsdp'=4] {'ctx','fsdp'}, use_global_device_ids=true, to_apply=%region_81.82 | all-reduce | flops 48 | bytes 384 | tf_op jit(solution)/shard_map/psum | solution.py:278
  667.7 4.6 fusion.150
  677.1 73.7 %all-reduce.2.cloned.1.call-done = f32[2,6,2048]{2,1,0:T(8,128)} async-done(((f32[2,6,2048]{2,1,0:T(8,128)}), f32[2,6,2048]{2,1,0:T(8,128)}) %all-reduce.2.cloned.1.call-update) | async-done | bytes 98320 | tf_op jit(solution)/shard_map/psum | solution.py:278
  752.5 89.3 %reduce-scatter.19.cloned.1.call-done = bf16[1,2048,256]{1,2,0:T(8,128)(2,1)} async-done(((bf16[8,2048,256]{1,2,0:T(8,128)(2,1)}), bf16[1,2048,256]{1,2,0:T(8,128)(2,1)}) %reduce-scatter.19.cloned.1.call-update) | async-done | bytes 1048592 | tf_op jit(solution)/shard_map/reduce_scatter | solution.py:112
  841.8 90.1 %reduce-scatter.21.cloned.1.call-done = bf16[1,2048,256]{1,2,0:T(8,128)(2,1)} async-done(((bf16[8,2048,256]{1,2,0:T(8,128)(2,1)}), bf16[1,2048,256]{1,2,0:T(8,128)(2,1)}) %reduce-scatter.21.cloned.1.call-update) | async-done | bytes 1048592 | tf_op jit(solution)/shard_map/reduce_scatter | solution.py:112
  931.9 90.1 %reduce-scatter.23.cloned.1.call-done = bf16[1,2048,256]{1,2,0:T(8,128)(2,1)} async-done(((bf16[8,2048,256]{1,2,0:T(8,128)(2,1)}), bf16[1,2048,256]{1,2,0:T(8,128)(2,1)}) %reduce-scatter.23.cloned.1.call-update) | async-done | bytes 1048592 | tf_op jit(solution)/shard_map/reduce_scatter | solution.py:112
  1022.1 5.0 maximum_convert_fusion
  1027.1 6.6 copy.43
  (386 shorter events, 98.9 us)
Async XLA Ops:
  7.2 68.5 %all-gather.10.cloned.1.call-start = ((), (), s32[]{:S(2)}) async-start(), calls=%async_computation.12 | async-start | bytes 3932160 | tf_op jit(solution)/shard_map/all_gather | solution.py:108
  29.0 96.0 %all-gather.8.cloned.1.call-start = ((), (), s32[]{:S(2)}) async-start(), calls=%async_computation.11 | async-start | bytes 4718592 | tf_op jit(solution)/shard_map/all_gather | solution.py:108
  36.1 177.6 %copy-start.52 = (f32[128]{0:T(128)}, f32[128]{0:T(128)S(1)}, u32[]{:S(2)}) copy-start(f32[128]{0:T(128)S(1)} %get-tuple-element.169) | copy-start | bytes 1540
  36.1 177.6 %copy-start.54 = (f32[128]{0:T(128)}, f32[128]{0:T(128)S(1)}, u32[]{:S(2)}) copy-start(f32[128]{0:T(128)S(1)} %get-tuple-element.172) | copy-start | bytes 1540
  36.1 177.6 %copy-start.66 = (f32[128]{0:T(128)}, f32[128]{0:T(128)S(1)}, u32[]{:S(2)}) copy-start(f32[128]{0:T(128)S(1)} %get-tuple-element.170) | copy-start | bytes 1540
  36.1 177.6 %copy-start.68 = (f32[128]{0:T(128)}, f32[128]{0:T(128)S(1)}, u32[]{:S(2)}) copy-start(f32[128]{0:T(128)S(1)} %get-tuple-element.171) | copy-start | bytes 1540
  36.1 177.6 %copy-start.101 = (f32[128]{0:T(128)}, f32[128]{0:T(128)S(1)}, u32[]{:S(2)}) copy-start(f32[128]{0:T(128)S(1)} %get-tuple-element.168) | copy-start | bytes 1540
  36.1 185.4 %copy-start.50 = (f32[128]{0:T(128)}, f32[128]{0:T(128)S(1)}, u32[]{:S(2)}) copy-start(f32[128]{0:T(128)S(1)} %get-tuple-element.167) | copy-start | bytes 1540
  36.1 185.4 %copy-start.56 = (f32[128]{0:T(128)}, f32[128]{0:T(128)S(1)}, u32[]{:S(2)}) copy-start(f32[128]{0:T(128)S(1)} %get-tuple-element.174) | copy-start | bytes 1540
  36.1 185.4 %copy-start.58 = (f32[128]{0:T(128)}, f32[128]{0:T(128)S(1)}, u32[]{:S(2)}) copy-start(f32[128]{0:T(128)S(1)} %get-tuple-element.178) | copy-start | bytes 1540
  36.1 185.4 %copy-start.60 = (f32[128]{0:T(128)}, f32[128]{0:T(128)S(1)}, u32[]{:S(2)}) copy-start(f32[128]{0:T(128)S(1)} %get-tuple-element.181) | copy-start | bytes 1540
  36.1 185.4 %copy-start.70 = (f32[128]{0:T(128)}, f32[128]{0:T(128)S(1)}, u32[]{:S(2)}) copy-start(f32[128]{0:T(128)S(1)} %get-tuple-element.175) | copy-start | bytes 1540
  36.2 185.4 %copy-start.72 = (f32[128]{0:T(128)}, f32[128]{0:T(128)S(1)}, u32[]{:S(2)}) copy-start(f32[128]{0:T(128)S(1)} %get-tuple-element.176) | copy-start | bytes 1540
  36.2 185.4 %copy-start.74 = (f32[128]{0:T(128)}, f32[128]{0:T(128)S(1)}, u32[]{:S(2)}) copy-start(f32[128]{0:T(128)S(1)} %get-tuple-element.179) | copy-start | bytes 1540
  36.2 185.4 %copy-start.76 = (f32[128]{0:T(128)}, f32[128]{0:T(128)S(1)}, u32[]{:S(2)}) copy-start(f32[128]{0:T(128)S(1)} %get-tuple-element.180) | copy-start | bytes 1540
  36.2 185.4 %copy-start.103 = (f32[128]{0:T(128)}, f32[128]{0:T(128)S(1)}, u32[]{:S(2)}) copy-start(f32[128]{0:T(128)S(1)} %get-tuple-element.173) | copy-start | bytes 1540
  38.6 175.1 %all-gather.18.cloned.1.call-start = ((), (), s32[]{:S(2)}) async-start(), calls=%async_computation.25 | async-start | bytes 10485760 | tf_op jit(solution)/shard_map/all_gather | solution.py:108
  43.4 88.1 %copy-start.24 = (f32[1024,64]{0,1:T(8,128)}, f32[1024,64]{0,1:T(8,128)S(1)}, u32[]{:S(2)}) copy-start(f32[1024,64]{0,1:T(8,128)S(1)} %get-tuple-element.192) | copy-start | bytes 786436
  140.5 18.8 %all-to-all-start = ((bf16[8,128,256]{1,2,0:T(8,128)(2,1)}), bf16[8,128,256]{1,2,0:T(8,128)(2,1)S(1)}, u32[]{:S(2)}, u32[]{:S(2)}) async-start(bf16[8,128,256]{1,2,0:T(8,128)(2,1)} %pad_maximum_fusion.5), calls=%async_computation | async-start | bytes 1048576 | tf_op jit(solution)/shard_map/all_to_all | solution.py:176
  144.0 125.6 %all-gather.12.cloned.1.call-start = ((), (), s32[]{:S(2)}) async-start(), calls=%async_computation.13 | async-start | bytes 2621440 | tf_op jit(solution)/shard_map/all_gather | solution.py:108
  148.7 72.9 %copy-start.82 = (f32[128]{0:T(128)}, f32[128]{0:T(128)S(1)}, u32[]{:S(2)}) copy-start(f32[128]{0:T(128)S(1)} %get-tuple-element.186) | copy-start | bytes 1540
  148.7 72.9 %copy-start.84 = (f32[128]{0:T(128)}, f32[128]{0:T(128)S(1)}, u32[]{:S(2)}) copy-start(f32[128]{0:T(128)S(1)} %get-tuple-element.188) | copy-start | bytes 1540
  148.7 72.9 %copy-start.86 = (f32[128]{0:T(128)}, f32[128]{0:T(128)S(1)}, u32[]{:S(2)}) copy-start(f32[128]{0:T(128)S(1)} %get-tuple-element.189) | copy-start | bytes 1540
  148.7 72.9 %copy-start.88 = (f32[128]{0:T(128)}, f32[128]{0:T(128)S(1)}, u32[]{:S(2)}) copy-start(f32[128]{0:T(128)S(1)} %get-tuple-element.190) | copy-start | bytes 1540
  148.8 72.9 %copy-start.105 = (f32[128]{0:T(128)}, f32[128]{0:T(128)S(1)}, u32[]{:S(2)}) copy-start(f32[128]{0:T(128)S(1)} %get-tuple-element.187) | copy-start | bytes 1540
  159.3 62.2 %copy-start.22 = (bf16[8,128,256]{1,2,0:T(8,128)(2,1)}, bf16[8,128,256]{1,2,0:T(8,128)(2,1)S(1)}, u32[]{:S(2)}) copy-start(bf16[8,128,256]{1,2,0:T(8,128)(2,1)S(1)} %all-to-all-done) | copy-start | bytes 1572868
  234.2 73.1 %all-gather.14.cloned.1.call-start = ((), (), s32[]{:S(2)}) async-start(), calls=%async_computation.15 | async-start | bytes 2621440 | tf_op jit(solution)/shard_map/all_gather | solution.py:108
  237.6 140.2 %reduce-scatter.11.cloned.1.call-start = ((), (), s32[]{:S(2)}) async-start(), calls=%async_computation.16 | async-start | bytes 2621440 | tf_op jit(solution)/shard_map/reduce_scatter | solution.py:112
  342.4 74.4 %reduce-scatter.9.cloned.1.call-start = ((), (), s32[]{:S(2)}) async-start(), calls=%async_computation.14 | async-start | bytes 2621440 | tf_op jit(solution)/shard_map/reduce_scatter | solution.py:112
  380.6 43.5 %copy-start.116 = (f32[128]{0:T(128)S(1)}, f32[128]{0:T(128)}, u32[]{:S(2)}) copy-start(f32[128]{0:T(128)} %get-tuple-element.74) | copy-start | bytes 1540
  380.6 43.5 %copy-start.117 = (f32[128]{0:T(128)S(1)}, f32[128]{0:T(128)}, u32[]{:S(2)}) copy-start(f32[128]{0:T(128)} %get-tuple-element.75) | copy-start | bytes 1540
  445.2 20.1 %all-to-all-start.1 = ((bf16[128,8,256]{2,0,1:T(8,128)(2,1)}), bf16[128,8,256]{2,0,1:T(8,128)(2,1)}, u32[]{:S(2)}, u32[]{:S(2)}) async-start(bf16[128,8,256]{2,0,1:T(8,128)(2,1)} %bitcast.724), calls=%async_computation.3 | async-start | bytes 1048576 | tf_op jit(solution)/shard_map/all_to_all | solution.py:249
  449.8 59.9 %all-gather.16.cloned.1.call-start = ((), (), s32[]{:S(2)}) async-start(), calls=%async_computation.19 | async-start | bytes 2621440 | tf_op jit(solution)/shard_map/all_gather | solution.py:108
  450.5 90.7 %reduce-scatter.13.cloned.1.call-start = ((), (), s32[]{:S(2)}) async-start(), calls=%async_computation.17 | async-start | bytes 4718592 | tf_op jit(solution)/shard_map/reduce_scatter | solution.py:112
  486.5 105.4 %reduce-scatter.15.cloned.1.call-start = ((), (), s32[]{:S(2)}) async-start(), calls=%async_computation.18 | async-start | bytes 3932160 | tf_op jit(solution)/shard_map/reduce_scatter | solution.py:112
  494.7 129.5 %reduce-scatter.17.cloned.1.call-start = ((), (), s32[]{:S(2)}) async-start(), calls=%async_computation.20 | async-start | bytes 2359296 | tf_op jit(solution)/shard_map/reduce_scatter | solution.py:112
  518.0 232.9 %all-reduce.2.cloned.1.call-start = ((), (), s32[]{:S(2)}) async-start(), calls=%async_computation.24 | async-start | bytes 262144 | tf_op jit(solution)/shard_map/psum | solution.py:278
  551.9 289.9 %reduce-scatter.19.cloned.1.call-start = ((), (), s32[]{:S(2)}) async-start(), calls=%async_computation.21 | async-start | bytes 9437184 | tf_op jit(solution)/shard_map/reduce_scatter | solution.py:112
  561.9 370.0 %reduce-scatter.21.cloned.1.call-start = ((), (), s32[]{:S(2)}) async-start(), calls=%async_computation.22 | async-start | bytes 9437184 | tf_op jit(solution)/shard_map/reduce_scatter | solution.py:112
  572.4 449.7 %reduce-scatter.23.cloned.1.call-start = ((), (), s32[]{:S(2)}) async-start(), calls=%async_computation.23 | async-start | bytes 9437184 | tf_op jit(solution)/shard_map/reduce_scatter | solution.py:112
  591.9 75.8 %copy-start.16 = (bf16[1,4,128,2048]{3,2,1,0:T(8,128)(2,1)S(1)}, bf16[1,4,128,2048]{3,2,1,0:T(8,128)(2,1)}, u32[]{:S(2)}) copy-start(bf16[1,4,128,2048]{3,2,1,0:T(8,128)(2,1)} %param.7) | copy-start | bytes 6291460
  591.9 75.8 %copy-start.39 = (f32[1,6,2048]{2,0,1:T(1,128)S(1)}, f32[1,6,2048]{2,0,1:T(1,128)}, u32[]{:S(2)}) copy-start(f32[1,6,2048]{2,0,1:T(1,128)} %copy-done.38) | copy-start | bytes 147460
  629.5 43.0 %copy-start.73 = (f32[128]{0:T(128)S(1)}, f32[128]{0:T(128)}, u32[]{:S(2)}) copy-start(f32[128]{0:T(128)} %copy-done.72) | copy-start | bytes 1540
  629.5 43.0 %copy-start.75 = (f32[128]{0:T(128)S(1)}, f32[128]{0:T(128)}, u32[]{:S(2)}) copy-start(f32[128]{0:T(128)} %copy-done.74) | copy-start | bytes 1540
  629.5 43.0 %copy-start.77 = (f32[128]{0:T(128)S(1)}, f32[128]{0:T(128)}, u32[]{:S(2)}) copy-start(f32[128]{0:T(128)} %copy-done.76) | copy-start | bytes 1540
  629.6 43.0 %copy-start.79 = (f32[128]{0:T(128)S(1)}, f32[128]{0:T(128)}, u32[]{:S(2)}) copy-start(f32[128]{0:T(128)} %copy-done.78) | copy-start | bytes 1540
  629.6 43.0 %copy-start.81 = (f32[128]{0:T(128)S(1)}, f32[128]{0:T(128)}, u32[]{:S(2)}) copy-start(f32[128]{0:T(128)} %copy-done.80) | copy-start | bytes 1540
  629.6 43.0 %copy-start.87 = (f32[128]{0:T(128)S(1)}, f32[128]{0:T(128)}, u32[]{:S(2)}) copy-start(f32[128]{0:T(128)} %copy-done.86) | copy-start | bytes 1540
  (94 other events, 617.5 us)
Sparse Core Ops, SparseCore 0:
  29.1 46.5 all-gather.9
  77.9 47.1 all-gather.7
  127.5 86.1 all-gather.17
  234.3 35.3 all-gather.11
  271.9 35.2 all-gather.13
  342.5 35.1 reduce-scatter.10
  381.6 35.1 reduce-scatter.8
  452.4 35.7 all-gather.15
  491.1 49.9 reduce-scatter.12
  544.0 42.1 reduce-scatter.14
  588.4 35.7 reduce-scatter.16
  629.6 121.1 all-reduce.1
  753.1 88.6 reduce-scatter.18
  843.9 87.9 reduce-scatter.20
  934.1 87.9 reduce-scatter.22

commit v2 on v1

--- a/solution.py
+++ b/solution.py
@@ -3,6 +3,8 @@
 import jax
 import jax.numpy as jnp
 from jax import lax
+from jax.experimental import pallas as pl
+from jax.experimental.pallas import tpu as pltpu
 from jax.sharding import PartitionSpec as P
 
 HEADS = 16
@@ -135,6 +137,621 @@
     )
 
 
+MESH = pl.DeviceIdType.MESH
+VMEM_LIMIT = 56 * 1024 * 1024
+
+
+def place(n_ctx):
+    ctx = lax.axis_index("ctx")
+    return (ctx // 2, ctx % 2, lax.axis_index("fsdp"), n_ctx // 2)
+
+
+def greet(peers):
+    barrier = pltpu.get_barrier_semaphore()
+    for peer in peers:
+        pl.semaphore_signal(barrier, inc=1, device_id=peer, device_id_type=MESH)
+    pl.semaphore_wait(barrier, len(peers))
+
+
+def send(source, target, sems, index, peer):
+    return pltpu.make_async_remote_copy(
+        src_ref=source,
+        dst_ref=target,
+        send_sem=sems[0].at[index],
+        recv_sem=sems[1].at[index],
+        device_id=peer,
+        device_id_type=MESH,
+    )
+
+
+def fsdp_neighbours(fsdp):
+    first = fsdp + 1 - 2 * (fsdp % 2)
+    second = (fsdp + 2) % 4
+    return (first, second, (first + 2) % 4)
+
+
+def fsdp_peers(n_fsdp, ctx, fsdp):
+    if n_fsdp == 4:
+        first, second, _ = fsdp_neighbours(fsdp)
+        return [(ctx, first), (ctx, second)]
+    return [(ctx, (fsdp + j) % n_fsdp) for j in range(1, n_fsdp)]
+
+
+def line_peers(chip, core, fsdp, length):
+    return [
+        (chip * 2 + 1 - core, fsdp),
+        ((chip + 1) % length * 2 + core, fsdp),
+        ((chip + length - 1) % length * 2 + core, fsdp),
+    ]
+
+
+def line_gather(own_ref, all_ref, sems, where):
+    chip, core, fsdp, length = where
+    right_sems, left_sems, core_sems = sems
+    sibling = (chip * 2 + 1 - core, fsdp)
+    right = ((chip + 1) % length * 2 + core, fsdp)
+    left = ((chip + length - 1) % length * 2 + core, fsdp)
+
+    def block(index):
+        return all_ref.at[(index + length) % length * 2 + core]
+
+    def pass_on(index, source):
+        return send(source, block(index), core_sems, (index + length) % length, sibling)
+
+    pass_on(chip, own_ref).start()
+    for step in range(length - 1):
+        for sign, peer, way in ((-1, right, right_sems), (1, left, left_sems)):
+            at = chip + sign * step
+            held = (at >= 0) & (at < length)
+            if step > 0:
+
+                @pl.when(held)
+                def _():
+                    send(block(at), block(at), way, step - 1, peer).wait_recv()
+                    pass_on(at, block(at)).start()
+
+            more = (chip < length - 1) if sign < 0 else (chip > 0)
+
+            @pl.when(held & more)
+            def _():
+                send(own_ref if step == 0 else block(at), block(at), way, step, peer).start()
+
+        yield
+    last = length - 1
+    for sign, peer, way in ((-1, right, right_sems), (1, left, left_sems)):
+        at = chip + sign * last
+
+        @pl.when((at >= 0) & (at < length))
+        def _():
+            send(block(at), block(at), way, last - 1, peer).wait_recv()
+            pass_on(at, block(at)).start()
+
+    yield
+    for step in range(length - 1):
+        for sign, peer, way in ((-1, right, right_sems), (1, left, left_sems)):
+            at = chip + sign * step
+            more = (chip < length - 1) if sign < 0 else (chip > 0)
+
+            @pl.when((at >= 0) & (at < length) & more)
+            def _():
+                send(block(at), block(at), way, step, peer).wait_send()
+
+    for index in range(length):
+        pass_on(index, block(index)).wait_send()
+        other = all_ref.at[index * 2 + 1 - core]
+        send(other, other, core_sems, index, sibling).wait_recv()
+
+
+def square_gather(own_ref, all_ref, sems, ctx, fsdp, n_fsdp, passed=None):
+    if n_fsdp != 4:
+        copies = [
+            send(own_ref, all_ref.at[fsdp], sems, j - 1, (ctx, (fsdp + j) % n_fsdp)) for j in range(1, n_fsdp)
+        ]
+        for copy in copies:
+            copy.start()
+        yield
+        for j, copy in enumerate(copies):
+            copy.wait()
+            if passed:
+                passed(all_ref.at[(fsdp + n_fsdp - j - 1) % n_fsdp], (fsdp + n_fsdp - j - 1) % n_fsdp, None, j)
+        return
+    first, second, corner = fsdp_neighbours(fsdp)
+    half = own_ref.shape[0] // 2
+    top, low_half = pl.ds(0, half), pl.ds(half, half)
+    to_first, to_second = (ctx, first), (ctx, second)
+
+    def copy(index, owner, part, peer, source=None):
+        source = all_ref.at[owner, part] if source is None else source
+        return send(source, all_ref.at[owner, part], sems, index, peer)
+
+    starts = [
+        copy(0, fsdp, top, to_first, own_ref.at[top]),
+        copy(1, fsdp, low_half, to_second, own_ref.at[low_half]),
+        copy(2, fsdp, low_half, to_first, own_ref.at[low_half]),
+        copy(3, fsdp, top, to_second, own_ref.at[top]),
+        copy(4, first, top, to_second),
+        copy(5, second, low_half, to_first),
+    ]
+    arrivals = [
+        (0, first, top),
+        (1, second, low_half),
+        (2, first, low_half),
+        (3, second, top),
+        (4, corner, top),
+        (5, corner, low_half),
+    ]
+    for each in starts[:4]:
+        each.start()
+    yield
+    for index, owner, part in arrivals:
+        copy(index, owner, part, to_first).wait_recv()
+        if index < 2:
+            starts[4 + index].start()
+        if passed:
+            passed(all_ref.at[owner, part], owner, part, index)
+        yield
+    for each in starts:
+        each.wait_send()
+
+
+def run_all(*parts):
+    parts = list(parts)
+    while parts:
+        for part in list(parts):
+            try:
+                next(part)
+            except StopIteration:
+                parts.remove(part)
+
+
+def dma_pair(count):
+    return [pltpu.SemaphoreType.DMA((count,)), pltpu.SemaphoreType.DMA((count,))]
+
+
+def any_specs(count):
+    return [pl.BlockSpec(memory_space=pl.ANY)] * count
+
+
+def params(collective_id=None, **more):
+    if collective_id is not None:
+        more.update(collective_id=collective_id, has_side_effects=True)
+    return pltpu.CompilerParams(vmem_limit_bytes=VMEM_LIMIT, **more)
+
+
+def attention_gather(n_ctx, n_fsdp, rows, weights):
+    def kernel(
+        rows_ref, weights_ref, all_rows, all_weights, right_s, right_r, left_s, left_r, core_s, core_r, sq_s, sq_r, own
+    ):
+        where = place(n_ctx)
+        chip, core, fsdp, length = where
+        ctx = chip * 2 + core
+        greet(line_peers(*where) + fsdp_peers(n_fsdp, ctx, fsdp))
+        mine = [
+            pltpu.make_async_copy(weights_ref, all_weights.at[fsdp], own.at[0]),
+            pltpu.make_async_copy(rows_ref, all_rows.at[ctx], own.at[1]),
+        ]
+        for copy in mine:
+            copy.start()
+        run_all(
+            line_gather(rows_ref, all_rows, ((right_s, right_r), (left_s, left_r), (core_s, core_r)), where),
+            square_gather(weights_ref, all_weights, (sq_s, sq_r), ctx, fsdp, n_fsdp),
+        )
+        for copy in mine:
+            copy.wait()
+
+    length = n_ctx // 2
+    return pl.pallas_call(
+        kernel,
+        out_shape=(
+            jax.ShapeDtypeStruct((n_ctx,) + rows.shape, rows.dtype),
+            jax.ShapeDtypeStruct((n_fsdp,) + weights.shape, weights.dtype),
+        ),
+        in_specs=any_specs(2),
+        out_specs=tuple(any_specs(2)),
+        scratch_shapes=dma_pair(length)
+        + dma_pair(length)
+        + dma_pair(length)
+        + dma_pair(max(6, n_fsdp))
+        + [pltpu.SemaphoreType.DMA((2,))],
+        compiler_params=params(0),
+        name="attention_gather",
+    )(rows, weights)
+
+
+def square_rows(n_ctx, n_fsdp, rows):
+    def kernel(rows_ref, all_ref, sq_s, sq_r, own):
+        chip, core, fsdp, _ = place(n_ctx)
+        ctx = chip * 2 + core
+        greet(fsdp_peers(n_fsdp, ctx, fsdp))
+        mine = pltpu.make_async_copy(rows_ref, all_ref.at[fsdp], own)
+        mine.start()
+        run_all(square_gather(rows_ref, all_ref, (sq_s, sq_r), ctx, fsdp, n_fsdp))
+        mine.wait()
+
+    return pl.pallas_call(
+        kernel,
+        out_shape=jax.ShapeDtypeStruct((n_fsdp,) + rows.shape, rows.dtype),
+        in_specs=any_specs(1),
+        out_specs=pl.BlockSpec(memory_space=pl.ANY),
+        scratch_shapes=dma_pair(max(6, n_fsdp)) + [pltpu.SemaphoreType.DMA],
+        compiler_params=params(7),
+        name="square_rows",
+    )(rows)
+
+
+def square_core_gather(n_ctx, n_fsdp, rows):
+    def kernel(rows_ref, all_ref, sq_s, sq_r, core_s, core_r, own):
+        chip, core, fsdp, _ = place(n_ctx)
+        ctx = chip * 2 + core
+        sibling = (chip * 2 + 1 - core, fsdp)
+        greet([sibling] + fsdp_peers(n_fsdp, ctx, fsdp))
+        mine = pltpu.make_async_copy(rows_ref, all_ref.at[core, fsdp], own)
+        mine.start()
+        handed = [send(rows_ref, all_ref.at[core, fsdp], (core_s, core_r), 0, sibling)]
+        handed[0].start()
+        arriving = [send(rows_ref, all_ref.at[1 - core, fsdp], (core_s, core_r), 0, sibling)]
+
+        def passed(source, owner, part, index):
+            target = all_ref.at[core, owner] if part is None else all_ref.at[core, owner, part]
+            handed.append(send(source, target, (core_s, core_r), index + 1, sibling))
+            handed[-1].start()
+            target = all_ref.at[1 - core, owner] if part is None else all_ref.at[1 - core, owner, part]
+            arriving.append(send(source, target, (core_s, core_r), index + 1, sibling))
+
+        run_all(square_gather(rows_ref, all_ref.at[core], (sq_s, sq_r), ctx, fsdp, n_fsdp, passed))
+        for out, back in zip(handed, arriving):
+            out.wait_send()
+            back.wait_recv()
+        mine.wait()
+
+    return pl.pallas_call(
+        kernel,
+        out_shape=jax.ShapeDtypeStruct((2, n_fsdp) + rows.shape, rows.dtype),
+        in_specs=any_specs(1),
+        out_specs=pl.BlockSpec(memory_space=pl.ANY),
+        scratch_shapes=dma_pair(max(6, n_fsdp)) + dma_pair(max(7, n_fsdp)) + [pltpu.SemaphoreType.DMA],
+        compiler_params=params(1),
+        name="square_core_gather",
+    )(rows)
+
+
+def add_into(target, *sources, chunk=64):
+    @pl.loop(0, target.shape[0] // chunk)
+    def _(step):
+        rows = pl.ds(pl.multiple_of(step * chunk, chunk), chunk)
+        total = target[rows].astype(jnp.float32)
+        for source in sources:
+            total = total + source[rows].astype(jnp.float32)
+        target[rows] = total.astype(target.dtype)
+
+
+def square_sum(n_ctx, n_fsdp, partial, with_core, collective_id):
+    rows, columns = partial.shape[-2:]
+    half = rows // 2
+
+    def kernel(partial_ref, out_ref, held, core_in, square_in, load, core_s, core_r, sq_s, sq_r):
+        chip, core, fsdp, _ = place(n_ctx)
+        ctx = chip * 2 + core
+        sibling = (chip * 2 + 1 - core, fsdp)
+        greet(([sibling] if with_core else []) + fsdp_peers(n_fsdp, ctx, fsdp))
+        if n_fsdp == 4:
+            first, second, corner = fsdp_neighbours(fsdp)
+            order = [corner, first, second, fsdp]
+        else:
+            order = [(fsdp + j) % n_fsdp for j in range(1, n_fsdp + 1)]
+        mine, others = [], []
+        for j, owner in enumerate(order):
+            source = partial_ref.at[core, owner] if with_core else partial_ref.at[owner]
+            mine.append(pltpu.make_async_copy(source, held.at[owner], load.at[j]))
+            if with_core:
+                others.append(
+                    send(partial_ref.at[1 - core, owner], core_in.at[owner], (core_s, core_r), j, sibling)
+                )
+                others[-1].start()
+            mine[-1].start()
+
+        def ready(j):
+            mine[j].wait()
+            if with_core:
+                others[j].wait_recv()
+                add_into(held.at[order[j]], core_in.at[order[j]])
+
+        if n_fsdp != 4:
+            copies = []
+            for j in range(n_fsdp - 1):
+                ready(j)
+                copies.append(
+                    send(held.at[order[j]], square_in.at[j], (sq_s, sq_r), j, (ctx, order[j]))
+                )
+                copies[-1].start()
+            ready(n_fsdp - 1)
+            total = held.at[fsdp]
+            for j, copy in enumerate(copies):
+                copy.wait()
+            @pl.loop(0, rows // 64)
+            def _(step):
+                at = pl.ds(pl.multiple_of(step * 64, 64), 64)
+                value = total[at].astype(jnp.float32)
+                for j in range(n_fsdp - 1):
+                    value = value + square_in[j, at].astype(jnp.float32)
+                out_ref[at] = value
+        else:
+            top, low_half = pl.ds(0, half), pl.ds(half, half)
+            to_first, to_second = (ctx, first), (ctx, second)
+
+            def copy(index, owner, part, peer):
+                return send(
+                    held.at[owner, part], square_in.at[index], (sq_s, sq_r), index, peer
+                )
+
+            copies = [
+                copy(0, corner, top, to_first),
+                copy(1, corner, low_half, to_second),
+                copy(2, first, top, to_first),
+                copy(3, second, low_half, to_second),
+                copy(4, second, top, to_second),
+                copy(5, first, low_half, to_first),
+            ]
+            ready(0)
+            copies[0].start()
+            copies[1].start()
+            ready(1)
+            copies[2].start()
+            ready(2)
+            copies[3].start()
+            copies[0].wait_recv()
+            add_into(held.at[second, top], square_in.at[0])
+            copies[4].start()
+            copies[1].wait_recv()
+            add_into(held.at[first, low_half], square_in.at[1])
+            copies[5].start()
+            ready(3)
+            for j in range(2, 6):
+                copies[j].wait_recv()
+            for part, sources in ((0, (2, 4)), (half, (3, 5))):
+
+                @pl.loop(0, half // 64)
+                def _(step):
+                    at = pl.ds(pl.multiple_of(part + step * 64, 64), 64)
+                    from_at = pl.ds(pl.multiple_of(step * 64, 64), 64)
+                    value = held[fsdp, at].astype(jnp.float32)
+                    for j in sources:
+                        value = value + square_in[j, from_at].astype(jnp.float32)
+                    out_ref[at] = value
+
+            for each in copies:
+                each.wait_send()
+        for each in others:
+            each.wait_send()
+
+    pieces = (6, half, columns) if n_fsdp == 4 else (n_fsdp - 1, rows, columns)
+    return pl.pallas_call(
+        kernel,
+        out_shape=jax.ShapeDtypeStruct((rows, columns), jnp.float32),
+        in_specs=any_specs(1),
+        out_specs=pl.BlockSpec(memory_space=pltpu.VMEM),
+        scratch_shapes=[
+            pltpu.VMEM((n_fsdp, rows, columns), partial.dtype),
+            pltpu.VMEM((n_fsdp, rows, columns) if with_core else (1, 16, 128), partial.dtype),
+            pltpu.VMEM(pieces, partial.dtype),
+            pltpu.SemaphoreType.DMA((n_fsdp,)),
+        ]
+        + dma_pair(n_fsdp)
+        + dma_pair(max(6, n_fsdp)),
+        compiler_params=params(collective_id),
+        name="square_sum",
+    )(partial)
+
+
+def line_sum(n_ctx, partial, collective_id):
+    rows, columns = partial.shape[-2:]
+    length = n_ctx // 2
+
+    def kernel(partial_ref, out_ref, held, core_in, right_in, left_in, load, core_s, core_r, right_s, right_r, left_s, left_r):
+        where = place(n_ctx)
+        chip, core, fsdp, _ = where
+        sibling, right, left = line_peers(*where)
+        greet([sibling, right, left])
+        order = [(chip + length - 1 - j) % length for j in range(length)]
+        mine, others = [], []
+        for j, owner in enumerate(order):
+            mine.append(pltpu.make_async_copy(partial_ref.at[owner * 2 + core], held.at[owner], load.at[j]))
+            others.append(
+                send(partial_ref.at[owner * 2 + 1 - core], core_in.at[owner], (core_s, core_r), j, sibling)
+            )
+            others[-1].start()
+            mine[-1].start()
+        for j, owner in enumerate(order):
+            mine[j].wait()
+            others[j].wait_recv()
+            add_into(held.at[owner], core_in.at[owner])
+        ways = ((1, right, right_in, (right_s, right_r)), (-1, left, left_in, (left_s, left_r)))
+        for step in range(length - 1):
+            for sign, peer, arrived, sems in ways:
+                block = chip + sign * (length - 1 - step)
+                inside = (block >= 0) & (block < length)
+
+                came = (chip >= 1) if sign > 0 else (chip < length - 1)
+                if step > 0:
+
+                    @pl.when(inside & came)
+                    def _():
+                        send(held.at[block], arrived.at[step - 1], sems, step - 1, peer).wait_recv()
+                        add_into(held.at[block], arrived.at[step - 1])
+
+                @pl.when(inside)
+                def _():
+                    send(held.at[block], arrived.at[step], sems, step, peer).start()
+
+        last = length - 2
+        for sign, peer, arrived, sems in ways:
+            came = (chip >= 1) if sign > 0 else (chip < length - 1)
+
+            @pl.when(came)
+            def _():
+                send(held.at[chip], arrived.at[last], sems, last, peer).wait_recv()
+                add_into(held.at[chip], arrived.at[last])
+
+        @pl.loop(0, rows // 64)
+        def _(step):
+            at = pl.ds(pl.multiple_of(step * 64, 64), 64)
+            out_ref[at] = held[chip, at].astype(jnp.float32)
+
+        for step in range(length - 1):
+            for sign, peer, arrived, sems in ways:
+                block = chip + sign * (length - 1 - step)
+
+                @pl.when((block >= 0) & (block < length))
+                def _():
+                    send(held.at[block], arrived.at[step], sems, step, peer).wait_send()
+
+        for each in others:
+            each.wait_send()
+
+    return pl.pallas_call(
+        kernel,
+        out_shape=jax.ShapeDtypeStruct((rows, columns), jnp.float32),
+        in_specs=any_specs(1),
+        out_specs=pl.BlockSpec(memory_space=pltpu.VMEM),
+        scratch_shapes=[
+            pltpu.VMEM((length, rows, columns), partial.dtype),
+            pltpu.VMEM((length, rows, columns), partial.dtype),
+            pltpu.VMEM((length - 1, rows, columns), partial.dtype),
+            pltpu.VMEM((length - 1, rows, columns), partial.dtype),
+            pltpu.SemaphoreType.DMA((length,)),
+        ]
+        + dma_pair(length)
+        + dma_pair(length)
+        + dma_pair(length),
+        compiler_params=params(collective_id),
+        name="line_sum",
+    )(partial)
+
+
+def sum_everywhere(n_ctx, n_fsdp, values):
+    ctx_steps = [1 << i for i in range(n_ctx.bit_length() - 1)]
+    fsdp_steps = [1 << i for i in range(n_fsdp.bit_length() - 1)]
+    rounds = len(ctx_steps) + len(fsdp_steps)
+
+    def kernel(values_ref, out_ref, out_buf, arrived, sent_s, sent_r):
+        ctx = lax.axis_index("ctx")
+        fsdp = lax.axis_index("fsdp")
+        peers = [(ctx + s - 2 * s * (ctx // s % 2), fsdp) for s in ctx_steps]
+        peers += [(ctx, fsdp + s - 2 * s * (fsdp // s % 2)) for s in fsdp_steps]
+        greet(peers)
+        out_buf[0] = values_ref[...]
+        for j, peer in enumerate(peers):
+            copy = send(out_buf.at[j], arrived.at[j], (sent_s, sent_r), j, peer)
+            copy.start()
+            copy.wait()
+            out_buf[j + 1] = out_buf[j] + arrived[j]
+        out_ref[...] = out_buf[rounds]
+
+    return pl.pallas_call(
+        kernel,
+        out_shape=jax.ShapeDtypeStruct(values.shape, values.dtype),
+        in_specs=[pl.BlockSpec(memory_space=pltpu.VMEM)],
+        out_specs=pl.BlockSpec(memory_space=pltpu.VMEM),
+        scratch_shapes=[
+            pltpu.VMEM((rounds + 1,) + values.shape, values.dtype),
+            pltpu.VMEM((rounds,) + values.shape, values.dtype),
+        ]
+        + dma_pair(rounds),
+        compiler_params=params(2),
+        name="sum_everywhere",
+    )(values)
+
+
+def ffn_forward(rows, planes, core, length, n_own, chunk=256):
+    blocks, _, tokens, features = rows.shape
+    total = blocks * tokens
+    wide = features // length
+    steps = n_own // chunk
+    group = max(1, 256 // tokens)
+
+    def kernel(core_ref, rows_ref, gate_ref, up_ref, down_ref, hidden_ref, grad_gate_ref, grad_up_ref, weight_ref):
+        for at in range(0, blocks, group):
+            here = rows_ref[at : at + group, 0].reshape(group * tokens, features)
+            back = rows_ref[at : at + group, 1].reshape(group * tokens, features)
+            gate = mm(here, gate_ref[0], CONTRACT_LAST)
+            up = mm(here, up_ref[0], CONTRACT_LAST)
+            grad_hidden = mm(back, down_ref[0], CONTRACT_LAST)
+            sigmoid = jax.nn.sigmoid(gate)
+            activated = gate * sigmoid
+            span = pl.ds(at * tokens, group * tokens)
+            hidden_ref[span] = low(activated * up)
+            grad_gate_ref[span] = low(grad_hidden * up * sigmoid * (1.0 + gate * (1.0 - sigmoid)))
+            grad_up_ref[span] = low(grad_hidden * activated)
+        for plane, (left, which) in enumerate(((grad_gate_ref, 0), (grad_up_ref, 0), (hidden_ref, 1))):
+            left = left[...]
+            for z in range(length):
+                right = rows_ref[:, which, :, z * wide : (z + 1) * wide].reshape(total, wide)
+                weight_ref[z, plane] = low(mm(left, right, CONTRACT_FIRST))
+
+    def weight_spec(plane):
+        return pl.BlockSpec((1, chunk, features), lambda j, core_ref: (plane, core_ref[0] * steps + j, 0))
+
+    act = jax.ShapeDtypeStruct((total, n_own), jnp.bfloat16)
+    act_spec = pl.BlockSpec((total, chunk), lambda j, core_ref: (0, j))
+    return pl.pallas_call(
+        kernel,
+        grid_spec=pltpu.PrefetchScalarGridSpec(
+            num_scalar_prefetch=1,
+            grid=(steps,),
+            in_specs=[
+                pl.BlockSpec(rows.shape, lambda j, core_ref: (0, 0, 0, 0), pipeline_mode=pl.Buffered(1)),
+                weight_spec(0),
+                weight_spec(1),
+                weight_spec(2),
+            ],
+            out_specs=[
+                act_spec,
+                act_spec,
+                act_spec,
+                pl.BlockSpec((length, 3, chunk, wide), lambda j, core_ref: (0, 0, j, 0)),
+            ],
+        ),
+        out_shape=[act, act, act, jax.ShapeDtypeStruct((length, 3, n_own, wide), jnp.bfloat16)],
+        compiler_params=params(),
+        cost_estimate=pl.CostEstimate(
+            flops=12 * total * n_own * features, bytes_accessed=40 * 1024 * 1024, transcendentals=total * n_own
+        ),
+        name="ffn_forward",
+    )(core, rows, planes, planes, planes)
+
+
+def ffn_back(hidden, grad_gate, grad_up, planes, core, blocks, wide=512):
+    total, n_own = hidden.shape
+    features = planes.shape[2]
+    tokens = total // blocks
+
+    def kernel(core_ref, hidden_ref, grad_gate_ref, grad_up_ref, gate_ref, up_ref, down_ref, out_ref):
+        out = mm(hidden_ref[...], down_ref[0])
+        out_ref[:, 0] = low(out).reshape(blocks, tokens, wide)
+        back = mm(grad_gate_ref[...], gate_ref[0]) + mm(grad_up_ref[...], up_ref[0])
+        out_ref[:, 1] = low(back).reshape(blocks, tokens, wide)
+
+    def weight_spec(plane):
+        return pl.BlockSpec((1, n_own, wide), lambda j, core_ref: (plane, core_ref[0], j))
+
+    act_spec = pl.BlockSpec((total, n_own), lambda j, core_ref: (0, 0), pipeline_mode=pl.Buffered(1))
+    return pl.pallas_call(
+        kernel,
+        grid_spec=pltpu.PrefetchScalarGridSpec(
+            num_scalar_prefetch=1,
+            grid=(features // wide,),
+            in_specs=[act_spec, act_spec, act_spec, weight_spec(0), weight_spec(1), weight_spec(2)],
+            out_specs=pl.BlockSpec((blocks, 2, tokens, wide), lambda j, core_ref: (0, 0, 0, j)),
+        ),
+        out_shape=jax.ShapeDtypeStruct((blocks, 2, tokens, features), jnp.bfloat16),
+        compiler_params=params(),
+        cost_estimate=pl.CostEstimate(
+            flops=6 * total * n_own * features, bytes_accessed=30 * 1024 * 1024, transcendentals=0
+        ),
+        name="ffn_back",
+    )(core, hidden, grad_gate, grad_up, planes, planes, planes)
+
+
 def local(n_ctx, n_fsdp, streams, w_attn, w_ffn, hc_dynamic, hc_static, cotangent, pair_order):
     number = streams.shape[1]
     length = streams.shape[2]
@@ -146,12 +763,22 @@
     own_rows = w_attn.shape[0]
     ctx = lax.axis_index("ctx")
     fsdp = lax.axis_index("fsdp")
-    both = ("ctx", "fsdp")
+    core = ctx % 2
+    chips = n_ctx // 2
+    core_index = jnp.reshape(core, (1,)).astype(jnp.int32)
+
+    def in_order(mine, other, axis):
+        return jnp.where(
+            core == 0, jnp.concatenate([mine, other], axis=axis), jnp.concatenate([other, mine], axis=axis)
+        )
+
 
     w_planes = jnp.moveaxis(w_attn, 1, 0)
     w_own = lax.dynamic_slice_in_dim(w_planes[0:3], ctx * own, own, 2)
-    w_qkv = gather(jnp.moveaxis(w_own, 0, 1).reshape(own_rows, 3 * own), "fsdp")
-    w_out = gather(w_planes[3], "fsdp")
+    w_own = jnp.moveaxis(w_own, 0, 1).reshape(own_rows, 3 * own)
+    half = features // 2
+    w_out_mine = gather(lax.dynamic_slice_in_dim(w_planes[3], core * half, half, 1), "fsdp")
+    w_out_other = lax.ppermute(w_out_mine, "ctx", [(i, i ^ 1) for i in range(n_ctx)])
 
     positions = block_positions(pair_order, length)
     cosine_table, sine_table = rope_tables(positions, size)
@@ -162,7 +789,9 @@
     mixed_one = branch_input(inputs, coef_one)
     attn_normed, attn_inverse = normalize(mixed_one)
     attn_low = low(attn_normed)
-    attn_all = gather(attn_low, "ctx")
+    attn_all, w_qkv = attention_gather(n_ctx, n_fsdp, attn_low, w_own)
+    attn_all = attn_all.reshape(rows, features)
+    w_qkv = w_qkv.reshape(features, 3 * own)
     qkv = mm(attn_all, w_qkv).reshape(rows, 3, heads, size)
     query = low(rotate(qkv[:, 0], cosine_table, sine_table))
     key = low(rotate(qkv[:, 1], cosine_table, sine_table))
@@ -174,7 +803,7 @@
         logs.append(log_total)
     attended = low(jnp.concatenate(outs, axis=1))
     attended_rows = lax.all_to_all(attended, "ctx", 0, 1, tiled=True)
-    attn_branch = mm(attended_rows, w_out)
+    attn_branch = in_order(mm(attended_rows, w_out_mine), mm(attended_rows, w_out_other), 1)
     attended_cols = lax.all_to_all(attended_rows, "fsdp", 1, 0, tiled=True)
 
     first_out = mix_output(inputs, coef_one, attn_branch)
@@ -185,29 +814,22 @@
     grad_final = cotangent[0].astype(jnp.float32)
     grad_ffn = low(sum((coef_two[j, :, 0:1] * grad_final[j] for j in range(number))))
 
-    ffn_rows = gather(ffn_low, "fsdp")
-    grad_rows = gather(grad_ffn, "fsdp")
-    gate = mm(ffn_rows, w_ffn[:, 0], CONTRACT_LAST)
-    up_part = mm(ffn_rows, w_ffn[:, 1], CONTRACT_LAST)
-    grad_hidden = mm(grad_rows, w_ffn[:, 2], CONTRACT_LAST)
-    sigmoid_gate = jax.nn.sigmoid(gate)
-    activated = gate * sigmoid_gate
-    hidden_low = low(activated * up_part)
-    grad_gate = low(grad_hidden * up_part * sigmoid_gate * (1.0 + gate * (1.0 - sigmoid_gate)))
-    grad_up = low(grad_hidden * activated)
-    ffn_branch = scatter(low(mm(hidden_low, w_ffn[:, 2])), "fsdp").astype(jnp.float32)
-    grad_ffn_normed = scatter(
-        low(mm(grad_gate, w_ffn[:, 0]) + mm(grad_up, w_ffn[:, 1])), "fsdp"
-    ).astype(jnp.float32)
-
-    def weight_part(left, right):
-        blocks = right.reshape(right.shape[0], n_ctx, own)
-        return scatter(low(jnp.einsum("tn,tke->kne", left, blocks, preferred_element_type=jnp.float32)), "ctx")[0]
-
-    down_grad = weight_part(hidden_low, grad_rows)
-    gate_grad = weight_part(grad_gate, ffn_rows)
-    up_grad = weight_part(grad_up, ffn_rows)
-    ffn_grad = jnp.stack([gate_grad, up_grad, down_grad], axis=1).astype(jnp.float32)
+    planes = jnp.moveaxis(w_ffn, 1, 0)
+    n_own = planes.shape[1] // 2
+    blocks = 2 * n_fsdp
+    ffn_rows = square_core_gather(n_ctx, n_fsdp, jnp.stack([ffn_low, grad_ffn]).reshape(2 * length, features))
+    ffn_rows = ffn_rows.reshape(blocks, 2, length, features)
+    hidden, grad_gate, grad_up, weight_parts = ffn_forward(ffn_rows, planes, core_index, chips, n_own)
+    lines = [[2 * i + j for i in range(chips)] for j in range(2)]
+    weight_cols = lax.psum_scatter(weight_parts, "ctx", scatter_dimension=0, axis_index_groups=lines)
+    sums = ffn_back(hidden, grad_gate, grad_up, planes, core_index, blocks)
+    sums = square_sum(n_ctx, n_fsdp, sums.reshape(2, n_fsdp, 2 * length, features), True, 3)
+    ffn_branch = sums[:length]
+    grad_ffn_normed = sums[length:]
+    mine = lax.dynamic_slice_in_dim(weight_cols, core * own, own, 2)
+    other = lax.dynamic_slice_in_dim(weight_cols, (1 - core) * own, own, 2)
+    other = lax.ppermute(other, "ctx", [(i, i ^ 1) for i in range(n_ctx)])
+    ffn_grad = jnp.moveaxis(in_order(mine, other, 1), 0, 1).astype(jnp.float32)
 
     second_out = mix_output(first_out, coef_two, ffn_branch)
     streams_out = low(second_out)[None]
@@ -245,10 +867,14 @@
     )
 
     grad_attn = low(sum((coef_one[j, :, 0:1] * grad_first[j] for j in range(number))))
-    grad_attended = low(mm(grad_attn, w_out, CONTRACT_LAST))
+    grad_attended = low(
+        mm(lax.dynamic_slice_in_dim(grad_attn, core * half, half, 1), w_out_mine, CONTRACT_LAST)
+        + mm(lax.dynamic_slice_in_dim(grad_attn, (1 - core) * half, half, 1), w_out_other, CONTRACT_LAST)
+    )
     grad_heads = lax.all_to_all(grad_attended, "ctx", 1, 0, tiled=True)
-    grad_attn_rows = gather(grad_attn, "fsdp")
-    out_grad = weight_part(attended_cols, grad_attn_rows)
+    grad_attn_rows = square_rows(n_ctx, n_fsdp, grad_attn).reshape(n_fsdp * length, n_ctx, own)
+    out_part = low(jnp.einsum("tn,tke->kne", attended_cols, grad_attn_rows, preferred_element_type=jnp.float32))
+    out_grad = line_sum(n_ctx, out_part, 4)
     parts = []
     for h in range(heads):
         parts.append(
@@ -267,21 +893,29 @@
             axis=1,
         ).reshape(rows, 3 * own)
     )
-    grad_attn_normed = scatter(low(mm(qkv_grad, w_qkv, CONTRACT_LAST)), "ctx").astype(jnp.float32)
-    inner_grad = scatter(low(mm(attn_all, qkv_grad, CONTRACT_FIRST)), "fsdp").reshape(own_rows, 3, own)
+    attn_part = low(mm(qkv_grad, w_qkv, CONTRACT_LAST)).reshape(n_ctx, length, features)
+    grad_attn_normed = line_sum(n_ctx, attn_part, 5)
+    inner_part = low(mm(attn_all, qkv_grad, CONTRACT_FIRST)).reshape(n_fsdp, own_rows, 3 * own)
+    inner_grad = square_sum(n_ctx, n_fsdp, inner_part, False, 6).reshape(own_rows, 3, own)
     attn_grad = jnp.concatenate([inner_grad, out_grad[:, None]], axis=1).astype(jnp.float32)
 
     grad_mixed_one = normalize_back(attn_normed, attn_inverse, grad_attn_normed)
     grad_inputs, dynamic_grad_one, static_grad_one = connect_back(
         inputs, normed_one, inverse_one, dynamic_one, coef_one, hc_dynamic[0], attn_branch, grad_first, grad_mixed_one
     )
-    dynamic_total, static_total = lax.psum(
-        (
-            jnp.stack([dynamic_grad_one, dynamic_grad_two]),
-            jnp.stack([static_grad_one, static_grad_two]),
-        ),
-        both,
-    )
+    small = jnp.concatenate(
+        [
+            dynamic_grad_one,
+            dynamic_grad_two,
+            jnp.pad(
+                jnp.concatenate([static_grad_one.reshape(1, -1), static_grad_two.reshape(1, -1)]),
+                ((0, 2), (0, features - 6 * number)),
+            ),
+        ]
+    )
+    small = sum_everywhere(n_ctx, n_fsdp, small)
+    dynamic_total = small[:12].reshape(2, 6, features)
+    static_total = small[12:14, : 6 * number].reshape(2, number, 6)
     return (streams_out, grad_inputs[None], attn_grad, ffn_grad, dynamic_total, static_total)
 
 

time: 1050 us -> 659 us (0.63)
  waiting for transfers between devices: 669 us -> 21.6 us
  Pallas kernels: 0 us -> 383 us
  matrix products: 164 us -> 74.4 us
  blocking collectives: 50.9 us -> 0 us
    pallas_call x0 -> x10, Pallas kernels: none -> 383 us  [the longest x2 106 us: line_sum(): pl.pallas_call(kernel, out_shape=jax.ShapeDtypeStruct((rows, columns), jn...]
    reduce_scatter x8 -> x1, waiting for transfers between devices: 374 us -> 0.01 us  [local(): lax.psum_scatter(weight_parts, 'ctx', scatter_dimension=0, axis_index_gro...]
    all_gather x6 -> x1, waiting for transfers between devices: 195 us -> 0.01 us  [gather(): return lax.all_gather(values, axis, axis=dim, tiled=True)]
    psum x1 -> x0, waiting for transfers between devices: 73.7 us -> none  [local(): lax.psum((jnp.stack([dynamic_grad_one, dynamic_grad_two]), jnp.stack([sta...]
    psum x1 -> x0, blocking collectives: 38 us -> none  [local(): lax.psum((jnp.stack([dynamic_grad_one, dynamic_grad_two]), jnp.stack([sta...]
    dot_general x4 -> x1, matrix products: 34.3 us -> 2.65 us  [local(): jnp.einsum('tn,tke->kne', attended_cols, grad_attn_rows, preferred_elemen...]
    dot_general x9 -> x7, matrix products: 44.6 us -> 15.8 us  [mm(): return jnp.dot(a, b, preferred_element_type=jnp.float32)]
    dot_general x14 -> x12, matrix products: 58 us -> 29.3 us  [mm(): return lax.dot_general(a, b, dims, preferred_element_type=jnp.float32)]
  transfers between devices with their start and end apart: 17 -> 7, of which waited for: 15 -> 2; matrix products, arithmetic and copies ran while one was open for 17% -> 24% of each run, Pallas kernels for 0% -> 46%
where the time goes in v2:
time: 659 us; the launch traced here: 649 us
  Pallas kernels  383 us (58%)
  matrix products  74.4 us (11%)
  local copies, waits for them, and re-layouts  71.9 us (11%)
  other arithmetic  68.8 us (10%)
  waiting for transfers between devices  21.6 us (3%)
  between operations  17.1 us (3%)
  starting transfers between devices  11.9 us (2%)
    pallas_call x2, Pallas kernels, line_sum(): pl.pallas_call(kernel, out_shape=jax.ShapeDtypeStruct((rows, columns), jn...  106 us
    pallas_call x2, Pallas kernels, square_sum(): pl.pallas_call(kernel, out_shape=jax.ShapeDtypeStruct((rows, columns), jn...  72.6 us
    pallas_call x1, Pallas kernels, attention_gather(): pl.pallas_call(kernel, out_shape=(jax.ShapeDtypeStruct((n_ctx,) + rows.sh...  51.8 us
    pallas_call x1, Pallas kernels, ffn_forward(): pl.pallas_call(kernel, grid_spec=pltpu.PrefetchScalarGridSpec(num_scalar_...  46.2 us
    pallas_call x1, Pallas kernels, square_core_gather(): pl.pallas_call(kernel, out_shape=jax.ShapeDtypeStruct((2, n_fsdp) + rows....  39.8 us
    unnamed x346, local copies, waits for them, and re-layouts  30 us
    dot_general x12, matrix products, mm(): return lax.dot_general(a, b, dims, preferred_element_type=jnp.float32)  29.3 us
    pallas_call x1, Pallas kernels, sum_everywhere(): pl.pallas_call(kernel, out_shape=jax.ShapeDtypeStruct(values.shape, value...  27.3 us
  transfers between devices with their start and end apart: 7, of which 2 were waited for; matrix products, arithmetic and copies ran while one was open for 24% of the time, Pallas kernels for 46%

profile of v2, /device:TPU:0, one launch (start us, length us, event | category | flops | bytes accessed | tf_op | source)
XLA Modules:
  0.0 649.1 jit_solution(3175823630307792772)
XLA Ops:
  7.2 13.7 %copy.26 = bf16[512,4,2048]{0,2,1:T(8,128)(2,1)} copy(bf16[512,4,2048]{2,1,0:T(4,128)(2,1)} %param.8) | data formatting | bytes 16777216 | tf_op args[1]
  20.9 3.2 slice.580
  26.8 2.7 convert_element_type.102
  31.3 3.1 slice.566
  38.2 4.7 broadcast_add_fusion.1
  45.4 51.8 %attention_gather.1 = (bf16[8,128,2048]{2,1,0:T(8,128)(2,1)}, bf16[4,512,768]{2,1,0:T(8,128)(2,1)}) custom-call(bf16[128,2048]{1,0:T(8,128)(2,1)} %fusion.161.rows_ref, bf16[512,768]{1,0:T(8,128)(2,1)} %copy.27.weights_ref), custom_call_target="tpu_custom_call" | custom-call | tf_op jit(solution)/shard_map/attention_gather/pallas_call | solution.py:343
  97.2 3.2 copy.28
  101.6 5.4 fusion.223
  108.8 2.9 fusion.221
  111.7 6.6 %copy.29 = bf16[1,2048,1024]{2,1,0:T(8,128)(2,1)} copy(bf16[1,2048,1024]{1,2,0:T(8,128)(2,1)} %all-gather.3.cloned.1.call-done) | data formatting | bytes 8388608 | tf_op jit(solution)/shard_map/all_gather | solution.py:110
  119.9 3.3 fusion.14
  129.4 3.5 all-to-all-start
  135.4 12.7 %all-to-all-done = bf16[8,128,256]{1,2,0:T(8,128)(2,1)S(1)} async-done(((bf16[8,128,256]{1,2,0:T(8,128)(2,1)}), bf16[8,128,256]{1,2,0:T(8,128)(2,1)S(1)}, u32[]{:S(2)}, u32[]{:S(2)}) %all-to-all-start) | async-done | bytes 524320 | tf_op jit(solution)/shard_map/all_to_all | solution.py:805
  148.2 3.9 fusion.3
  152.1 3.1 fusion.224
  158.3 4.6 broadcast_add_fusion
  164.3 3.0 fusion.212
  171.4 39.8 %square_core_gather.1 = bf16[2,4,256,2048]{3,2,1,0:T(8,128)(2,1)} custom-call(bf16[256,2048]{1,0:T(8,128)(2,1)} %bitcast.896), custom_call_target="tpu_custom_call" | custom-call | tf_op jit(solution)/shard_map/square_core_gather/pallas_call | solution.py:407
  211.2 46.2 %ffn_forward.1 = (bf16[1024,1024]{1,0:T(8,128)(2,1)}, bf16[1024,1024]{1,0:T(8,128)(2,1)}, bf16[1024,1024]{1,0:T(8,128)(2,1)}, bf16[4,3,1024,512]{3,2,1,0:T(8,128)(2,1)}) custom-call(s32[1]{0:T(128)} %bitcast.74.core_ref, bf16[8,2,128,2048]{3,2,1,0:T(8,128)(2,1)} %bitcast.892, bf16[3,2048,2048]{2,1,0:T(8,128)(2,1)} %bitcast.872, ...), custom_call_target="tpu_custom_call" | custom-call | flops 25769803776 | bytes 41943040 | tf_op jit(solution)/shard_map/ffn_forward/pallas_call | solution.py:696
  257.4 4.1 all-to-all-start.2
  261.6 8.9 %all-to-all-done.2 = bf16[128,4,512]{0,2,1:T(8,128)(2,1)} async-done(((bf16[128,4,512]{0,2,1:T(8,128)(2,1)}), bf16[128,4,512]{0,2,1:T(8,128)(2,1)}, u32[]{:S(2)}, u32[]{:S(2)}) %all-to-all-start.2) | async-done | bytes 524320 | tf_op jit(solution)/shard_map/all_to_all | solution.py:807
  272.5 19.4 %ffn_back.1 = bf16[8,2,128,2048]{3,2,1,0:T(8,128)(2,1)} custom-call(s32[1]{0:T(128)} %bitcast.74.core_ref, bf16[1024,1024]{1,0:T(8,128)(2,1)} %get-tuple-element.14.hidden_ref, bf16[1024,1024]{1,0:T(8,128)(2,1)} %get-tuple-element.15.grad_gate_ref, bf16[1024,1024]{1,0:T(8,128)(2,1)} %get-tuple-element.16.grad_up_ref, bf16[3,2048,2048]{2,1,0:T(8,128)(2,1)} %bitcast.875, ...), custom_call_target="tpu_custom_call" | custom-call | flops 12884901888 | bytes 31457280 | tf_op jit(solution)/shard_map/ffn_back/pallas_call | solution.py:738
  291.9 41.6 %square_sum.2 = f32[256,2048]{1,0:T(8,128)} custom-call(bf16[2,4,256,2048]{3,2,1,0:T(8,128)(2,1)} %bitcast.878), custom_call_target="tpu_custom_call" | custom-call | tf_op jit(solution)/shard_map/square_sum/pallas_call | solution.py:528
  333.6 3.8 fusion.74
  337.5 3.0 fusion.75
  343.3 6.5 %fusion.210 = (f32[4,128]{1,0:T(4,128)S(1)}, f32[4,128]{1,0:T(4,128)S(1)}, f32[4,128,2048]{2,1,0:T(8,128)S(1)}) fusion(f32[4,128]{1,0:T(4,128)S(1)} %copy-done.111, f32[4,128]{1,0:T(4,128)S(1)} %broadcast_multiply_fusion.4, f32[1,128,2048]{2,1,0:T(8,128)} %copy-done.21, f32[1,128,2048]{2,1,0:T(8,128)} %copy-done.18, f32[1,128,2048]{2,1,0:T(8,128)S(1)} %fusion.148, ...), kind=kOutput, calls=%fused_computation.472 | convolution fusion | flops 83903488 | bytes 8470528 | tf_op jit(solution)/shard_map/stk,kd->std/dot_general | solution.py:860
  355.1 2.6 fusion.144
  357.8 20.1 %square_rows.1 = bf16[4,128,2048]{2,1,0:T(8,128)(2,1)} custom-call(bf16[128,2048]{1,0:T(8,128)(2,1)} %get-tuple-element.125.rows_ref), custom_call_target="tpu_custom_call" | custom-call | tf_op jit(solution)/shard_map/square_rows/pallas_call | solution.py:371
  379.5 3.7 fusion.19
  384.1 4.1 all-to-all-start.1
  394.9 2.7 convert_bitcast_fusion.1.partial_ref
  398.3 61.6 %line_sum.3 = f32[512,256]{1,0:T(8,128)} custom-call(bf16[8,512,256]{2,1,0:T(8,128)(2,1)} %convert_bitcast_fusion.1.partial_ref), custom_call_target="tpu_custom_call" | custom-call | tf_op jit(solution)/shard_map/line_sum/pallas_call | solution.py:611
  462.1 2.7 multiply_reduce_fusion.9
  468.9 3.2 fusion.55
  485.6 5.2 convolution_convert_fusion
  490.9 44.7 %line_sum.2 = f32[128,2048]{1,0:T(8,128)} custom-call(bf16[8,128,2048]{2,1,0:T(8,128)(2,1)} %bitcast.895), custom_call_target="tpu_custom_call" | custom-call | tf_op jit(solution)/shard_map/line_sum/pallas_call | solution.py:611
  535.6 4.9 convolution_convert_fusion.1
  540.5 31.0 %square_sum.3 = f32[512,768]{1,0:T(8,128)} custom-call(bf16[4,512,768]{2,1,0:T(8,128)(2,1)} %bitcast.901), custom_call_target="tpu_custom_call" | custom-call | tf_op jit(solution)/shard_map/square_sum/pallas_call | solution.py:528
  571.5 3.0 copy.36
  575.0 5.4 fusion.143
  580.8 5.9 fusion.209
  586.7 2.5 fusion.20
  592.1 3.9 dynamic-slice_bitcast_fusion.1
  597.5 3.1 copy.41
  600.7 27.3 %sum_everywhere.1 = f32[16,2048]{1,0:T(8,128)} custom-call(f32[16,2048]{1,0:T(8,128)} %pad_maximum_fusion.10.values_ref), custom_call_target="tpu_custom_call" | custom-call | tf_op jit(solution)/shard_map/sum_everywhere/pallas_call | solution.py:650
  631.0 3.4 add_bitcast_fusion.3
  634.5 2.8 fusion
  637.3 4.5 convert_bitcast_fusion
  (458 shorter events, 78.9 us)
Async XLA Ops:
  7.2 104.5 %all-gather.3.cloned.1.call-start = ((), (), s32[]{:S(2)}) async-start(), calls=%async_computation.5 | async-start | bytes 5242880 | tf_op jit(solution)/shard_map/all_gather | solution.py:110
  42.9 121.3 %copy-start.80 = (f32[128]{0:T(128)}, f32[128]{0:T(128)S(1)}, u32[]{:S(2)}) copy-start(f32[128]{0:T(128)S(1)} %get-tuple-element.191) | copy-start | bytes 1540
  42.9 54.3 %copy-start.117 = (f32[128]{0:T(128)}, f32[128]{0:T(128)S(1)}, u32[]{:S(2)}) copy-start(f32[128]{0:T(128)S(1)} %get-tuple-element.185) | copy-start | bytes 1540
  42.9 54.3 %copy-start.119 = (f32[128]{0:T(128)}, f32[128]{0:T(128)S(1)}, u32[]{:S(2)}) copy-start(f32[128]{0:T(128)S(1)} %get-tuple-element.186) | copy-start | bytes 1540
  42.9 54.3 %copy-start.121 = (f32[128]{0:T(128)}, f32[128]{0:T(128)S(1)}, u32[]{:S(2)}) copy-start(f32[128]{0:T(128)S(1)} %get-tuple-element.187) | copy-start | bytes 1540
  42.9 112.3 %copy-start.99 = (f32[128]{0:T(128)}, f32[128]{0:T(128)S(1)}, u32[]{:S(2)}) copy-start(f32[128]{0:T(128)S(1)} %get-tuple-element.180) | copy-start | bytes 1540
  43.0 112.9 %copy-start.96 = (f32[128]{0:T(128)}, f32[128]{0:T(128)S(1)}, u32[]{:S(2)}) copy-start(f32[128]{0:T(128)S(1)} %get-tuple-element.175) | copy-start | bytes 1540
  43.0 121.3 %copy-start.82 = (f32[128]{0:T(128)}, f32[128]{0:T(128)S(1)}, u32[]{:S(2)}) copy-start(f32[128]{0:T(128)S(1)} %get-tuple-element.169) | copy-start | bytes 1540
  43.0 121.3 %copy-start.84 = (f32[128]{0:T(128)}, f32[128]{0:T(128)S(1)}, u32[]{:S(2)}) copy-start(f32[128]{0:T(128)S(1)} %get-tuple-element.171) | copy-start | bytes 1540
  43.0 121.3 %copy-start.86 = (f32[128]{0:T(128)}, f32[128]{0:T(128)S(1)}, u32[]{:S(2)}) copy-start(f32[128]{0:T(128)S(1)} %get-tuple-element.174) | copy-start | bytes 1540
  43.0 121.3 %copy-start.88 = (f32[128]{0:T(128)}, f32[128]{0:T(128)S(1)}, u32[]{:S(2)}) copy-start(f32[128]{0:T(128)S(1)} %get-tuple-element.176) | copy-start | bytes 1540
  43.0 121.3 %copy-start.90 = (f32[128]{0:T(128)}, f32[128]{0:T(128)S(1)}, u32[]{:S(2)}) copy-start(f32[128]{0:T(128)S(1)} %get-tuple-element.179) | copy-start | bytes 1540
  43.0 121.3 %copy-start.92 = (f32[128]{0:T(128)}, f32[128]{0:T(128)S(1)}, u32[]{:S(2)}) copy-start(f32[128]{0:T(128)S(1)} %get-tuple-element.181) | copy-start | bytes 1540
  43.0 121.3 %copy-start.94 = (f32[128]{0:T(128)}, f32[128]{0:T(128)S(1)}, u32[]{:S(2)}) copy-start(f32[128]{0:T(128)S(1)} %get-tuple-element.184) | copy-start | bytes 1540
  44.5 56.0 %copy-start.113 = (f32[128]{0:T(128)}, f32[128]{0:T(128)S(1)}, u32[]{:S(2)}) copy-start(f32[128]{0:T(128)S(1)} %add_rsqrt_fusion.3) | copy-start | bytes 1540
  45.4 55.0 %copy-start.169 = (s32[8]{0:T(128)S(1)}, s32[8]{0:T(128)}, u32[]{:S(2)}) copy-start(s32[8]{0:T(128)} %param.13) | copy-start | bytes 100
  108.8 15.9 %copy-start.54 = (bf16[1024,2,64]{0,2,1:T(8,128)(2,1)}, bf16[1024,2,64]{0,2,1:T(8,128)(2,1)S(1)}, u32[]{:S(2)}) copy-start(bf16[1024,2,64]{0,2,1:T(8,128)(2,1)S(1)} %get-tuple-element.136) | copy-start | bytes 786436
  108.8 16.0 %copy-start.56 = (bf16[1024,2,64]{0,2,1:T(8,128)(2,1)}, bf16[1024,2,64]{0,2,1:T(8,128)(2,1)S(1)}, u32[]{:S(2)}) copy-start(bf16[1024,2,64]{0,2,1:T(8,128)(2,1)S(1)} %get-tuple-element.141) | copy-start | bytes 786436
  108.8 16.0 %copy-start.58 = (bf16[1024,2,64]{0,2,1:T(8,128)(2,1)}, bf16[1024,2,64]{0,2,1:T(8,128)(2,1)S(1)}, u32[]{:S(2)}) copy-start(bf16[1024,2,64]{0,2,1:T(8,128)(2,1)S(1)} %get-tuple-element.142) | copy-start | bytes 786436
  118.3 33.8 %collective-permute-start = (bf16[2048,1024]{1,0:T(8,128)(2,1)}, bf16[2048,1024]{1,0:T(8,128)(2,1)}, u32[]{:S(2)}, u32[]{:S(2)}) collective-permute-start(bf16[2048,1024]{1,0:T(8,128)(2,1)} %bitcast.897), channel_id=1, source_target_pairs={{0,4},{4,0},{8,12},{12,8},{16,20},{20,16},{24,28},{28,24},{1,5},{5... | collective-permute-start | bytes 12582920 | tf_op jit(solution)/shard_map/ppermute | solution.py:781
  129.4 18.8 %all-to-all-start = ((bf16[8,128,256]{1,2,0:T(8,128)(2,1)}), bf16[8,128,256]{1,2,0:T(8,128)(2,1)S(1)}, u32[]{:S(2)}, u32[]{:S(2)}) async-start(bf16[8,128,256]{1,2,0:T(8,128)(2,1)} %pad_maximum_fusion.7), calls=%async_computation | async-start | bytes 1048576 | tf_op jit(solution)/shard_map/all_to_all | solution.py:805
  132.9 459.2 %reduce-scatter.2.cloned.1.call-start = ((), (), s32[]{:S(2)}) async-start(), calls=%async_computation.4 | async-start | bytes 15728640 | tf_op jit(solution)/shard_map/reduce_scatter | solution.py:824
  152.1 12.2 %copy-start.27 = (f32[128,1024]{1,0:T(8,128)}, f32[128,1024]{1,0:T(8,128)S(1)}, u32[]{:S(2)}) copy-start(f32[128,1024]{1,0:T(8,128)S(1)} %fusion.3) | copy-start | bytes 1572868
  257.4 13.0 %all-to-all-start.2 = ((bf16[128,4,512]{0,2,1:T(8,128)(2,1)}), bf16[128,4,512]{0,2,1:T(8,128)(2,1)}, u32[]{:S(2)}, u32[]{:S(2)}) async-start(bf16[128,4,512]{0,2,1:T(8,128)(2,1)} %bitcast.891), calls=%async_computation.2 | async-start | bytes 1048576 | tf_op jit(solution)/shard_map/all_to_all | solution.py:807
  291.9 41.6 %copy-start.4 = (f32[1,4,128,2048]{3,2,1,0:T(8,128)S(1)}, f32[1,4,128,2048]{3,2,1,0:T(8,128)}, u32[]{:S(2)}) copy-start(f32[1,4,128,2048]{3,2,1,0:T(8,128)} %convert_element_type.110) | copy-start | bytes 12582916
  355.1 22.7 %copy-start.14 = (bf16[1,2048,1024]{1,2,0:T(8,128)(2,1)S(1)}, bf16[1,2048,1024]{1,2,0:T(8,128)(2,1)}, u32[]{:S(2)}) copy-start(bf16[1,2048,1024]{1,2,0:T(8,128)(2,1)} %all-gather.3.cloned.1.call-done) | copy-start | bytes 12582916
  357.7 21.7 %copy-start.46 = (bf16[128,2048]{1,0:T(8,128)(2,1)S(1)}, bf16[128,2048]{1,0:T(8,128)(2,1)}, u32[]{:S(2)}) copy-start(bf16[128,2048]{1,0:T(8,128)(2,1)} %get-tuple-element.125.rows_ref) | copy-start | bytes 1572868
  384.1 84.7 %all-to-all-start.1 = ((bf16[128,8,256]{2,0,1:T(8,128)(2,1)}), bf16[128,8,256]{2,0,1:T(8,128)(2,1)}, u32[]{:S(2)}, u32[]{:S(2)}) async-start(bf16[128,8,256]{2,0,1:T(8,128)(2,1)} %bitcast.908), calls=%async_computation.1 | async-start | bytes 1048576 | tf_op jit(solution)/shard_map/all_to_all | solution.py:874
  394.9 67.1 %copy-start.28 = (f32[128,1024]{1,0:T(8,128)S(1)}, f32[128,1024]{1,0:T(8,128)}, u32[]{:S(2)}) copy-start(f32[128,1024]{1,0:T(8,128)} %copy-done.27) | copy-start | bytes 1572868
  394.9 67.1 %copy-start.30 = (f32[128,1024]{1,0:T(8,128)S(1)}, f32[128,1024]{1,0:T(8,128)}, u32[]{:S(2)}) copy-start(f32[128,1024]{1,0:T(8,128)} %copy-done.29) | copy-start | bytes 1572868
  398.3 66.5 %copy-start.64 = (bf16[1,1,128,2048]{3,2,1,0:T(8,128)(2,1)S(1)}, bf16[1,1,128,2048]{3,2,1,0:T(8,128)(2,1)}, u32[]{:S(2)}) copy-start(bf16[1,1,128,2048]{3,2,1,0:T(8,128)(2,1)} %get-tuple-element.114) | copy-start | bytes 1572868
  398.3 66.5 %copy-start.65 = (bf16[1,1,128,2048]{3,2,1,0:T(8,128)(2,1)S(1)}, bf16[1,1,128,2048]{3,2,1,0:T(8,128)(2,1)}, u32[]{:S(2)}) copy-start(bf16[1,1,128,2048]{3,2,1,0:T(8,128)(2,1)} %get-tuple-element.115) | copy-start | bytes 1572868
  490.8 44.7 %copy-start.168 = (bf16[8,128,2048]{2,1,0:T(8,128)(2,1)S(1)}, bf16[8,128,2048]{2,1,0:T(8,128)(2,1)}, u32[]{:S(2)}) copy-start(bf16[8,128,2048]{2,1,0:T(8,128)(2,1)} %get-tuple-element.12) | copy-start | bytes 12582916
  540.5 34.0 %copy-start.17 = (f32[128,2048]{1,0:T(8,128)S(1)}, f32[128,2048]{1,0:T(8,128)}, u32[]{:S(2)}) copy-start(f32[128,2048]{1,0:T(8,128)} %copy-done.16) | copy-start | bytes 3145732
  540.5 34.0 %copy-start.42 = (f32[128,2048]{1,0:T(8,128)S(1)}, f32[128,2048]{1,0:T(8,128)}, u32[]{:S(2)}) copy-start(f32[128,2048]{1,0:T(8,128)} %line_sum.2) | copy-start | bytes 3145732
  540.5 34.0 %copy-start.79 = (f32[128]{0:T(128)S(1)}, f32[128]{0:T(128)}, u32[]{:S(2)}) copy-start(f32[128]{0:T(128)} %copy-done.78) | copy-start | bytes 1540
  540.5 34.0 %copy-start.114 = (f32[128]{0:T(128)S(1)}, f32[128]{0:T(128)}, u32[]{:S(2)}) copy-start(f32[128]{0:T(128)} %copy-done.113) | copy-start | bytes 1540
  595.9 41.4 %collective-permute-start.1 = (bf16[3,1024,256]{2,1,0:T(8,128)(2,1)}, bf16[3,1024,256]{2,1,0:T(8,128)(2,1)}, u32[]{:S(2)}, u32[]{:S(2)}) collective-permute-start(bf16[3,1024,256]{2,1,0:T(8,128)(2,1)} %get-tuple-element.127), channel_id=1, source_target_pairs={{0,4},{4,0},{8,12},{12,8},{16,20},{20,16},{24,28},{28,24},{1,5},{5... | collective-permute-start | bytes 4718600 | tf_op jit(solution)/shard_map/ppermute | solution.py:831
  596.0 35.0 %copy-start.81 = (f32[128]{0:T(128)S(1)}, f32[128]{0:T(128)}, u32[]{:S(2)}) copy-start(f32[128]{0:T(128)} %copy-done.80) | copy-start | bytes 1540
  596.0 35.0 %copy-start.83 = (f32[128]{0:T(128)S(1)}, f32[128]{0:T(128)}, u32[]{:S(2)}) copy-start(f32[128]{0:T(128)} %copy-done.82) | copy-start | bytes 1540
  596.0 35.0 %copy-start.85 = (f32[128]{0:T(128)S(1)}, f32[128]{0:T(128)}, u32[]{:S(2)}) copy-start(f32[128]{0:T(128)} %copy-done.84) | copy-start | bytes 1540
  596.0 35.0 %copy-start.87 = (f32[128]{0:T(128)S(1)}, f32[128]{0:T(128)}, u32[]{:S(2)}) copy-start(f32[128]{0:T(128)} %copy-done.86) | copy-start | bytes 1540
  596.0 35.0 %copy-start.89 = (f32[128]{0:T(128)S(1)}, f32[128]{0:T(128)}, u32[]{:S(2)}) copy-start(f32[128]{0:T(128)} %copy-done.88) | copy-start | bytes 1540
  596.0 35.0 %copy-start.91 = (f32[128]{0:T(128)S(1)}, f32[128]{0:T(128)}, u32[]{:S(2)}) copy-start(f32[128]{0:T(128)} %copy-done.90) | copy-start | bytes 1540
  596.0 35.0 %copy-start.93 = (f32[128]{0:T(128)S(1)}, f32[128]{0:T(128)}, u32[]{:S(2)}) copy-start(f32[128]{0:T(128)} %copy-done.92) | copy-start | bytes 1540
  596.0 35.0 %copy-start.95 = (f32[128]{0:T(128)S(1)}, f32[128]{0:T(128)}, u32[]{:S(2)}) copy-start(f32[128]{0:T(128)} %copy-done.94) | copy-start | bytes 1540
  596.0 35.0 %copy-start.116 = (f32[128]{0:T(128)S(1)}, f32[128]{0:T(128)}, u32[]{:S(2)}) copy-start(f32[128]{0:T(128)} %copy-done.115) | copy-start | bytes 1540
  596.0 35.0 %copy-start.118 = (f32[128]{0:T(128)S(1)}, f32[128]{0:T(128)}, u32[]{:S(2)}) copy-start(f32[128]{0:T(128)} %copy-done.117) | copy-start | bytes 1540
  (130 other events, 582.8 us)
Sparse Core Ops, SparseCore 0:
  26.5 74.1 all-gather.2
  257.5 233.8 reduce-scatter.1

commit v3 on v2

v3 whole, which is shorter than its diff:
```python
import functools

import jax
import jax.numpy as jnp
from jax import lax
from jax.experimental import pallas as pl
from jax.experimental.pallas import tpu as pltpu
from jax.sharding import PartitionSpec as P

HEADS = 16
HEAD_DIM = 128


EPS = 1e-05
THETA = 10000.0
HIGH = lax.Precision.HIGHEST
MASKED = -1e30
CONTRACT_LAST = (((1,), (1,)), ((), ()))
CONTRACT_FIRST = (((0,), (0,)), ((), ()))


def normalize(values):
    centered = values - jnp.mean(values, axis=-1, keepdims=True)
    inverse = lax.rsqrt(jnp.mean(centered * centered, axis=-1, keepdims=True) + EPS)
    return (centered * inverse, inverse)


def normalize_back(normed, inverse, gradient):
    inner = jnp.mean(gradient * normed, axis=-1, keepdims=True)
    return inverse * (gradient - jnp.mean(gradient, axis=-1, keepdims=True) - normed * inner)


def block_positions(pair_order, length):
    half_size = length // 2
    offsets = jnp.arange(half_size, dtype=jnp.int32)
    mirror = 2 * pair_order.shape[0] - 1 - pair_order
    first_half = pair_order[:, None] * half_size + offsets[None, :]
    second_half = mirror[:, None] * half_size + offsets[None, :]
    return jnp.concatenate([first_half, second_half], axis=1).reshape(-1)


def low(values):
    return values.astype(jnp.bfloat16)


def mm(a, b, dims=None):
    if dims is None:
        return jnp.dot(a, b, preferred_element_type=jnp.float32)
    return lax.dot_general(a, b, dims, preferred_element_type=jnp.float32)


def gather(values, axis, dim=0):
    return lax.all_gather(values, axis, axis=dim, tiled=True)


def scatter(values, axis, dim=0):
    return lax.psum_scatter(values, axis, scatter_dimension=dim, tiled=True)


MESH = pl.DeviceIdType.MESH
VMEM_LIMIT = 60 * 1024 * 1024


def place(n_ctx):
    ctx = lax.axis_index("ctx")
    return (ctx // 2, ctx % 2, lax.axis_index("fsdp"), n_ctx // 2)


def greet(peers):
    barrier = pltpu.get_barrier_semaphore()
    for peer in peers:
        pl.semaphore_signal(barrier, inc=1, device_id=peer, device_id_type=MESH)
    pl.semaphore_wait(barrier, len(peers))


def send(source, target, sems, index, peer):
    return pltpu.make_async_remote_copy(
        src_ref=source,
        dst_ref=target,
        send_sem=sems[0].at[index],
        recv_sem=sems[1].at[index],
        device_id=peer,
        device_id_type=MESH,
    )


def fsdp_neighbours(fsdp):
    first = fsdp + 1 - 2 * (fsdp % 2)
    second = (fsdp + 2) % 4
    return (first, second, (first + 2) % 4)


def fsdp_peers(n_fsdp, ctx, fsdp):
    if n_fsdp == 4:
        first, second, _ = fsdp_neighbours(fsdp)
        return [(ctx, first), (ctx, second)]
    return [(ctx, (fsdp + j) % n_fsdp) for j in range(1, n_fsdp)]


def line_peers(chip, core, fsdp, length):
    return [
        (chip * 2 + 1 - core, fsdp),
        ((chip + 1) % length * 2 + core, fsdp),
        ((chip + length - 1) % length * 2 + core, fsdp),
    ]


def line_gather(own_ref, all_ref, sems, where):
    chip, core, fsdp, length = where
    right_sems, left_sems, core_sems = sems
    sibling = (chip * 2 + 1 - core, fsdp)
    right = ((chip + 1) % length * 2 + core, fsdp)
    left = ((chip + length - 1) % length * 2 + core, fsdp)

    def block(index):
        return all_ref.at[(index + length) % length * 2 + core]

    def pass_on(index, source):
        return send(source, block(index), core_sems, (index + length) % length, sibling)

    pass_on(chip, own_ref).start()
    for step in range(length - 1):
        for sign, peer, way in ((-1, right, right_sems), (1, left, left_sems)):
            at = chip + sign * step
            held = (at >= 0) & (at < length)
            if step > 0:

                @pl.when(held)
                def _():
                    send(block(at), block(at), way, step - 1, peer).wait_recv()
                    pass_on(at, block(at)).start()

            more = (chip < length - 1) if sign < 0 else (chip > 0)

            @pl.when(held & more)
            def _():
                send(own_ref if step == 0 else block(at), block(at), way, step, peer).start()

        yield
    last = length - 1
    for sign, peer, way in ((-1, right, right_sems), (1, left, left_sems)):
        at = chip + sign * last

        @pl.when((at >= 0) & (at < length))
        def _():
            send(block(at), block(at), way, last - 1, peer).wait_recv()
            pass_on(at, block(at)).start()

    yield
    for step in range(length - 1):
        for sign, peer, way in ((-1, right, right_sems), (1, left, left_sems)):
            at = chip + sign * step
            more = (chip < length - 1) if sign < 0 else (chip > 0)

            @pl.when((at >= 0) & (at < length) & more)
            def _():
                send(block(at), block(at), way, step, peer).wait_send()

    for index in range(length):
        pass_on(index, block(index)).wait_send()
        other = all_ref.at[index * 2 + 1 - core]
        send(other, other, core_sems, index, sibling).wait_recv()


def square_gather(own_ref, all_ref, sems, ctx, fsdp, n_fsdp, passed=None):
    if n_fsdp != 4:
        copies = [
            send(own_ref, all_ref.at[fsdp], sems, j - 1, (ctx, (fsdp + j) % n_fsdp)) for j in range(1, n_fsdp)
        ]
        for copy in copies:
            copy.start()
        yield
        for j, copy in enumerate(copies):
            copy.wait()
            if passed:
                passed(all_ref.at[(fsdp + n_fsdp - j - 1) % n_fsdp], (fsdp + n_fsdp - j - 1) % n_fsdp, None, j)
        return
    first, second, corner = fsdp_neighbours(fsdp)
    half = own_ref.shape[0] // 2
    top, low_half = pl.ds(0, half), pl.ds(half, half)
    to_first, to_second = (ctx, first), (ctx, second)

    def copy(index, owner, part, peer, source=None):
        source = all_ref.at[owner, part] if source is None else source
        return send(source, all_ref.at[owner, part], sems, index, peer)

    starts = [
        copy(0, fsdp, top, to_first, own_ref.at[top]),
        copy(1, fsdp, low_half, to_second, own_ref.at[low_half]),
        copy(2, fsdp, low_half, to_first, own_ref.at[low_half]),
        copy(3, fsdp, top, to_second, own_ref.at[top]),
        copy(4, first, top, to_second),
        copy(5, second, low_half, to_first),
    ]
    arrivals = [
        (0, first, top),
        (1, second, low_half),
        (2, first, low_half),
        (3, second, top),
        (4, corner, top),
        (5, corner, low_half),
    ]
    for each in starts[:4]:
        each.start()
    yield
    for index, owner, part in arrivals:
        copy(index, owner, part, to_first).wait_recv()
        if index < 2:
            starts[4 + index].start()
        if passed:
            passed(all_ref.at[owner, part], owner, part, index)
        yield
    for each in starts:
        each.wait_send()


def run_all(*parts):
    parts = list(parts)
    while parts:
        for part in list(parts):
            try:
                next(part)
            except StopIteration:
                parts.remove(part)


def dma_pair(count):
    return [pltpu.SemaphoreType.DMA((count,)), pltpu.SemaphoreType.DMA((count,))]


def any_specs(count):
    return [pl.BlockSpec(memory_space=pl.ANY)] * count


def params(collective_id=None, **more):
    if collective_id is not None:
        more.update(collective_id=collective_id, has_side_effects=True)
    return pltpu.CompilerParams(vmem_limit_bytes=VMEM_LIMIT, **more)


def passing(own_ref, all_ref, sems, core, fsdp, sibling):
    handed = [send(own_ref, all_ref.at[core, fsdp], sems, 0, sibling)]
    handed[0].start()
    arriving = [send(own_ref, all_ref.at[1 - core, fsdp], sems, 0, sibling)]

    def passed(source, owner, part, index):
        for side, copies in ((core, handed), (1 - core, arriving)):
            target = all_ref.at[side, owner] if part is None else all_ref.at[side, owner, part]
            copies.append(send(source, target, sems, index + 1, sibling))
        handed[-1].start()

    def finish():
        for out, back in zip(handed, arriving):
            out.wait_send()
            back.wait_recv()

    return (passed, finish)


def line_rows(n_ctx, rows):
    def kernel(rows_ref, all_rows, right_s, right_r, left_s, left_r, core_s, core_r, own):
        where = place(n_ctx)
        chip, core, fsdp, length = where
        greet(line_peers(*where))
        mine = pltpu.make_async_copy(rows_ref, all_rows.at[chip * 2 + core], own)
        mine.start()
        run_all(line_gather(rows_ref, all_rows, ((right_s, right_r), (left_s, left_r), (core_s, core_r)), where))
        mine.wait()

    length = n_ctx // 2
    return pl.pallas_call(
        kernel,
        out_shape=jax.ShapeDtypeStruct((n_ctx,) + rows.shape, rows.dtype),
        in_specs=any_specs(1),
        out_specs=pl.BlockSpec(memory_space=pl.ANY),
        scratch_shapes=dma_pair(length) + dma_pair(length) + dma_pair(length) + [pltpu.SemaphoreType.DMA],
        compiler_params=params(0),
        name="line_rows",
    )(rows)


def square_core_gather(n_ctx, n_fsdp, rows):
    def kernel(rows_ref, all_ref, sq_s, sq_r, core_s, core_r, own):
        chip, core, fsdp, _ = place(n_ctx)
        ctx = chip * 2 + core
        sibling = (chip * 2 + 1 - core, fsdp)
        greet([sibling] + fsdp_peers(n_fsdp, ctx, fsdp))
        mine = pltpu.make_async_copy(rows_ref, all_ref.at[core, fsdp], own)
        mine.start()
        passed, finish = passing(rows_ref, all_ref, (core_s, core_r), core, fsdp, sibling)
        run_all(square_gather(rows_ref, all_ref.at[core], (sq_s, sq_r), ctx, fsdp, n_fsdp, passed))
        finish()
        mine.wait()

    return pl.pallas_call(
        kernel,
        out_shape=jax.ShapeDtypeStruct((2, n_fsdp) + rows.shape, rows.dtype),
        in_specs=any_specs(1),
        out_specs=pl.BlockSpec(memory_space=pl.ANY),
        scratch_shapes=dma_pair(max(6, n_fsdp)) + dma_pair(max(7, n_fsdp)) + [pltpu.SemaphoreType.DMA],
        compiler_params=params(1),
        name="square_core_gather",
    )(rows)


def add_into(target, *sources, chunk=64):
    @pl.loop(0, target.shape[0] // chunk)
    def _(step):
        rows = pl.ds(pl.multiple_of(step * chunk, chunk), chunk)
        total = target[rows].astype(jnp.float32)
        for source in sources:
            total = total + source[rows].astype(jnp.float32)
        target[rows] = total.astype(target.dtype)


def square_sum_stages(n_ctx, n_fsdp, partial_ref, out_ref, held, core_in, square_in, load, core_sems, sems):
    rows = partial_ref.shape[-2]
    half = rows // 2
    chip, core, fsdp, _ = place(n_ctx)
    ctx = chip * 2 + core
    sibling = (chip * 2 + 1 - core, fsdp)
    if n_fsdp == 4:
        first, second, corner = fsdp_neighbours(fsdp)
        order = [corner, first, second, fsdp]
    else:
        order = [(fsdp + j) % n_fsdp for j in range(1, n_fsdp + 1)]
    mine = [
        pltpu.make_async_copy(partial_ref.at[core, owner], held.at[owner], load.at[j])
        for j, owner in enumerate(order)
    ]
    others = [
        send(partial_ref.at[1 - core, owner], core_in.at[owner], core_sems, j, sibling)
        for j, owner in enumerate(order)
    ]

    def ready(j):
        mine[j].wait()
        others[j].wait_recv()
        add_into(held.at[order[j]], core_in.at[order[j]])

    def total(parts, sources):
        @pl.loop(0, parts[1] // 64)
        def _(step):
            at = pl.ds(pl.multiple_of(parts[0] + step * 64, 64), 64)
            from_at = pl.ds(pl.multiple_of(step * 64, 64), 64)
            value = held[fsdp, at].astype(jnp.float32)
            for j in sources:
                value = value + square_in[j, from_at].astype(jnp.float32)
            out_ref[at] = value

    def begin():
        greet([sibling] + fsdp_peers(n_fsdp, ctx, fsdp))
        for j in range(n_fsdp):
            others[j].start()
            mine[j].start()

    if n_fsdp != 4:
        copies = [
            send(held.at[order[j]], square_in.at[j], sems, j, (ctx, order[j])) for j in range(n_fsdp - 1)
        ]

        def spread():
            for j in range(n_fsdp):
                ready(j)
                if j < n_fsdp - 1:
                    copies[j].start()

        def finish():
            for copy in copies:
                copy.wait()
            total((0, rows), range(n_fsdp - 1))
            for each in others:
                each.wait_send()

        return [begin, spread, finish]

    top, low_half = pl.ds(0, half), pl.ds(half, half)
    to_first, to_second = (ctx, first), (ctx, second)

    def copy(index, owner, part, peer):
        return send(held.at[owner, part], square_in.at[index], sems, index, peer)

    copies = [
        copy(0, corner, top, to_first),
        copy(1, corner, low_half, to_second),
        copy(2, first, top, to_first),
        copy(3, second, low_half, to_second),
        copy(4, second, top, to_second),
        copy(5, first, low_half, to_first),
    ]

    def spread():
        ready(0)
        copies[0].start()
        copies[1].start()
        ready(1)
        copies[2].start()
        ready(2)
        copies[3].start()
        ready(3)

    def pass_on():
        copies[0].wait_recv()
        add_into(held.at[second, top], square_in.at[0])
        copies[4].start()
        copies[1].wait_recv()
        add_into(held.at[first, low_half], square_in.at[1])
        copies[5].start()

    def finish():
        for j in range(2, 6):
            copies[j].wait_recv()
        total((0, half), (2, 4))
        total((half, half), (3, 5))
        for each in copies:
            each.wait_send()
        for each in others:
            each.wait_send()

    return [begin, spread, pass_on, finish]


def square_sum_scratch(n_fsdp, partial):
    rows, columns = partial.shape[-2:]
    pieces = (6, rows // 2, columns) if n_fsdp == 4 else (n_fsdp - 1, rows, columns)
    return (
        [
            pltpu.VMEM((n_fsdp, rows, columns), partial.dtype),
            pltpu.VMEM((n_fsdp, rows, columns), partial.dtype),
            pltpu.VMEM(pieces, partial.dtype),
            pltpu.SemaphoreType.DMA((n_fsdp,)),
        ]
        + dma_pair(n_fsdp)
        + dma_pair(max(6, n_fsdp))
    )


def square_sum(n_ctx, n_fsdp, partial):
    def kernel(partial_ref, out_ref, held, core_in, square_in, load, core_s, core_r, sq_s, sq_r):
        for stage in square_sum_stages(
            n_ctx, n_fsdp, partial_ref, out_ref, held, core_in, square_in, load, (core_s, core_r), (sq_s, sq_r)
        ):
            stage()

    return pl.pallas_call(
        kernel,
        out_shape=jax.ShapeDtypeStruct(partial.shape[-2:], jnp.float32),
        in_specs=any_specs(1),
        out_specs=pl.BlockSpec(memory_space=pltpu.VMEM),
        scratch_shapes=square_sum_scratch(n_fsdp, partial),
        compiler_params=params(1),
        name="square_sum",
    )(partial)


def line_sum(n_ctx, partial, collective_id):
    rows, columns = partial.shape[-2:]
    length = n_ctx // 2

    def kernel(partial_ref, out_ref, held, core_in, right_in, left_in, load, core_s, core_r, right_s, right_r, left_s, left_r):
        where = place(n_ctx)
        chip, core, fsdp, _ = where
        sibling, right, left = line_peers(*where)
        greet([sibling, right, left])
        order = [(chip + length - 1 - j) % length for j in range(length)]
        mine, others = [], []
        for j, owner in enumerate(order):
            mine.append(pltpu.make_async_copy(partial_ref.at[owner * 2 + core], held.at[owner], load.at[j]))
            others.append(
                send(partial_ref.at[owner * 2 + 1 - core], core_in.at[owner], (core_s, core_r), j, sibling)
            )
            others[-1].start()
            mine[-1].start()
        for j, owner in enumerate(order):
            mine[j].wait()
            others[j].wait_recv()
            add_into(held.at[owner], core_in.at[owner])
        ways = ((1, right, right_in, (right_s, right_r)), (-1, left, left_in, (left_s, left_r)))
        for step in range(length - 1):
            for sign, peer, arrived, sems in ways:
                block = chip + sign * (length - 1 - step)
                inside = (block >= 0) & (block < length)

                came = (chip >= 1) if sign > 0 else (chip < length - 1)
                if step > 0:

                    @pl.when(inside & came)
                    def _():
                        send(held.at[block], arrived.at[step - 1], sems, step - 1, peer).wait_recv()
                        add_into(held.at[block], arrived.at[step - 1])

                @pl.when(inside)
                def _():
                    send(held.at[block], arrived.at[step], sems, step, peer).start()

        last = length - 2
        for sign, peer, arrived, sems in ways:
            came = (chip >= 1) if sign > 0 else (chip < length - 1)

            @pl.when(came)
            def _():
                send(held.at[chip], arrived.at[last], sems, last, peer).wait_recv()
                add_into(held.at[chip], arrived.at[last])

        @pl.loop(0, rows // 64)
        def _(step):
            at = pl.ds(pl.multiple_of(step * 64, 64), 64)
            out_ref[at] = held[chip, at].astype(jnp.float32)

        for step in range(length - 1):
            for sign, peer, arrived, sems in ways:
                block = chip + sign * (length - 1 - step)

                @pl.when((block >= 0) & (block < length))
                def _():
                    send(held.at[block], arrived.at[step], sems, step, peer).wait_send()

        for each in others:
            each.wait_send()

    return pl.pallas_call(
        kernel,
        out_shape=jax.ShapeDtypeStruct((rows, columns), jnp.float32),
        in_specs=any_specs(1),
        out_specs=pl.BlockSpec(memory_space=pltpu.VMEM),
        scratch_shapes=[
            pltpu.VMEM((length, rows, columns), partial.dtype),
            pltpu.VMEM((length, rows, columns), partial.dtype),
            pltpu.VMEM((length - 1, rows, columns), partial.dtype),
            pltpu.VMEM((length - 1, rows, columns), partial.dtype),
            pltpu.SemaphoreType.DMA((length,)),
        ]
        + dma_pair(length)
        + dma_pair(length)
        + dma_pair(length),
        compiler_params=params(collective_id),
        name="line_sum",
    )(partial)


def sum_everywhere(n_ctx, n_fsdp, values):
    block = values.shape[1:]

    def kernel(values_ref, out_ref, along_ctx, along_fsdp, result, ctx_s, ctx_r, fsdp_s, fsdp_r, back_s, back_r):
        ctx = lax.axis_index("ctx")
        fsdp = lax.axis_index("fsdp")
        ctx_peers = [((ctx + j) % n_ctx, fsdp) for j in range(1, n_ctx)]
        fsdp_peers = [(ctx, (fsdp + j) % n_fsdp) for j in range(1, n_fsdp)]
        greet(ctx_peers + fsdp_peers)

        def exchange(copies):
            for copy in copies:
                copy.start()
            for copy in copies:
                copy.wait()

        def total(slots, count):
            value = slots[0]
            for j in range(1, count):
                value = value + slots[j]
            return value

        along_ctx[ctx] = values_ref[ctx]
        exchange(
            [
                send(values_ref.at[peer[0]], along_ctx.at[ctx], (ctx_s, ctx_r), j, peer)
                for j, peer in enumerate(ctx_peers)
            ]
        )
        along_fsdp[fsdp] = total(along_ctx, n_ctx)
        exchange(
            [
                send(along_fsdp.at[fsdp], along_fsdp.at[fsdp], (fsdp_s, fsdp_r), j, peer)
                for j, peer in enumerate(fsdp_peers)
            ]
        )
        result[ctx] = total(along_fsdp, n_fsdp)
        exchange(
            [send(result.at[ctx], result.at[ctx], (back_s, back_r), j, peer) for j, peer in enumerate(ctx_peers)]
        )
        out_ref[...] = result[...]

    return pl.pallas_call(
        kernel,
        out_shape=jax.ShapeDtypeStruct(values.shape, values.dtype),
        in_specs=[pl.BlockSpec(memory_space=pltpu.VMEM)],
        out_specs=pl.BlockSpec(memory_space=pltpu.VMEM),
        scratch_shapes=[
            pltpu.VMEM((n_ctx,) + block, values.dtype),
            pltpu.VMEM((n_fsdp,) + block, values.dtype),
            pltpu.VMEM((n_ctx,) + block, values.dtype),
        ]
        + dma_pair(n_ctx)
        + dma_pair(n_fsdp)
        + dma_pair(n_ctx),
        compiler_params=params(2),
        name="sum_everywhere",
    )(values)


def hidden_units(here, back, gate_ref, up_ref, down_ref):
    gate = mm(here, gate_ref[0], CONTRACT_LAST)
    up = mm(here, up_ref[0], CONTRACT_LAST)
    grad_hidden = mm(back, down_ref[0], CONTRACT_LAST)
    sigmoid = jax.nn.sigmoid(gate)
    activated = gate * sigmoid
    return (
        low(activated * up),
        low(grad_hidden * up * sigmoid * (1.0 + gate * (1.0 - sigmoid))),
        low(grad_hidden * activated),
    )


def ffn_forward(rows, planes, core, n_own, chunk=256):
    blocks, _, tokens, features = rows.shape
    total = blocks * tokens
    steps = n_own // chunk
    group = max(1, 256 // tokens)

    def kernel(core_ref, rows_ref, gate_ref, up_ref, down_ref, *outs):
        for at in range(0, blocks, group):
            here = rows_ref[at : at + group, 0].reshape(group * tokens, features)
            back = rows_ref[at : at + group, 1].reshape(group * tokens, features)
            span = pl.ds(at * tokens, group * tokens)
            for out, value in zip(outs, hidden_units(here, back, gate_ref, up_ref, down_ref)):
                out[span] = value

    def weight_spec(plane):
        return pl.BlockSpec((1, chunk, features), lambda j, core_ref: (plane, core_ref[0] * steps + j, 0))

    act = jax.ShapeDtypeStruct((total, n_own), jnp.bfloat16)
    act_spec = pl.BlockSpec((total, chunk), lambda j, core_ref: (0, j))
    return pl.pallas_call(
        kernel,
        grid_spec=pltpu.PrefetchScalarGridSpec(
            num_scalar_prefetch=1,
            grid=(steps,),
            in_specs=[
                pl.BlockSpec(rows.shape, lambda j, core_ref: (0, 0, 0, 0), pipeline_mode=pl.Buffered(1)),
                weight_spec(0),
                weight_spec(1),
                weight_spec(2),
            ],
            out_specs=[act_spec, act_spec, act_spec],
        ),
        out_shape=[act, act, act],
        compiler_params=params(),
        cost_estimate=pl.CostEstimate(
            flops=6 * total * n_own * features, bytes_accessed=30 * 1024 * 1024, transcendentals=total * n_own
        ),
        name="ffn_forward",
    )(core, rows, planes, planes, planes)


def mirror_gather(all_ref, arrivals, sems, pass_sems, ctx, core, fsdp, sibling):
    first, second, corner = fsdp_neighbours(fsdp)
    half = all_ref.shape[2] // 2
    parts = [pl.ds(0, half), pl.ds(half, half)]
    to_first, to_second = (ctx, first), (ctx, second)

    def copy(index, owner, part, peer):
        place_ref = all_ref.at[core, owner, parts[part]]
        return send(place_ref, place_ref, sems, index, peer)

    copies = [
        copy(0, fsdp, 0, to_first),
        copy(1, fsdp, 0, to_second),
        copy(2, fsdp, 1, to_first),
        copy(3, fsdp, 1, to_second),
        copy(4, first, 0, to_second),
        copy(5, second, 1, to_first),
    ]
    passes = [(fsdp, 0), (fsdp, 1), (first, 0), (second, 0), (first, 1), (second, 1), (corner, 0), (corner, 1)]

    def passing_copy(number, side):
        owner, part = passes[number]
        place_ref = all_ref.at[side, owner, parts[part]]
        return send(place_ref, place_ref, pass_sems, number, sibling)

    for part in range(2):
        arrivals[part].wait_recv()
        copies[2 * part].start()
        copies[2 * part + 1].start()
        passing_copy(part, core).start()
        yield
    for index, number, then in ((0, 2, 4), (1, 3, None), (2, 4, None), (3, 5, 5), (4, 6, None), (5, 7, None)):
        owner, part = passes[number]
        copy(index, owner, part, to_first).wait_recv()
        if then is not None:
            copies[then].start()
        passing_copy(number, core).start()
        yield
    for each in copies:
        each.wait_send()
    for number in range(8):
        passing_copy(number, core).wait_send()
        passing_copy(number, 1 - core).wait_recv()


def ffn_rows(n_ctx, own, planes, n_own, chunk=256, wide=512):
    n_fsdp = 4
    size, features = own.shape
    tokens = size // 2
    total = 2 * n_fsdp * tokens

    def kernel(
        own_ref, planes_ref, all_ref, mirror_ref, hidden_a, hidden_b, hidden_c, partial_ref,
        rows, weights, hidden, partial, load, sq_s, sq_r, core_s, core_r, far_s, far_r, mi_s, mi_r, mc_s, mc_r, out_sem,
    ):
        chip, core, fsdp, length = place(n_ctx)
        ctx = chip * 2 + core
        sibling = (chip * 2 + 1 - core, fsdp)
        mirror = ((length - 1 - chip) * 2 + core, fsdp)
        first, second, corner = fsdp_neighbours(fsdp)
        greet([sibling, mirror] + fsdp_peers(n_fsdp, ctx, fsdp))
        mine = pltpu.make_async_copy(own_ref, rows.at[core, fsdp], load.at[3])
        mine.start()
        start = pl.multiple_of(core * n_own, n_own)
        loads = [
            pltpu.make_async_copy(planes_ref.at[p, pl.ds(start, n_own)], weights.at[p], load.at[p]) for p in range(3)
        ]
        handed, arriving = [], []

        def hand(source, owner, part, index):
            for side, copies in ((core, handed), (1 - core, arriving)):
                target = rows.at[side, owner] if part is None else rows.at[side, owner, part]
                copies.append(send(source, target, (core_s, core_r), index + 1, sibling))
            handed[-1].start()

        gathering = square_gather(own_ref, rows.at[core], (sq_s, sq_r), ctx, fsdp, n_fsdp, hand)
        next(gathering)
        hand(own_ref, fsdp, None, -1)
        for each in loads:
            each.start()
        far = [
            send(
                own_ref.at[pl.ds(part * tokens, tokens)],
                mirror_ref.at[core, fsdp, pl.ds(part * tokens, tokens)],
                (far_s, far_r),
                part,
                mirror,
            )
            for part in range(2)
        ]
        for each in far:
            each.start()
        mirroring = mirror_gather(mirror_ref, far, (mi_s, mi_r), (mc_s, mc_r), ctx, core, fsdp, sibling)
        outs = []

        def group(number, owner):
            slot = number % 2
            if number >= 2:
                for each in outs[number - 2]:
                    each.wait()
            here = jnp.concatenate([rows[0, owner, :tokens], rows[1, owner, :tokens]])
            back = jnp.concatenate([rows[0, owner, tokens:], rows[1, owner, tokens:]])

            @pl.loop(0, n_own // chunk)
            def _(step):
                at = pl.ds(pl.multiple_of(step * chunk, chunk), chunk)
                parts = [weights.at[pl.ds(p, 1), at] for p in range(3)]
                for q, value in enumerate(hidden_units(here, back, *parts)):
                    hidden[slot, q, :, at] = value

            @pl.loop(0, features // wide)
            def _(step):
                at = pl.ds(pl.multiple_of(step * wide, wide), wide)
                out = low(mm(hidden[slot, 0], weights[2, :, at]))
                below = low(mm(hidden[slot, 1], weights[0, :, at]) + mm(hidden[slot, 2], weights[1, :, at]))
                for k in range(2):
                    partial[slot, k, :tokens, at] = out[k * tokens : (k + 1) * tokens]
                    partial[slot, k, tokens:, at] = below[k * tokens : (k + 1) * tokens]

            pairs = []
            for k in range(2):
                pairs.append((rows.at[k, owner], all_ref.at[k, owner]))
                pairs.append((partial.at[slot, k], partial_ref.at[k, owner]))
                at = pl.ds(pl.multiple_of((k * n_fsdp + owner) * tokens, tokens), tokens)
                for q, target in enumerate((hidden_a, hidden_b, hidden_c)):
                    pairs.append((hidden.at[slot, q, pl.ds(k * tokens, tokens)], target.at[at]))
            outs.append(
                [pltpu.make_async_copy(a, b, out_sem.at[slot, j]) for j, (a, b) in enumerate(pairs)]
            )
            for each in outs[-1]:
                each.start()

        mine.wait()
        arriving[0].wait_recv()
        for each in loads:
            each.wait()
        group(0, fsdp)
        for _ in range(4):
            next(gathering)
        arriving[1].wait_recv()
        arriving[3].wait_recv()
        group(1, first)
        next(mirroring)
        for _ in range(2):
            next(gathering)
        arriving[2].wait_recv()
        arriving[4].wait_recv()
        group(2, second)
        for _ in range(3):
            next(mirroring)
        arriving[5].wait_recv()
        arriving[6].wait_recv()
        group(3, corner)
        run_all(mirroring, gathering)
        for each in handed:
            each.wait_send()
        for each in far:
            each.wait_send()
        for group_outs in outs[2:]:
            for each in group_outs:
                each.wait()

    act = jax.ShapeDtypeStruct((total, n_own), own.dtype)
    all_rows = jax.ShapeDtypeStruct((2, n_fsdp) + own.shape, own.dtype)
    return pl.pallas_call(
        kernel,
        in_specs=any_specs(2),
        out_specs=any_specs(6),
        out_shape=[all_rows, all_rows, act, act, act, all_rows],
        scratch_shapes=[
            pltpu.VMEM((2, n_fsdp) + own.shape, own.dtype),
            pltpu.VMEM((3, n_own, features), own.dtype),
            pltpu.VMEM((2, 3, 2 * tokens, n_own), own.dtype),
            pltpu.VMEM((2, 2) + own.shape, own.dtype),
            pltpu.SemaphoreType.DMA((4,)),
        ]
        + dma_pair(6)
        + dma_pair(7)
        + dma_pair(2)
        + dma_pair(6)
        + dma_pair(8)
        + [pltpu.SemaphoreType.DMA((2, 10))],
        compiler_params=params(6),
        cost_estimate=pl.CostEstimate(
            flops=12 * total * n_own * features, bytes_accessed=50 * 1024 * 1024, transcendentals=total * n_own
        ),
        name="ffn_rows",
    )(own, planes)


def ffn_weights(n_ctx, n_fsdp, partial, rows, rows_mirror, hidden, planes, n_own, chunk=256):
    blocks, _, tokens, features = rows.shape
    total = blocks * tokens
    steps = n_own // chunk
    group = max(1, 256 // tokens)
    half = features // 2
    sides = n_ctx // 4
    wide = half // sides
    fused = partial is not None

    def kernel(*refs):
        rows_ref, refs = refs[0], refs[1:]
        mirror_refs, refs = refs[: len(rows_mirror)], refs[len(rows_mirror) :]
        mirror_blocks = [ref.at[b] for ref in mirror_refs for b in range(ref.shape[0])]
        hidden_ref, grad_gate_ref, grad_up_ref, planes_ref, *refs = refs
        if fused:
            partial_ref, weight_ref, out_ref, *refs = refs
        else:
            weight_ref, *refs = refs
        mirror, (weights, weight_sems), refs = refs[:3], refs[3:5], refs[5:]
        chip, core, _, length = place(n_ctx)
        side = chip // sides
        step = pl.program_id(0)
        stages = [lambda: None] * 2
        if fused:
            held, core_in, square_in, load, core_s, core_r, sq_s, sq_r = refs
            stages = square_sum_stages(
                n_ctx, n_fsdp, partial_ref, out_ref, held, core_in, square_in, load, (core_s, core_r), (sq_s, sq_r)
            )

        def fetch(at, slot):
            start = pl.multiple_of((core * steps + at) * chunk, chunk)
            return pltpu.make_async_copy(planes_ref.at[:, pl.ds(start, chunk)], weights.at[slot], weight_sems.at[slot])

        @pl.when(step == 0)
        def _():
            fetch(0, 0).start()
            stages[0]()

        @pl.when(step + 1 < steps)
        def _():
            fetch(step + 1, (step + 1) % 2).start()

        slot = step % 2
        fetch(step, slot).wait()
        gate_ref, up_ref, down_ref = (weights.at[slot, pl.ds(plane, 1)] for plane in range(3))
        for at in range(0, blocks, group):
            here = jnp.concatenate([ref[0] for ref in mirror_blocks[at : at + group]])
            back = jnp.concatenate([ref[1] for ref in mirror_blocks[at : at + group]])
            span = pl.ds(at * tokens, group * tokens)
            for out, value in zip(mirror, hidden_units(here, back, gate_ref, up_ref, down_ref)):
                out[span] = value

        @pl.when(step == 0)
        def _():
            stages[1]()

        lefts = ((grad_gate_ref, mirror[1], 0), (grad_up_ref, mirror[2], 0), (hidden_ref, mirror[0], 1))
        for plane, (left, left_mirror, which) in enumerate(lefts):
            left = left[...]
            left_mirror = left_mirror[...]
            for z in range(sides):
                cols = pl.ds(pl.multiple_of(side * half + z * wide, wide), wide)
                right = rows_ref[:, which, :, cols].reshape(total, wide)
                right_mirror = jnp.concatenate([ref[which, :, cols] for ref in mirror_blocks])
                weight_ref[z, plane] = low(
                    mm(left, right, CONTRACT_FIRST) + mm(left_mirror, right_mirror, CONTRACT_FIRST)
                )

        for at, stage in ((1, 2), (steps - 1, 3)):
            if stage < len(stages):

                @pl.when(step == min(at, steps - 1))
                def _():
                    stages[stage]()

    act_spec = pl.BlockSpec((total, chunk), lambda j: (0, j))
    once = dict(pipeline_mode=pl.Buffered(1))
    operands = [rows, *rows_mirror, *hidden, planes]
    in_specs = [whole_block(rows.shape, **once)] + [whole_block(part.shape, **once) for part in rows_mirror]
    in_specs += [act_spec] * 3 + any_specs(1)
    out_specs = [pl.BlockSpec((sides, 3, chunk, wide), lambda j: (0, 0, j, 0))]
    out_shape = [jax.ShapeDtypeStruct((sides, 3, n_own, wide), jnp.bfloat16)]
    scratch = [pltpu.VMEM((total, chunk), jnp.bfloat16)] * 3
    scratch += [pltpu.VMEM((2, 3, chunk, features), jnp.bfloat16), pltpu.SemaphoreType.DMA((2,))]
    if fused:
        operands.append(partial)
        in_specs += any_specs(1)
        out_specs.append(whole_block(partial.shape[-2:], **once))
        out_shape.append(jax.ShapeDtypeStruct(partial.shape[-2:], jnp.float32))
        scratch += square_sum_scratch(n_fsdp, partial)
    return pl.pallas_call(
        kernel,
        grid=(steps,),
        in_specs=in_specs,
        out_specs=out_specs,
        out_shape=out_shape,
        scratch_shapes=scratch,
        compiler_params=params(3) if fused else params(),
        cost_estimate=pl.CostEstimate(
            flops=12 * total * n_own * features, bytes_accessed=50 * 1024 * 1024, transcendentals=total * n_own
        ),
        name="ffn_weights",
    )(*operands)


def ffn_back(hidden, grad_gate, grad_up, planes, core, blocks, wide=512):
    total, n_own = hidden.shape
    features = planes.shape[2]
    tokens = total // blocks

    def kernel(core_ref, hidden_ref, grad_gate_ref, grad_up_ref, gate_ref, up_ref, down_ref, out_ref):
        out = mm(hidden_ref[...], down_ref[0])
        out_ref[:, 0] = low(out).reshape(blocks, tokens, wide)
        back = mm(grad_gate_ref[...], gate_ref[0]) + mm(grad_up_ref[...], up_ref[0])
        out_ref[:, 1] = low(back).reshape(blocks, tokens, wide)

    def weight_spec(plane):
        return pl.BlockSpec((1, n_own, wide), lambda j, core_ref: (plane, core_ref[0], j))

    act_spec = pl.BlockSpec((total, n_own), lambda j, core_ref: (0, 0), pipeline_mode=pl.Buffered(1))
    return pl.pallas_call(
        kernel,
        grid_spec=pltpu.PrefetchScalarGridSpec(
            num_scalar_prefetch=1,
            grid=(features // wide,),
            in_specs=[act_spec, act_spec, act_spec, weight_spec(0), weight_spec(1), weight_spec(2)],
            out_specs=pl.BlockSpec((blocks, 2, tokens, wide), lambda j, core_ref: (0, 0, 0, j)),
        ),
        out_shape=jax.ShapeDtypeStruct((blocks, 2, tokens, features), jnp.bfloat16),
        compiler_params=params(),
        cost_estimate=pl.CostEstimate(
            flops=6 * total * n_own * features, bytes_accessed=30 * 1024 * 1024, transcendentals=0
        ),
        name="ffn_back",
    )(core, hidden, grad_gate, grad_up, planes, planes, planes)


SPAN = 256


def turn(values, cosine, sine):
    return values * cosine + pltpu.roll(values, HEAD_DIM // 2, 1) * sine


def attention_forward(rows, w_qkv, cosine, sine, place_column, place_row, heads):
    total, features = rows.shape
    own = heads * HEAD_DIM
    steps = total // SPAN
    scale = HEAD_DIM ** (-0.5)

    def kernel(
        rows_ref, w_ref, cosine_ref, sine_ref, column_ref, row_ref, query_ref, key_ref, value_ref, out_ref, log_ref
    ):
        step = pl.program_id(0)
        span = pl.ds(pl.multiple_of(step * SPAN, SPAN), SPAN)
        qkv = mm(rows_ref[...], w_ref[...])
        cosine = cosine_ref[span]
        sine = sine_ref[span]
        for h in range(heads):
            at = slice(h * HEAD_DIM, (h + 1) * HEAD_DIM)
            query_ref[span, at] = low(turn(qkv[:, at], cosine, sine))
            key_ref[span, at] = low(turn(qkv[:, own + h * HEAD_DIM : own + (h + 1) * HEAD_DIM], cosine, sine))
        value_ref[span] = low(qkv[:, 2 * own :])

        @pl.when(step == steps - 1)
        def _():
            for h in range(heads):
                at = slice(h * HEAD_DIM, (h + 1) * HEAD_DIM)

                @pl.loop(0, steps)
                def _(block):
                    here = pl.ds(pl.multiple_of(block * SPAN, SPAN), SPAN)
                    scores = mm(query_ref[here, at], key_ref[:, at], CONTRACT_LAST) * scale
                    scores = jnp.where(column_ref[here] >= row_ref[...], scores, MASKED)
                    highest = jnp.max(scores, axis=-1, keepdims=True)
                    exponent = jnp.exp(scores - highest)
                    sums = jnp.sum(exponent, axis=-1, keepdims=True)
                    out_ref[here, at] = low(mm(low(exponent * (1.0 / sums)), value_ref[:, at]))
                    log_ref[h, here] = highest + jnp.log(sums)

    act = jax.ShapeDtypeStruct((total, own), jnp.bfloat16)
    return pl.pallas_call(
        kernel,
        grid=(steps,),
        in_specs=[pl.BlockSpec((SPAN, features), lambda r: (r, 0))]
        + [whole_block(a.shape) for a in (w_qkv, cosine, sine, place_column, place_row)],
        out_specs=[whole_block((total, own))] * 4 + [whole_block((heads, total, 1))],
        out_shape=[act] * 4 + [jax.ShapeDtypeStruct((heads, total, 1), jnp.float32)],
        compiler_params=params(),
        name="attention_forward",
    )(rows, w_qkv, cosine, sine, place_column, place_row)


def attention_backward(query, key, value, grad, logs, w_qkv, cosine, sine, place_column, place_row, heads):
    total, own = query.shape
    features = w_qkv.shape[0]
    steps = total // SPAN
    scale = HEAD_DIM ** (-0.5)

    def kernel(
        query_ref, key_ref, value_ref, grad_ref, log_ref, w_ref, cosine_ref, sine_ref, column_ref, row_ref,
        qkv_ref, out_ref, key_sum, value_sum,
    ):
        step = pl.program_id(0)

        @pl.when(step == 0)
        def _():
            for h in range(heads):
                at = slice(h * HEAD_DIM, (h + 1) * HEAD_DIM)
                key_sum[...] = jnp.zeros_like(key_sum)
                value_sum[...] = jnp.zeros_like(value_sum)

                @pl.loop(0, steps)
                def _(block):
                    here = pl.ds(pl.multiple_of(block * SPAN, SPAN), SPAN)
                    queries = query_ref[here, at]
                    grads = grad_ref[here, at]
                    scores = mm(queries, key_ref[:, at], CONTRACT_LAST) * scale
                    scores = jnp.where(column_ref[here] >= row_ref[...], scores, MASKED)
                    probs = jnp.exp(scores - log_ref[h, here])
                    probs_grad = mm(grads, value_ref[:, at], CONTRACT_LAST)
                    centre = jnp.sum(probs * probs_grad, axis=-1, keepdims=True)
                    scores_grad = low(probs * (probs_grad - centre))
                    query_grad = mm(scores_grad, key_ref[:, at]) * scale
                    qkv_ref[here, at] = low(turn(query_grad, cosine_ref[here], -sine_ref[here]))
                    key_sum[...] += mm(scores_grad, queries, CONTRACT_FIRST)
                    value_sum[...] += mm(low(probs), grads, CONTRACT_FIRST)

                qkv_ref[:, own + h * HEAD_DIM : own + (h + 1) * HEAD_DIM] = low(
                    turn(key_sum[...] * scale, cosine_ref[...], -sine_ref[...])
                )
                qkv_ref[:, 2 * own + h * HEAD_DIM : 2 * own + (h + 1) * HEAD_DIM] = low(value_sum[...])

        span = pl.ds(pl.multiple_of(step * SPAN, SPAN), SPAN)
        out_ref[...] = low(mm(qkv_ref[span], w_ref[...], CONTRACT_LAST))

    return pl.pallas_call(
        kernel,
        grid=(steps,),
        in_specs=[
            whole_block(a.shape)
            for a in (query, key, value, grad, logs, w_qkv, cosine, sine, place_column, place_row)
        ],
        out_specs=[whole_block((total, 3 * own)), pl.BlockSpec((SPAN, features), lambda r: (r, 0))],
        out_shape=[
            jax.ShapeDtypeStruct((total, 3 * own), jnp.bfloat16),
            jax.ShapeDtypeStruct((total, features), jnp.bfloat16),
        ],
        scratch_shapes=[pltpu.VMEM((total, HEAD_DIM), jnp.float32)] * 2,
        compiler_params=params(),
        name="attention_backward",
    )(query, key, value, grad, logs, w_qkv, cosine, sine, place_column, place_row)


ROWS = 32


def row_blocks(count, features):
    return pl.BlockSpec((count, ROWS, features), lambda r, *_: (0, r, 0))


def whole_block(shape, **more):
    zeros = (0,) * len(shape)
    return pl.BlockSpec(shape, lambda r, *_: zeros, **more)


def connect_coefficients(values, dynamic_ref, static_ref, coef_ref, dyn_ref):
    lane = lax.broadcasted_iota(jnp.int32, (values[0].shape[0], 8), 1)
    columns = []
    for i, value in enumerate(values):
        mean = jnp.mean(value, axis=-1, keepdims=True)
        centered = value - mean
        inverse = lax.rsqrt(jnp.mean(centered * centered, axis=-1, keepdims=True) + EPS)
        normed = centered * inverse
        projected = 0.0
        for k in range(6):
            part = jnp.sum(normed * dynamic_ref[k : k + 1], axis=-1, keepdims=True)
            projected = jnp.where(lane == k, part, projected)
        dynamic_part = jnp.tanh(projected)
        coefficient = dynamic_part + static_ref[i : i + 1]
        dyn_ref[i] = dynamic_part
        coef_ref[i] = jnp.where(lane == 6, mean, jnp.where(lane == 7, inverse, coefficient))
        columns.append(coefficient)
    return columns


def connect_first(streams, dynamic, static):
    number, rows, features = streams.shape

    def kernel(streams_ref, dynamic_ref, static_ref, coef_ref, dyn_ref, low_ref):
        values = [streams_ref[i].astype(jnp.float32) for i in range(number)]
        columns = connect_coefficients(values, dynamic_ref, static_ref, coef_ref, dyn_ref)
        mixed = sum((columns[i][:, 1:2] * values[i] for i in range(number)))
        low_ref[...] = low(normalize(mixed)[0])

    small = jax.ShapeDtypeStruct((number, rows, 8), jnp.float32)
    return pl.pallas_call(
        kernel,
        grid=(rows // ROWS,),
        out_shape=(small, small, jax.ShapeDtypeStruct((rows, features), jnp.bfloat16)),
        in_specs=[row_blocks(number, features), whole_block(dynamic.shape), whole_block(static.shape)],
        out_specs=(
            row_blocks(number, 8),
            row_blocks(number, 8),
            pl.BlockSpec((ROWS, features), lambda r: (r, 0)),
        ),
        compiler_params=params(),
        name="connect_first",
    )(streams, dynamic, static)


def connect_middle(streams, coef, attended, w_mine, w_other, cotangent, dynamic, static, core_fsdp, where, depth):
    number, rows, features = streams.shape
    half = features // 2
    count = len(w_mine)

    def kernel(core_ref, streams_ref, coef_ref, attended_ref, *refs):
        weights, refs = refs[: 2 * count], refs[2 * count :]
        cotangent_ref, dynamic_ref, static_ref = refs[:3]
        first_ref, branch_ref, coef_two_ref, dyn_ref, own_ref, projected = refs[3:]
        step = pl.program_id(0)

        @pl.when(step == 0)
        def _():
            for side in range(2):
                total = 0.0
                for j, (d, offset) in enumerate(where):
                    size = w_mine[j].shape[0]
                    columns = pl.ds(pl.multiple_of((core_ref[1] ^ d) * depth + offset, size), size)
                    total = total + mm(attended_ref[:, columns], weights[side * count + j][...])
                projected[core_ref[0] if side == 0 else 1 - core_ref[0]] = total

        span = pl.ds(pl.multiple_of(step * ROWS, ROWS), ROWS)
        branch = jnp.concatenate([projected[0, span], projected[1, span]], axis=1)
        branch_ref[...] = branch
        inputs = [streams_ref[i].astype(jnp.float32) for i in range(number)]
        outs = []
        for j in range(number):
            out = sum((coef_ref[i][:, 2 + j : 3 + j] * inputs[i] for i in range(number)))
            outs.append(out + coef_ref[j][:, 0:1] * branch)
            first_ref[j] = outs[-1]
        columns = connect_coefficients(outs, dynamic_ref, static_ref, coef_two_ref, dyn_ref)
        mixed = sum((columns[i][:, 1:2] * outs[i] for i in range(number)))
        own_ref[0] = low(normalize(mixed)[0])
        own_ref[1] = low(sum((columns[j][:, 0:1] * cotangent_ref[j].astype(jnp.float32) for j in range(number))))

    small = jax.ShapeDtypeStruct((number, rows, 8), jnp.float32)
    once = dict(pipeline_mode=pl.Buffered(1))
    return pl.pallas_call(
        kernel,
        grid_spec=pltpu.PrefetchScalarGridSpec(
            num_scalar_prefetch=1,
            grid=(rows // ROWS,),
            in_specs=[
                row_blocks(number, features),
                row_blocks(number, 8),
                whole_block(attended.shape, **once),
                *[whole_block(w.shape, **once) for w in w_mine + w_other],
                row_blocks(number, features),
                whole_block(dynamic.shape),
                whole_block(static.shape),
            ],
            out_specs=(
                row_blocks(number, features),
                pl.BlockSpec((ROWS, features), lambda r, *_: (r, 0)),
                row_blocks(number, 8),
                row_blocks(number, 8),
                row_blocks(2, features),
            ),
            scratch_shapes=[pltpu.VMEM((2, rows, half), jnp.float32)],
        ),
        out_shape=(
            jax.ShapeDtypeStruct((number, rows, features), jnp.float32),
            jax.ShapeDtypeStruct((rows, features), jnp.float32),
            small,
            small,
            jax.ShapeDtypeStruct((2, rows, features), jnp.bfloat16),
        ),
        compiler_params=params(),
        name="connect_middle",
    )(core_fsdp, streams, coef, attended, *w_mine, *w_other, cotangent, dynamic, static)


def attention_weights(rows, grads, attended, grad_cols):
    total, features = rows.shape
    parts, _, own = attended.shape
    wide = grads.shape[1]

    def kernel(rows_ref, grads_ref, attended_ref, cols_ref, out_ref):
        out_ref[:, :wide] = low(mm(rows_ref[...], grads_ref[...], CONTRACT_FIRST))
        out_ref[:, wide:] = low(mm(attended_ref[0], cols_ref[...], CONTRACT_FIRST))

    return pl.pallas_call(
        kernel,
        grid=(parts,),
        in_specs=[
            pl.BlockSpec((total, own), lambda k: (0, k)),
            whole_block(grads.shape),
            pl.BlockSpec((1, total, own), lambda k: (k, 0, 0)),
            whole_block(grad_cols.shape),
        ],
        out_specs=pl.BlockSpec((own, wide + own), lambda k: (k, 0)),
        out_shape=jax.ShapeDtypeStruct((features, wide + own), jnp.bfloat16),
        compiler_params=params(),
        cost_estimate=pl.CostEstimate(
            flops=2 * total * features * (wide + own), bytes_accessed=16 * 1024 * 1024, transcendentals=0
        ),
        name="attention_weights",
    )(rows, grads, attended, grad_cols)


def project_back(grad, w_mine, w_other, core_fsdp, n_ctx, where, depth):
    rows, features = grad.shape
    half = features // 2
    count = len(w_mine)
    own = features // n_ctx

    def kernel(core_ref, grad_ref, *refs):
        weights, (out_ref, cols_ref) = refs[: 2 * count], refs[2 * count :]
        first = grad_ref[:, pl.ds(pl.multiple_of(core_ref[0] * half, half), half)]
        second = grad_ref[:, pl.ds(pl.multiple_of((1 - core_ref[0]) * half, half), half)]
        for j, (d, offset) in enumerate(where):
            out = low(
                mm(first, weights[j][...], CONTRACT_LAST) + mm(second, weights[count + j][...], CONTRACT_LAST)
            )
            for q in range(w_mine[j].shape[0] // own):
                at = (core_ref[1] ^ d) * (depth // own) + offset // own + q
                out_ref[at] = out[:, q * own : (q + 1) * own]
        for index in range(n_ctx):
            cols_ref[index] = grad_ref[:, index * own : (index + 1) * own]

    return pl.pallas_call(
        kernel,
        grid_spec=pltpu.PrefetchScalarGridSpec(
            num_scalar_prefetch=1,
            grid=(1,),
            in_specs=[whole_block(a.shape) for a in [grad] + w_mine + w_other],
            out_specs=[whole_block((n_ctx, rows, own))] * 2,
        ),
        out_shape=[jax.ShapeDtypeStruct((n_ctx, rows, own), grad.dtype)] * 2,
        compiler_params=params(),
        name="project_back",
    )(core_fsdp, grad, *w_mine, *w_other)


def connect_back(values, coef, dyn, branch, grads, grad_normed, dynamic, coef_before=None):
    number, rows, features = values.shape
    steps = rows // ROWS
    more = coef_before is not None

    def kernel(*refs):
        values_ref, coef_ref, dyn_ref, branch_ref, grads_ref, normed_ref, dynamic_ref = refs[:7]
        refs = refs[7:]
        if more:
            before_ref, refs = refs[0], refs[1:]
        out_ref, dynamic_out, static_out = refs[:3]
        if more:
            forward_ref, grad_low_ref = refs[3:5]
        dynamic_sum = refs[-1]
        step = pl.program_id(0)

        @pl.when(step == 0)
        def _():
            dynamic_sum[...] = jnp.zeros_like(dynamic_sum)
            static_out[...] = jnp.zeros_like(static_out)

        branch = branch_ref[...]
        mixed = sum((coef_ref[i][:, 1:2] * values_ref[i].astype(jnp.float32) for i in range(number)))
        normed, inverse = normalize(mixed)
        grad_mixed = normalize_back(normed, inverse, normed_ref[...])
        lane = lax.broadcasted_iota(jnp.int32, (ROWS, 8), 1)
        totals = [0.0] * 6
        befores = 0.0
        for i in range(number):
            value = values_ref[i].astype(jnp.float32)
            grad_own = grads_ref[i].astype(jnp.float32)
            columns = [
                jnp.sum(grad_own * branch, axis=-1, keepdims=True),
                jnp.sum(grad_mixed * value, axis=-1, keepdims=True),
            ]
            out = coef_ref[i][:, 1:2] * grad_mixed
            for j in range(number):
                grad = grads_ref[j].astype(jnp.float32)
                columns.append(jnp.sum(grad * value, axis=-1, keepdims=True))
                out = out + coef_ref[i][:, 2 + j : 3 + j] * grad
            normed = (value - coef_ref[i][:, 6:7]) * coef_ref[i][:, 7:8]
            normed_grad = 0.0
            coef_grad = jnp.zeros((ROWS, 8), jnp.float32)
            for k in range(6):
                part = dyn_ref[i][:, k : k + 1]
                pre_grad = columns[k] * (1.0 - part * part)
                normed_grad = normed_grad + pre_grad * dynamic_ref[k : k + 1]
                totals[k] = totals[k] + pre_grad * normed
                coef_grad = jnp.where(lane == k, columns[k], coef_grad)
            out = out + normalize_back(normed, coef_ref[i][:, 7:8], normed_grad)
            out_ref[i] = out
            static_out[i : i + 1] += jnp.sum(coef_grad, axis=0, keepdims=True)
            if more:
                befores = befores + before_ref[i][:, 0:1] * out
        for k in range(6):
            dynamic_sum[k] += jnp.sum(totals[k].reshape(ROWS // 8, 8, features), axis=0)
        if more:
            grad_low_ref[...] = low(befores)
            for j in range(number):
                out = coef_ref[j][:, 0:1] * branch
                for i in range(number):
                    out = out + coef_ref[i][:, 2 + j : 3 + j] * values_ref[i].astype(jnp.float32)
                forward_ref[j] = low(out)

        @pl.when(step == steps - 1)
        def _():
            for k in range(6):
                dynamic_out[k : k + 1] = jnp.sum(dynamic_sum[k], axis=0, keepdims=True)
            dynamic_out[6:8] = jnp.zeros((2, features), jnp.float32)

    rows_spec = pl.BlockSpec((ROWS, features), lambda r: (r, 0))
    out_shape = [
        jax.ShapeDtypeStruct((number, rows, features), jnp.float32),
        jax.ShapeDtypeStruct((8, features), jnp.float32),
        jax.ShapeDtypeStruct((8, 8), jnp.float32),
    ]
    out_specs = [row_blocks(number, features), whole_block((8, features)), whole_block((8, 8))]
    operands = [values, coef, dyn, branch, grads, grad_normed, dynamic]
    in_specs = [
        row_blocks(number, features),
        row_blocks(number, 8),
        row_blocks(number, 8),
        rows_spec,
        row_blocks(number, features),
        rows_spec,
        whole_block(dynamic.shape),
    ]
    if more:
        operands.append(coef_before)
        in_specs.append(row_blocks(number, 8))
        out_shape.append(jax.ShapeDtypeStruct((number, rows, features), jnp.bfloat16))
        out_specs.append(row_blocks(number, features))
        out_shape.append(jax.ShapeDtypeStruct((rows, features), jnp.bfloat16))
        out_specs.append(rows_spec)
    return pl.pallas_call(
        kernel,
        grid=(steps,),
        in_specs=in_specs,
        out_specs=out_specs,
        out_shape=out_shape,
        scratch_shapes=[pltpu.VMEM((6, 8, features), jnp.float32)],
        compiler_params=params(),
        name="connect_back",
    )(*operands)


def local(n_ctx, n_fsdp, streams, w_attn, w_ffn, hc_dynamic, hc_static, cotangent, pair_order):
    number = streams.shape[1]
    length = streams.shape[2]
    features = streams.shape[3]
    size = HEAD_DIM
    own = features // n_ctx
    heads = own // size
    rows = length * n_ctx
    own_rows = w_attn.shape[0]
    ctx = lax.axis_index("ctx")
    fsdp = lax.axis_index("fsdp")
    core = ctx % 2
    chips = n_ctx // 2
    core_index = jnp.reshape(core, (1,)).astype(jnp.int32)

    def in_order(mine, other, axis):
        return jnp.where(
            core == 0, jnp.concatenate([mine, other], axis=axis), jnp.concatenate([other, mine], axis=axis)
        )


    w_own = lax.dynamic_slice_in_dim(w_attn, ctx * own, own, 2)[:, 0:3].reshape(own_rows, 3 * own)
    w_qkv = gather(w_own, "fsdp")
    half = features // 2
    w_half = lax.dynamic_slice_in_dim(w_attn, core * half, half, 2)[:, 3]
    siblings = [(i, i ^ 1) for i in range(n_ctx)]
    core_fsdp = jnp.stack([core, fsdp]).astype(jnp.int32)

    def exchange(values, most=0):
        return [values] + [
            lax.ppermute(values, "fsdp", [(i, i ^ d) for i in range(n_fsdp)])
            for d in range(1, most + 1 if most else n_fsdp)
        ]

    def swap(blocks):
        return [lax.ppermute(block, "ctx", siblings) for block in blocks]


    positions = block_positions(pair_order, length)
    frequency = THETA ** (-(jnp.arange(size // 2, dtype=jnp.float32) * 2.0) / size)
    angles = positions.astype(jnp.float32)[:, None] * jnp.concatenate([frequency, frequency])[None, :]
    signs = jnp.where(jnp.arange(size) < size // 2, -1.0, 1.0)
    tables = (jnp.cos(angles), jnp.sin(angles) * signs[None, :], positions[:, None], positions[None, :])

    dynamics = jnp.pad(hc_dynamic, ((0, 0), (0, 2), (0, 0)))
    statics = jnp.pad(hc_static, ((0, 0), (0, 0), (0, 2)))
    coef_one, dyn_one, attn_low = connect_first(streams[0], dynamics[0], statics[0])
    attn_low, w_half = lax.optimization_barrier((attn_low, w_half))
    w_out_mine = exchange(w_half, 2 if n_fsdp == 4 else 0)
    attn_all = line_rows(n_ctx, attn_low).reshape(rows, features)
    w_out_where = [(d, 0) for d in range(len(w_out_mine))]
    if n_fsdp == 4:
        attn_all, *w_out_mine = lax.optimization_barrier((attn_all, *w_out_mine))
        middle = own_rows // 2
        w_out_mine.append(lax.ppermute(w_out_mine[1][:middle], "fsdp", [(i, i ^ 2) for i in range(4)]))
        w_out_mine.append(lax.ppermute(w_out_mine[2][middle:], "fsdp", [(i, i ^ 1) for i in range(4)]))
        w_out_where += [(3, 0), (3, middle)]
    query, key, value, attended, logs = attention_forward(attn_all, w_qkv, *tables, heads)
    attended, w_out_mine = lax.optimization_barrier((attended, w_out_mine))
    w_out_other = swap(w_out_mine)
    attended_rows = lax.all_to_all(attended, "ctx", 0, 1, tiled=True)

    first_out, attn_branch, coef_two, dyn_two, ffn_own = connect_middle(
        streams[0], coef_one, attended_rows, w_out_mine, w_out_other, cotangent[0], dynamics[1], statics[1], core_fsdp,
        w_out_where, own_rows,
    )
    ffn_own = ffn_own.reshape(2 * length, features)

    planes = jnp.moveaxis(w_ffn, 1, 0)
    n_own = planes.shape[1] // 2
    blocks = 2 * n_fsdp
    if n_fsdp == 4:
        ffn_all, mirror_rows, *hidden, sums = ffn_rows(n_ctx, ffn_own, planes, n_own)
        ffn_all, mirror_rows = (part.reshape(blocks, 2, length, features) for part in (ffn_all, mirror_rows))
        mirror_rows = [mirror_rows]
        attended, sums = lax.optimization_barrier((attended, sums))
        attended_all = gather(attended, "ctx").reshape(n_ctx, rows, own)
        *weight_parts, sums = ffn_weights(n_ctx, n_fsdp, sums, ffn_all, mirror_rows, hidden, planes, n_own)
    else:
        ffn_mirror = lax.ppermute(ffn_own, "ctx", [(i, n_ctx - 2 - i + 2 * (i % 2)) for i in range(n_ctx)])
        ffn_all = square_core_gather(n_ctx, n_fsdp, ffn_own).reshape(blocks, 2, length, features)
        attended_all = gather(attended, "ctx").reshape(n_ctx, rows, own)
        mirror_mine = exchange(ffn_mirror)
        hidden = ffn_forward(ffn_all, planes, core_index, n_own)
        sums = ffn_back(*hidden, planes, core_index, blocks)
        mirror_rows = [part.reshape(1, 2, length, features) for part in mirror_mine + swap(mirror_mine)]
        sums = square_sum(n_ctx, n_fsdp, sums.reshape(2, n_fsdp, 2 * length, features))
        weight_parts = ffn_weights(n_ctx, n_fsdp, None, ffn_all, mirror_rows, hidden, planes, n_own)
    sides = chips // 2
    lines = [[2 * (sides * side + i) + j for i in range(sides)] for side in range(2) for j in range(2)]
    weight_cols = lax.psum_scatter(weight_parts[0], "ctx", scatter_dimension=0, axis_index_groups=lines)
    ffn_branch = sums[:length]
    grad_ffn_normed = sums[length:]

    grad_first, dynamic_grad_two, static_grad_two, streams_out, grad_attn = connect_back(
        first_out, coef_two, dyn_two, ffn_branch, cotangent[0], grad_ffn_normed, dynamics[1], coef_one
    )
    grad_heads, grad_cols = project_back(grad_attn, w_out_mine, w_out_other, core_fsdp, n_ctx, w_out_where, own_rows)
    grad_heads = lax.all_to_all(grad_heads, "ctx", 0, 0, tiled=True).reshape(rows, own)
    grad_heads, grad_cols = lax.optimization_barrier((grad_heads, grad_cols))
    grad_cols = lax.all_to_all(grad_cols, "ctx", 0, 0, tiled=True).reshape(rows, own)
    qkv_grad, attn_part = attention_backward(query, key, value, grad_heads, logs, w_qkv, *tables, heads)
    attn_part = attn_part.reshape(n_ctx, length, features)
    grad_attn_normed = line_sum(n_ctx, attn_part, 5)
    grad_attn_normed, weight_cols = lax.optimization_barrier((grad_attn_normed, weight_cols))
    mine = lax.dynamic_slice_in_dim(weight_cols, core * own, own, 2)
    other = lax.dynamic_slice_in_dim(weight_cols, (1 - core) * own, own, 2)
    other = lax.ppermute(other, "ctx", siblings)
    ffn_grad = jnp.moveaxis(in_order(mine, other, 1), 0, 1).astype(jnp.float32)
    weight_part = attention_weights(attn_all, qkv_grad, attended_all, grad_cols)
    attn_grad = scatter(weight_part, "fsdp")

    grad_inputs, dynamic_grad_one, static_grad_one = connect_back(
        streams[0], coef_one, dyn_one, attn_branch, grad_first, grad_attn_normed, dynamics[0]
    )
    static_grads = jnp.concatenate([static_grad_one[:number, :6].reshape(1, -1), static_grad_two[:number, :6].reshape(1, -1)])
    small = jnp.concatenate(
        [
            dynamic_grad_one[:6],
            dynamic_grad_two[:6],
            jnp.pad(static_grads, ((0, 2), (0, features - 6 * number))),
        ]
    )
    small = sum_everywhere(n_ctx, n_fsdp, small.reshape(n_ctx, 8, -1))
    small, attn_grad = lax.optimization_barrier((small, attn_grad))
    small = small.reshape(16, features)
    attn_grad = attn_grad.astype(jnp.float32).reshape(own_rows, 4, own)
    dynamic_total = small[:12].reshape(2, 6, features)
    static_total = small[12:14, : 6 * number].reshape(2, number, 6)
    return (streams_out[None], grad_inputs[None], attn_grad, ffn_grad, dynamic_total, static_total)


def solution(mesh):
    return jax.shard_map(
        functools.partial(local, mesh.shape["ctx"], mesh.shape["fsdp"]),
        mesh=mesh,
        in_specs=(
            P("fsdp", None, "ctx", None),
            P("fsdp", None, None),
            P("fsdp", None, None),
            P(),
            P(),
            P("fsdp", None, "ctx", None),
            P(),
        ),
        out_specs=(
            P("fsdp", None, "ctx", None),
            P("fsdp", None, "ctx", None),
            P("fsdp", None, "ctx"),
            P("fsdp", None, "ctx"),
            P(),
            P(),
        ),
        check_vma=False,
    )
```

time: 659 us -> 455 us (0.69)
  matrix products: 74.4 us -> 0 us
  other arithmetic: 68.8 us -> 7.83 us
  Pallas kernels: 383 us -> 340 us
  local copies, waits for them, and re-layouts: 71.9 us -> 29 us
  blocking collectives: 0 us -> 25.3 us
  waiting for transfers between devices: 21.6 us -> 14.8 us
    dot_general x26 -> x0, matrix products: 74.4 us -> none  [the longest x12 29.3 us: mm(): return lax.dot_general(a, b, dims, preferred_element_type=jnp.float32)]
    pallas_call x2 -> x1, Pallas kernels: 106 us -> 47.8 us  [line_sum(): pl.pallas_call(kernel, out_shape=jax.ShapeDtypeStruct((rows, columns), jn...]
    reduce_sum x18 -> x0, other arithmetic: 28.2 us -> none  [the longest x4 14.9 us: connect_back(): jnp.sum(grad_out[j] * values[i], axis=-1)]
    unnamed x346 -> x28, local copies, waits for them, and re-layouts: 30 us -> 4.46 us
    all_to_all x0 -> x1, blocking collectives: none -> 25.3 us  [local(): lax.all_to_all(grad_heads, 'ctx', 0, 0, tiled=True).reshape(rows, own)]
    pallas_call x7 -> x11, Pallas kernels: 250 us -> 274 us  [the longest x1 76.3 us: ffn_rows(): pl.pallas_call(kernel, in_specs=any_specs(2), out_specs=any_specs(6), out...]
    another operation x14 -> x1, other arithmetic: 14.7 us -> 0.59 us  [local(): core_fsdp = jnp.stack([core, fsdp]).astype(jnp.int32)]
    convert_element_type x10 -> x1, other arithmetic: 10.2 us -> 0.08 us  [local(): positions.astype(jnp.float32)[:, None]]
  transfers between devices with their start and end apart: 7 -> 16, of which waited for: 2 -> 2; matrix products, arithmetic and copies ran while one was open for 24% -> 6% of each run, Pallas kernels for 46% -> 56%
where the time goes in v3:
time: 455 us; the launch traced here: 447 us
  Pallas kernels  340 us (75%)
  local copies, waits for them, and re-layouts  29 us (6%)
  blocking collectives  25.3 us (6%)
  starting transfers between devices  15.3 us (3%)
  waiting for transfers between devices  14.8 us (3%)
  between operations  14.5 us (3%)
  other arithmetic  7.83 us (2%)
    pallas_call x1, Pallas kernels, ffn_rows(): pl.pallas_call(kernel, in_specs=any_specs(2), out_specs=any_specs(6), out...  76.3 us
    pallas_call x1, Pallas kernels, ffn_weights(): pl.pallas_call(kernel, grid=(steps,), in_specs=in_specs, out_specs=out_sp...  51.4 us
    pallas_call x1, Pallas kernels, line_sum(): pl.pallas_call(kernel, out_shape=jax.ShapeDtypeStruct((rows, columns), jn...  47.8 us
    pallas_call x1, Pallas kernels, line_rows(): pl.pallas_call(kernel, out_shape=jax.ShapeDtypeStruct((n_ctx,) + rows.sha...  42.9 us
    pallas_call x2, Pallas kernels, connect_back(): pl.pallas_call(kernel, grid=(steps,), in_specs=in_specs, out_specs=out_sp...  31.3 us
    all_to_all x1, blocking collectives, local(): lax.all_to_all(grad_heads, 'ctx', 0, 0, tiled=True).reshape(rows, own)  25.3 us
    pallas_call x1, Pallas kernels, attention_backward(): pl.pallas_call(kernel, grid=(steps,), in_specs=[whole_block(a.shape) for...  18.1 us
    pallas_call x1, Pallas kernels, sum_everywhere(): pl.pallas_call(kernel, out_shape=jax.ShapeDtypeStruct(values.shape, value...  17.8 us
  transfers between devices with their start and end apart: 16, of which 2 were waited for; matrix products, arithmetic and copies ran while one was open for 6% of the time, Pallas kernels for 56%

profile of v3, /device:TPU:0, one launch (start us, length us, event | category | flops | bytes accessed | tf_op | source)
XLA Modules:
  0.0 446.5 jit_solution(16218413766367010895)
XLA Ops:
  7.2 1.6 constant_dynamic-slice_fusion.2
  8.8 0.9 copy.36
  9.7 1.2 copy.28
  10.9 5.8 %constant_dynamic-slice_fusion.3 = bf16[512,1,1024]{2,1,0:T(2,128)(2,1)S(1)} fusion(bf16[512,4,2048]{2,1,0:T(4,128)(2,1)} %param.8, s32[]{:T(128)S(6)} %add.65, s32[]{:T(128)S(6)} %select_n.36), kind=kLoop, calls=%fused_computation.26 | loop fusion | bytes 2097160 | tf_op jit(solution)/shard_map/slice | solution.py:1421
  16.7 0.4 copy.39
  17.2 0.7 fusion.4
  17.9 0.7 fusion.2
  18.6 6.4 %connect_first.1 = (f32[4,128,8]{2,1,0:T(8,128)}, f32[4,128,8]{2,1,0:T(8,128)}, bf16[128,2048]{1,0:T(8,128)(2,1)}) custom-call(bf16[4,128,2048]{2,1,0:T(8,128)(2,1)} %bitcast.40, f32[8,2048]{1,0:T(8,128)} %get-tuple-element.137.dynamic_ref.refs_6_, f32[4,8]{1,0:T(4,128)} %get-tuple-element.141.static_ref), custom_call_target="tpu_custom_call" | custom-call | tf_op jit(solution)/shard_map/connect_first/pallas_call | solution.py:1142
  24.9 3.0 collective-permute-start
  27.9 1.5 collective-permute-start.1
  29.4 42.9 %line_rows.1 = bf16[8,128,2048]{2,1,0:T(8,128)(2,1)} custom-call(bf16[128,2048]{1,0:T(8,128)(2,1)} %get-tuple-element.61.rows_ref), custom_call_target="tpu_custom_call" | custom-call | tf_op jit(solution)/shard_map/line_rows/pallas_call | solution.py:271
  72.5 0.9 slice.55
  73.4 0.5 collective-permute-start.2
  73.9 0.8 slice.56
  74.7 0.5 collective-permute-start.3
  75.3 1.0 copy.29.column_ref
  76.5 3.1 fusion
  79.6 15.3 %attention_forward.1 = (bf16[1024,256]{1,0:T(8,128)(2,1)}, bf16[1024,256]{1,0:T(8,128)(2,1)}, bf16[1024,256]{1,0:T(8,128)(2,1)}, bf16[1024,256]{1,0:T(8,128)(2,1)}, f32[2,1024,1]{2,1,0:T(8,128)}) custom-call(bf16[1024,2048]{1,0:T(8,128)(2,1)} %bitcast.43, bf16[2048,768]{1,0:T(8,128)(2,1)} %all-gather.3.cloned.1.call-done.w_ref, ...), custom_call_target="tpu_custom_call" | custom-call | tf_op jit(solution)/shard_map/attention_forward/pallas_call | solution.py:1027
  95.0 0.5 collective-permute-start.5
  95.6 4.1 all-to-all-start
  100.0 0.4 collective-permute-start.7
  100.5 0.6 pad_add_fusion.1.core_ref
  101.1 14.0 %all-to-all-done = bf16[8,128,256]{2,1,0:T(8,128)(2,1)} async-done(((bf16[8,128,256]{2,1,0:T(8,128)(2,1)}), bf16[8,128,256]{2,1,0:T(8,128)(2,1)}, u32[]{:S(2)}, u32[]{:S(2)}) %all-to-all-start) | async-done | bytes 524320 | tf_op jit(solution)/shard_map/all_to_all | solution.py:1457
  115.1 1.9 copy.37
  117.0 13.6 %connect_middle.1 = (f32[4,128,2048]{2,1,0:T(8,128)}, f32[128,2048]{1,0:T(8,128)}, f32[4,128,8]{2,1,0:T(8,128)}, f32[4,128,8]{2,1,0:T(8,128)}, bf16[2,128,2048]{2,1,0:T(8,128)(2,1)}) custom-call(s32[2]{0:T(128)} %pad_add_fusion.1.core_ref, bf16[4,128,2048]{2,1,0:T(8,128)(2,1)} %bitcast.41, f32[4,128,8]{2,1,0:T(8,128)} %get-tuple-element.59.coef_ref.refs_7_.refs_1_, ...), custom_call_target="tpu_custom_call" | custom-call | tf_op jit(solution)/shard_map/connect_middle/pallas_call | solution.py:1194
  130.6 76.3 %ffn_rows.1 = (bf16[2,4,256,2048]{3,2,1,0:T(8,128)(2,1)}, bf16[2,4,256,2048]{3,2,1,0:T(8,128)(2,1)}, bf16[1024,1024]{1,0:T(8,128)(2,1)}, bf16[1024,1024]{1,0:T(8...) custom-call(bf16[256,2048]{1,0:T(8,128)(2,1)} %bitcast.69, bf16[3,2048,2048]{2,1,0:T(8,128)(2,1)} %bitcast.64), custom_call_target="tpu_custom_call" | custom-call | flops 25769803776 | bytes 52428800 | tf_op jit(solution)/shard_map/ffn_rows/pallas_call | solution.py:819
  207.2 51.4 %ffn_weights.1 = (bf16[2,3,1024,512]{3,2,1,0:T(8,128)(2,1)}, f32[256,2048]{1,0:T(8,128)}) custom-call(bf16[8,2,128,2048]{3,2,1,0:T(8,128)(2,1)} %bitcast.70, bf16[8,2,128,2048]{3,2,1,0:T(8,128)(2,1)} %bitcast.71, bf16[1024,1024]{1,0:T(8,128)(2,1)} %get-tuple-element.80.refs_2_, bf16[1024,1024]{1,0:T(8,128)(2,1)} %get-tuple-element.81.refs_3_, ...), custom_call_target="tpu_custom_call" | custom-call | flops 25769803776 | bytes 52428800 | tf_op jit(solution)/shard_map/ffn_weights/pallas_call | solution.py:936
  258.7 1.6 copy-done.3
  260.2 1.5 fusion.5
  261.7 17.0 %connect_back.2 = (f32[4,128,2048]{2,1,0:T(8,128)}, f32[8,2048]{1,0:T(8,128)}, f32[8,8]{1,0:T(8,128)}, bf16[4,128,2048]{2,1,0:T(8,128)(2,1)}, bf16[128,2048]{1,0:T(8,128)(2,1)}) custom-call(f32[4,128,2048]{2,1,0:T(8,128)} %get-tuple-element.74.refs_0_, f32[4,128,8]{2,1,0:T(8,128)} %get-tuple-element.75.refs_1_, f32[4,128,8]{2,1,0:T(8,128)} %get-tuple-element.76.refs_2_, ...), custom_call_target="tpu_custom_call" | custom-call | tf_op jit(solution)/shard_map/connect_back/pallas_call | solution.py:1385
  278.7 7.9 %project_back.1 = (bf16[8,128,256]{2,1,0:T(8,128)(2,1)}, bf16[8,128,256]{2,1,0:T(8,128)(2,1)}) custom-call(s32[2]{0:T(128)} %pad_add_fusion.1.core_ref, bf16[128,2048]{1,0:T(8,128)(2,1)} %get-tuple-element.93.grad_ref, bf16[512,1024]{1,0:T(8,128)(2,1)} %bitcast.49, bf16[512,1024]{1,0:T(8,128)(2,1)} %copy-done.1, bf16[512,1024]{1,0:T(8,128)(2,1)} %copy-done.2, ...), custom_call_target="tpu_custom_call" | custom-call | tf_op jit(solution)/shard_map/project_back/pallas_call | solution.py:1277
  286.5 25.3 %all_to_all.29 = bf16[8,128,256]{2,1,0:T(8,128)(2,1)} all-to-all(bf16[8,128,256]{2,1,0:T(8,128)(2,1)} %get-tuple-element.94), channel_id=1, replica_groups=mesh['ctx'=8,'fsdp'=4] {'ctx'}, dimensions={0} | all-to-all | bytes 1048576 | tf_op jit(solution)/shard_map/all_to_all | solution.py:1495
  311.8 3.8 all-to-all-start.2
  315.7 18.1 %attention_backward.1 = (bf16[1024,768]{1,0:T(8,128)(2,1)}, bf16[1024,2048]{1,0:T(8,128)(2,1)}) custom-call(bf16[1024,256]{1,0:T(8,128)(2,1)} %get-tuple-element.90.query_ref, bf16[1024,256]{1,0:T(8,128)(2,1)} %get-tuple-element.91.key_ref, bf16[1024,256]{1,0:T(8,128)(2,1)} %get-tuple-element.92.value_ref, bf16[1024,256]{1,0:T(8,128)(2,1)} %bitcast.56, ...), custom_call_target="tpu_custom_call" | custom-call | tf_op jit(solution)/shard_map/attention_backward/pallas_call | solution.py:1082
  333.8 0.7 all-to-all-done.2
  334.5 0.8 copy-done.5
  335.3 11.1 %attention_weights.1 = bf16[2048,1024]{1,0:T(8,128)(2,1)} custom-call(bf16[1024,2048]{1,0:T(8,128)(2,1)} %bitcast.44, bf16[1024,768]{1,0:T(8,128)(2,1)} %get-tuple-element.106.grads_ref, bf16[8,1024,256]{2,1,0:T(8,128)(2,1)} %bitcast.66, bf16[1024,256]{1,0:T(8,128)(2,1)} %bitcast.58), custom_call_target="tpu_custom_call" | custom-call | flops 4294967296 | bytes 16777216 | tf_op jit(solution)/shard_map/attention_weights/pallas_call | solution.py:1238
  346.4 47.8 %line_sum.1.refs_5_ = f32[128,2048]{1,0:T(8,128)} custom-call(bf16[8,128,2048]{2,1,0:T(8,128)(2,1)} %bitcast.52), custom_call_target="tpu_custom_call" | custom-call | tf_op jit(solution)/shard_map/line_sum/pallas_call | solution.py:521
  394.2 3.3 constant_dynamic-slice_fusion.1
  397.5 14.3 %connect_back.3 = (f32[4,128,2048]{2,1,0:T(8,128)}, f32[8,2048]{1,0:T(8,128)}, f32[8,8]{1,0:T(8,128)}) custom-call(bf16[4,128,2048]{2,1,0:T(8,128)(2,1)} %bitcast.42, f32[4,128,8]{2,1,0:T(8,128)} %get-tuple-element.59.coef_ref.refs_7_.refs_1_, f32[4,128,8]{2,1,0:T(8,128)} %get-tuple-element.87.refs_2_, f32[128,2048]{1,0:T(8,128)} %get-tuple-element.88.refs_3_, ...), custom_call_target="tpu_custom_call" | custom-call | tf_op jit(solution)/shard_map/connect_back/pallas_call | solution.py:1385
  411.8 0.7 slice.63
  412.6 0.9 pad_maximum_fusion
  413.5 0.7 reshape.97.values_ref
  414.2 17.8 %sum_everywhere.1 = f32[8,8,512]{2,1,0:T(8,128)} custom-call(f32[8,8,512]{2,1,0:T(8,128)} %reshape.97.values_ref), custom_call_target="tpu_custom_call" | custom-call | tf_op jit(solution)/shard_map/sum_everywhere/pallas_call | solution.py:583
  432.1 3.0 convert_bitcast_fusion
  435.2 3.0 reshape.106
  438.2 0.7 copy.32
  438.9 0.7 reshape.104
  (63 shorter events, 1.6 us)
Async XLA Ops:
  7.2 72.4 %all-gather.3.cloned.1.call-start = ((), (), s32[]{:S(2)}) async-start(), calls=%async_computation.5 | async-start | bytes 3932160 | tf_op jit(solution)/shard_map/all_gather | solution.py:53
  10.9 6.2 %copy-start.6 = (f32[2,6,2048]{2,0,1:T(2,128)S(1)}, f32[2,6,2048]{2,0,1:T(2,128)}, u32[]{:S(2)}) copy-start(f32[2,6,2048]{2,0,1:T(2,128)} %param.10) | copy-start | bytes 294916
  10.9 6.3 %copy-start.9 = (f32[2,4,6]{2,1,0:T(4,128)S(1)}, f32[2,4,6]{2,1,0:T(4,128)}, u32[]{:S(2)}) copy-start(f32[2,4,6]{2,1,0:T(4,128)} %param.11) | copy-start | bytes 580
  17.1 77.8 %copy-start = (bf16[512,1,1024]{2,0,1:T(8,128)(2,1)}, bf16[512,1,1024]{2,0,1:T(8,128)(2,1)S(1)}, u32[]{:S(2)}) copy-start(bf16[512,1,1024]{2,0,1:T(8,128)(2,1)S(1)} %copy.39) | copy-start | bytes 3145732
  18.6 53.8 %copy-start.11 = (s32[8]{0:T(128)S(1)}, s32[8]{0:T(128)}, u32[]{:S(2)}) copy-start(s32[8]{0:T(128)} %param.13) | copy-start | bytes 100
  24.9 47.5 %collective-permute-start = (bf16[512,1024]{1,0:T(8,128)(2,1)S(1)}, bf16[512,1024]{1,0:T(8,128)(2,1)S(1)}, u32[]{:S(2)}, u32[]{:S(2)}) collective-permute-start(bf16[512,1024]{1,0:T(8,128)(2,1)S(1)} %bitcast.45), channel_id=1, source_target_pairs={{0,1},{1,0},{2,3},{3,2},{4,5},{5,4},{6,7},{7,6},{8,9},{9,8},{10,11... | collective-permute-start | bytes 3145736 | tf_op jit(solution)/shard_map/ppermute | solution.py:1427
  27.9 44.6 %collective-permute-start.1 = (bf16[512,1024]{1,0:T(8,128)(2,1)S(1)}, bf16[512,1024]{1,0:T(8,128)(2,1)S(1)}, u32[]{:S(2)}, u32[]{:S(2)}) collective-permute-start(bf16[512,1024]{1,0:T(8,128)(2,1)S(1)} %bitcast.46), channel_id=1, source_target_pairs={{0,2},{1,3},{2,0},{3,1},{4,6},{5,7},{6,4},{7,5},{8,10},{9,11},{10,... | collective-permute-start | bytes 3145736 | tf_op jit(solution)/shard_map/ppermute | solution.py:1427
  72.4 22.5 %copy-start.1 = (bf16[512,1024]{1,0:T(8,128)(2,1)}, bf16[512,1024]{1,0:T(8,128)(2,1)S(1)}, u32[]{:S(2)}) copy-start(bf16[512,1024]{1,0:T(8,128)(2,1)S(1)} %collective-permute-done.refs_1_) | copy-start | bytes 3145732
  72.5 23.0 %copy-start.2 = (bf16[512,1024]{1,0:T(8,128)(2,1)}, bf16[512,1024]{1,0:T(8,128)(2,1)S(1)}, u32[]{:S(2)}) copy-start(bf16[512,1024]{1,0:T(8,128)(2,1)S(1)} %collective-permute-done.1.refs_2_) | copy-start | bytes 3145732
  73.4 21.5 %collective-permute-start.2 = (bf16[256,1024]{1,0:T(8,128)(2,1)}, bf16[256,1024]{1,0:T(8,128)(2,1)}, u32[]{:S(2)}, u32[]{:S(2)}) collective-permute-start(bf16[256,1024]{1,0:T(8,128)(2,1)} %slice.55), channel_id=1, source_target_pairs={{0,2},{1,3},{2,0},{3,1},{4,6},{5,7},{6,4},{7,5},{8,10},{9,11},{10,... | collective-permute-start | bytes 1572872 | tf_op jit(solution)/shard_map/ppermute | solution.py:1451
  74.7 20.2 %collective-permute-start.3 = (bf16[256,1024]{1,0:T(8,128)(2,1)}, bf16[256,1024]{1,0:T(8,128)(2,1)}, u32[]{:S(2)}, u32[]{:S(2)}) collective-permute-start(bf16[256,1024]{1,0:T(8,128)(2,1)} %slice.56), channel_id=1, source_target_pairs={{0,1},{1,0},{2,3},{3,2},{4,5},{5,4},{6,7},{7,6},{8,9},{9,8},{10,11... | collective-permute-start | bytes 1572872 | tf_op jit(solution)/shard_map/ppermute | solution.py:1452
  75.3 4.2 copy-start.7
  94.9 22.1 %collective-permute-start.4 = (bf16[512,1024]{1,0:T(8,128)(2,1)S(1)}, bf16[512,1024]{1,0:T(8,128)(2,1)}, u32[]{:S(2)}, u32[]{:S(2)}) collective-permute-start(bf16[512,1024]{1,0:T(8,128)(2,1)S(1)} %bitcast.47), channel_id=1, source_target_pairs={{0,4},{4,0},{8,12},{12,8},{16,20},{20,16},{24,28},{28,24},{1,5},{5... | collective-permute-start | bytes 3145736 | tf_op jit(solution)/shard_map/ppermute | solution.py:1432
  95.0 22.0 %collective-permute-start.5 = (bf16[512,1024]{1,0:T(8,128)(2,1)S(1)}, bf16[512,1024]{1,0:T(8,128)(2,1)}, u32[]{:S(2)}, u32[]{:S(2)}) collective-permute-start(bf16[512,1024]{1,0:T(8,128)(2,1)S(1)} %collective-permute-done.refs_1_), channel_id=1, source_target_pairs={{0,4},{4,0},{8,12},{12,8},{16,20},{20,16},{24,28},{28,24},{1,5},{5... | collective-permute-start | bytes 3145736 | tf_op jit(solution)/shard_map/ppermute | solution.py:1432
  95.5 21.5 %collective-permute-start.6 = (bf16[512,1024]{1,0:T(8,128)(2,1)S(1)}, bf16[512,1024]{1,0:T(8,128)(2,1)}, u32[]{:S(2)}, u32[]{:S(2)}) collective-permute-start(bf16[512,1024]{1,0:T(8,128)(2,1)S(1)} %collective-permute-done.1.refs_2_), channel_id=1, source_target_pairs={{0,4},{4,0},{8,12},{12,8},{16,20},{20,16},{24,28},{28,24},{1,5},{5... | collective-permute-start | bytes 3145736 | tf_op jit(solution)/shard_map/ppermute | solution.py:1432
  95.6 19.5 %all-to-all-start = ((bf16[8,128,256]{2,1,0:T(8,128)(2,1)}), bf16[8,128,256]{2,1,0:T(8,128)(2,1)}, u32[]{:S(2)}, u32[]{:S(2)}) async-start(bf16[8,128,256]{2,1,0:T(8,128)(2,1)} %bitcast.57), calls=%async_computation | async-start | bytes 1048576 | tf_op jit(solution)/shard_map/all_to_all | solution.py:1457
  99.7 234.7 %all-gather.5.cloned.1.call-start = ((), (), s32[]{:S(2)}) async-start(), calls=%async_computation.7 | async-start | bytes 4718592 | tf_op jit(solution)/shard_map/all_gather | solution.py:53
  100.0 17.0 %collective-permute-start.7 = (bf16[256,1024]{1,0:T(8,128)(2,1)}, bf16[256,1024]{1,0:T(8,128)(2,1)}, u32[]{:S(2)}, u32[]{:S(2)}) collective-permute-start(bf16[256,1024]{1,0:T(8,128)(2,1)} %collective-permute-done.2.refs_3_), channel_id=1, source_target_pairs={{0,4},{4,0},{8,12},{12,8},{16,20},{20,16},{24,28},{28,24},{1,5},{5... | collective-permute-start | bytes 1572872 | tf_op jit(solution)/shard_map/ppermute | solution.py:1432
  100.4 16.6 %collective-permute-start.8 = (bf16[256,1024]{1,0:T(8,128)(2,1)}, bf16[256,1024]{1,0:T(8,128)(2,1)}, u32[]{:S(2)}, u32[]{:S(2)}) collective-permute-start(bf16[256,1024]{1,0:T(8,128)(2,1)} %collective-permute-done.3.refs_4_), channel_id=1, source_target_pairs={{0,4},{4,0},{8,12},{12,8},{16,20},{20,16},{24,28},{28,24},{1,5},{5... | collective-permute-start | bytes 1572872 | tf_op jit(solution)/shard_map/ppermute | solution.py:1432
  207.0 187.2 %reduce-scatter.3.cloned.1.call-start = ((), (), s32[]{:S(2)}) async-start(), calls=%async_computation.6 | async-start | bytes 9437184 | tf_op jit(solution)/shard_map/reduce_scatter | solution.py:1487
  258.6 1.6 copy-start.3
  311.8 22.6 %all-to-all-start.2 = ((bf16[8,128,256]{2,1,0:T(8,128)(2,1)}), bf16[8,128,256]{2,1,0:T(8,128)(2,1)S(1)}, u32[]{:S(2)}, u32[]{:S(2)}) async-start(bf16[8,128,256]{2,1,0:T(8,128)(2,1)} %get-tuple-element.108), calls=%async_computation.3 | async-start | bytes 1048576 | tf_op jit(solution)/shard_map/all_to_all | solution.py:1497
  315.6 119.5 %reduce-scatter.5.cloned.1.call-start = ((), (), s32[]{:S(2)}) async-start(), calls=%async_computation.8 | async-start | bytes 5242880 | tf_op jit(solution)/shard_map/reduce_scatter | solution.py:57
  334.5 0.8 copy-start.5
  394.2 3.3 copy-start.10
  397.4 34.6 %collective-permute-start.9 = (bf16[3,1024,256]{2,1,0:T(8,128)(2,1)}, bf16[3,1024,256]{2,1,0:T(8,128)(2,1)S(1)}, u32[]{:S(2)}, u32[]{:S(2)}) collective-permute-start(bf16[3,1024,256]{2,1,0:T(8,128)(2,1)} %get-tuple-element.133), channel_id=1, source_target_pairs={{0,4},{4,0},{8,12},{12,8},{16,20},{20,16},{24,28},{28,24},{1,5},{5... | collective-permute-start | bytes 4718600 | tf_op jit(solution)/shard_map/ppermute | solution.py:1504
  397.5 15.1 %copy-start.8 = (f32[8,2048]{1,0:T(8,128)S(1)}, f32[8,2048]{1,0:T(8,128)}, u32[]{:S(2)}) copy-start(f32[8,2048]{1,0:T(8,128)} %get-tuple-element.103) | copy-start | bytes 196612
  432.1 3.0 copy-start.4
  435.1 3.0 slice-start
Sparse Core Ops, SparseCore 0:
  11.0 61.5 all-gather.2
  207.1 47.3 all-gather.4
  258.8 93.9 reduce-scatter.2
  355.9 52.6 reduce-scatter.4

commit v4 on v3

--- a/solution.py
+++ b/solution.py
@@ -420,6 +420,75 @@
     return [begin, spread, pass_on, finish]
 
 
+def corner_sum_stages(n_ctx, partial_ref, out_ref, held, square_in, load, sems):
+    half = partial_ref.shape[1] // 2
+    chip, core, fsdp, _ = place(n_ctx)
+    ctx = chip * 2 + core
+    first, second, corner = fsdp_neighbours(fsdp)
+    top, low_half = pl.ds(0, half), pl.ds(half, half)
+    to_first, to_second = (ctx, first), (ctx, second)
+
+    def copy(index, source, peer):
+        return send(source, square_in.at[index], sems, index, peer)
+
+    copies = [
+        copy(0, partial_ref.at[corner, top], to_first),
+        copy(1, partial_ref.at[corner, low_half], to_second),
+        copy(2, partial_ref.at[first, top], to_first),
+        copy(3, partial_ref.at[second, low_half], to_second),
+        copy(4, held.at[0], to_second),
+        copy(5, held.at[1], to_first),
+    ]
+    mine = [
+        pltpu.make_async_copy(partial_ref.at[second, top], held.at[0], load.at[0]),
+        pltpu.make_async_copy(partial_ref.at[first, low_half], held.at[1], load.at[1]),
+        pltpu.make_async_copy(partial_ref.at[fsdp, top], held.at[2], load.at[2]),
+        pltpu.make_async_copy(partial_ref.at[fsdp, low_half], held.at[3], load.at[3]),
+    ]
+
+    def begin():
+        greet(fsdp_peers(4, ctx, fsdp))
+        for each in copies[:4]:
+            each.start()
+        for each in mine:
+            each.start()
+
+    def pass_on():
+        for index in range(2):
+            mine[index].wait()
+            copies[index].wait_recv()
+            add_into(held.at[index], square_in.at[index])
+            copies[4 + index].start()
+
+    def finish():
+        for part, sources in ((0, (2, 4)), (1, (3, 5))):
+            mine[2 + part].wait()
+            for j in sources:
+                copies[j].wait_recv()
+
+            @pl.loop(0, half // 64)
+            def _(step):
+                at = pl.ds(pl.multiple_of(step * 64, 64), 64)
+                value = held[2 + part, at].astype(jnp.float32)
+                for j in sources:
+                    value = value + square_in[j, at].astype(jnp.float32)
+                out_ref[pl.ds(pl.multiple_of(part * half + step * 64, 64), 64)] = value
+
+        for each in copies:
+            each.wait_send()
+
+    return [begin, pass_on, finish]
+
+
+def corner_sum_scratch(partial):
+    _, rows, columns = partial.shape
+    return [
+        pltpu.VMEM((4, rows // 2, columns), partial.dtype),
+        pltpu.VMEM((6, rows // 2, columns), partial.dtype),
+        pltpu.SemaphoreType.DMA((4,)),
+    ] + dma_pair(6)
+
+
 def square_sum_scratch(n_fsdp, partial):
     rows, columns = partial.shape[-2:]
     pieces = (6, rows // 2, columns) if n_fsdp == 4 else (n_fsdp - 1, rows, columns)
@@ -705,7 +774,7 @@
 
     def kernel(
         own_ref, planes_ref, all_ref, mirror_ref, hidden_a, hidden_b, hidden_c, partial_ref,
-        rows, weights, hidden, partial, load, sq_s, sq_r, core_s, core_r, far_s, far_r, mi_s, mi_r, mc_s, mc_r, out_sem,
+        rows, weights, hidden, partial, core_in, load, sq_s, sq_r, core_s, core_r, far_s, far_r, mi_s, mi_r, mc_s, mc_r, sum_s, sum_r, out_sem,
     ):
         chip, core, fsdp, length = place(n_ctx)
         ctx = chip * 2 + core
@@ -745,13 +814,23 @@
         for each in far:
             each.start()
         mirroring = mirror_gather(mirror_ref, far, (mi_s, mi_r), (mc_s, mc_r), ctx, core, fsdp, sibling)
-        outs = []
+        outs, summing, sums = [], [], []
+
+        def add_up(number, owner):
+            summing[number].wait_recv()
+            add_into(partial.at[number % 2, core], core_in.at[number])
+            sums.append(
+                pltpu.make_async_copy(partial.at[number % 2, core], partial_ref.at[owner], out_sem.at[number % 2, 8])
+            )
+            sums[-1].start()
 
         def group(number, owner):
             slot = number % 2
             if number >= 2:
                 for each in outs[number - 2]:
                     each.wait()
+                summing[number - 2].wait_send()
+                sums[number - 2].wait()
             here = jnp.concatenate([rows[0, owner, :tokens], rows[1, owner, :tokens]])
             back = jnp.concatenate([rows[0, owner, tokens:], rows[1, owner, tokens:]])
 
@@ -772,9 +851,10 @@
                     partial[slot, k, tokens:, at] = below[k * tokens : (k + 1) * tokens]
 
             pairs = []
+            summing.append(send(partial.at[slot, 1 - core], core_in.at[number], (sum_s, sum_r), number, sibling))
+            summing[-1].start()
             for k in range(2):
                 pairs.append((rows.at[k, owner], all_ref.at[k, owner]))
-                pairs.append((partial.at[slot, k], partial_ref.at[k, owner]))
                 at = pl.ds(pl.multiple_of((k * n_fsdp + owner) * tokens, tokens), tokens)
                 for q, target in enumerate((hidden_a, hidden_b, hidden_c)):
                     pairs.append((hidden.at[slot, q, pl.ds(k * tokens, tokens)], target.at[at]))
@@ -794,25 +874,31 @@
         arriving[1].wait_recv()
         arriving[3].wait_recv()
         group(1, first)
+        add_up(0, fsdp)
         next(mirroring)
         for _ in range(2):
             next(gathering)
         arriving[2].wait_recv()
         arriving[4].wait_recv()
         group(2, second)
+        add_up(1, first)
         for _ in range(3):
             next(mirroring)
         arriving[5].wait_recv()
         arriving[6].wait_recv()
         group(3, corner)
+        add_up(2, second)
+        next(mirroring)
+        add_up(3, corner)
         run_all(mirroring, gathering)
         for each in handed:
             each.wait_send()
         for each in far:
             each.wait_send()
-        for group_outs in outs[2:]:
-            for each in group_outs:
-                each.wait()
+        for each in outs[2] + outs[3] + sums[2:]:
+            each.wait()
+        for each in summing[2:]:
+            each.wait_send()
 
     act = jax.ShapeDtypeStruct((total, n_own), own.dtype)
     all_rows = jax.ShapeDtypeStruct((2, n_fsdp) + own.shape, own.dtype)
@@ -820,12 +906,13 @@
         kernel,
         in_specs=any_specs(2),
         out_specs=any_specs(6),
-        out_shape=[all_rows, all_rows, act, act, act, all_rows],
+        out_shape=[all_rows, all_rows, act, act, act, jax.ShapeDtypeStruct((n_fsdp,) + own.shape, own.dtype)],
         scratch_shapes=[
             pltpu.VMEM((2, n_fsdp) + own.shape, own.dtype),
             pltpu.VMEM((3, n_own, features), own.dtype),
             pltpu.VMEM((2, 3, 2 * tokens, n_own), own.dtype),
             pltpu.VMEM((2, 2) + own.shape, own.dtype),
+            pltpu.VMEM((n_fsdp,) + own.shape, own.dtype),
             pltpu.SemaphoreType.DMA((4,)),
         ]
         + dma_pair(6)
@@ -833,7 +920,8 @@
         + dma_pair(2)
         + dma_pair(6)
         + dma_pair(8)
-        + [pltpu.SemaphoreType.DMA((2, 10))],
+        + dma_pair(4)
+        + [pltpu.SemaphoreType.DMA((2, 9))],
         compiler_params=params(6),
         cost_estimate=pl.CostEstimate(
             flops=12 * total * n_own * features, bytes_accessed=50 * 1024 * 1024, transcendentals=total * n_own
@@ -865,12 +953,10 @@
         chip, core, _, length = place(n_ctx)
         side = chip // sides
         step = pl.program_id(0)
-        stages = [lambda: None] * 2
+        stages = [lambda: None]
         if fused:
-            held, core_in, square_in, load, core_s, core_r, sq_s, sq_r = refs
-            stages = square_sum_stages(
-                n_ctx, n_fsdp, partial_ref, out_ref, held, core_in, square_in, load, (core_s, core_r), (sq_s, sq_r)
-            )
+            held, square_in, load, sq_s, sq_r = refs
+            stages = corner_sum_stages(n_ctx, partial_ref, out_ref, held, square_in, load, (sq_s, sq_r))
 
         def fetch(at, slot):
             start = pl.multiple_of((core * steps + at) * chunk, chunk)
@@ -894,10 +980,6 @@
             span = pl.ds(at * tokens, group * tokens)
             for out, value in zip(mirror, hidden_units(here, back, gate_ref, up_ref, down_ref)):
                 out[span] = value
-
-        @pl.when(step == 0)
-        def _():
-            stages[1]()
 
         lefts = ((grad_gate_ref, mirror[1], 0), (grad_up_ref, mirror[2], 0), (hidden_ref, mirror[0], 1))
         for plane, (left, left_mirror, which) in enumerate(lefts):
@@ -911,7 +993,7 @@
                     mm(left, right, CONTRACT_FIRST) + mm(left_mirror, right_mirror, CONTRACT_FIRST)
                 )
 
-        for at, stage in ((1, 2), (steps - 1, 3)):
+        for at, stage in ((1, 1), (steps - 1, 2)):
             if stage < len(stages):
 
                 @pl.when(step == min(at, steps - 1))
@@ -932,7 +1014,7 @@
         in_specs += any_specs(1)
         out_specs.append(whole_block(partial.shape[-2:], **once))
         out_shape.append(jax.ShapeDtypeStruct(partial.shape[-2:], jnp.float32))
-        scratch += square_sum_scratch(n_fsdp, partial)
+        scratch += corner_sum_scratch(partial)
     return pl.pallas_call(
         kernel,
         grid=(steps,),
@@ -1288,7 +1370,7 @@
     )(core_fsdp, grad, *w_mine, *w_other)
 
 
-def connect_back(values, coef, dyn, branch, grads, grad_normed, dynamic, coef_before=None):
+def connect_back(values, coef, dyn, branch, grads, grad_normed, dynamic, coef_before=None, offset=0):
     number, rows, features = values.shape
     steps = rows // ROWS
     more = coef_before is not None
@@ -1372,7 +1454,7 @@
         row_blocks(number, 8),
         rows_spec,
         row_blocks(number, features),
-        rows_spec,
+        pl.BlockSpec((ROWS, features), lambda r: (offset // ROWS + r, 0)),
         whole_block(dynamic.shape),
     ]
     if more:
@@ -1485,11 +1567,9 @@
     sides = chips // 2
     lines = [[2 * (sides * side + i) + j for i in range(sides)] for side in range(2) for j in range(2)]
     weight_cols = lax.psum_scatter(weight_parts[0], "ctx", scatter_dimension=0, axis_index_groups=lines)
-    ffn_branch = sums[:length]
-    grad_ffn_normed = sums[length:]
 
     grad_first, dynamic_grad_two, static_grad_two, streams_out, grad_attn = connect_back(
-        first_out, coef_two, dyn_two, ffn_branch, cotangent[0], grad_ffn_normed, dynamics[1], coef_one
+        first_out, coef_two, dyn_two, sums, cotangent[0], sums, dynamics[1], coef_one, length
     )
     grad_heads, grad_cols = project_back(grad_attn, w_out_mine, w_out_other, core_fsdp, n_ctx, w_out_where, own_rows)
     grad_heads = lax.all_to_all(grad_heads, "ctx", 0, 0, tiled=True).reshape(rows, own)

time: 455 us -> 448 us (0.985)
    pallas_call x1, Pallas kernels: 51.4 us -> 46 us  [ffn_weights(): pl.pallas_call(kernel, grid=(steps,), in_specs=in_specs, out_specs=out_sp...]
where the time goes in v4:
time: 448 us; the launch traced here: 439 us
  Pallas kernels  336 us (75%)
  local copies, waits for them, and re-layouts  26 us (6%)
  blocking collectives  24.4 us (5%)
  starting transfers between devices  15.5 us (3%)
  waiting for transfers between devices  14.5 us (3%)
  between operations  14.5 us (3%)
  other arithmetic  7.8 us (2%)
    pallas_call x1, Pallas kernels, ffn_rows(): pl.pallas_call(kernel, in_specs=any_specs(2), out_specs=any_specs(6), out...  78.3 us
    pallas_call x1, Pallas kernels, line_sum(): pl.pallas_call(kernel, out_shape=jax.ShapeDtypeStruct((rows, columns), jn...  49.1 us
    pallas_call x1, Pallas kernels, ffn_weights(): pl.pallas_call(kernel, grid=(steps,), in_specs=in_specs, out_specs=out_sp...  46 us
    pallas_call x1, Pallas kernels, line_rows(): pl.pallas_call(kernel, out_shape=jax.ShapeDtypeStruct((n_ctx,) + rows.sha...  42.9 us
    pallas_call x2, Pallas kernels, connect_back(): pl.pallas_call(kernel, grid=(steps,), in_specs=in_specs, out_specs=out_sp...  31.3 us
    all_to_all x1, blocking collectives, local(): lax.all_to_all(grad_heads, 'ctx', 0, 0, tiled=True).reshape(rows, own)  24.4 us
    pallas_call x1, Pallas kernels, attention_backward(): pl.pallas_call(kernel, grid=(steps,), in_specs=[whole_block(a.shape) for...  18.1 us
    pallas_call x1, Pallas kernels, sum_everywhere(): pl.pallas_call(kernel, out_shape=jax.ShapeDtypeStruct(values.shape, value...  16.1 us
  transfers between devices with their start and end apart: 16, of which 2 were waited for; matrix products, arithmetic and copies ran while one was open for 6% of the time, Pallas kernels for 56%

profile of v4, /device:TPU:0, one launch (start us, length us, event | category | flops | bytes accessed | tf_op | source)
XLA Modules:
  0.0 439.2 jit_solution(18012453774347911935)
XLA Ops:
  7.2 1.6 constant_dynamic-slice_fusion.2
  8.8 0.9 copy.36
  9.7 1.2 copy.28
  10.9 5.8 %constant_dynamic-slice_fusion.3 = bf16[512,1,1024]{2,1,0:T(2,128)(2,1)S(1)} fusion(bf16[512,4,2048]{2,1,0:T(4,128)(2,1)} %param.8, s32[]{:T(128)S(6)} %add.65, s32[]{:T(128)S(6)} %select_n.36), kind=kLoop, calls=%fused_computation.26 | loop fusion | bytes 2097160 | tf_op jit(solution)/shard_map/slice | solution.py:1503
  16.7 0.4 copy.39
  17.2 0.7 fusion.4
  17.9 0.7 fusion.2
  18.6 6.4 %connect_first.1 = (f32[4,128,8]{2,1,0:T(8,128)}, f32[4,128,8]{2,1,0:T(8,128)}, bf16[128,2048]{1,0:T(8,128)(2,1)}) custom-call(bf16[4,128,2048]{2,1,0:T(8,128)(2,1)} %bitcast.40, f32[8,2048]{1,0:T(8,128)} %get-tuple-element.135.dynamic_ref.refs_6_, f32[4,8]{1,0:T(4,128)} %get-tuple-element.139.static_ref), custom_call_target="tpu_custom_call" | custom-call | tf_op jit(solution)/shard_map/connect_first/pallas_call | solution.py:1224
  24.9 3.0 collective-permute-start
  27.9 1.5 collective-permute-start.1
  29.4 42.9 %line_rows.1 = bf16[8,128,2048]{2,1,0:T(8,128)(2,1)} custom-call(bf16[128,2048]{1,0:T(8,128)(2,1)} %get-tuple-element.61.rows_ref), custom_call_target="tpu_custom_call" | custom-call | tf_op jit(solution)/shard_map/line_rows/pallas_call | solution.py:271
  72.5 0.9 slice.49
  73.4 0.5 collective-permute-start.2
  73.9 0.8 slice.50
  74.8 0.5 collective-permute-start.3
  75.4 1.1 copy.29.column_ref
  76.5 3.1 fusion
  79.6 15.4 %attention_forward.1 = (bf16[1024,256]{1,0:T(8,128)(2,1)}, bf16[1024,256]{1,0:T(8,128)(2,1)}, bf16[1024,256]{1,0:T(8,128)(2,1)}, bf16[1024,256]{1,0:T(8,128)(2,1)}, f32[2,1024,1]{2,1,0:T(8,128)}) custom-call(bf16[1024,2048]{1,0:T(8,128)(2,1)} %bitcast.43, bf16[2048,768]{1,0:T(8,128)(2,1)} %all-gather.3.cloned.1.call-done.w_ref, ...), custom_call_target="tpu_custom_call" | custom-call | tf_op jit(solution)/shard_map/attention_forward/pallas_call | solution.py:1109
  95.1 0.5 collective-permute-start.5
  95.7 4.1 all-to-all-start
  100.1 0.4 collective-permute-start.7
  100.6 0.6 pad_add_fusion.1.core_ref
  101.2 14.0 %all-to-all-done = bf16[8,128,256]{2,1,0:T(8,128)(2,1)} async-done(((bf16[8,128,256]{2,1,0:T(8,128)(2,1)}), bf16[8,128,256]{2,1,0:T(8,128)(2,1)}, u32[]{:S(2)}, u32[]{:S(2)}) %all-to-all-start) | async-done | bytes 524320 | tf_op jit(solution)/shard_map/all_to_all | solution.py:1539
  115.2 1.9 copy.37
  117.1 13.6 %connect_middle.1 = (f32[4,128,2048]{2,1,0:T(8,128)}, f32[128,2048]{1,0:T(8,128)}, f32[4,128,8]{2,1,0:T(8,128)}, f32[4,128,8]{2,1,0:T(8,128)}, bf16[2,128,2048]{2,1,0:T(8,128)(2,1)}) custom-call(s32[2]{0:T(128)} %pad_add_fusion.1.core_ref, bf16[4,128,2048]{2,1,0:T(8,128)(2,1)} %bitcast.41, f32[4,128,8]{2,1,0:T(8,128)} %get-tuple-element.59.coef_ref.refs_7_.refs_1_, ...), custom_call_target="tpu_custom_call" | custom-call | tf_op jit(solution)/shard_map/connect_middle/pallas_call | solution.py:1276
  130.7 78.3 %ffn_rows.1 = (bf16[2,4,256,2048]{3,2,1,0:T(8,128)(2,1)}, bf16[2,4,256,2048]{3,2,1,0:T(8,128)(2,1)}, bf16[1024,1024]{1,0:T(8,128)(2,1)}, bf16[1024,1024]{1,0:T(8...) custom-call(bf16[256,2048]{1,0:T(8,128)(2,1)} %bitcast.69, bf16[3,2048,2048]{2,1,0:T(8,128)(2,1)} %bitcast.64), custom_call_target="tpu_custom_call" | custom-call | flops 25769803776 | bytes 52428800 | tf_op jit(solution)/shard_map/ffn_rows/pallas_call | solution.py:905
  209.1 0.3 reduce-scatter.3.cloned.1.call-start
  209.3 46.0 %ffn_weights.1 = (bf16[2,3,1024,512]{3,2,1,0:T(8,128)(2,1)}, f32[256,2048]{1,0:T(8,128)}) custom-call(bf16[8,2,128,2048]{3,2,1,0:T(8,128)(2,1)} %bitcast.70, bf16[8,2,128,2048]{3,2,1,0:T(8,128)(2,1)} %bitcast.71, bf16[1024,1024]{1,0:T(8,128)(2,1)} %get-tuple-element.80.refs_2_, bf16[1024,1024]{1,0:T(8,128)(2,1)} %get-tuple-element.81.refs_3_, ...), custom_call_target="tpu_custom_call" | custom-call | flops 25769803776 | bytes 52428800 | tf_op jit(solution)/shard_map/ffn_weights/pallas_call | solution.py:1018
  255.4 17.0 %connect_back.2 = (f32[4,128,2048]{2,1,0:T(8,128)}, f32[8,2048]{1,0:T(8,128)}, f32[8,8]{1,0:T(8,128)}, bf16[4,128,2048]{2,1,0:T(8,128)(2,1)}, bf16[128,2048]{1,0:T(8,128)(2,1)}) custom-call(f32[4,128,2048]{2,1,0:T(8,128)} %get-tuple-element.74.refs_0_, f32[4,128,8]{2,1,0:T(8,128)} %get-tuple-element.75.refs_1_, f32[4,128,8]{2,1,0:T(8,128)} %get-tuple-element.76.refs_2_, ...), custom_call_target="tpu_custom_call" | custom-call | tf_op jit(solution)/shard_map/connect_back/pallas_call | solution.py:1467
  272.4 8.3 %project_back.1 = (bf16[8,128,256]{2,1,0:T(8,128)(2,1)}, bf16[8,128,256]{2,1,0:T(8,128)(2,1)}) custom-call(s32[2]{0:T(128)} %pad_add_fusion.1.core_ref, bf16[128,2048]{1,0:T(8,128)(2,1)} %get-tuple-element.93.grad_ref, bf16[512,1024]{1,0:T(8,128)(2,1)} %bitcast.49, bf16[512,1024]{1,0:T(8,128)(2,1)} %copy-done.1, bf16[512,1024]{1,0:T(8,128)(2,1)} %copy-done.2, ...), custom_call_target="tpu_custom_call" | custom-call | tf_op jit(solution)/shard_map/project_back/pallas_call | solution.py:1359
  280.7 24.4 %all_to_all.29 = bf16[8,128,256]{2,1,0:T(8,128)(2,1)} all-to-all(bf16[8,128,256]{2,1,0:T(8,128)(2,1)} %get-tuple-element.94), channel_id=1, replica_groups=mesh['ctx'=8,'fsdp'=4] {'ctx'}, dimensions={0} | all-to-all | bytes 1048576 | tf_op jit(solution)/shard_map/all_to_all | solution.py:1575
  305.1 3.8 all-to-all-start.2
  308.9 0.3 reduce-scatter.5.cloned.1.call-start
  309.2 18.1 %attention_backward.1 = (bf16[1024,768]{1,0:T(8,128)(2,1)}, bf16[1024,2048]{1,0:T(8,128)(2,1)}) custom-call(bf16[1024,256]{1,0:T(8,128)(2,1)} %get-tuple-element.90.query_ref, bf16[1024,256]{1,0:T(8,128)(2,1)} %get-tuple-element.91.key_ref, bf16[1024,256]{1,0:T(8,128)(2,1)} %get-tuple-element.92.value_ref, bf16[1024,256]{1,0:T(8,128)(2,1)} %bitcast.56, ...), custom_call_target="tpu_custom_call" | custom-call | tf_op jit(solution)/shard_map/attention_backward/pallas_call | solution.py:1164
  327.3 0.4 all-to-all-done.2
  327.7 0.8 copy-done.4
  328.5 10.9 %attention_weights.1 = bf16[2048,1024]{1,0:T(8,128)(2,1)} custom-call(bf16[1024,2048]{1,0:T(8,128)(2,1)} %bitcast.44, bf16[1024,768]{1,0:T(8,128)(2,1)} %get-tuple-element.106.grads_ref, bf16[8,1024,256]{2,1,0:T(8,128)(2,1)} %bitcast.66, bf16[1024,256]{1,0:T(8,128)(2,1)} %bitcast.58), custom_call_target="tpu_custom_call" | custom-call | flops 4294967296 | bytes 16777216 | tf_op jit(solution)/shard_map/attention_weights/pallas_call | solution.py:1320
  339.5 49.1 %line_sum.1.refs_5_ = f32[128,2048]{1,0:T(8,128)} custom-call(bf16[8,128,2048]{2,1,0:T(8,128)(2,1)} %bitcast.52), custom_call_target="tpu_custom_call" | custom-call | tf_op jit(solution)/shard_map/line_sum/pallas_call | solution.py:590
  388.6 3.2 constant_dynamic-slice_fusion.1
  391.9 14.3 %connect_back.3 = (f32[4,128,2048]{2,1,0:T(8,128)}, f32[8,2048]{1,0:T(8,128)}, f32[8,8]{1,0:T(8,128)}) custom-call(bf16[4,128,2048]{2,1,0:T(8,128)(2,1)} %bitcast.42, f32[4,128,8]{2,1,0:T(8,128)} %get-tuple-element.59.coef_ref.refs_7_.refs_1_, f32[4,128,8]{2,1,0:T(8,128)} %get-tuple-element.87.refs_2_, f32[128,2048]{1,0:T(8,128)} %get-tuple-element.88.refs_3_, ...), custom_call_target="tpu_custom_call" | custom-call | tf_op jit(solution)/shard_map/connect_back/pallas_call | solution.py:1467
  406.3 0.7 slice.55
  407.1 0.9 pad_maximum_fusion
  407.9 0.7 reshape.97.values_ref
  408.6 16.1 %sum_everywhere.1 = f32[8,8,512]{2,1,0:T(8,128)} custom-call(f32[8,8,512]{2,1,0:T(8,128)} %reshape.97.values_ref), custom_call_target="tpu_custom_call" | custom-call | tf_op jit(solution)/shard_map/sum_everywhere/pallas_call | solution.py:652
  424.8 3.0 convert_bitcast_fusion
  427.9 3.0 reshape.106
  430.9 0.7 copy.32
  431.6 0.7 reshape.104
  (60 shorter events, 1.3 us)
Async XLA Ops:
  7.2 72.4 %all-gather.3.cloned.1.call-start = ((), (), s32[]{:S(2)}) async-start(), calls=%async_computation.5 | async-start | bytes 3932160 | tf_op jit(solution)/shard_map/all_gather | solution.py:53
  10.9 6.2 %copy-start.5 = (f32[2,6,2048]{2,0,1:T(2,128)S(1)}, f32[2,6,2048]{2,0,1:T(2,128)}, u32[]{:S(2)}) copy-start(f32[2,6,2048]{2,0,1:T(2,128)} %param.10) | copy-start | bytes 294916
  10.9 6.3 %copy-start.8 = (f32[2,4,6]{2,1,0:T(4,128)S(1)}, f32[2,4,6]{2,1,0:T(4,128)}, u32[]{:S(2)}) copy-start(f32[2,4,6]{2,1,0:T(4,128)} %param.11) | copy-start | bytes 580
  17.1 77.9 %copy-start = (bf16[512,1,1024]{2,0,1:T(8,128)(2,1)}, bf16[512,1,1024]{2,0,1:T(8,128)(2,1)S(1)}, u32[]{:S(2)}) copy-start(bf16[512,1,1024]{2,0,1:T(8,128)(2,1)S(1)} %copy.39) | copy-start | bytes 3145732
  18.6 53.8 %copy-start.10 = (s32[8]{0:T(128)S(1)}, s32[8]{0:T(128)}, u32[]{:S(2)}) copy-start(s32[8]{0:T(128)} %param.13) | copy-start | bytes 100
  24.9 47.5 %collective-permute-start = (bf16[512,1024]{1,0:T(8,128)(2,1)S(1)}, bf16[512,1024]{1,0:T(8,128)(2,1)S(1)}, u32[]{:S(2)}, u32[]{:S(2)}) collective-permute-start(bf16[512,1024]{1,0:T(8,128)(2,1)S(1)} %bitcast.45), channel_id=1, source_target_pairs={{0,1},{1,0},{2,3},{3,2},{4,5},{5,4},{6,7},{7,6},{8,9},{9,8},{10,11... | collective-permute-start | bytes 3145736 | tf_op jit(solution)/shard_map/ppermute | solution.py:1509
  27.9 44.6 %collective-permute-start.1 = (bf16[512,1024]{1,0:T(8,128)(2,1)S(1)}, bf16[512,1024]{1,0:T(8,128)(2,1)S(1)}, u32[]{:S(2)}, u32[]{:S(2)}) collective-permute-start(bf16[512,1024]{1,0:T(8,128)(2,1)S(1)} %bitcast.46), channel_id=1, source_target_pairs={{0,2},{1,3},{2,0},{3,1},{4,6},{5,7},{6,4},{7,5},{8,10},{9,11},{10,... | collective-permute-start | bytes 3145736 | tf_op jit(solution)/shard_map/ppermute | solution.py:1509
  72.5 22.6 %copy-start.1 = (bf16[512,1024]{1,0:T(8,128)(2,1)}, bf16[512,1024]{1,0:T(8,128)(2,1)S(1)}, u32[]{:S(2)}) copy-start(bf16[512,1024]{1,0:T(8,128)(2,1)S(1)} %collective-permute-done.refs_1_) | copy-start | bytes 3145732
  72.5 23.1 %copy-start.2 = (bf16[512,1024]{1,0:T(8,128)(2,1)}, bf16[512,1024]{1,0:T(8,128)(2,1)S(1)}, u32[]{:S(2)}) copy-start(bf16[512,1024]{1,0:T(8,128)(2,1)S(1)} %collective-permute-done.1.refs_2_) | copy-start | bytes 3145732
  73.4 21.6 %collective-permute-start.2 = (bf16[256,1024]{1,0:T(8,128)(2,1)}, bf16[256,1024]{1,0:T(8,128)(2,1)}, u32[]{:S(2)}, u32[]{:S(2)}) collective-permute-start(bf16[256,1024]{1,0:T(8,128)(2,1)} %slice.49), channel_id=1, source_target_pairs={{0,2},{1,3},{2,0},{3,1},{4,6},{5,7},{6,4},{7,5},{8,10},{9,11},{10,... | collective-permute-start | bytes 1572872 | tf_op jit(solution)/shard_map/ppermute | solution.py:1533
  74.8 20.3 %collective-permute-start.3 = (bf16[256,1024]{1,0:T(8,128)(2,1)}, bf16[256,1024]{1,0:T(8,128)(2,1)}, u32[]{:S(2)}, u32[]{:S(2)}) collective-permute-start(bf16[256,1024]{1,0:T(8,128)(2,1)} %slice.50), channel_id=1, source_target_pairs={{0,1},{1,0},{2,3},{3,2},{4,5},{5,4},{6,7},{7,6},{8,9},{9,8},{10,11... | collective-permute-start | bytes 1572872 | tf_op jit(solution)/shard_map/ppermute | solution.py:1534
  75.4 4.2 copy-start.6
  95.0 22.1 %collective-permute-start.4 = (bf16[512,1024]{1,0:T(8,128)(2,1)S(1)}, bf16[512,1024]{1,0:T(8,128)(2,1)}, u32[]{:S(2)}, u32[]{:S(2)}) collective-permute-start(bf16[512,1024]{1,0:T(8,128)(2,1)S(1)} %bitcast.47), channel_id=1, source_target_pairs={{0,4},{4,0},{8,12},{12,8},{16,20},{20,16},{24,28},{28,24},{1,5},{5... | collective-permute-start | bytes 3145736 | tf_op jit(solution)/shard_map/ppermute | solution.py:1514
  95.1 22.0 %collective-permute-start.5 = (bf16[512,1024]{1,0:T(8,128)(2,1)S(1)}, bf16[512,1024]{1,0:T(8,128)(2,1)}, u32[]{:S(2)}, u32[]{:S(2)}) collective-permute-start(bf16[512,1024]{1,0:T(8,128)(2,1)S(1)} %collective-permute-done.refs_1_), channel_id=1, source_target_pairs={{0,4},{4,0},{8,12},{12,8},{16,20},{20,16},{24,28},{28,24},{1,5},{5... | collective-permute-start | bytes 3145736 | tf_op jit(solution)/shard_map/ppermute | solution.py:1514
  95.6 21.5 %collective-permute-start.6 = (bf16[512,1024]{1,0:T(8,128)(2,1)S(1)}, bf16[512,1024]{1,0:T(8,128)(2,1)}, u32[]{:S(2)}, u32[]{:S(2)}) collective-permute-start(bf16[512,1024]{1,0:T(8,128)(2,1)S(1)} %collective-permute-done.1.refs_2_), channel_id=1, source_target_pairs={{0,4},{4,0},{8,12},{12,8},{16,20},{20,16},{24,28},{28,24},{1,5},{5... | collective-permute-start | bytes 3145736 | tf_op jit(solution)/shard_map/ppermute | solution.py:1514
  95.7 19.5 %all-to-all-start = ((bf16[8,128,256]{2,1,0:T(8,128)(2,1)}), bf16[8,128,256]{2,1,0:T(8,128)(2,1)}, u32[]{:S(2)}, u32[]{:S(2)}) async-start(bf16[8,128,256]{2,1,0:T(8,128)(2,1)} %bitcast.57), calls=%async_computation | async-start | bytes 1048576 | tf_op jit(solution)/shard_map/all_to_all | solution.py:1539
  99.8 227.9 %all-gather.5.cloned.1.call-start = ((), (), s32[]{:S(2)}) async-start(), calls=%async_computation.7 | async-start | bytes 4718592 | tf_op jit(solution)/shard_map/all_gather | solution.py:53
  100.1 17.0 %collective-permute-start.7 = (bf16[256,1024]{1,0:T(8,128)(2,1)}, bf16[256,1024]{1,0:T(8,128)(2,1)}, u32[]{:S(2)}, u32[]{:S(2)}) collective-permute-start(bf16[256,1024]{1,0:T(8,128)(2,1)} %collective-permute-done.2.refs_3_), channel_id=1, source_target_pairs={{0,4},{4,0},{8,12},{12,8},{16,20},{20,16},{24,28},{28,24},{1,5},{5... | collective-permute-start | bytes 1572872 | tf_op jit(solution)/shard_map/ppermute | solution.py:1514
  100.5 16.6 %collective-permute-start.8 = (bf16[256,1024]{1,0:T(8,128)(2,1)}, bf16[256,1024]{1,0:T(8,128)(2,1)}, u32[]{:S(2)}, u32[]{:S(2)}) collective-permute-start(bf16[256,1024]{1,0:T(8,128)(2,1)} %collective-permute-done.3.refs_4_), channel_id=1, source_target_pairs={{0,4},{4,0},{8,12},{12,8},{16,20},{20,16},{24,28},{28,24},{1,5},{5... | collective-permute-start | bytes 1572872 | tf_op jit(solution)/shard_map/ppermute | solution.py:1514
  209.1 179.5 %reduce-scatter.3.cloned.1.call-start = ((), (), s32[]{:S(2)}) async-start(), calls=%async_computation.6 | async-start | bytes 9437184 | tf_op jit(solution)/shard_map/reduce_scatter | solution.py:1569
  305.1 22.6 %all-to-all-start.2 = ((bf16[8,128,256]{2,1,0:T(8,128)(2,1)}), bf16[8,128,256]{2,1,0:T(8,128)(2,1)S(1)}, u32[]{:S(2)}, u32[]{:S(2)}) async-start(bf16[8,128,256]{2,1,0:T(8,128)(2,1)} %get-tuple-element.108), calls=%async_computation.3 | async-start | bytes 1048576 | tf_op jit(solution)/shard_map/all_to_all | solution.py:1577
  308.9 118.9 %reduce-scatter.5.cloned.1.call-start = ((), (), s32[]{:S(2)}) async-start(), calls=%async_computation.8 | async-start | bytes 5242880 | tf_op jit(solution)/shard_map/reduce_scatter | solution.py:57
  327.7 0.8 copy-start.4
  388.6 3.3 copy-start.9
  391.8 32.9 %collective-permute-start.9 = (bf16[3,1024,256]{2,1,0:T(8,128)(2,1)}, bf16[3,1024,256]{2,1,0:T(8,128)(2,1)S(1)}, u32[]{:S(2)}, u32[]{:S(2)}) collective-permute-start(bf16[3,1024,256]{2,1,0:T(8,128)(2,1)} %get-tuple-element.133), channel_id=1, source_target_pairs={{0,4},{4,0},{8,12},{12,8},{16,20},{20,16},{24,28},{28,24},{1,5},{5... | collective-permute-start | bytes 4718600 | tf_op jit(solution)/shard_map/ppermute | solution.py:1584
  391.9 15.1 %copy-start.7 = (f32[8,2048]{1,0:T(8,128)S(1)}, f32[8,2048]{1,0:T(8,128)}, u32[]{:S(2)}) copy-start(f32[8,2048]{1,0:T(8,128)} %get-tuple-element.103) | copy-start | bytes 196612
  424.7 3.0 copy-start.3
  427.8 3.0 slice-start
Sparse Core Ops, SparseCore 0:
  11.0 61.4 all-gather.2
  209.2 46.1 all-gather.4
  257.7 92.6 reduce-scatter.2
  353.4 55.5 reduce-scatter.4

commit v5 on v4

--- a/solution.py
+++ b/solution.py
@@ -1065,20 +1065,55 @@
 SPAN = 256
 
 
+def ctx_peers(n_ctx):
+    ctx = lax.axis_index("ctx")
+    fsdp = lax.axis_index("fsdp")
+    return [((ctx + j) % n_ctx, fsdp) for j in range(1, n_ctx)]
+
+
+def deal(n_ctx, block, target, landed, sems, own_sem):
+    ctx = lax.axis_index("ctx")
+    fsdp = lax.axis_index("fsdp")
+
+    @pl.when(target != ctx)
+    def _():
+        send(block, landed.at[ctx], sems, (target - ctx + n_ctx) % n_ctx, (target, fsdp)).start()
+
+    @pl.when(target == ctx)
+    def _():
+        pltpu.make_async_copy(block, landed.at[ctx], own_sem).start()
+
+
+def dealt(n_ctx, block, landed, sems, own_sem):
+    ctx = lax.axis_index("ctx")
+    pltpu.make_async_copy(block, landed.at[ctx], own_sem).wait()
+    for j, peer in enumerate(ctx_peers(n_ctx)):
+        copy = send(block, landed.at[(ctx + n_ctx - j - 1) % n_ctx], sems, j + 1, peer)
+        copy.wait_send()
+        copy.wait_recv()
+
+
 def turn(values, cosine, sine):
     return values * cosine + pltpu.roll(values, HEAD_DIM // 2, 1) * sine
 
 
-def attention_forward(rows, w_qkv, cosine, sine, place_column, place_row, heads):
+def attention_forward(n_ctx, rows, w_qkv, cosine, sine, place_column, place_row, heads):
     total, features = rows.shape
     own = heads * HEAD_DIM
     steps = total // SPAN
+    length = total // n_ctx
     scale = HEAD_DIM ** (-0.5)
 
     def kernel(
-        rows_ref, w_ref, cosine_ref, sine_ref, column_ref, row_ref, query_ref, key_ref, value_ref, out_ref, log_ref
+        rows_ref, w_ref, cosine_ref, sine_ref, column_ref, row_ref,
+        query_ref, key_ref, value_ref, out_ref, log_ref, landed, deal_s, deal_r, own_sem,
     ):
         step = pl.program_id(0)
+
+        @pl.when(step == 0)
+        def _():
+            greet(ctx_peers(n_ctx))
+
         span = pl.ds(pl.multiple_of(step * SPAN, SPAN), SPAN)
         qkv = mm(rows_ref[...], w_ref[...])
         cosine = cosine_ref[span]
@@ -1091,12 +1126,11 @@
 
         @pl.when(step == steps - 1)
         def _():
-            for h in range(heads):
-                at = slice(h * HEAD_DIM, (h + 1) * HEAD_DIM)
-
-                @pl.loop(0, steps)
-                def _(block):
-                    here = pl.ds(pl.multiple_of(block * SPAN, SPAN), SPAN)
+            @pl.loop(0, steps)
+            def _(block):
+                here = pl.ds(pl.multiple_of(block * SPAN, SPAN), SPAN)
+                for h in range(heads):
+                    at = slice(h * HEAD_DIM, (h + 1) * HEAD_DIM)
                     scores = mm(query_ref[here, at], key_ref[:, at], CONTRACT_LAST) * scale
                     scores = jnp.where(column_ref[here] >= row_ref[...], scores, MASKED)
                     highest = jnp.max(scores, axis=-1, keepdims=True)
@@ -1104,6 +1138,11 @@
                     sums = jnp.sum(exponent, axis=-1, keepdims=True)
                     out_ref[here, at] = low(mm(low(exponent * (1.0 / sums)), value_ref[:, at]))
                     log_ref[h, here] = highest + jnp.log(sums)
+                for r in range(SPAN // length):
+                    mine = out_ref.at[pl.ds(pl.multiple_of(block * SPAN + r * length, length), length)]
+                    deal(n_ctx, mine, block * (SPAN // length) + r, landed, (deal_s, deal_r), own_sem)
+
+            dealt(n_ctx, out_ref.at[pl.ds(0, length)], landed, (deal_s, deal_r), own_sem)
 
     act = jax.ShapeDtypeStruct((total, own), jnp.bfloat16)
     return pl.pallas_call(
@@ -1111,9 +1150,14 @@
         grid=(steps,),
         in_specs=[pl.BlockSpec((SPAN, features), lambda r: (r, 0))]
         + [whole_block(a.shape) for a in (w_qkv, cosine, sine, place_column, place_row)],
-        out_specs=[whole_block((total, own))] * 4 + [whole_block((heads, total, 1))],
-        out_shape=[act] * 4 + [jax.ShapeDtypeStruct((heads, total, 1), jnp.float32)],
-        compiler_params=params(),
+        out_specs=[whole_block((total, own))] * 4 + [whole_block((heads, total, 1))] + any_specs(1),
+        out_shape=[act] * 4
+        + [
+            jax.ShapeDtypeStruct((heads, total, 1), jnp.float32),
+            jax.ShapeDtypeStruct((n_ctx, length, own), jnp.bfloat16),
+        ],
+        scratch_shapes=dma_pair(n_ctx) + [pltpu.SemaphoreType.DMA],
+        compiler_params=params(8),
         name="attention_forward",
     )(rows, w_qkv, cosine, sine, place_column, place_row)
 
@@ -1239,6 +1283,7 @@
 def connect_middle(streams, coef, attended, w_mine, w_other, cotangent, dynamic, static, core_fsdp, where, depth):
     number, rows, features = streams.shape
     half = features // 2
+    own = attended.shape[2]
     count = len(w_mine)
 
     def kernel(core_ref, streams_ref, coef_ref, attended_ref, *refs):
@@ -1252,9 +1297,9 @@
             for side in range(2):
                 total = 0.0
                 for j, (d, offset) in enumerate(where):
-                    size = w_mine[j].shape[0]
-                    columns = pl.ds(pl.multiple_of((core_ref[1] ^ d) * depth + offset, size), size)
-                    total = total + mm(attended_ref[:, columns], weights[side * count + j][...])
+                    for q in range(w_mine[j].shape[0] // own):
+                        part = attended_ref[(core_ref[1] ^ d) * (depth // own) + offset // own + q]
+                        total = total + mm(part, weights[side * count + j][q * own : (q + 1) * own])
                 projected[core_ref[0] if side == 0 else 1 - core_ref[0]] = total
 
         span = pl.ds(pl.multiple_of(step * ROWS, ROWS), ROWS)
@@ -1336,38 +1381,51 @@
     )(rows, grads, attended, grad_cols)
 
 
-def project_back(grad, w_mine, w_other, core_fsdp, n_ctx, where, depth):
+def flip(index, bits, count):
+    result = index
+    bit = 1
+    while bit < count:
+        if bits & bit:
+            result = result + bit - 2 * bit * (index // bit % 2)
+        bit *= 2
+    return result
+
+
+def project_back(n_ctx, n_fsdp, grad, w_mine, w_other, where, depth):
     rows, features = grad.shape
     half = features // 2
     count = len(w_mine)
     own = features // n_ctx
 
-    def kernel(core_ref, grad_ref, *refs):
-        weights, (out_ref, cols_ref) = refs[: 2 * count], refs[2 * count :]
-        first = grad_ref[:, pl.ds(pl.multiple_of(core_ref[0] * half, half), half)]
-        second = grad_ref[:, pl.ds(pl.multiple_of((1 - core_ref[0]) * half, half), half)]
+    def kernel(grad_ref, *refs):
+        weights, refs = refs[: 2 * count], refs[2 * count :]
+        landed, cols_ref, outs, deal_s, deal_r, own_sem = refs
+        _, core, fsdp, _ = place(n_ctx)
+        greet(ctx_peers(n_ctx))
+        first = grad_ref[:, pl.ds(pl.multiple_of(core * half, half), half)]
+        second = grad_ref[:, pl.ds(pl.multiple_of((1 - core) * half, half), half)]
         for j, (d, offset) in enumerate(where):
             out = low(
                 mm(first, weights[j][...], CONTRACT_LAST) + mm(second, weights[count + j][...], CONTRACT_LAST)
             )
             for q in range(w_mine[j].shape[0] // own):
-                at = (core_ref[1] ^ d) * (depth // own) + offset // own + q
-                out_ref[at] = out[:, q * own : (q + 1) * own]
+                at = flip(fsdp, d, n_fsdp) * (depth // own) + offset // own + q
+                outs[at] = out[:, q * own : (q + 1) * own]
+                deal(n_ctx, outs.at[at], at, landed, (deal_s, deal_r), own_sem)
         for index in range(n_ctx):
             cols_ref[index] = grad_ref[:, index * own : (index + 1) * own]
-
+        dealt(n_ctx, outs.at[0], landed, (deal_s, deal_r), own_sem)
+
+    shape = (n_ctx, rows, own)
     return pl.pallas_call(
         kernel,
-        grid_spec=pltpu.PrefetchScalarGridSpec(
-            num_scalar_prefetch=1,
-            grid=(1,),
-            in_specs=[whole_block(a.shape) for a in [grad] + w_mine + w_other],
-            out_specs=[whole_block((n_ctx, rows, own))] * 2,
-        ),
-        out_shape=[jax.ShapeDtypeStruct((n_ctx, rows, own), grad.dtype)] * 2,
-        compiler_params=params(),
+        in_specs=[pl.BlockSpec(memory_space=pltpu.VMEM)] * (1 + 2 * count),
+        out_specs=any_specs(1) + [pl.BlockSpec(memory_space=pltpu.VMEM)],
+        out_shape=[jax.ShapeDtypeStruct(shape, grad.dtype)] * 2,
+        scratch_shapes=[pltpu.VMEM(shape, grad.dtype)] + dma_pair(n_ctx) + [pltpu.SemaphoreType.DMA],
+        compiler_params=params(9),
         name="project_back",
-    )(core_fsdp, grad, *w_mine, *w_other)
+    )(grad, *w_mine, *w_other)
 
 
 def connect_back(values, coef, dyn, branch, grads, grad_normed, dynamic, coef_before=None, offset=0):
@@ -1527,16 +1585,20 @@
     w_out_mine = exchange(w_half, 2 if n_fsdp == 4 else 0)
     attn_all = line_rows(n_ctx, attn_low).reshape(rows, features)
     w_out_where = [(d, 0) for d in range(len(w_out_mine))]
+    attn_all, *w_out_mine = lax.optimization_barrier((attn_all, *w_out_mine))
+    w_out_other = swap(w_out_mine)
     if n_fsdp == 4:
-        attn_all, *w_out_mine = lax.optimization_barrier((attn_all, *w_out_mine))
         middle = own_rows // 2
-        w_out_mine.append(lax.ppermute(w_out_mine[1][:middle], "fsdp", [(i, i ^ 2) for i in range(4)]))
-        w_out_mine.append(lax.ppermute(w_out_mine[2][middle:], "fsdp", [(i, i ^ 1) for i in range(4)]))
+        corners = [
+            lax.ppermute(w_out_mine[1][:middle], "fsdp", [(i, i ^ 2) for i in range(4)]),
+            lax.ppermute(w_out_mine[2][middle:], "fsdp", [(i, i ^ 1) for i in range(4)]),
+        ]
         w_out_where += [(3, 0), (3, middle)]
-    query, key, value, attended, logs = attention_forward(attn_all, w_qkv, *tables, heads)
-    attended, w_out_mine = lax.optimization_barrier((attended, w_out_mine))
-    w_out_other = swap(w_out_mine)
-    attended_rows = lax.all_to_all(attended, "ctx", 0, 1, tiled=True)
+    query, key, value, attended, logs, attended_rows = attention_forward(n_ctx, attn_all, w_qkv, *tables, heads)
+    if n_fsdp == 4:
+        attended, *corners = lax.optimization_barrier((attended, *corners))
+        w_out_mine += corners
+        w_out_other += swap(corners)
 
     first_out, attn_branch, coef_two, dyn_two, ffn_own = connect_middle(
         streams[0], coef_one, attended_rows, w_out_mine, w_out_other, cotangent[0], dynamics[1], statics[1], core_fsdp,
@@ -1571,8 +1633,8 @@
     grad_first, dynamic_grad_two, static_grad_two, streams_out, grad_attn = connect_back(
         first_out, coef_two, dyn_two, sums, cotangent[0], sums, dynamics[1], coef_one, length
     )
-    grad_heads, grad_cols = project_back(grad_attn, w_out_mine, w_out_other, core_fsdp, n_ctx, w_out_where, own_rows)
-    grad_heads = lax.all_to_all(grad_heads, "ctx", 0, 0, tiled=True).reshape(rows, own)
+    grad_heads, grad_cols = project_back(n_ctx, n_fsdp, grad_attn, w_out_mine, w_out_other, w_out_where, own_rows)
+    grad_heads = grad_heads.reshape(rows, own)
     grad_heads, grad_cols = lax.optimization_barrier((grad_heads, grad_cols))
     grad_cols = lax.all_to_all(grad_cols, "ctx", 0, 0, tiled=True).reshape(rows, own)
     qkv_grad, attn_part = attention_backward(query, key, value, grad_heads, logs, w_qkv, *tables, heads)

time: 448 us -> 438 us (0.978)
  Pallas kernels: 336 us -> 371 us
  blocking collectives: 24.4 us -> 0 us
  waiting for transfers between devices: 14.5 us -> 2.59 us
    all_to_all x1 -> x0, blocking collectives: 24.4 us -> none  [local(): lax.all_to_all(grad_heads, 'ctx', 0, 0, tiled=True).reshape(rows, own)]
    pallas_call x1, Pallas kernels: 8.28 us -> 25.2 us  [project_back(): pl.pallas_call(kernel, in_specs=[pl.BlockSpec(memory_space=pltpu.VMEM)] *...]
    all_to_all x1 -> x0, waiting for transfers between devices: 14 us -> none  [local(): attended_rows = lax.all_to_all(attended, 'ctx', 0, 1, tiled=True)]
    pallas_call x1, Pallas kernels: 15.4 us -> 22.1 us  [attention_forward(): pl.pallas_call(kernel, grid=(steps,), in_specs=[pl.BlockSpec((SPAN, featu...]
    pallas_call x1, Pallas kernels: 78.3 us -> 83.8 us  [ffn_rows(): pl.pallas_call(kernel, in_specs=any_specs(2), out_specs=any_specs(6), out...]
    pallas_call x1, Pallas kernels: 49.1 us -> 53.8 us  [line_sum(): pl.pallas_call(kernel, out_shape=jax.ShapeDtypeStruct((rows, columns), jn...]
  transfers between devices with their start and end apart: 16 -> 15, of which waited for: 2 -> 3; matrix products, arithmetic and copies ran while one was open for 6% -> 5% of each run, Pallas kernels for 56% -> 63%
where the time goes in v5:
time: 438 us; the launch traced here: 433 us
  Pallas kernels  371 us (85%)
  local copies, waits for them, and re-layouts  24.1 us (6%)
  between operations  14.3 us (3%)
  starting transfers between devices  12.6 us (3%)
  other arithmetic  7.81 us (2%)
    pallas_call x1, Pallas kernels, ffn_rows(): pl.pallas_call(kernel, in_specs=any_specs(2), out_specs=any_specs(6), out...  83.8 us
    pallas_call x1, Pallas kernels, line_sum(): pl.pallas_call(kernel, out_shape=jax.ShapeDtypeStruct((rows, columns), jn...  53.8 us
    pallas_call x1, Pallas kernels, ffn_weights(): pl.pallas_call(kernel, grid=(steps,), in_specs=in_specs, out_specs=out_sp...  46.7 us
    pallas_call x1, Pallas kernels, line_rows(): pl.pallas_call(kernel, out_shape=jax.ShapeDtypeStruct((n_ctx,) + rows.sha...  43 us
    pallas_call x2, Pallas kernels, connect_back(): pl.pallas_call(kernel, grid=(steps,), in_specs=in_specs, out_specs=out_sp...  31.3 us
    pallas_call x1, Pallas kernels, project_back(): pl.pallas_call(kernel, in_specs=[pl.BlockSpec(memory_space=pltpu.VMEM)] *...  25.2 us
    pallas_call x1, Pallas kernels, attention_forward(): pl.pallas_call(kernel, grid=(steps,), in_specs=[pl.BlockSpec((SPAN, featu...  22.1 us
    pallas_call x1, Pallas kernels, attention_backward(): pl.pallas_call(kernel, grid=(steps,), in_specs=[whole_block(a.shape) for...  18.3 us
  transfers between devices with their start and end apart: 15, of which 3 were waited for; matrix products, arithmetic and copies ran while one was open for 5% of the time, Pallas kernels for 63%

profile of v5, /device:TPU:0, one launch (start us, length us, event | category | flops | bytes accessed | tf_op | source)
XLA Modules:
  0.0 432.6 jit_solution(12132392681465325246)
XLA Ops:
  7.2 1.6 constant_dynamic-slice_fusion.2
  8.8 0.9 copy.26
  9.7 1.2 copy.19
  11.0 5.8 %constant_dynamic-slice_fusion.3 = bf16[512,1,1024]{2,1,0:T(2,128)(2,1)S(1)} fusion(bf16[512,4,2048]{2,1,0:T(4,128)(2,1)} %param.8, s32[]{:T(128)S(6)} %add.65, s32[]{:T(128)S(6)} %select_n.36), kind=kLoop, calls=%fused_computation.26 | loop fusion | bytes 2097160 | tf_op jit(solution)/shard_map/slice | solution.py:1561
  16.8 0.4 copy.28
  17.3 0.7 fusion.4
  18.0 0.7 fusion.2
  18.6 6.5 %connect_first.1 = (f32[4,128,8]{2,1,0:T(8,128)}, f32[4,128,8]{2,1,0:T(8,128)}, bf16[128,2048]{1,0:T(8,128)(2,1)}) custom-call(bf16[4,128,2048]{2,1,0:T(8,128)(2,1)} %bitcast.36, f32[8,2048]{1,0:T(8,128)} %get-tuple-element.125.dynamic_ref.refs_6_, f32[4,8]{1,0:T(4,128)} %get-tuple-element.129.static_ref), custom_call_target="tpu_custom_call" | custom-call | tf_op jit(solution)/shard_map/connect_first/pallas_call | solution.py:1268
  25.1 3.0 collective-permute-start
  28.1 1.5 collective-permute-start.1
  29.6 43.0 %line_rows.1 = bf16[8,128,2048]{2,1,0:T(8,128)(2,1)} custom-call(bf16[128,2048]{1,0:T(8,128)(2,1)} %get-tuple-element.59.rows_ref), custom_call_target="tpu_custom_call" | custom-call | tf_op jit(solution)/shard_map/line_rows/pallas_call | solution.py:271
  72.7 0.9 slice.49
  73.6 0.4 collective-permute-start.5
  74.0 0.8 slice.50
  74.8 0.1 collective-permute-start.6
  75.0 0.5 collective-permute-start.2
  75.5 0.5 collective-permute-start.3
  76.1 1.1 copy.20.column_ref
  77.2 3.1 fusion
  80.3 22.1 %attention_forward.1 = (bf16[1024,256]{1,0:T(8,128)(2,1)}, bf16[1024,256]{1,0:T(8,128)(2,1)}, bf16[1024,256]{1,0:T(8,128)(2,1)}, bf16[1024,256]{1,0:T(8,128)(2,1...) custom-call(bf16[1024,2048]{1,0:T(8,128)(2,1)} %bitcast.39, ...), custom_call_target="tpu_custom_call" | custom-call | tf_op jit(solution)/shard_map/attention_forward/pallas_call | solution.py:1148
  102.5 1.3 collective-permute-start.7
  103.8 0.1 collective-permute-start.8
  103.8 0.6 pad_add_fusion.1.core_ref
  104.4 1.2 collective-permute-done.7.refs_8_
  105.6 0.7 collective-permute-done.8.refs_9_
  106.4 13.6 %connect_middle.1 = (f32[4,128,2048]{2,1,0:T(8,128)}, f32[128,2048]{1,0:T(8,128)}, f32[4,128,8]{2,1,0:T(8,128)}, f32[4,128,8]{2,1,0:T(8,128)}, bf16[2,128,2048]{2,1,0:T(8,128)(2,1)}) custom-call(s32[2]{0:T(128)} %pad_add_fusion.1.core_ref, bf16[4,128,2048]{2,1,0:T(8,128)(2,1)} %bitcast.37, f32[4,128,8]{2,1,0:T(8,128)} %get-tuple-element.57.coef_ref.refs_7_.refs_1_, ...), custom_call_target="tpu_custom_call" | custom-call | tf_op jit(solution)/shard_map/connect_middle/pallas_call | solution.py:1321
  120.0 83.8 %ffn_rows.1 = (bf16[2,4,256,2048]{3,2,1,0:T(8,128)(2,1)}, bf16[2,4,256,2048]{3,2,1,0:T(8,128)(2,1)}, bf16[1024,1024]{1,0:T(8,128)(2,1)}, bf16[1024,1024]{1,0:T(8...) custom-call(bf16[256,2048]{1,0:T(8,128)(2,1)} %bitcast.63, bf16[3,2048,2048]{2,1,0:T(8,128)(2,1)} %bitcast.58), custom_call_target="tpu_custom_call" | custom-call | flops 25769803776 | bytes 52428800 | tf_op jit(solution)/shard_map/ffn_rows/pallas_call | solution.py:905
  203.9 46.7 %ffn_weights.1 = (bf16[2,3,1024,512]{3,2,1,0:T(8,128)(2,1)}, f32[256,2048]{1,0:T(8,128)}) custom-call(bf16[8,2,128,2048]{3,2,1,0:T(8,128)(2,1)} %bitcast.64, bf16[8,2,128,2048]{3,2,1,0:T(8,128)(2,1)} %bitcast.65, bf16[1024,1024]{1,0:T(8,128)(2,1)} %get-tuple-element.75.refs_2_, bf16[1024,1024]{1,0:T(8,128)(2,1)} %get-tuple-element.76.refs_3_, ...), custom_call_target="tpu_custom_call" | custom-call | flops 25769803776 | bytes 52428800 | tf_op jit(solution)/shard_map/ffn_weights/pallas_call | solution.py:1018
  250.6 17.0 %connect_back.2 = (f32[4,128,2048]{2,1,0:T(8,128)}, f32[8,2048]{1,0:T(8,128)}, f32[8,8]{1,0:T(8,128)}, bf16[4,128,2048]{2,1,0:T(8,128)(2,1)}, bf16[128,2048]{1,0:T(8,128)(2,1)}) custom-call(f32[4,128,2048]{2,1,0:T(8,128)} %get-tuple-element.69.refs_0_, f32[4,128,8]{2,1,0:T(8,128)} %get-tuple-element.70.refs_1_, f32[4,128,8]{2,1,0:T(8,128)} %get-tuple-element.71.refs_2_, ...), custom_call_target="tpu_custom_call" | custom-call | tf_op jit(solution)/shard_map/connect_back/pallas_call | solution.py:1525
  267.6 25.2 %project_back.1 = (bf16[8,128,256]{2,1,0:T(8,128)(2,1)}, bf16[8,128,256]{2,1,0:T(8,128)(2,1)}) custom-call(bf16[128,2048]{1,0:T(8,128)(2,1)} %get-tuple-element.89.grad_ref, bf16[512,1024]{1,0:T(8,128)(2,1)} %bitcast.45, bf16[512,1024]{1,0:T(8,128)(2,1)} %copy-done.1, bf16[512,1024]{1,0:T(8,128)(2,1)} %copy-done.2, ...), custom_call_target="tpu_custom_call" | custom-call | tf_op jit(solution)/shard_map/project_back/pallas_call | solution.py:1420
  292.8 5.1 %all-to-all-start = ((bf16[8,128,256]{2,1,0:T(8,128)(2,1)}), bf16[8,128,256]{2,1,0:T(8,128)(2,1)S(1)}, u32[]{:S(2)}, u32[]{:S(2)}) async-start(bf16[8,128,256]{2,1,0:T(8,128)(2,1)} %get-tuple-element.104), calls=%async_computation.1 | async-start | bytes 1048576 | tf_op jit(solution)/shard_map/all_to_all | solution.py:1639
  297.9 18.3 %attention_backward.1 = (bf16[1024,768]{1,0:T(8,128)(2,1)}, bf16[1024,2048]{1,0:T(8,128)(2,1)}) custom-call(bf16[1024,256]{1,0:T(8,128)(2,1)} %get-tuple-element.86.query_ref, bf16[1024,256]{1,0:T(8,128)(2,1)} %get-tuple-element.87.key_ref, bf16[1024,256]{1,0:T(8,128)(2,1)} %get-tuple-element.88.value_ref, bf16[1024,256]{1,0:T(8,128)(2,1)} %bitcast.51, ...), custom_call_target="tpu_custom_call" | custom-call | tf_op jit(solution)/shard_map/attention_backward/pallas_call | solution.py:1208
  316.2 0.5 all-to-all-done
  316.8 0.8 copy-done.4
  317.6 11.0 %attention_weights.1 = bf16[2048,1024]{1,0:T(8,128)(2,1)} custom-call(bf16[1024,2048]{1,0:T(8,128)(2,1)} %bitcast.40, bf16[1024,768]{1,0:T(8,128)(2,1)} %get-tuple-element.102.grads_ref, bf16[8,1024,256]{2,1,0:T(8,128)(2,1)} %bitcast.60, bf16[1024,256]{1,0:T(8,128)(2,1)} %bitcast.52), custom_call_target="tpu_custom_call" | custom-call | flops 4294967296 | bytes 16777216 | tf_op jit(solution)/shard_map/attention_weights/pallas_call | solution.py:1365
  328.6 53.8 %line_sum.1.refs_5_ = f32[128,2048]{1,0:T(8,128)} custom-call(bf16[8,128,2048]{2,1,0:T(8,128)(2,1)} %bitcast.48), custom_call_target="tpu_custom_call" | custom-call | tf_op jit(solution)/shard_map/line_sum/pallas_call | solution.py:590
  382.4 3.2 constant_dynamic-slice_fusion.1
  385.7 0.1 reshape.93
  385.8 14.3 %connect_back.3 = (f32[4,128,2048]{2,1,0:T(8,128)}, f32[8,2048]{1,0:T(8,128)}, f32[8,8]{1,0:T(8,128)}) custom-call(bf16[4,128,2048]{2,1,0:T(8,128)(2,1)} %bitcast.38, f32[4,128,8]{2,1,0:T(8,128)} %get-tuple-element.57.coef_ref.refs_7_.refs_1_, f32[4,128,8]{2,1,0:T(8,128)} %get-tuple-element.83.refs_2_, f32[128,2048]{1,0:T(8,128)} %get-tuple-element.84.refs_3_, ...), custom_call_target="tpu_custom_call" | custom-call | tf_op jit(solution)/shard_map/connect_back/pallas_call | solution.py:1525
  400.1 0.7 slice.55
  400.8 0.1 reshape.92
  400.9 0.9 pad_maximum_fusion
  401.8 0.7 reshape.94.values_ref
  402.4 15.9 %sum_everywhere.1 = f32[8,8,512]{2,1,0:T(8,128)} custom-call(f32[8,8,512]{2,1,0:T(8,128)} %reshape.94.values_ref), custom_call_target="tpu_custom_call" | custom-call | tf_op jit(solution)/shard_map/sum_everywhere/pallas_call | solution.py:652
  418.3 3.0 convert_bitcast_fusion
  421.4 3.0 reshape.103
  424.4 0.7 copy.22
  425.2 0.7 reshape.101
  (56 shorter events, 0.8 us)
Async XLA Ops:
  7.2 73.1 %all-gather.3.cloned.1.call-start = ((), (), s32[]{:S(2)}) async-start(), calls=%async_computation.3 | async-start | bytes 3932160 | tf_op jit(solution)/shard_map/all_gather | solution.py:53
  10.9 305.9 %all-gather.5.cloned.1.call-start = ((), (), s32[]{:S(2)}) async-start(), calls=%async_computation.5 | async-start | bytes 4718592 | tf_op jit(solution)/shard_map/all_gather | solution.py:53
  11.0 6.2 %copy-start.5 = (f32[2,6,2048]{2,0,1:T(2,128)S(1)}, f32[2,6,2048]{2,0,1:T(2,128)}, u32[]{:S(2)}) copy-start(f32[2,6,2048]{2,0,1:T(2,128)} %param.10) | copy-start | bytes 294916
  11.0 6.3 %copy-start.8 = (f32[2,4,6]{2,1,0:T(4,128)S(1)}, f32[2,4,6]{2,1,0:T(4,128)}, u32[]{:S(2)}) copy-start(f32[2,4,6]{2,1,0:T(4,128)} %param.11) | copy-start | bytes 580
  17.2 58.8 %copy-start = (bf16[512,1,1024]{2,0,1:T(8,128)(2,1)}, bf16[512,1,1024]{2,0,1:T(8,128)(2,1)S(1)}, u32[]{:S(2)}) copy-start(bf16[512,1,1024]{2,0,1:T(8,128)(2,1)S(1)} %copy.28) | copy-start | bytes 3145732
  18.6 54.0 %copy-start.10 = (s32[8]{0:T(128)S(1)}, s32[8]{0:T(128)}, u32[]{:S(2)}) copy-start(s32[8]{0:T(128)} %param.13) | copy-start | bytes 100
  25.1 47.6 %collective-permute-start = (bf16[512,1024]{1,0:T(8,128)(2,1)S(1)}, bf16[512,1024]{1,0:T(8,128)(2,1)S(1)}, u32[]{:S(2)}, u32[]{:S(2)}) collective-permute-start(bf16[512,1024]{1,0:T(8,128)(2,1)S(1)} %bitcast.41), channel_id=1, source_target_pairs={{0,1},{1,0},{2,3},{3,2},{4,5},{5,4},{6,7},{7,6},{8,9},{9,8},{10,11... | collective-permute-start | bytes 3145736 | tf_op jit(solution)/shard_map/ppermute | solution.py:1567
  28.1 44.6 %collective-permute-start.1 = (bf16[512,1024]{1,0:T(8,128)(2,1)S(1)}, bf16[512,1024]{1,0:T(8,128)(2,1)S(1)}, u32[]{:S(2)}, u32[]{:S(2)}) collective-permute-start(bf16[512,1024]{1,0:T(8,128)(2,1)S(1)} %bitcast.42), channel_id=1, source_target_pairs={{0,2},{1,3},{2,0},{3,1},{4,6},{5,7},{6,4},{7,5},{8,10},{9,11},{10,... | collective-permute-start | bytes 3145736 | tf_op jit(solution)/shard_map/ppermute | solution.py:1567
  72.7 29.7 %copy-start.1 = (bf16[512,1024]{1,0:T(8,128)(2,1)}, bf16[512,1024]{1,0:T(8,128)(2,1)S(1)}, u32[]{:S(2)}) copy-start(bf16[512,1024]{1,0:T(8,128)(2,1)S(1)} %collective-permute-done.refs_1_) | copy-start | bytes 3145732
  72.7 29.7 %copy-start.2 = (bf16[512,1024]{1,0:T(8,128)(2,1)}, bf16[512,1024]{1,0:T(8,128)(2,1)S(1)}, u32[]{:S(2)}) copy-start(bf16[512,1024]{1,0:T(8,128)(2,1)S(1)} %collective-permute-done.1.refs_2_) | copy-start | bytes 3145732
  73.6 30.8 %collective-permute-start.5 = (bf16[512,1024]{1,0:T(8,128)(2,1)S(1)}, bf16[512,1024]{1,0:T(8,128)(2,1)}, u32[]{:S(2)}, u32[]{:S(2)}) collective-permute-start(bf16[512,1024]{1,0:T(8,128)(2,1)S(1)} %collective-permute-done.refs_1_), channel_id=1, source_target_pairs={{0,4},{4,0},{8,12},{12,8},{16,20},{20,16},{24,28},{28,24},{1,5},{5... | collective-permute-start | bytes 3145736 | tf_op jit(solution)/shard_map/ppermute | solution.py:1572
  74.8 29.6 %collective-permute-start.6 = (bf16[512,1024]{1,0:T(8,128)(2,1)S(1)}, bf16[512,1024]{1,0:T(8,128)(2,1)}, u32[]{:S(2)}, u32[]{:S(2)}) collective-permute-start(bf16[512,1024]{1,0:T(8,128)(2,1)S(1)} %collective-permute-done.1.refs_2_), channel_id=1, source_target_pairs={{0,4},{4,0},{8,12},{12,8},{16,20},{20,16},{24,28},{28,24},{1,5},{5... | collective-permute-start | bytes 3145736 | tf_op jit(solution)/shard_map/ppermute | solution.py:1572
  75.0 27.5 %collective-permute-start.2 = (bf16[256,1024]{1,0:T(8,128)(2,1)}, bf16[256,1024]{1,0:T(8,128)(2,1)}, u32[]{:S(2)}, u32[]{:S(2)}) collective-permute-start(bf16[256,1024]{1,0:T(8,128)(2,1)} %slice.49), channel_id=1, source_target_pairs={{0,2},{1,3},{2,0},{3,1},{4,6},{5,7},{6,4},{7,5},{8,10},{9,11},{10,... | collective-permute-start | bytes 1572872 | tf_op jit(solution)/shard_map/ppermute | solution.py:1593
  75.5 27.0 %collective-permute-start.3 = (bf16[256,1024]{1,0:T(8,128)(2,1)}, bf16[256,1024]{1,0:T(8,128)(2,1)}, u32[]{:S(2)}, u32[]{:S(2)}) collective-permute-start(bf16[256,1024]{1,0:T(8,128)(2,1)} %slice.50), channel_id=1, source_target_pairs={{0,1},{1,0},{2,3},{3,2},{4,5},{5,4},{6,7},{7,6},{8,9},{9,8},{10,11... | collective-permute-start | bytes 1572872 | tf_op jit(solution)/shard_map/ppermute | solution.py:1594
  76.0 28.4 %collective-permute-start.4 = (bf16[512,1024]{1,0:T(8,128)(2,1)S(1)}, bf16[512,1024]{1,0:T(8,128)(2,1)}, u32[]{:S(2)}, u32[]{:S(2)}) collective-permute-start(bf16[512,1024]{1,0:T(8,128)(2,1)S(1)} %bitcast.43), channel_id=1, source_target_pairs={{0,4},{4,0},{8,12},{12,8},{16,20},{20,16},{24,28},{28,24},{1,5},{5... | collective-permute-start | bytes 3145736 | tf_op jit(solution)/shard_map/ppermute | solution.py:1572
  76.1 4.2 copy-start.6
  102.5 3.2 collective-permute-start.7
  103.8 2.6 collective-permute-start.8
  203.8 178.6 %reduce-scatter.3.cloned.1.call-start = ((), (), s32[]{:S(2)}) async-start(), calls=%async_computation.4 | async-start | bytes 9437184 | tf_op jit(solution)/shard_map/reduce_scatter | solution.py:1631
  292.8 24.0 %all-to-all-start = ((bf16[8,128,256]{2,1,0:T(8,128)(2,1)}), bf16[8,128,256]{2,1,0:T(8,128)(2,1)S(1)}, u32[]{:S(2)}, u32[]{:S(2)}) async-start(bf16[8,128,256]{2,1,0:T(8,128)(2,1)} %get-tuple-element.104), calls=%async_computation.1 | async-start | bytes 1048576 | tf_op jit(solution)/shard_map/all_to_all | solution.py:1639
  297.9 123.5 %reduce-scatter.5.cloned.1.call-start = ((), (), s32[]{:S(2)}) async-start(), calls=%async_computation.6 | async-start | bytes 5242880 | tf_op jit(solution)/shard_map/reduce_scatter | solution.py:57
  316.7 0.8 copy-start.4
  382.4 3.3 copy-start.9
  385.7 32.6 %collective-permute-start.9 = (bf16[3,1024,256]{2,1,0:T(8,128)(2,1)}, bf16[3,1024,256]{2,1,0:T(8,128)(2,1)S(1)}, u32[]{:S(2)}, u32[]{:S(2)}) collective-permute-start(bf16[3,1024,256]{2,1,0:T(8,128)(2,1)} %get-tuple-element.123), channel_id=1, source_target_pairs={{0,4},{4,0},{8,12},{12,8},{16,20},{20,16},{24,28},{28,24},{1,5},{5... | collective-permute-start | bytes 4718600 | tf_op jit(solution)/shard_map/ppermute | solution.py:1646
  385.8 15.1 %copy-start.7 = (f32[8,2048]{1,0:T(8,128)S(1)}, f32[8,2048]{1,0:T(8,128)}, u32[]{:S(2)}) copy-start(f32[8,2048]{1,0:T(8,128)} %get-tuple-element.99) | copy-start | bytes 196612
  418.3 3.0 copy-start.3
  421.4 3.0 slice-start
Sparse Core Ops, SparseCore 0:
  11.0 61.5 all-gather.2
  203.9 45.3 all-gather.4
  251.6 92.6 reduce-scatter.2
  347.4 60.4 reduce-scatter.4

commit v6 on v5

--- a/solution.py
+++ b/solution.py
@@ -446,12 +446,12 @@
         pltpu.make_async_copy(partial_ref.at[fsdp, low_half], held.at[3], load.at[3]),
     ]
 
-    def begin():
-        greet(fsdp_peers(4, ctx, fsdp))
-        for each in copies[:4]:
-            each.start()
-        for each in mine:
-            each.start()
+    starts = [
+        [copies[0].start, copies[1].start],
+        [copies[2].start, mine[1].start],
+        [copies[3].start, mine[0].start],
+        [mine[2].start, mine[3].start],
+    ]
 
     def pass_on():
         for index in range(2):
@@ -477,7 +477,7 @@
         for each in copies:
             each.wait_send()
 
-    return [begin, pass_on, finish]
+    return [starts, pass_on, finish]
 
 
 def corner_sum_scratch(partial):
@@ -522,89 +522,164 @@
     )(partial)
 
 
-def line_sum(n_ctx, partial, collective_id):
+def line_sum_steps(n_ctx, partial_ref, out_ref, held, core_in, right_in, left_in, load, core_sems, right_sems, left_sems):
+    rows = partial_ref.shape[1]
+    where = place(n_ctx)
+    chip, core, fsdp, length = where
+    sibling, right, left = line_peers(*where)
+    order = [(chip + length - 1 - j) % length for j in range(length)]
+    mine, others = [], []
+    for j, owner in enumerate(order):
+        mine.append(pltpu.make_async_copy(partial_ref.at[owner * 2 + core], held.at[owner], load.at[j]))
+        others.append(send(partial_ref.at[owner * 2 + 1 - core], core_in.at[owner], core_sems, j, sibling))
+        others[-1].start()
+        mine[-1].start()
+    yield
+    for j, owner in enumerate(order):
+        mine[j].wait()
+        others[j].wait_recv()
+        add_into(held.at[owner], core_in.at[owner])
+    ways = ((1, right, right_in, right_sems), (-1, left, left_in, left_sems))
+    for step in range(length - 1):
+        for sign, peer, arrived, sems in ways:
+            block = chip + sign * (length - 1 - step)
+            inside = (block >= 0) & (block < length)
+            came = (chip >= 1) if sign > 0 else (chip < length - 1)
+            if step > 0:
+
+                @pl.when(inside & came)
+                def _():
+                    send(held.at[block], arrived.at[step - 1], sems, step - 1, peer).wait_recv()
+                    add_into(held.at[block], arrived.at[step - 1])
+
+            @pl.when(inside)
+            def _():
+                send(held.at[block], arrived.at[step], sems, step, peer).start()
+
+        yield
+    last = length - 2
+    for sign, peer, arrived, sems in ways:
+        came = (chip >= 1) if sign > 0 else (chip < length - 1)
+
+        @pl.when(came)
+        def _():
+            send(held.at[chip], arrived.at[last], sems, last, peer).wait_recv()
+            add_into(held.at[chip], arrived.at[last])
+
+    @pl.loop(0, rows // 64)
+    def _(step):
+        at = pl.ds(pl.multiple_of(step * 64, 64), 64)
+        out_ref[at] = held[chip, at].astype(jnp.float32)
+
+    for step in range(length - 1):
+        for sign, peer, arrived, sems in ways:
+            block = chip + sign * (length - 1 - step)
+
+            @pl.when((block >= 0) & (block < length))
+            def _():
+                send(held.at[block], arrived.at[step], sems, step, peer).wait_send()
+
+    for each in others:
+        each.wait_send()
+
+
+def line_sum_scratch(n_ctx, partial):
     rows, columns = partial.shape[-2:]
     length = n_ctx // 2
-
+    return [
+        pltpu.VMEM((length, rows, columns), partial.dtype),
+        pltpu.VMEM((length, rows, columns), partial.dtype),
+        pltpu.VMEM((length - 1, rows, columns), partial.dtype),
+        pltpu.VMEM((length - 1, rows, columns), partial.dtype),
+        pltpu.SemaphoreType.DMA((length,)),
+    ] + dma_pair(length) * 3
+
+
+def line_sum(n_ctx, partial):
     def kernel(partial_ref, out_ref, held, core_in, right_in, left_in, load, core_s, core_r, right_s, right_r, left_s, left_r):
+        greet(line_peers(*place(n_ctx)))
+        run_all(
+            line_sum_steps(
+                n_ctx, partial_ref, out_ref, held, core_in, right_in, left_in, load,
+                (core_s, core_r), (right_s, right_r), (left_s, left_r),
+            )
+        )
+
+    return pl.pallas_call(
+        kernel,
+        out_shape=jax.ShapeDtypeStruct(partial.shape[-2:], jnp.float32),
+        in_specs=any_specs(1),
+        out_specs=pl.BlockSpec(memory_space=pltpu.VMEM),
+        scratch_shapes=line_sum_scratch(n_ctx, partial),
+        compiler_params=params(5),
+        name="line_sum",
+    )(partial)
+
+
+def attention_sums(n_ctx, partial, rows, grads, attended, grad_cols):
+    total, features = rows.shape
+    parts, _, own = attended.shape
+    wide = grads.shape[1]
+    depth = features // 4
+    weight_shape = jax.ShapeDtypeStruct((4, depth, wide + own), jnp.bfloat16)
+    inputs = (rows, grads, attended, grad_cols)
+
+    def kernel(partial_ref, *refs):
+        inputs_refs, refs = refs[:4], refs[4:]
+        out_ref, weight_ref, rows_v, grads_v, attended_v, cols_v, weights, in_sem, *refs = refs
+        line_refs, refs = refs[:5], refs[5:]
+        core_s, core_r, right_s, right_r, left_s, left_r, *refs = refs
+        held, square_in, load, sq_s, sq_r = refs
         where = place(n_ctx)
         chip, core, fsdp, _ = where
-        sibling, right, left = line_peers(*where)
-        greet([sibling, right, left])
-        order = [(chip + length - 1 - j) % length for j in range(length)]
-        mine, others = [], []
-        for j, owner in enumerate(order):
-            mine.append(pltpu.make_async_copy(partial_ref.at[owner * 2 + core], held.at[owner], load.at[j]))
-            others.append(
-                send(partial_ref.at[owner * 2 + 1 - core], core_in.at[owner], (core_s, core_r), j, sibling)
-            )
-            others[-1].start()
-            mine[-1].start()
-        for j, owner in enumerate(order):
-            mine[j].wait()
-            others[j].wait_recv()
-            add_into(held.at[owner], core_in.at[owner])
-        ways = ((1, right, right_in, (right_s, right_r)), (-1, left, left_in, (left_s, left_r)))
-        for step in range(length - 1):
-            for sign, peer, arrived, sems in ways:
-                block = chip + sign * (length - 1 - step)
-                inside = (block >= 0) & (block < length)
-
-                came = (chip >= 1) if sign > 0 else (chip < length - 1)
-                if step > 0:
-
-                    @pl.when(inside & came)
-                    def _():
-                        send(held.at[block], arrived.at[step - 1], sems, step - 1, peer).wait_recv()
-                        add_into(held.at[block], arrived.at[step - 1])
-
-                @pl.when(inside)
-                def _():
-                    send(held.at[block], arrived.at[step], sems, step, peer).start()
-
-        last = length - 2
-        for sign, peer, arrived, sems in ways:
-            came = (chip >= 1) if sign > 0 else (chip < length - 1)
-
-            @pl.when(came)
-            def _():
-                send(held.at[chip], arrived.at[last], sems, last, peer).wait_recv()
-                add_into(held.at[chip], arrived.at[last])
-
-        @pl.loop(0, rows // 64)
-        def _(step):
-            at = pl.ds(pl.multiple_of(step * 64, 64), 64)
-            out_ref[at] = held[chip, at].astype(jnp.float32)
-
-        for step in range(length - 1):
-            for sign, peer, arrived, sems in ways:
-                block = chip + sign * (length - 1 - step)
-
-                @pl.when((block >= 0) & (block < length))
-                def _():
-                    send(held.at[block], arrived.at[step], sems, step, peer).wait_send()
-
-        for each in others:
-            each.wait_send()
+        loads = [
+            pltpu.make_async_copy(a, b, in_sem.at[j])
+            for j, (a, b) in enumerate(zip(inputs_refs, (rows_v, grads_v, attended_v, cols_v)))
+        ]
+        for each in loads:
+            each.start()
+        greet(line_peers(*where) + fsdp_peers(4, chip * 2 + core, fsdp))
+        line = line_sum_steps(
+            n_ctx, partial_ref, out_ref, *line_refs, (core_s, core_r), (right_s, right_r), (left_s, left_r)
+        )
+        next(line)
+        starts, pass_on, finish = corner_sum_stages(n_ctx, weights, weight_ref, held, square_in, load, (sq_s, sq_r))
+        for each in loads:
+            each.wait()
+        first, second, corner = fsdp_neighbours(fsdp)
+        for number, owner in enumerate((corner, first, second, fsdp)):
+            at = pl.ds(pl.multiple_of(owner * depth, depth), depth)
+            weights[owner, :, :wide] = low(mm(rows_v[:, at], grads_v[...], CONTRACT_FIRST))
+            for q in range(depth // own):
+                weights[owner, q * own : (q + 1) * own, wide:] = low(
+                    mm(attended_v[owner * (depth // own) + q], cols_v[...], CONTRACT_FIRST)
+                )
+            for start in starts[number]:
+                start()
+            if number < 2:
+                next(line)
+        pass_on()
+        run_all(line)
+        finish()
 
     return pl.pallas_call(
         kernel,
-        out_shape=jax.ShapeDtypeStruct((rows, columns), jnp.float32),
-        in_specs=any_specs(1),
-        out_specs=pl.BlockSpec(memory_space=pltpu.VMEM),
-        scratch_shapes=[
-            pltpu.VMEM((length, rows, columns), partial.dtype),
-            pltpu.VMEM((length, rows, columns), partial.dtype),
-            pltpu.VMEM((length - 1, rows, columns), partial.dtype),
-            pltpu.VMEM((length - 1, rows, columns), partial.dtype),
-            pltpu.SemaphoreType.DMA((length,)),
-        ]
-        + dma_pair(length)
-        + dma_pair(length)
-        + dma_pair(length),
-        compiler_params=params(collective_id),
-        name="line_sum",
-    )(partial)
+        out_shape=[
+            jax.ShapeDtypeStruct(partial.shape[-2:], jnp.float32),
+            jax.ShapeDtypeStruct(weight_shape.shape[1:], jnp.float32),
+        ],
+        in_specs=any_specs(5),
+        out_specs=[pl.BlockSpec(memory_space=pltpu.VMEM)] * 2,
+        scratch_shapes=[pltpu.VMEM(a.shape, a.dtype) for a in inputs]
+        + [pltpu.VMEM(weight_shape.shape, weight_shape.dtype), pltpu.SemaphoreType.DMA((4,))]
+        + line_sum_scratch(n_ctx, partial)
+        + corner_sum_scratch(weight_shape),
+        compiler_params=params(4),
+        cost_estimate=pl.CostEstimate(
+            flops=2 * total * features * (wide + own), bytes_accessed=16 * 1024 * 1024, transcendentals=0
+        ),
+        name="attention_sums",
+    )(partial, *inputs)
 
 
 def sum_everywhere(n_ctx, n_fsdp, values):
@@ -953,10 +1028,10 @@
         chip, core, _, length = place(n_ctx)
         side = chip // sides
         step = pl.program_id(0)
-        stages = [lambda: None]
+        stages = []
         if fused:
             held, square_in, load, sq_s, sq_r = refs
-            stages = corner_sum_stages(n_ctx, partial_ref, out_ref, held, square_in, load, (sq_s, sq_r))
+            starts, *stages = corner_sum_stages(n_ctx, partial_ref, out_ref, held, square_in, load, (sq_s, sq_r))
 
         def fetch(at, slot):
             start = pl.multiple_of((core * steps + at) * chunk, chunk)
@@ -965,7 +1040,10 @@
         @pl.when(step == 0)
         def _():
             fetch(0, 0).start()
-            stages[0]()
+            if fused:
+                greet(fsdp_peers(4, chip * 2 + core, lax.axis_index("fsdp")))
+                for start in sum(starts, []):
+                    start()
 
         @pl.when(step + 1 < steps)
         def _():
@@ -993,7 +1071,7 @@
                     mm(left, right, CONTRACT_FIRST) + mm(left_mirror, right_mirror, CONTRACT_FIRST)
                 )
 
-        for at, stage in ((1, 1), (steps - 1, 2)):
+        for at, stage in ((1, 0), (steps - 1, 1)):
             if stage < len(stages):
 
                 @pl.when(step == min(at, steps - 1))
@@ -1235,21 +1313,35 @@
     return pl.BlockSpec(shape, lambda r, *_: zeros, **more)
 
 
+def split(values):
+    high = low(values)
+    return (high, low(values - high.astype(jnp.float32)))
+
+
 def connect_coefficients(values, dynamic_ref, static_ref, coef_ref, dyn_ref):
-    lane = lax.broadcasted_iota(jnp.int32, (values[0].shape[0], 8), 1)
-    columns = []
-    for i, value in enumerate(values):
+    rows = values[0].shape[0]
+    lane = lax.broadcasted_iota(jnp.int32, (rows, 8), 1)
+    stats, highs, lows = [], [], []
+    for value in values:
         mean = jnp.mean(value, axis=-1, keepdims=True)
         centered = value - mean
         inverse = lax.rsqrt(jnp.mean(centered * centered, axis=-1, keepdims=True) + EPS)
-        normed = centered * inverse
-        projected = 0.0
-        for k in range(6):
-            part = jnp.sum(normed * dynamic_ref[k : k + 1], axis=-1, keepdims=True)
-            projected = jnp.where(lane == k, part, projected)
-        dynamic_part = jnp.tanh(projected)
-        coefficient = dynamic_part + static_ref[i : i + 1]
-        dyn_ref[i] = dynamic_part
+        stats.append((mean, inverse))
+        high, rest = split(centered * inverse)
+        highs.append(high)
+        lows.append(rest)
+    dynamic, dynamic_rest = split(dynamic_ref[...])
+    highs = jnp.concatenate(highs)
+    projected = (
+        mm(highs, dynamic, CONTRACT_LAST)
+        + mm(highs, dynamic_rest, CONTRACT_LAST)
+        + mm(jnp.concatenate(lows), dynamic, CONTRACT_LAST)
+    )
+    columns = []
+    for i, (mean, inverse) in enumerate(stats):
+        part = projected[i * rows : (i + 1) * rows]
+        coefficient = jnp.tanh(part) + static_ref[i : i + 1]
+        dyn_ref[i] = part
         coef_ref[i] = jnp.where(lane == 6, mean, jnp.where(lane == 7, inverse, coefficient))
         columns.append(coefficient)
     return columns
@@ -1428,62 +1520,69 @@
     )(grad, *w_mine, *w_other)
 
 
-def connect_back(values, coef, dyn, branch, grads, grad_normed, dynamic, coef_before=None, offset=0):
+def connect_back(values, coef, dyn, branch, grads, grad_normed, dynamic, means, coef_before=None, offset=0):
     number, rows, features = values.shape
     steps = rows // ROWS
     more = coef_before is not None
 
     def kernel(*refs):
-        values_ref, coef_ref, dyn_ref, branch_ref, grads_ref, normed_ref, dynamic_ref = refs[:7]
-        refs = refs[7:]
+        values_ref, coef_ref, dyn_ref, branch_ref, grads_ref, normed_ref, dynamic_ref, means_ref = refs[:8]
+        refs = refs[8:]
         if more:
             before_ref, refs = refs[0], refs[1:]
         out_ref, dynamic_out, static_out = refs[:3]
         if more:
             forward_ref, grad_low_ref = refs[3:5]
-        dynamic_sum = refs[-1]
         step = pl.program_id(0)
 
         @pl.when(step == 0)
         def _():
-            dynamic_sum[...] = jnp.zeros_like(dynamic_sum)
+            dynamic_out[...] = jnp.zeros_like(dynamic_out)
             static_out[...] = jnp.zeros_like(static_out)
 
         branch = branch_ref[...]
+        grads = [grads_ref[j].astype(jnp.float32) for j in range(number)]
         mixed = sum((coef_ref[i][:, 1:2] * values_ref[i].astype(jnp.float32) for i in range(number)))
         normed, inverse = normalize(mixed)
         grad_mixed = normalize_back(normed, inverse, normed_ref[...])
         lane = lax.broadcasted_iota(jnp.int32, (ROWS, 8), 1)
-        totals = [0.0] * 6
+        pre_grads, highs, lows = [], [], []
+        for i in range(number):
+            value = values_ref[i].astype(jnp.float32)
+            columns = [grads[i] * branch, grad_mixed * value] + [grads[j] * value for j in range(number)]
+            coef_grad = jnp.zeros((ROWS, 8), jnp.float32)
+            for k, column in enumerate(columns):
+                coef_grad = jnp.where(lane == k, jnp.sum(column, axis=-1, keepdims=True), coef_grad)
+            static_out[i : i + 1] += jnp.sum(coef_grad, axis=0, keepdims=True)
+            part = jnp.tanh(dyn_ref[i])
+            pre_grads.append(coef_grad * (1.0 - part * part))
+            high, rest = split((value - coef_ref[i][:, 6:7]) * coef_ref[i][:, 7:8])
+            highs.append(high)
+            lows.append(rest)
+        pre, pre_rest = split(jnp.concatenate(pre_grads))
+        dynamic, dynamic_rest = split(dynamic_ref[...])
+        normed_grads = mm(
+            jnp.concatenate([pre, pre_rest, pre], axis=1), jnp.concatenate([dynamic, dynamic, dynamic_rest], axis=0)
+        )
+        highs = jnp.concatenate(highs)
+        dynamic_out[...] += (
+            mm(pre, highs, CONTRACT_FIRST)
+            + mm(pre_rest, highs, CONTRACT_FIRST)
+            + mm(pre, jnp.concatenate(lows), CONTRACT_FIRST)
+        )
         befores = 0.0
         for i in range(number):
-            value = values_ref[i].astype(jnp.float32)
-            grad_own = grads_ref[i].astype(jnp.float32)
-            columns = [
-                jnp.sum(grad_own * branch, axis=-1, keepdims=True),
-                jnp.sum(grad_mixed * value, axis=-1, keepdims=True),
-            ]
-            out = coef_ref[i][:, 1:2] * grad_mixed
+            coef = coef_ref[i]
+            mean_grad = jnp.sum(pre_grads[i] * means_ref[...], axis=-1, keepdims=True)
+            inner = jnp.sum(pre_grads[i] * dyn_ref[i], axis=-1, keepdims=True) / features
+            normed = (values_ref[i].astype(jnp.float32) - coef[:, 6:7]) * coef[:, 7:8]
+            out = coef[:, 7:8] * (normed_grads[i * ROWS : (i + 1) * ROWS] - mean_grad - normed * inner)
+            out = out + coef[:, 1:2] * grad_mixed
             for j in range(number):
-                grad = grads_ref[j].astype(jnp.float32)
-                columns.append(jnp.sum(grad * value, axis=-1, keepdims=True))
-                out = out + coef_ref[i][:, 2 + j : 3 + j] * grad
-            normed = (value - coef_ref[i][:, 6:7]) * coef_ref[i][:, 7:8]
-            normed_grad = 0.0
-            coef_grad = jnp.zeros((ROWS, 8), jnp.float32)
-            for k in range(6):
-                part = dyn_ref[i][:, k : k + 1]
-                pre_grad = columns[k] * (1.0 - part * part)
-                normed_grad = normed_grad + pre_grad * dynamic_ref[k : k + 1]
-                totals[k] = totals[k] + pre_grad * normed
-                coef_grad = jnp.where(lane == k, columns[k], coef_grad)
-            out = out + normalize_back(normed, coef_ref[i][:, 7:8], normed_grad)
+                out = out + coef[:, 2 + j : 3 + j] * grads[j]
             out_ref[i] = out
-            static_out[i : i + 1] += jnp.sum(coef_grad, axis=0, keepdims=True)
             if more:
                 befores = befores + before_ref[i][:, 0:1] * out
-        for k in range(6):
-            dynamic_sum[k] += jnp.sum(totals[k].reshape(ROWS // 8, 8, features), axis=0)
         if more:
             grad_low_ref[...] = low(befores)
             for j in range(number):
@@ -1492,12 +1591,6 @@
                     out = out + coef_ref[i][:, 2 + j : 3 + j] * values_ref[i].astype(jnp.float32)
                 forward_ref[j] = low(out)
 
-        @pl.when(step == steps - 1)
-        def _():
-            for k in range(6):
-                dynamic_out[k : k + 1] = jnp.sum(dynamic_sum[k], axis=0, keepdims=True)
-            dynamic_out[6:8] = jnp.zeros((2, features), jnp.float32)
-
     rows_spec = pl.BlockSpec((ROWS, features), lambda r: (r, 0))
     out_shape = [
         jax.ShapeDtypeStruct((number, rows, features), jnp.float32),
@@ -1505,7 +1598,7 @@
         jax.ShapeDtypeStruct((8, 8), jnp.float32),
     ]
     out_specs = [row_blocks(number, features), whole_block((8, features)), whole_block((8, 8))]
-    operands = [values, coef, dyn, branch, grads, grad_normed, dynamic]
+    operands = [values, coef, dyn, branch, grads, grad_normed, dynamic, means]
     in_specs = [
         row_blocks(number, features),
         row_blocks(number, 8),
@@ -1514,6 +1607,7 @@
         row_blocks(number, features),
         pl.BlockSpec((ROWS, features), lambda r: (offset // ROWS + r, 0)),
         whole_block(dynamic.shape),
+        whole_block(means.shape),
     ]
     if more:
         operands.append(coef_before)
@@ -1528,7 +1622,6 @@
         in_specs=in_specs,
         out_specs=out_specs,
         out_shape=out_shape,
-        scratch_shapes=[pltpu.VMEM((6, 8, features), jnp.float32)],
         compiler_params=params(),
         name="connect_back",
     )(*operands)
@@ -1579,6 +1672,7 @@
     tables = (jnp.cos(angles), jnp.sin(angles) * signs[None, :], positions[:, None], positions[None, :])
 
     dynamics = jnp.pad(hc_dynamic, ((0, 0), (0, 2), (0, 0)))
+    means = jnp.mean(dynamics, axis=-1)
     statics = jnp.pad(hc_static, ((0, 0), (0, 0), (0, 2)))
     coef_one, dyn_one, attn_low = connect_first(streams[0], dynamics[0], statics[0])
     attn_low, w_half = lax.optimization_barrier((attn_low, w_half))
@@ -1631,7 +1725,7 @@
     weight_cols = lax.psum_scatter(weight_parts[0], "ctx", scatter_dimension=0, axis_index_groups=lines)
 
     grad_first, dynamic_grad_two, static_grad_two, streams_out, grad_attn = connect_back(
-        first_out, coef_two, dyn_two, sums, cotangent[0], sums, dynamics[1], coef_one, length
+        first_out, coef_two, dyn_two, sums, cotangent[0], sums, dynamics[1], means[1:], coef_one, length
     )
     grad_heads, grad_cols = project_back(n_ctx, n_fsdp, grad_attn, w_out_mine, w_out_other, w_out_where, own_rows)
     grad_heads = grad_heads.reshape(rows, own)
@@ -1639,17 +1733,18 @@
     grad_cols = lax.all_to_all(grad_cols, "ctx", 0, 0, tiled=True).reshape(rows, own)
     qkv_grad, attn_part = attention_backward(query, key, value, grad_heads, logs, w_qkv, *tables, heads)
     attn_part = attn_part.reshape(n_ctx, length, features)
-    grad_attn_normed = line_sum(n_ctx, attn_part, 5)
+    if n_fsdp == 4:
+        grad_attn_normed, attn_grad = attention_sums(n_ctx, attn_part, attn_all, qkv_grad, attended_all, grad_cols)
+    else:
+        grad_attn_normed = line_sum(n_ctx, attn_part)
+        attn_grad = scatter(attention_weights(attn_all, qkv_grad, attended_all, grad_cols), "fsdp").astype(jnp.float32)
     grad_attn_normed, weight_cols = lax.optimization_barrier((grad_attn_normed, weight_cols))
     mine = lax.dynamic_slice_in_dim(weight_cols, core * own, own, 2)
     other = lax.dynamic_slice_in_dim(weight_cols, (1 - core) * own, own, 2)
     other = lax.ppermute(other, "ctx", siblings)
     ffn_grad = jnp.moveaxis(in_order(mine, other, 1), 0, 1).astype(jnp.float32)
-    weight_part = attention_weights(attn_all, qkv_grad, attended_all, grad_cols)
-    attn_grad = scatter(weight_part, "fsdp")
-
     grad_inputs, dynamic_grad_one, static_grad_one = connect_back(
-        streams[0], coef_one, dyn_one, attn_branch, grad_first, grad_attn_normed, dynamics[0]
+        streams[0], coef_one, dyn_one, attn_branch, grad_first, grad_attn_normed, dynamics[0], means[:1]
     )
     static_grads = jnp.concatenate([static_grad_one[:number, :6].reshape(1, -1), static_grad_two[:number, :6].reshape(1, -1)])
     small = jnp.concatenate(
@@ -1660,9 +1755,8 @@
         ]
     )
     small = sum_everywhere(n_ctx, n_fsdp, small.reshape(n_ctx, 8, -1))
-    small, attn_grad = lax.optimization_barrier((small, attn_grad))
     small = small.reshape(16, features)
-    attn_grad = attn_grad.astype(jnp.float32).reshape(own_rows, 4, own)
+    attn_grad = attn_grad.reshape(own_rows, 4, own)
     dynamic_total = small[:12].reshape(2, 6, features)
     static_total = small[12:14, : 6 * number].reshape(2, number, 6)
     return (streams_out[None], grad_inputs[None], attn_grad, ffn_grad, dynamic_total, static_total)

time: 438 us -> 436 us (level)
    pallas_call x2, Pallas kernels: 31.3 us -> 24.3 us  [connect_back(): pl.pallas_call(kernel, grid=(steps,), in_specs=in_specs, out_specs=out_sp...]
    pallas_call x2 -> x1, Pallas kernels: 64.8 us -> 66.9 us  [attention_sums(): pl.pallas_call(kernel, out_shape=[jax.ShapeDtypeStruct(partial.shape[-2:]...]
  transfers between devices with their start and end apart: 15 -> 14, of which waited for: 3 -> 3; matrix products, arithmetic and copies ran while one was open for 5% -> 6% of each run, Pallas kernels for 63% -> 62%
where the time goes in v6:
time: 436 us; the launch traced here: 431 us
  Pallas kernels  367 us (84%)
  local copies, waits for them, and re-layouts  26.7 us (6%)
  between operations  14.2 us (3%)
  starting transfers between devices  13.1 us (3%)
  other arithmetic  7.88 us (2%)
    pallas_call x1, Pallas kernels, ffn_rows(): pl.pallas_call(kernel, in_specs=any_specs(2), out_specs=any_specs(6), out...  83.7 us
    pallas_call x1, Pallas kernels, attention_sums(): pl.pallas_call(kernel, out_shape=[jax.ShapeDtypeStruct(partial.shape[-2:]...  66.9 us
    pallas_call x1, Pallas kernels, ffn_weights(): pl.pallas_call(kernel, grid=(steps,), in_specs=in_specs, out_specs=out_sp...  46.1 us
    pallas_call x1, Pallas kernels, line_rows(): pl.pallas_call(kernel, out_shape=jax.ShapeDtypeStruct((n_ctx,) + rows.sha...  43 us
    pallas_call x1, Pallas kernels, project_back(): pl.pallas_call(kernel, in_specs=[pl.BlockSpec(memory_space=pltpu.VMEM)] *...  25 us
    pallas_call x2, Pallas kernels, connect_back(): pl.pallas_call(kernel, grid=(steps,), in_specs=in_specs, out_specs=out_sp...  24.3 us
    pallas_call x1, Pallas kernels, attention_forward(): pl.pallas_call(kernel, grid=(steps,), in_specs=[pl.BlockSpec((SPAN, featu...  22.1 us
    pallas_call x1, Pallas kernels, attention_backward(): pl.pallas_call(kernel, grid=(steps,), in_specs=[whole_block(a.shape) for...  18.2 us
  transfers between devices with their start and end apart: 14, of which 3 were waited for; matrix products, arithmetic and copies ran while one was open for 6% of the time, Pallas kernels for 62%

profile of v6, /device:TPU:0, one launch (start us, length us, event | category | flops | bytes accessed | tf_op | source)
XLA Modules:
  0.0 431.1 jit_solution(3948956345851028984)
XLA Ops:
  7.2 1.6 constant_dynamic-slice_fusion.2
  8.9 0.9 copy.26
  9.8 1.2 copy.19
  11.1 5.8 %constant_dynamic-slice_fusion.3 = bf16[512,1,1024]{2,1,0:T(2,128)(2,1)S(1)} fusion(bf16[512,4,2048]{2,1,0:T(4,128)(2,1)} %param.8, s32[]{:T(128)S(6)} %add.63, s32[]{:T(128)S(6)} %select_n.36), kind=kLoop, calls=%fused_computation.27 | loop fusion | bytes 2097160 | tf_op jit(solution)/shard_map/slice | solution.py:1654
  16.9 0.4 copy.28
  17.3 0.7 fusion.4
  17.9 0.7 fusion.2
  18.6 6.7 %connect_first.1 = (f32[4,128,8]{2,1,0:T(8,128)}, f32[4,128,8]{2,1,0:T(8,128)}, bf16[128,2048]{1,0:T(8,128)(2,1)}) custom-call(bf16[4,128,2048]{2,1,0:T(8,128)(2,1)} %bitcast.36, f32[8,2048]{1,0:T(8,128)} %get-tuple-element.125.dynamic_ref.refs_6_, f32[4,8]{1,0:T(4,128)} %get-tuple-element.129.static_ref), custom_call_target="tpu_custom_call" | custom-call | tf_op jit(solution)/shard_map/connect_first/pallas_call | solution.py:1360
  25.2 3.0 collective-permute-start.1
  28.2 1.5 collective-permute-start
  29.7 43.0 %line_rows.1 = bf16[8,128,2048]{2,1,0:T(8,128)(2,1)} custom-call(bf16[128,2048]{1,0:T(8,128)(2,1)} %get-tuple-element.59.rows_ref), custom_call_target="tpu_custom_call" | custom-call | tf_op jit(solution)/shard_map/line_rows/pallas_call | solution.py:271
  72.9 0.9 slice.55
  73.8 0.4 collective-permute-start.5
  74.2 0.8 slice.56
  75.0 0.1 collective-permute-start.6
  75.2 0.5 collective-permute-start.3
  75.7 0.5 collective-permute-start.2
  76.3 1.1 copy.20.column_ref
  77.4 3.1 fusion
  80.5 22.1 %attention_forward.1 = (bf16[1024,256]{1,0:T(8,128)(2,1)}, bf16[1024,256]{1,0:T(8,128)(2,1)}, bf16[1024,256]{1,0:T(8,128)(2,1)}, bf16[1024,256]{1,0:T(8,128)(2,1...) custom-call(bf16[1024,2048]{1,0:T(8,128)(2,1)} %bitcast.39, ...), custom_call_target="tpu_custom_call" | custom-call | tf_op jit(solution)/shard_map/attention_forward/pallas_call | solution.py:1226
  102.6 1.3 collective-permute-start.7
  104.0 0.6 pad_add_fusion.1.core_ref
  104.6 1.2 collective-permute-done.7.refs_8_
  105.8 0.7 collective-permute-done.8.refs_9_
  106.6 13.6 %connect_middle.1 = (f32[4,128,2048]{2,1,0:T(8,128)}, f32[128,2048]{1,0:T(8,128)}, f32[4,128,8]{2,1,0:T(8,128)}, f32[4,128,8]{2,1,0:T(8,128)}, bf16[2,128,2048]{2,1,0:T(8,128)(2,1)}) custom-call(s32[2]{0:T(128)} %pad_add_fusion.1.core_ref, bf16[4,128,2048]{2,1,0:T(8,128)(2,1)} %bitcast.37, f32[4,128,8]{2,1,0:T(8,128)} %get-tuple-element.57.coef_ref.refs_8_.refs_1_, ...), custom_call_target="tpu_custom_call" | custom-call | tf_op jit(solution)/shard_map/connect_middle/pallas_call | solution.py:1413
  120.2 83.7 %ffn_rows.1 = (bf16[2,4,256,2048]{3,2,1,0:T(8,128)(2,1)}, bf16[2,4,256,2048]{3,2,1,0:T(8,128)(2,1)}, bf16[1024,1024]{1,0:T(8,128)(2,1)}, bf16[1024,1024]{1,0:T(8...) custom-call(bf16[256,2048]{1,0:T(8,128)(2,1)} %bitcast.63, bf16[3,2048,2048]{2,1,0:T(8,128)(2,1)} %bitcast.57), custom_call_target="tpu_custom_call" | custom-call | flops 25769803776 | bytes 52428800 | tf_op jit(solution)/shard_map/ffn_rows/pallas_call | solution.py:980
  204.0 46.1 %ffn_weights.1 = (bf16[2,3,1024,512]{3,2,1,0:T(8,128)(2,1)}, f32[256,2048]{1,0:T(8,128)}) custom-call(bf16[8,2,128,2048]{3,2,1,0:T(8,128)(2,1)} %bitcast.64, bf16[8,2,128,2048]{3,2,1,0:T(8,128)(2,1)} %bitcast.65, bf16[1024,1024]{1,0:T(8,128)(2,1)} %get-tuple-element.75.refs_2_, bf16[1024,1024]{1,0:T(8,128)(2,1)} %get-tuple-element.76.refs_3_, ...), custom_call_target="tpu_custom_call" | custom-call | flops 25769803776 | bytes 52428800 | tf_op jit(solution)/shard_map/ffn_weights/pallas_call | solution.py:1096
  250.1 0.1 pad_reduce_fusion
  250.2 0.6 fusion.5
  250.8 13.2 %connect_back.2 = (f32[4,128,2048]{2,1,0:T(8,128)}, f32[8,2048]{1,0:T(8,128)}, f32[8,8]{1,0:T(8,128)}, bf16[4,128,2048]{2,1,0:T(8,128)(2,1)}, bf16[128,2048]{1,0:T(8,128)(2,1)}) custom-call(f32[4,128,2048]{2,1,0:T(8,128)} %get-tuple-element.69.refs_0_, f32[4,128,8]{2,1,0:T(8,128)} %get-tuple-element.70.refs_1_, f32[4,128,8]{2,1,0:T(8,128)} %get-tuple-element.71.refs_2_, ...), custom_call_target="tpu_custom_call" | custom-call | tf_op jit(solution)/shard_map/connect_back/pallas_call | solution.py:1619
  263.9 25.0 %project_back.1 = (bf16[8,128,256]{2,1,0:T(8,128)(2,1)}, bf16[8,128,256]{2,1,0:T(8,128)(2,1)}) custom-call(bf16[128,2048]{1,0:T(8,128)(2,1)} %get-tuple-element.89.grad_ref, bf16[512,1024]{1,0:T(8,128)(2,1)} %bitcast.45, bf16[512,1024]{1,0:T(8,128)(2,1)} %copy-done.2, bf16[512,1024]{1,0:T(8,128)(2,1)} %copy-done.1, ...), custom_call_target="tpu_custom_call" | custom-call | tf_op jit(solution)/shard_map/project_back/pallas_call | solution.py:1512
  289.0 5.5 %all-to-all-start = ((bf16[8,128,256]{2,1,0:T(8,128)(2,1)}), bf16[8,128,256]{2,1,0:T(8,128)(2,1)S(1)}, u32[]{:S(2)}, u32[]{:S(2)}) async-start(bf16[8,128,256]{2,1,0:T(8,128)(2,1)} %get-tuple-element.97), calls=%async_computation | async-start | bytes 1048576 | tf_op jit(solution)/shard_map/all_to_all | solution.py:1733
  294.6 18.2 %attention_backward.1 = (bf16[1024,768]{1,0:T(8,128)(2,1)}, bf16[1024,2048]{1,0:T(8,128)(2,1)}) custom-call(bf16[1024,256]{1,0:T(8,128)(2,1)} %get-tuple-element.86.query_ref, bf16[1024,256]{1,0:T(8,128)(2,1)} %get-tuple-element.87.key_ref, bf16[1024,256]{1,0:T(8,128)(2,1)} %get-tuple-element.88.value_ref, bf16[1024,256]{1,0:T(8,128)(2,1)} %bitcast.50, ...), custom_call_target="tpu_custom_call" | custom-call | tf_op jit(solution)/shard_map/attention_backward/pallas_call | solution.py:1286
  312.7 0.6 all-to-all-done
  313.4 0.8 copy-done.3
  314.2 66.9 %attention_sums.1 = (f32[128,2048]{1,0:T(8,128)}, f32[512,1024]{1,0:T(8,128)}) custom-call(bf16[8,128,2048]{2,1,0:T(8,128)(2,1)} %bitcast.61, bf16[1024,2048]{1,0:T(8,128)(2,1)} %bitcast.40, bf16[1024,768]{1,0:T(8,128)(2,1)} %get-tuple-element.95.refs_1_, bf16[8,1024,256]{2,1,0:T(8,128)(2,1)} %bitcast.59, bf16[1024,256]{1,0:T(8,128)(2,1)} %bitcast.51), custom_call_target="tpu_custom_call" | custom-call | flops 4294967296 | bytes 16777216 | tf_op jit(solution)/shard_map/attention_sums/pallas_call | solution.py:665
  381.1 3.2 constant_dynamic-slice_fusion.1
  384.4 3.2 reshape.91
  387.6 11.1 %connect_back.3 = (f32[4,128,2048]{2,1,0:T(8,128)}, f32[8,2048]{1,0:T(8,128)}, f32[8,8]{1,0:T(8,128)}) custom-call(bf16[4,128,2048]{2,1,0:T(8,128)(2,1)} %bitcast.38, f32[4,128,8]{2,1,0:T(8,128)} %get-tuple-element.57.coef_ref.refs_8_.refs_1_, f32[4,128,8]{2,1,0:T(8,128)} %get-tuple-element.83.refs_2_, f32[128,2048]{1,0:T(8,128)} %get-tuple-element.84.refs_3_, ...), custom_call_target="tpu_custom_call" | custom-call | tf_op jit(solution)/shard_map/connect_back/pallas_call | solution.py:1619
  398.7 0.7 slice.63
  399.5 0.9 pad_maximum_fusion
  400.4 0.7 reshape.94.values_ref
  401.1 16.9 %sum_everywhere.1 = f32[8,8,512]{2,1,0:T(8,128)} custom-call(f32[8,8,512]{2,1,0:T(8,128)} %reshape.94.values_ref), custom_call_target="tpu_custom_call" | custom-call | tf_op jit(solution)/shard_map/sum_everywhere/pallas_call | solution.py:727
  418.0 0.9 slice.65
  418.9 1.0 reshape.96
  419.9 0.7 reshape.97
  420.6 0.7 copy.22
  421.4 3.0 convert_bitcast_fusion
  (52 shorter events, 0.9 us)
Async XLA Ops:
  7.2 73.3 %all-gather.3.cloned.1.call-start = ((), (), s32[]{:S(2)}) async-start(), calls=%async_computation.2 | async-start | bytes 3932160 | tf_op jit(solution)/shard_map/all_gather | solution.py:53
  7.2 3.8 copy-start.4
  10.9 302.4 %all-gather.5.cloned.1.call-start = ((), (), s32[]{:S(2)}) async-start(), calls=%async_computation.3 | async-start | bytes 4718592 | tf_op jit(solution)/shard_map/all_gather | solution.py:53
  11.1 6.2 %copy-start.7 = (f32[2,4,6]{2,1,0:T(4,128)S(1)}, f32[2,4,6]{2,1,0:T(4,128)}, u32[]{:S(2)}) copy-start(f32[2,4,6]{2,1,0:T(4,128)} %param.11) | copy-start | bytes 580
  17.3 58.9 %copy-start = (bf16[512,1,1024]{2,0,1:T(8,128)(2,1)}, bf16[512,1,1024]{2,0,1:T(8,128)(2,1)S(1)}, u32[]{:S(2)}) copy-start(bf16[512,1,1024]{2,0,1:T(8,128)(2,1)S(1)} %copy.28) | copy-start | bytes 3145732
  18.6 54.2 %copy-start.9 = (s32[8]{0:T(128)S(1)}, s32[8]{0:T(128)}, u32[]{:S(2)}) copy-start(s32[8]{0:T(128)} %param.13) | copy-start | bytes 100
  25.2 47.6 %collective-permute-start.1 = (bf16[512,1024]{1,0:T(8,128)(2,1)S(1)}, bf16[512,1024]{1,0:T(8,128)(2,1)S(1)}, u32[]{:S(2)}, u32[]{:S(2)}) collective-permute-start(bf16[512,1024]{1,0:T(8,128)(2,1)S(1)} %bitcast.41), channel_id=1, source_target_pairs={{0,2},{1,3},{2,0},{3,1},{4,6},{5,7},{6,4},{7,5},{8,10},{9,11},{10,... | collective-permute-start | bytes 3145736 | tf_op jit(solution)/shard_map/ppermute | solution.py:1660
  28.2 44.6 %collective-permute-start = (bf16[512,1024]{1,0:T(8,128)(2,1)S(1)}, bf16[512,1024]{1,0:T(8,128)(2,1)S(1)}, u32[]{:S(2)}, u32[]{:S(2)}) collective-permute-start(bf16[512,1024]{1,0:T(8,128)(2,1)S(1)} %bitcast.42), channel_id=1, source_target_pairs={{0,1},{1,0},{2,3},{3,2},{4,5},{5,4},{6,7},{7,6},{8,9},{9,8},{10,11... | collective-permute-start | bytes 3145736 | tf_op jit(solution)/shard_map/ppermute | solution.py:1660
  72.9 29.7 %copy-start.1 = (bf16[512,1024]{1,0:T(8,128)(2,1)}, bf16[512,1024]{1,0:T(8,128)(2,1)S(1)}, u32[]{:S(2)}) copy-start(bf16[512,1024]{1,0:T(8,128)(2,1)S(1)} %collective-permute-done.1.refs_2_) | copy-start | bytes 3145732
  72.9 29.7 %copy-start.2 = (bf16[512,1024]{1,0:T(8,128)(2,1)}, bf16[512,1024]{1,0:T(8,128)(2,1)S(1)}, u32[]{:S(2)}) copy-start(bf16[512,1024]{1,0:T(8,128)(2,1)S(1)} %collective-permute-done.refs_1_) | copy-start | bytes 3145732
  73.8 30.8 %collective-permute-start.5 = (bf16[512,1024]{1,0:T(8,128)(2,1)S(1)}, bf16[512,1024]{1,0:T(8,128)(2,1)}, u32[]{:S(2)}, u32[]{:S(2)}) collective-permute-start(bf16[512,1024]{1,0:T(8,128)(2,1)S(1)} %collective-permute-done.refs_1_), channel_id=1, source_target_pairs={{0,4},{4,0},{8,12},{12,8},{16,20},{20,16},{24,28},{28,24},{1,5},{5... | collective-permute-start | bytes 3145736 | tf_op jit(solution)/shard_map/ppermute | solution.py:1665
  75.0 29.6 %collective-permute-start.6 = (bf16[512,1024]{1,0:T(8,128)(2,1)S(1)}, bf16[512,1024]{1,0:T(8,128)(2,1)}, u32[]{:S(2)}, u32[]{:S(2)}) collective-permute-start(bf16[512,1024]{1,0:T(8,128)(2,1)S(1)} %collective-permute-done.1.refs_2_), channel_id=1, source_target_pairs={{0,4},{4,0},{8,12},{12,8},{16,20},{20,16},{24,28},{28,24},{1,5},{5... | collective-permute-start | bytes 3145736 | tf_op jit(solution)/shard_map/ppermute | solution.py:1665
  75.2 27.5 %collective-permute-start.3 = (bf16[256,1024]{1,0:T(8,128)(2,1)}, bf16[256,1024]{1,0:T(8,128)(2,1)}, u32[]{:S(2)}, u32[]{:S(2)}) collective-permute-start(bf16[256,1024]{1,0:T(8,128)(2,1)} %slice.56), channel_id=1, source_target_pairs={{0,1},{1,0},{2,3},{3,2},{4,5},{5,4},{6,7},{7,6},{8,9},{9,8},{10,11... | collective-permute-start | bytes 1572872 | tf_op jit(solution)/shard_map/ppermute | solution.py:1688
  75.7 26.9 %collective-permute-start.2 = (bf16[256,1024]{1,0:T(8,128)(2,1)}, bf16[256,1024]{1,0:T(8,128)(2,1)}, u32[]{:S(2)}, u32[]{:S(2)}) collective-permute-start(bf16[256,1024]{1,0:T(8,128)(2,1)} %slice.55), channel_id=1, source_target_pairs={{0,2},{1,3},{2,0},{3,1},{4,6},{5,7},{6,4},{7,5},{8,10},{9,11},{10,... | collective-permute-start | bytes 1572872 | tf_op jit(solution)/shard_map/ppermute | solution.py:1687
  76.2 28.4 %collective-permute-start.4 = (bf16[512,1024]{1,0:T(8,128)(2,1)S(1)}, bf16[512,1024]{1,0:T(8,128)(2,1)}, u32[]{:S(2)}, u32[]{:S(2)}) collective-permute-start(bf16[512,1024]{1,0:T(8,128)(2,1)S(1)} %bitcast.43), channel_id=1, source_target_pairs={{0,4},{4,0},{8,12},{12,8},{16,20},{20,16},{24,28},{28,24},{1,5},{5... | collective-permute-start | bytes 3145736 | tf_op jit(solution)/shard_map/ppermute | solution.py:1665
  76.3 4.2 copy-start.5
  102.6 3.2 collective-permute-start.7
  103.9 2.6 collective-permute-start.8
  203.9 177.2 %reduce-scatter.2.cloned.1.call-start = ((), (), s32[]{:S(2)}) async-start(), calls=%async_computation.4 | async-start | bytes 9437184 | tf_op jit(solution)/shard_map/reduce_scatter | solution.py:1725
  289.0 24.4 %all-to-all-start = ((bf16[8,128,256]{2,1,0:T(8,128)(2,1)}), bf16[8,128,256]{2,1,0:T(8,128)(2,1)S(1)}, u32[]{:S(2)}, u32[]{:S(2)}) async-start(bf16[8,128,256]{2,1,0:T(8,128)(2,1)} %get-tuple-element.97), calls=%async_computation | async-start | bytes 1048576 | tf_op jit(solution)/shard_map/all_to_all | solution.py:1733
  313.4 0.8 copy-start.3
  381.1 3.3 copy-start.8
  384.3 37.0 %collective-permute-start.9 = (bf16[3,1024,256]{2,1,0:T(8,128)(2,1)}, bf16[3,1024,256]{2,1,0:T(8,128)(2,1)S(1)}, u32[]{:S(2)}, u32[]{:S(2)}) collective-permute-start(bf16[3,1024,256]{2,1,0:T(8,128)(2,1)} %get-tuple-element.123), channel_id=1, source_target_pairs={{0,4},{4,0},{8,12},{12,8},{16,20},{20,16},{24,28},{28,24},{1,5},{5... | collective-permute-start | bytes 4718600 | tf_op jit(solution)/shard_map/ppermute | solution.py:1744
  387.6 11.9 %copy-start.6 = (f32[8,2048]{1,0:T(8,128)S(1)}, f32[8,2048]{1,0:T(8,128)}, u32[]{:S(2)}) copy-start(f32[8,2048]{1,0:T(8,128)} %get-tuple-element.105) | copy-start | bytes 196612
Sparse Core Ops, SparseCore 0:
  11.1 61.4 all-gather.2
  204.0 45.3 all-gather.4
  251.8 106.9 reduce-scatter.1

commit v7 on v6

--- a/solution.py
+++ b/solution.py
@@ -1014,6 +1014,8 @@
     sides = n_ctx // 4
     wide = half // sides
     fused = partial is not None
+    early = steps // 2 if fused else 0
+    assert not fused or sides == 2
 
     def kernel(*refs):
         rows_ref, refs = refs[0], refs[1:]
@@ -1021,7 +1023,7 @@
         mirror_blocks = [ref.at[b] for ref in mirror_refs for b in range(ref.shape[0])]
         hidden_ref, grad_gate_ref, grad_up_ref, planes_ref, *refs = refs
         if fused:
-            partial_ref, weight_ref, out_ref, *refs = refs
+            partial_ref, weight_ref, out_ref, early_ref, *refs = refs
         else:
             weight_ref, *refs = refs
         mirror, (weights, weight_sems), refs = refs[:3], refs[3:5], refs[5:]
@@ -1030,7 +1032,12 @@
         step = pl.program_id(0)
         stages = []
         if fused:
-            held, square_in, load, sq_s, sq_r = refs
+            keep, give, take, side_s, side_r, held, square_in, load, sq_s, sq_r = refs
+            member = chip % 2
+            other = (chip + 1 - 2 * member) * 2 + core
+            crossing = [
+                send(give.at[j], take.at[j], (side_s, side_r), j, (other, lax.axis_index("fsdp"))) for j in range(early)
+            ]
             starts, *stages = corner_sum_stages(n_ctx, partial_ref, out_ref, held, square_in, load, (sq_s, sq_r))
 
         def fetch(at, slot):
@@ -1041,7 +1048,8 @@
         def _():
             fetch(0, 0).start()
             if fused:
-                greet(fsdp_peers(4, chip * 2 + core, lax.axis_index("fsdp")))
+                fsdp = lax.axis_index("fsdp")
+                greet(fsdp_peers(4, chip * 2 + core, fsdp) + [(other, fsdp)])
                 for start in sum(starts, []):
                     start()
 
@@ -1067,9 +1075,28 @@
                 cols = pl.ds(pl.multiple_of(side * half + z * wide, wide), wide)
                 right = rows_ref[:, which, :, cols].reshape(total, wide)
                 right_mirror = jnp.concatenate([ref[which, :, cols] for ref in mirror_blocks])
-                weight_ref[z, plane] = low(
-                    mm(left, right, CONTRACT_FIRST) + mm(left_mirror, right_mirror, CONTRACT_FIRST)
-                )
+                value = mm(left, right, CONTRACT_FIRST) + mm(left_mirror, right_mirror, CONTRACT_FIRST)
+                if not fused:
+                    weight_ref[z, plane] = low(value)
+                    continue
+
+                @pl.when((step < early) & (z == member))
+                def _():
+                    keep[step % early, plane] = value
+
+                @pl.when((step < early) & (z != member))
+                def _():
+                    give[step % early, plane] = low(value)
+
+                @pl.when(step >= early)
+                def _():
+                    weight_ref[z, plane] = low(value)
+
+        for j in range(early):
+
+            @pl.when(step == j)
+            def _():
+                crossing[j].start()
 
         for at, stage in ((1, 0), (steps - 1, 1)):
             if stage < len(stages):
@@ -1077,14 +1104,25 @@
                 @pl.when(step == min(at, steps - 1))
                 def _():
                     stages[stage]()
+
+        if fused:
+
+            @pl.when(step == steps - 1)
+            def _():
+                for j in range(early):
+                    crossing[j].wait()
+                    for plane in range(3):
+                        early_ref[plane, j * chunk : (j + 1) * chunk] = low(
+                            keep[j, plane] + take[j, plane].astype(jnp.float32)
+                        )
 
     act_spec = pl.BlockSpec((total, chunk), lambda j: (0, j))
     once = dict(pipeline_mode=pl.Buffered(1))
     operands = [rows, *rows_mirror, *hidden, planes]
     in_specs = [whole_block(rows.shape, **once)] + [whole_block(part.shape, **once) for part in rows_mirror]
     in_specs += [act_spec] * 3 + any_specs(1)
-    out_specs = [pl.BlockSpec((sides, 3, chunk, wide), lambda j: (0, 0, j, 0))]
-    out_shape = [jax.ShapeDtypeStruct((sides, 3, n_own, wide), jnp.bfloat16)]
+    out_specs = [pl.BlockSpec((sides, 3, chunk, wide), lambda j: (0, 0, jnp.maximum(j - early, 0), 0))]
+    out_shape = [jax.ShapeDtypeStruct((sides, 3, n_own - early * chunk, wide), jnp.bfloat16)]
     scratch = [pltpu.VMEM((total, chunk), jnp.bfloat16)] * 3
     scratch += [pltpu.VMEM((2, 3, chunk, features), jnp.bfloat16), pltpu.SemaphoreType.DMA((2,))]
     if fused:
@@ -1092,6 +1130,10 @@
         in_specs += any_specs(1)
         out_specs.append(whole_block(partial.shape[-2:], **once))
         out_shape.append(jax.ShapeDtypeStruct(partial.shape[-2:], jnp.float32))
+        out_specs.append(whole_block((3, early * chunk, wide), **once))
+        out_shape.append(jax.ShapeDtypeStruct((3, early * chunk, wide), jnp.bfloat16))
+        scratch.append(pltpu.VMEM((early, 3, chunk, wide), jnp.float32))
+        scratch += [pltpu.VMEM((early, 3, chunk, wide), jnp.bfloat16)] * 2 + dma_pair(early)
         scratch += corner_sum_scratch(partial)
     return pl.pallas_call(
         kernel,
@@ -1319,29 +1361,19 @@
 
 
 def connect_coefficients(values, dynamic_ref, static_ref, coef_ref, dyn_ref):
-    rows = values[0].shape[0]
-    lane = lax.broadcasted_iota(jnp.int32, (rows, 8), 1)
-    stats, highs, lows = [], [], []
-    for value in values:
+    lane = lax.broadcasted_iota(jnp.int32, (values[0].shape[0], 8), 1)
+    columns = []
+    for i, value in enumerate(values):
         mean = jnp.mean(value, axis=-1, keepdims=True)
         centered = value - mean
         inverse = lax.rsqrt(jnp.mean(centered * centered, axis=-1, keepdims=True) + EPS)
-        stats.append((mean, inverse))
-        high, rest = split(centered * inverse)
-        highs.append(high)
-        lows.append(rest)
-    dynamic, dynamic_rest = split(dynamic_ref[...])
-    highs = jnp.concatenate(highs)
-    projected = (
-        mm(highs, dynamic, CONTRACT_LAST)
-        + mm(highs, dynamic_rest, CONTRACT_LAST)
-        + mm(jnp.concatenate(lows), dynamic, CONTRACT_LAST)
-    )
-    columns = []
-    for i, (mean, inverse) in enumerate(stats):
-        part = projected[i * rows : (i + 1) * rows]
-        coefficient = jnp.tanh(part) + static_ref[i : i + 1]
-        dyn_ref[i] = part
+        normed = centered * inverse
+        projected = jnp.zeros(lane.shape, jnp.float32)
+        for k in range(6):
+            part = jnp.sum(normed * dynamic_ref[k : k + 1], axis=-1, keepdims=True)
+            projected = jnp.where(lane == k, part, projected)
+        coefficient = jnp.tanh(projected) + static_ref[i : i + 1]
+        dyn_ref[i] = projected
         coef_ref[i] = jnp.where(lane == 6, mean, jnp.where(lane == 7, inverse, coefficient))
         columns.append(coefficient)
     return columns
@@ -1707,9 +1739,10 @@
         ffn_all, mirror_rows, *hidden, sums = ffn_rows(n_ctx, ffn_own, planes, n_own)
         ffn_all, mirror_rows = (part.reshape(blocks, 2, length, features) for part in (ffn_all, mirror_rows))
         mirror_rows = [mirror_rows]
-        attended, sums = lax.optimization_barrier((attended, sums))
         attended_all = gather(attended, "ctx").reshape(n_ctx, rows, own)
-        *weight_parts, sums = ffn_weights(n_ctx, n_fsdp, sums, ffn_all, mirror_rows, hidden, planes, n_own)
+        weight_parts, sums, weight_early = ffn_weights(
+            n_ctx, n_fsdp, sums, ffn_all, mirror_rows, hidden, planes, n_own
+        )
     else:
         ffn_mirror = lax.ppermute(ffn_own, "ctx", [(i, n_ctx - 2 - i + 2 * (i % 2)) for i in range(n_ctx)])
         ffn_all = square_core_gather(n_ctx, n_fsdp, ffn_own).reshape(blocks, 2, length, features)
@@ -1719,10 +1752,10 @@
         sums = ffn_back(*hidden, planes, core_index, blocks)
         mirror_rows = [part.reshape(1, 2, length, features) for part in mirror_mine + swap(mirror_mine)]
         sums = square_sum(n_ctx, n_fsdp, sums.reshape(2, n_fsdp, 2 * length, features))
-        weight_parts = ffn_weights(n_ctx, n_fsdp, None, ffn_all, mirror_rows, hidden, planes, n_own)
+        (weight_parts,) = ffn_weights(n_ctx, n_fsdp, None, ffn_all, mirror_rows, hidden, planes, n_own)
     sides = chips // 2
     lines = [[2 * (sides * side + i) + j for i in range(sides)] for side in range(2) for j in range(2)]
-    weight_cols = lax.psum_scatter(weight_parts[0], "ctx", scatter_dimension=0, axis_index_groups=lines)
+    weight_cols = lax.psum_scatter(weight_parts, "ctx", scatter_dimension=0, axis_index_groups=lines)
 
     grad_first, dynamic_grad_two, static_grad_two, streams_out, grad_attn = connect_back(
         first_out, coef_two, dyn_two, sums, cotangent[0], sums, dynamics[1], means[1:], coef_one, length
@@ -1739,6 +1772,8 @@
         grad_attn_normed = line_sum(n_ctx, attn_part)
         attn_grad = scatter(attention_weights(attn_all, qkv_grad, attended_all, grad_cols), "fsdp").astype(jnp.float32)
     grad_attn_normed, weight_cols = lax.optimization_barrier((grad_attn_normed, weight_cols))
+    if n_fsdp == 4:
+        weight_cols = jnp.concatenate([weight_early, weight_cols], axis=1)
     mine = lax.dynamic_slice_in_dim(weight_cols, core * own, own, 2)
     other = lax.dynamic_slice_in_dim(weight_cols, (1 - core) * own, own, 2)
     other = lax.ppermute(other, "ctx", siblings)

time: 436 us -> 454 us (1.041)
  Pallas kernels: 367 us -> 377 us
    pallas_call x1, Pallas kernels: 46.1 us -> 74.7 us  [ffn_weights(): pl.pallas_call(kernel, grid=(steps,), in_specs=in_specs, out_specs=out_sp...]
    pallas_call x1, Pallas kernels: 66.9 us -> 49.1 us  [attention_sums(): pl.pallas_call(kernel, out_shape=[jax.ShapeDtypeStruct(partial.shape[-2:]...]
  transfers between devices with their start and end apart: 14 -> 14, of which waited for: 3 -> 3; matrix products, arithmetic and copies ran while one was open for 6% -> 6% of each run, Pallas kernels for 62% -> 84%
where the time goes in v7:
time: 454 us; the launch traced here: 446 us
  Pallas kernels  377 us (83%)
  local copies, waits for them, and re-layouts  27.7 us (6%)
  between operations  14.6 us (3%)
  starting transfers between devices  13.6 us (3%)
  other arithmetic  7.94 us (2%)
  waiting for transfers between devices  5.42 us (1%)
    pallas_call x1, Pallas kernels, ffn_rows(): pl.pallas_call(kernel, in_specs=any_specs(2), out_specs=any_specs(6), out...  83.9 us
    pallas_call x1, Pallas kernels, ffn_weights(): pl.pallas_call(kernel, grid=(steps,), in_specs=in_specs, out_specs=out_sp...  74.7 us
    pallas_call x1, Pallas kernels, attention_sums(): pl.pallas_call(kernel, out_shape=[jax.ShapeDtypeStruct(partial.shape[-2:]...  49.1 us
    pallas_call x1, Pallas kernels, line_rows(): pl.pallas_call(kernel, out_shape=jax.ShapeDtypeStruct((n_ctx,) + rows.sha...  42.9 us
    pallas_call x1, Pallas kernels, project_back(): pl.pallas_call(kernel, in_specs=[pl.BlockSpec(memory_space=pltpu.VMEM)] *...  24.8 us
    pallas_call x2, Pallas kernels, connect_back(): pl.pallas_call(kernel, grid=(steps,), in_specs=in_specs, out_specs=out_sp...  24.3 us
    pallas_call x1, Pallas kernels, attention_forward(): pl.pallas_call(kernel, grid=(steps,), in_specs=[pl.BlockSpec((SPAN, featu...  22 us
    pallas_call x1, Pallas kernels, attention_backward(): pl.pallas_call(kernel, grid=(steps,), in_specs=[whole_block(a.shape) for...  18.1 us
  transfers between devices with their start and end apart: 14, of which 3 were waited for; matrix products, arithmetic and copies ran while one was open for 6% of the time, Pallas kernels for 84%

profile of v7, /device:TPU:0, one launch (start us, length us, event | category | flops | bytes accessed | tf_op | source)
XLA Modules:
  0.0 446.3 jit_solution(2367631080962374215)
XLA Ops:
  7.2 1.6 constant_dynamic-slice_fusion.2
  8.8 0.9 copy.26
  9.7 1.2 copy.19
  11.0 5.8 %constant_dynamic-slice_fusion.3 = bf16[512,1,1024]{2,1,0:T(2,128)(2,1)S(1)} fusion(bf16[512,4,2048]{2,1,0:T(4,128)(2,1)} %param.8, s32[]{:T(128)S(6)} %add.63, s32[]{:T(128)S(6)} %select_n.36), kind=kLoop, calls=%fused_computation.29 | loop fusion | bytes 2097160 | tf_op jit(solution)/shard_map/slice | solution.py:1686
  16.8 0.4 copy.28
  17.3 0.7 fusion.4
  18.0 0.7 fusion.2
  18.7 6.4 %connect_first.1 = (f32[4,128,8]{2,1,0:T(8,128)}, f32[4,128,8]{2,1,0:T(8,128)}, bf16[128,2048]{1,0:T(8,128)(2,1)}) custom-call(bf16[4,128,2048]{2,1,0:T(8,128)(2,1)} %bitcast.36, f32[8,2048]{1,0:T(8,128)} %get-tuple-element.123.dynamic_ref.refs_6_, f32[4,8]{1,0:T(4,128)} %get-tuple-element.127.static_ref), custom_call_target="tpu_custom_call" | custom-call | tf_op jit(solution)/shard_map/connect_first/pallas_call | solution.py:1392
  25.0 3.0 collective-permute-start
  28.0 1.5 collective-permute-start.1
  29.5 42.9 %line_rows.1 = bf16[8,128,2048]{2,1,0:T(8,128)(2,1)} custom-call(bf16[128,2048]{1,0:T(8,128)(2,1)} %get-tuple-element.58.rows_ref), custom_call_target="tpu_custom_call" | custom-call | tf_op jit(solution)/shard_map/line_rows/pallas_call | solution.py:271
  72.5 0.9 slice.55
  73.5 0.5 collective-permute-start.2
  74.0 0.8 slice.56
  74.8 0.6 collective-permute-start.3
  75.4 1.1 copy.20.column_ref
  76.6 3.1 fusion
  79.7 22.0 %attention_forward.1 = (bf16[1024,256]{1,0:T(8,128)(2,1)}, bf16[1024,256]{1,0:T(8,128)(2,1)}, bf16[1024,256]{1,0:T(8,128)(2,1)}, bf16[1024,256]{1,0:T(8,128)(2,1...) custom-call(bf16[1024,2048]{1,0:T(8,128)(2,1)} %bitcast.39, ...), custom_call_target="tpu_custom_call" | custom-call | tf_op jit(solution)/shard_map/attention_forward/pallas_call | solution.py:1268
  102.0 1.3 collective-permute-start.4
  103.4 0.4 collective-permute-start.6
  103.9 0.4 collective-permute-start.8
  104.3 0.6 pad_add_fusion.1.core_ref
  104.9 0.8 collective-permute-done.4.refs_5_
  105.7 3.0 collective-permute-done.5.refs_6_
  108.7 1.5 collective-permute-done.6.refs_7_
  110.2 13.9 %connect_middle.1 = (f32[4,128,2048]{2,1,0:T(8,128)}, f32[128,2048]{1,0:T(8,128)}, f32[4,128,8]{2,1,0:T(8,128)}, f32[4,128,8]{2,1,0:T(8,128)}, bf16[2,128,2048]{2,1,0:T(8,128)(2,1)}) custom-call(s32[2]{0:T(128)} %pad_add_fusion.1.core_ref, bf16[4,128,2048]{2,1,0:T(8,128)(2,1)} %bitcast.37, f32[4,128,8]{2,1,0:T(8,128)} %get-tuple-element.56.coef_ref.refs_8_.refs_1_, ...), custom_call_target="tpu_custom_call" | custom-call | tf_op jit(solution)/shard_map/connect_middle/pallas_call | solution.py:1445
  124.1 83.9 %ffn_rows.1 = (bf16[2,4,256,2048]{3,2,1,0:T(8,128)(2,1)}, bf16[2,4,256,2048]{3,2,1,0:T(8,128)(2,1)}, bf16[1024,1024]{1,0:T(8,128)(2,1)}, bf16[1024,1024]{1,0:T(8...) custom-call(bf16[256,2048]{1,0:T(8,128)(2,1)} %bitcast.62, bf16[3,2048,2048]{2,1,0:T(8,128)(2,1)} %bitcast.56), custom_call_target="tpu_custom_call" | custom-call | flops 25769803776 | bytes 52428800 | tf_op jit(solution)/shard_map/ffn_rows/pallas_call | solution.py:980
  208.1 74.7 %ffn_weights.1 = (bf16[2,3,512,512]{3,2,1,0:T(8,128)(2,1)}, f32[256,2048]{1,0:T(8,128)}, bf16[3,512,512]{2,1,0:T(8,128)(2,1)}) custom-call(bf16[8,2,128,2048]{3,2,1,0:T(8,128)(2,1)} %bitcast.63, bf16[8,2,128,2048]{3,2,1,0:T(8,128)(2,1)} %bitcast.64, bf16[1024,1024]{1,0:T(8,128)(2,1)} %get-tuple-element.74.refs_2_, ...), custom_call_target="tpu_custom_call" | custom-call | flops 25769803776 | bytes 52428800 | tf_op jit(solution)/shard_map/ffn_weights/pallas_call | solution.py:1138
  282.9 0.6 fusion.5
  283.5 13.2 %connect_back.2 = (f32[4,128,2048]{2,1,0:T(8,128)}, f32[8,2048]{1,0:T(8,128)}, f32[8,8]{1,0:T(8,128)}, bf16[4,128,2048]{2,1,0:T(8,128)(2,1)}, bf16[128,2048]{1,0:T(8,128)(2,1)}) custom-call(f32[4,128,2048]{2,1,0:T(8,128)} %get-tuple-element.68.refs_0_, f32[4,128,8]{2,1,0:T(8,128)} %get-tuple-element.69.refs_1_, f32[4,128,8]{2,1,0:T(8,128)} %get-tuple-element.70.refs_2_, ...), custom_call_target="tpu_custom_call" | custom-call | tf_op jit(solution)/shard_map/connect_back/pallas_call | solution.py:1651
  296.7 24.8 %project_back.1 = (bf16[8,128,256]{2,1,0:T(8,128)(2,1)}, bf16[8,128,256]{2,1,0:T(8,128)(2,1)}) custom-call(bf16[128,2048]{1,0:T(8,128)(2,1)} %get-tuple-element.86.grad_ref, bf16[512,1024]{1,0:T(8,128)(2,1)} %bitcast.45, bf16[512,1024]{1,0:T(8,128)(2,1)} %copy-done.1, bf16[512,1024]{1,0:T(8,128)(2,1)} %copy-done.2, ...), custom_call_target="tpu_custom_call" | custom-call | tf_op jit(solution)/shard_map/project_back/pallas_call | solution.py:1544
  321.5 5.4 %all-to-all-start = ((bf16[8,128,256]{2,1,0:T(8,128)(2,1)}), bf16[8,128,256]{2,1,0:T(8,128)(2,1)}, u32[]{:S(2)}, u32[]{:S(2)}) async-start(bf16[8,128,256]{2,1,0:T(8,128)(2,1)} %get-tuple-element.94), calls=%async_computation | async-start | bytes 1048576 | tf_op jit(solution)/shard_map/all_to_all | solution.py:1766
  326.9 18.1 %attention_backward.1 = (bf16[1024,768]{1,0:T(8,128)(2,1)}, bf16[1024,2048]{1,0:T(8,128)(2,1)}) custom-call(bf16[1024,256]{1,0:T(8,128)(2,1)} %get-tuple-element.83.query_ref, bf16[1024,256]{1,0:T(8,128)(2,1)} %get-tuple-element.84.key_ref, bf16[1024,256]{1,0:T(8,128)(2,1)} %get-tuple-element.85.value_ref, bf16[1024,256]{1,0:T(8,128)(2,1)} %bitcast.50, ...), custom_call_target="tpu_custom_call" | custom-call | tf_op jit(solution)/shard_map/attention_backward/pallas_call | solution.py:1328
  345.0 1.5 constant_dynamic-update-slice_fusion.1
  346.6 49.1 %attention_sums.1 = (f32[128,2048]{1,0:T(8,128)}, f32[512,1024]{1,0:T(8,128)}) custom-call(bf16[8,128,2048]{2,1,0:T(8,128)(2,1)} %bitcast.60, bf16[1024,2048]{1,0:T(8,128)(2,1)} %bitcast.40, bf16[1024,768]{1,0:T(8,128)(2,1)} %get-tuple-element.92.refs_1_, bf16[8,1024,256]{2,1,0:T(8,128)(2,1)} %bitcast.58, bf16[1024,256]{1,0:T(8,128)(2,1)} %bitcast.22.refs_3_), custom_call_target="tpu_custom_call" | custom-call | flops 4294967296 | bytes 16777216 | tf_op jit(solution)/shard_map/attention_sums/pallas_call | solution.py:665
  395.8 1.5 constant_dynamic-update-slice_fusion
  397.3 1.9 constant_dynamic-slice_fusion.1
  399.2 11.2 %connect_back.3 = (f32[4,128,2048]{2,1,0:T(8,128)}, f32[8,2048]{1,0:T(8,128)}, f32[8,8]{1,0:T(8,128)}) custom-call(bf16[4,128,2048]{2,1,0:T(8,128)(2,1)} %bitcast.38, f32[4,128,8]{2,1,0:T(8,128)} %get-tuple-element.56.coef_ref.refs_8_.refs_1_, f32[4,128,8]{2,1,0:T(8,128)} %get-tuple-element.80.refs_2_, f32[128,2048]{1,0:T(8,128)} %get-tuple-element.81.refs_3_, ...), custom_call_target="tpu_custom_call" | custom-call | tf_op jit(solution)/shard_map/connect_back/pallas_call | solution.py:1651
  410.4 0.8 slice.63
  411.3 0.9 pad_maximum_fusion
  412.2 0.7 reshape.94.values_ref
  412.9 16.9 %sum_everywhere.1 = f32[8,8,512]{2,1,0:T(8,128)} custom-call(f32[8,8,512]{2,1,0:T(8,128)} %reshape.94.values_ref), custom_call_target="tpu_custom_call" | custom-call | tf_op jit(solution)/shard_map/sum_everywhere/pallas_call | solution.py:727
  429.8 0.9 slice.65
  430.7 1.0 reshape.96
  431.7 0.7 copy.22
  432.4 0.7 reshape.97
  433.1 3.2 reshape.91
  436.2 3.0 convert_bitcast_fusion
  (54 shorter events, 1.3 us)
Async XLA Ops:
  7.2 72.5 %all-gather.3.cloned.1.call-start = ((), (), s32[]{:S(2)}) async-start(), calls=%async_computation.2 | async-start | bytes 3932160 | tf_op jit(solution)/shard_map/all_gather | solution.py:53
  10.9 335.7 %all-gather.5.cloned.1.call-start = ((), (), s32[]{:S(2)}) async-start(), calls=%async_computation.3 | async-start | bytes 4718592 | tf_op jit(solution)/shard_map/all_gather | solution.py:53
  11.0 6.2 %copy-start.4 = (f32[2,6,2048]{2,0,1:T(2,128)S(1)}, f32[2,6,2048]{2,0,1:T(2,128)}, u32[]{:S(2)}) copy-start(f32[2,6,2048]{2,0,1:T(2,128)} %param.10) | copy-start | bytes 294916
  11.0 6.3 %copy-start.7 = (f32[2,4,6]{2,1,0:T(4,128)S(1)}, f32[2,4,6]{2,1,0:T(4,128)}, u32[]{:S(2)}) copy-start(f32[2,4,6]{2,1,0:T(4,128)} %param.11) | copy-start | bytes 580
  17.2 84.8 %copy-start = (bf16[512,1,1024]{2,0,1:T(8,128)(2,1)}, bf16[512,1,1024]{2,0,1:T(8,128)(2,1)S(1)}, u32[]{:S(2)}) copy-start(bf16[512,1,1024]{2,0,1:T(8,128)(2,1)S(1)} %copy.28) | copy-start | bytes 3145732
  18.7 53.8 %copy-start.9 = (s32[8]{0:T(128)S(1)}, s32[8]{0:T(128)}, u32[]{:S(2)}) copy-start(s32[8]{0:T(128)} %param.13) | copy-start | bytes 100
  25.0 47.5 %collective-permute-start = (bf16[512,1024]{1,0:T(8,128)(2,1)S(1)}, bf16[512,1024]{1,0:T(8,128)(2,1)S(1)}, u32[]{:S(2)}, u32[]{:S(2)}) collective-permute-start(bf16[512,1024]{1,0:T(8,128)(2,1)S(1)} %bitcast.41), channel_id=1, source_target_pairs={{0,1},{1,0},{2,3},{3,2},{4,5},{5,4},{6,7},{7,6},{8,9},{9,8},{10,11... | collective-permute-start | bytes 3145736 | tf_op jit(solution)/shard_map/ppermute | solution.py:1692
  28.0 44.5 %collective-permute-start.1 = (bf16[512,1024]{1,0:T(8,128)(2,1)S(1)}, bf16[512,1024]{1,0:T(8,128)(2,1)S(1)}, u32[]{:S(2)}, u32[]{:S(2)}) collective-permute-start(bf16[512,1024]{1,0:T(8,128)(2,1)S(1)} %bitcast.42), channel_id=1, source_target_pairs={{0,2},{1,3},{2,0},{3,1},{4,6},{5,7},{6,4},{7,5},{8,10},{9,11},{10,... | collective-permute-start | bytes 3145736 | tf_op jit(solution)/shard_map/ppermute | solution.py:1692
  72.5 30.8 %copy-start.1 = (bf16[512,1024]{1,0:T(8,128)(2,1)}, bf16[512,1024]{1,0:T(8,128)(2,1)S(1)}, u32[]{:S(2)}) copy-start(bf16[512,1024]{1,0:T(8,128)(2,1)S(1)} %collective-permute-done.refs_1_) | copy-start | bytes 3145732
  72.5 30.9 %copy-start.2 = (bf16[512,1024]{1,0:T(8,128)(2,1)}, bf16[512,1024]{1,0:T(8,128)(2,1)S(1)}, u32[]{:S(2)}) copy-start(bf16[512,1024]{1,0:T(8,128)(2,1)S(1)} %collective-permute-done.1.refs_2_) | copy-start | bytes 3145732
  73.5 28.3 %collective-permute-start.2 = (bf16[256,1024]{1,0:T(8,128)(2,1)}, bf16[256,1024]{1,0:T(8,128)(2,1)}, u32[]{:S(2)}, u32[]{:S(2)}) collective-permute-start(bf16[256,1024]{1,0:T(8,128)(2,1)} %slice.55), channel_id=1, source_target_pairs={{0,2},{1,3},{2,0},{3,1},{4,6},{5,7},{6,4},{7,5},{8,10},{9,11},{10,... | collective-permute-start | bytes 1572872 | tf_op jit(solution)/shard_map/ppermute | solution.py:1719
  74.8 26.9 %collective-permute-start.3 = (bf16[256,1024]{1,0:T(8,128)(2,1)}, bf16[256,1024]{1,0:T(8,128)(2,1)}, u32[]{:S(2)}, u32[]{:S(2)}) collective-permute-start(bf16[256,1024]{1,0:T(8,128)(2,1)} %slice.56), channel_id=1, source_target_pairs={{0,1},{1,0},{2,3},{3,2},{4,5},{5,4},{6,7},{7,6},{8,9},{9,8},{10,11... | collective-permute-start | bytes 1572872 | tf_op jit(solution)/shard_map/ppermute | solution.py:1720
  75.4 4.3 copy-start.5
  101.8 294.0 %reduce-scatter.2.cloned.1.call-start = ((), (), s32[]{:S(2)}) async-start(), calls=%async_computation.4 | async-start | bytes 4718592 | tf_op jit(solution)/shard_map/reduce_scatter | solution.py:1758
  102.0 3.7 collective-permute-start.4
  103.3 5.4 %collective-permute-start.5 = (bf16[512,1024]{1,0:T(8,128)(2,1)S(1)}, bf16[512,1024]{1,0:T(8,128)(2,1)}, u32[]{:S(2)}, u32[]{:S(2)}) collective-permute-start(bf16[512,1024]{1,0:T(8,128)(2,1)S(1)} %collective-permute-done.refs_1_), channel_id=1, source_target_pairs={{0,4},{4,0},{8,12},{12,8},{16,20},{20,16},{24,28},{28,24},{1,5},{5... | collective-permute-start | bytes 3145736 | tf_op jit(solution)/shard_map/ppermute | solution.py:1697
  103.4 6.8 %collective-permute-start.6 = (bf16[512,1024]{1,0:T(8,128)(2,1)S(1)}, bf16[512,1024]{1,0:T(8,128)(2,1)}, u32[]{:S(2)}, u32[]{:S(2)}) collective-permute-start(bf16[512,1024]{1,0:T(8,128)(2,1)S(1)} %collective-permute-done.1.refs_2_), channel_id=1, source_target_pairs={{0,4},{4,0},{8,12},{12,8},{16,20},{20,16},{24,28},{28,24},{1,5},{5... | collective-permute-start | bytes 3145736 | tf_op jit(solution)/shard_map/ppermute | solution.py:1697
  103.8 6.4 %collective-permute-start.7 = (bf16[256,1024]{1,0:T(8,128)(2,1)}, bf16[256,1024]{1,0:T(8,128)(2,1)}, u32[]{:S(2)}, u32[]{:S(2)}) collective-permute-start(bf16[256,1024]{1,0:T(8,128)(2,1)} %collective-permute-done.2.refs_3_), channel_id=1, source_target_pairs={{0,4},{4,0},{8,12},{12,8},{16,20},{20,16},{24,28},{28,24},{1,5},{5... | collective-permute-start | bytes 1572872 | tf_op jit(solution)/shard_map/ppermute | solution.py:1697
  103.9 6.3 %collective-permute-start.8 = (bf16[256,1024]{1,0:T(8,128)(2,1)}, bf16[256,1024]{1,0:T(8,128)(2,1)}, u32[]{:S(2)}, u32[]{:S(2)}) collective-permute-start(bf16[256,1024]{1,0:T(8,128)(2,1)} %collective-permute-done.3.refs_4_), channel_id=1, source_target_pairs={{0,4},{4,0},{8,12},{12,8},{16,20},{20,16},{24,28},{28,24},{1,5},{5... | collective-permute-start | bytes 1572872 | tf_op jit(solution)/shard_map/ppermute | solution.py:1697
  321.5 25.1 %all-to-all-start = ((bf16[8,128,256]{2,1,0:T(8,128)(2,1)}), bf16[8,128,256]{2,1,0:T(8,128)(2,1)}, u32[]{:S(2)}, u32[]{:S(2)}) async-start(bf16[8,128,256]{2,1,0:T(8,128)(2,1)} %get-tuple-element.94), calls=%async_computation | async-start | bytes 1048576 | tf_op jit(solution)/shard_map/all_to_all | solution.py:1766
  397.3 1.9 copy-start.8
  399.1 37.1 %collective-permute-start.9 = (bf16[3,1024,256]{2,1,0:T(8,128)(2,1)}, bf16[3,1024,256]{2,1,0:T(8,128)(2,1)S(1)}, u32[]{:S(2)}, u32[]{:S(2)}) collective-permute-start(bf16[3,1024,256]{2,1,0:T(8,128)(2,1)} %get-tuple-element.121), channel_id=1, source_target_pairs={{0,4},{4,0},{8,12},{12,8},{16,20},{20,16},{24,28},{28,24},{1,5},{5... | collective-permute-start | bytes 4718600 | tf_op jit(solution)/shard_map/ppermute | solution.py:1779
  399.2 12.1 %copy-start.6 = (f32[8,2048]{1,0:T(8,128)S(1)}, f32[8,2048]{1,0:T(8,128)}, u32[]{:S(2)}) copy-start(f32[8,2048]{1,0:T(8,128)} %get-tuple-element.103) | copy-start | bytes 196612
  410.4 25.9 %copy-start.3 = (bf16[3,1024,256]{2,1,0:T(8,128)(2,1)S(1)}, bf16[3,1024,256]{2,1,0:T(8,128)(2,1)}, u32[]{:S(2)}) copy-start(bf16[3,1024,256]{2,1,0:T(8,128)(2,1)} %get-tuple-element.120) | copy-start | bytes 4718596
Sparse Core Ops, SparseCore 0:
  11.0 61.5 all-gather.2
  101.9 85.4 all-gather.4
  282.9 50.5 reduce-scatter.1

commit v8 on v7

--- a/solution.py
+++ b/solution.py
@@ -1014,7 +1014,7 @@
     sides = n_ctx // 4
     wide = half // sides
     fused = partial is not None
-    early = steps // 2 if fused else 0
+    early = 1 if fused else 0
     assert not fused or sides == 2
 
     def kernel(*refs):
@@ -1739,6 +1739,7 @@
         ffn_all, mirror_rows, *hidden, sums = ffn_rows(n_ctx, ffn_own, planes, n_own)
         ffn_all, mirror_rows = (part.reshape(blocks, 2, length, features) for part in (ffn_all, mirror_rows))
         mirror_rows = [mirror_rows]
+        attended, sums = lax.optimization_barrier((attended, sums))
         attended_all = gather(attended, "ctx").reshape(n_ctx, rows, own)
         weight_parts, sums, weight_early = ffn_weights(
             n_ctx, n_fsdp, sums, ffn_all, mirror_rows, hidden, planes, n_own

time: 454 us -> 441 us (0.971)
  Pallas kernels: 377 us -> 367 us
    pallas_call x1, Pallas kernels: 74.7 us -> 61.7 us  [ffn_weights(): pl.pallas_call(kernel, grid=(steps,), in_specs=in_specs, out_specs=out_sp...]
  transfers between devices with their start and end apart: 14 -> 14, of which waited for: 3 -> 2; matrix products, arithmetic and copies ran while one was open for 6% -> 6% of each run, Pallas kernels for 84% -> 62%
where the time goes in v8:
time: 441 us; the launch traced here: 435 us
  Pallas kernels  367 us (83%)
  local copies, waits for them, and re-layouts  30.7 us (7%)
  between operations  14.2 us (3%)
  starting transfers between devices  13 us (3%)
  other arithmetic  7.87 us (2%)
    pallas_call x1, Pallas kernels, ffn_rows(): pl.pallas_call(kernel, in_specs=any_specs(2), out_specs=any_specs(6), out...  83.7 us
    pallas_call x1, Pallas kernels, ffn_weights(): pl.pallas_call(kernel, grid=(steps,), in_specs=in_specs, out_specs=out_sp...  61.7 us
    pallas_call x1, Pallas kernels, attention_sums(): pl.pallas_call(kernel, out_shape=[jax.ShapeDtypeStruct(partial.shape[-2:]...  52 us
    pallas_call x1, Pallas kernels, line_rows(): pl.pallas_call(kernel, out_shape=jax.ShapeDtypeStruct((n_ctx,) + rows.sha...  43 us
    pallas_call x1, Pallas kernels, project_back(): pl.pallas_call(kernel, in_specs=[pl.BlockSpec(memory_space=pltpu.VMEM)] *...  26.2 us
    pallas_call x2, Pallas kernels, connect_back(): pl.pallas_call(kernel, grid=(steps,), in_specs=in_specs, out_specs=out_sp...  24.3 us
    pallas_call x1, Pallas kernels, attention_forward(): pl.pallas_call(kernel, grid=(steps,), in_specs=[pl.BlockSpec((SPAN, featu...  22.1 us
    pallas_call x1, Pallas kernels, attention_backward(): pl.pallas_call(kernel, grid=(steps,), in_specs=[whole_block(a.shape) for...  18.2 us
  transfers between devices with their start and end apart: 14, of which 2 were waited for; matrix products, arithmetic and copies ran while one was open for 6% of the time, Pallas kernels for 62%

profile of v8, /device:TPU:0, one launch (start us, length us, event | category | flops | bytes accessed | tf_op | source)
XLA Modules:
  0.0 435.2 jit_solution(13221166863843053849)
XLA Ops:
  7.2 1.6 constant_dynamic-slice_fusion.2
  8.9 0.9 copy.26
  9.8 1.2 copy.19
  11.1 5.8 %constant_dynamic-slice_fusion.3 = bf16[512,1,1024]{2,1,0:T(2,128)(2,1)S(1)} fusion(bf16[512,4,2048]{2,1,0:T(4,128)(2,1)} %param.8, s32[]{:T(128)S(6)} %add.63, s32[]{:T(128)S(6)} %select_n.36), kind=kLoop, calls=%fused_computation.29 | loop fusion | bytes 2097160 | tf_op jit(solution)/shard_map/slice | solution.py:1686
  16.9 0.4 copy.28
  17.3 0.7 fusion.4
  17.9 0.6 fusion.2
  18.6 6.5 %connect_first.1 = (f32[4,128,8]{2,1,0:T(8,128)}, f32[4,128,8]{2,1,0:T(8,128)}, bf16[128,2048]{1,0:T(8,128)(2,1)}) custom-call(bf16[4,128,2048]{2,1,0:T(8,128)(2,1)} %bitcast.36, f32[8,2048]{1,0:T(8,128)} %get-tuple-element.127.dynamic_ref.refs_6_, f32[4,8]{1,0:T(4,128)} %get-tuple-element.131.static_ref), custom_call_target="tpu_custom_call" | custom-call | tf_op jit(solution)/shard_map/connect_first/pallas_call | solution.py:1392
  25.1 3.0 collective-permute-start.1
  28.1 1.5 collective-permute-start
  29.6 43.0 %line_rows.1 = bf16[8,128,2048]{2,1,0:T(8,128)(2,1)} custom-call(bf16[128,2048]{1,0:T(8,128)(2,1)} %get-tuple-element.60.rows_ref), custom_call_target="tpu_custom_call" | custom-call | tf_op jit(solution)/shard_map/line_rows/pallas_call | solution.py:271
  72.7 0.9 slice.55
  73.6 0.4 collective-permute-start.5
  74.0 0.8 slice.56
  74.8 0.1 collective-permute-start.6
  74.9 0.5 collective-permute-start.3
  75.4 0.5 collective-permute-start.2
  76.0 1.0 copy.20.column_ref
  77.1 3.0 fusion
  80.2 22.1 %attention_forward.1 = (bf16[1024,256]{1,0:T(8,128)(2,1)}, bf16[1024,256]{1,0:T(8,128)(2,1)}, bf16[1024,256]{1,0:T(8,128)(2,1)}, bf16[1024,256]{1,0:T(8,128)(2,1...) custom-call(bf16[1024,2048]{1,0:T(8,128)(2,1)} %bitcast.39, ...), custom_call_target="tpu_custom_call" | custom-call | tf_op jit(solution)/shard_map/attention_forward/pallas_call | solution.py:1268
  102.3 1.3 collective-permute-start.7
  103.7 0.6 pad_add_fusion.1.core_ref
  104.3 1.2 collective-permute-done.7.refs_8_
  105.5 0.7 collective-permute-done.8.refs_9_
  106.2 13.6 %connect_middle.1 = (f32[4,128,2048]{2,1,0:T(8,128)}, f32[128,2048]{1,0:T(8,128)}, f32[4,128,8]{2,1,0:T(8,128)}, f32[4,128,8]{2,1,0:T(8,128)}, bf16[2,128,2048]{2,1,0:T(8,128)(2,1)}) custom-call(s32[2]{0:T(128)} %pad_add_fusion.1.core_ref, bf16[4,128,2048]{2,1,0:T(8,128)(2,1)} %bitcast.37, f32[4,128,8]{2,1,0:T(8,128)} %get-tuple-element.58.coef_ref.refs_8_.refs_1_, ...), custom_call_target="tpu_custom_call" | custom-call | tf_op jit(solution)/shard_map/connect_middle/pallas_call | solution.py:1445
  119.9 83.7 %ffn_rows.1 = (bf16[2,4,256,2048]{3,2,1,0:T(8,128)(2,1)}, bf16[2,4,256,2048]{3,2,1,0:T(8,128)(2,1)}, bf16[1024,1024]{1,0:T(8,128)(2,1)}, bf16[1024,1024]{1,0:T(8...) custom-call(bf16[256,2048]{1,0:T(8,128)(2,1)} %bitcast.63, bf16[3,2048,2048]{2,1,0:T(8,128)(2,1)} %bitcast.57), custom_call_target="tpu_custom_call" | custom-call | flops 25769803776 | bytes 52428800 | tf_op jit(solution)/shard_map/ffn_rows/pallas_call | solution.py:980
  203.7 61.7 %ffn_weights.1 = (bf16[2,3,768,512]{3,2,1,0:T(8,128)(2,1)}, f32[256,2048]{1,0:T(8,128)}, bf16[3,256,512]{2,1,0:T(8,128)(2,1)}) custom-call(bf16[8,2,128,2048]{3,2,1,0:T(8,128)(2,1)} %bitcast.64, bf16[8,2,128,2048]{3,2,1,0:T(8,128)(2,1)} %bitcast.65, bf16[1024,1024]{1,0:T(8,128)(2,1)} %get-tuple-element.76.refs_2_, ...), custom_call_target="tpu_custom_call" | custom-call | flops 25769803776 | bytes 52428800 | tf_op jit(solution)/shard_map/ffn_weights/pallas_call | solution.py:1138
  265.5 0.5 fusion.5
  266.0 13.2 %connect_back.2 = (f32[4,128,2048]{2,1,0:T(8,128)}, f32[8,2048]{1,0:T(8,128)}, f32[8,8]{1,0:T(8,128)}, bf16[4,128,2048]{2,1,0:T(8,128)(2,1)}, bf16[128,2048]{1,0:T(8,128)(2,1)}) custom-call(f32[4,128,2048]{2,1,0:T(8,128)} %get-tuple-element.70.refs_0_, f32[4,128,8]{2,1,0:T(8,128)} %get-tuple-element.71.refs_1_, f32[4,128,8]{2,1,0:T(8,128)} %get-tuple-element.72.refs_2_, ...), custom_call_target="tpu_custom_call" | custom-call | tf_op jit(solution)/shard_map/connect_back/pallas_call | solution.py:1651
  279.2 26.2 %project_back.1 = (bf16[8,128,256]{2,1,0:T(8,128)(2,1)}, bf16[8,128,256]{2,1,0:T(8,128)(2,1)}) custom-call(bf16[128,2048]{1,0:T(8,128)(2,1)} %get-tuple-element.90.grad_ref, bf16[512,1024]{1,0:T(8,128)(2,1)} %bitcast.45, bf16[512,1024]{1,0:T(8,128)(2,1)} %copy-done.2, bf16[512,1024]{1,0:T(8,128)(2,1)} %copy-done.1, ...), custom_call_target="tpu_custom_call" | custom-call | tf_op jit(solution)/shard_map/project_back/pallas_call | solution.py:1544
  305.5 5.5 %all-to-all-start = ((bf16[8,128,256]{2,1,0:T(8,128)(2,1)}), bf16[8,128,256]{2,1,0:T(8,128)(2,1)S(1)}, u32[]{:S(2)}, u32[]{:S(2)}) async-start(bf16[8,128,256]{2,1,0:T(8,128)(2,1)} %get-tuple-element.98), calls=%async_computation | async-start | bytes 1048576 | tf_op jit(solution)/shard_map/all_to_all | solution.py:1767
  311.0 18.2 %attention_backward.1 = (bf16[1024,768]{1,0:T(8,128)(2,1)}, bf16[1024,2048]{1,0:T(8,128)(2,1)}) custom-call(bf16[1024,256]{1,0:T(8,128)(2,1)} %get-tuple-element.87.query_ref, bf16[1024,256]{1,0:T(8,128)(2,1)} %get-tuple-element.88.key_ref, bf16[1024,256]{1,0:T(8,128)(2,1)} %get-tuple-element.89.value_ref, bf16[1024,256]{1,0:T(8,128)(2,1)} %bitcast.50, ...), custom_call_target="tpu_custom_call" | custom-call | tf_op jit(solution)/shard_map/attention_backward/pallas_call | solution.py:1328
  329.2 1.0 constant_dynamic-update-slice_fusion.1
  330.2 0.8 copy-done.4
  331.0 52.0 %attention_sums.1 = (f32[128,2048]{1,0:T(8,128)}, f32[512,1024]{1,0:T(8,128)}) custom-call(bf16[8,128,2048]{2,1,0:T(8,128)(2,1)} %bitcast.61, bf16[1024,2048]{1,0:T(8,128)(2,1)} %bitcast.40, bf16[1024,768]{1,0:T(8,128)(2,1)} %get-tuple-element.96.refs_1_, bf16[8,1024,256]{2,1,0:T(8,128)(2,1)} %bitcast.59, bf16[1024,256]{1,0:T(8,128)(2,1)} %bitcast.51), custom_call_target="tpu_custom_call" | custom-call | flops 4294967296 | bytes 16777216 | tf_op jit(solution)/shard_map/attention_sums/pallas_call | solution.py:665
  383.0 3.2 constant_dynamic-update-slice_fusion
  386.3 3.2 constant_dynamic-slice_fusion.1
  389.6 3.2 reshape.91
  392.8 11.1 %connect_back.3 = (f32[4,128,2048]{2,1,0:T(8,128)}, f32[8,2048]{1,0:T(8,128)}, f32[8,8]{1,0:T(8,128)}) custom-call(bf16[4,128,2048]{2,1,0:T(8,128)(2,1)} %bitcast.38, f32[4,128,8]{2,1,0:T(8,128)} %get-tuple-element.58.coef_ref.refs_8_.refs_1_, f32[4,128,8]{2,1,0:T(8,128)} %get-tuple-element.84.refs_2_, f32[128,2048]{1,0:T(8,128)} %get-tuple-element.85.refs_3_, ...), custom_call_target="tpu_custom_call" | custom-call | tf_op jit(solution)/shard_map/connect_back/pallas_call | solution.py:1651
  403.9 0.7 slice.63
  404.7 0.9 pad_maximum_fusion
  405.6 0.7 reshape.94.values_ref
  406.3 15.9 %sum_everywhere.1 = f32[8,8,512]{2,1,0:T(8,128)} custom-call(f32[8,8,512]{2,1,0:T(8,128)} %reshape.94.values_ref), custom_call_target="tpu_custom_call" | custom-call | tf_op jit(solution)/shard_map/sum_everywhere/pallas_call | solution.py:727
  422.2 0.9 slice.65
  423.1 1.0 reshape.96
  424.0 0.7 reshape.97
  424.8 0.7 copy.22
  425.5 3.0 convert_bitcast_fusion
  (56 shorter events, 1.0 us)
Async XLA Ops:
  7.2 73.0 %all-gather.3.cloned.1.call-start = ((), (), s32[]{:S(2)}) async-start(), calls=%async_computation.2 | async-start | bytes 3932160 | tf_op jit(solution)/shard_map/all_gather | solution.py:53
  7.2 3.8 copy-start.5
  10.9 319.2 %all-gather.5.cloned.1.call-start = ((), (), s32[]{:S(2)}) async-start(), calls=%async_computation.3 | async-start | bytes 4718592 | tf_op jit(solution)/shard_map/all_gather | solution.py:53
  11.1 6.2 %copy-start.8 = (f32[2,4,6]{2,1,0:T(4,128)S(1)}, f32[2,4,6]{2,1,0:T(4,128)}, u32[]{:S(2)}) copy-start(f32[2,4,6]{2,1,0:T(4,128)} %param.11) | copy-start | bytes 580
  17.3 58.7 %copy-start = (bf16[512,1,1024]{2,0,1:T(8,128)(2,1)}, bf16[512,1,1024]{2,0,1:T(8,128)(2,1)S(1)}, u32[]{:S(2)}) copy-start(bf16[512,1,1024]{2,0,1:T(8,128)(2,1)S(1)} %copy.28) | copy-start | bytes 3145732
  18.6 54.0 %copy-start.10 = (s32[8]{0:T(128)S(1)}, s32[8]{0:T(128)}, u32[]{:S(2)}) copy-start(s32[8]{0:T(128)} %param.13) | copy-start | bytes 100
  25.1 47.6 %collective-permute-start.1 = (bf16[512,1024]{1,0:T(8,128)(2,1)S(1)}, bf16[512,1024]{1,0:T(8,128)(2,1)S(1)}, u32[]{:S(2)}, u32[]{:S(2)}) collective-permute-start(bf16[512,1024]{1,0:T(8,128)(2,1)S(1)} %bitcast.41), channel_id=1, source_target_pairs={{0,2},{1,3},{2,0},{3,1},{4,6},{5,7},{6,4},{7,5},{8,10},{9,11},{10,... | collective-permute-start | bytes 3145736 | tf_op jit(solution)/shard_map/ppermute | solution.py:1692
  28.1 44.6 %collective-permute-start = (bf16[512,1024]{1,0:T(8,128)(2,1)S(1)}, bf16[512,1024]{1,0:T(8,128)(2,1)S(1)}, u32[]{:S(2)}, u32[]{:S(2)}) collective-permute-start(bf16[512,1024]{1,0:T(8,128)(2,1)S(1)} %bitcast.42), channel_id=1, source_target_pairs={{0,1},{1,0},{2,3},{3,2},{4,5},{5,4},{6,7},{7,6},{8,9},{9,8},{10,11... | collective-permute-start | bytes 3145736 | tf_op jit(solution)/shard_map/ppermute | solution.py:1692
  72.7 29.6 %copy-start.1 = (bf16[512,1024]{1,0:T(8,128)(2,1)}, bf16[512,1024]{1,0:T(8,128)(2,1)S(1)}, u32[]{:S(2)}) copy-start(bf16[512,1024]{1,0:T(8,128)(2,1)S(1)} %collective-permute-done.1.refs_2_) | copy-start | bytes 3145732
  72.7 29.6 %copy-start.2 = (bf16[512,1024]{1,0:T(8,128)(2,1)}, bf16[512,1024]{1,0:T(8,128)(2,1)S(1)}, u32[]{:S(2)}) copy-start(bf16[512,1024]{1,0:T(8,128)(2,1)S(1)} %collective-permute-done.refs_1_) | copy-start | bytes 3145732
  73.6 30.7 %collective-permute-start.5 = (bf16[512,1024]{1,0:T(8,128)(2,1)S(1)}, bf16[512,1024]{1,0:T(8,128)(2,1)}, u32[]{:S(2)}, u32[]{:S(2)}) collective-permute-start(bf16[512,1024]{1,0:T(8,128)(2,1)S(1)} %collective-permute-done.refs_1_), channel_id=1, source_target_pairs={{0,4},{4,0},{8,12},{12,8},{16,20},{20,16},{24,28},{28,24},{1,5},{5... | collective-permute-start | bytes 3145736 | tf_op jit(solution)/shard_map/ppermute | solution.py:1697
  74.8 29.5 %collective-permute-start.6 = (bf16[512,1024]{1,0:T(8,128)(2,1)S(1)}, bf16[512,1024]{1,0:T(8,128)(2,1)}, u32[]{:S(2)}, u32[]{:S(2)}) collective-permute-start(bf16[512,1024]{1,0:T(8,128)(2,1)S(1)} %collective-permute-done.1.refs_2_), channel_id=1, source_target_pairs={{0,4},{4,0},{8,12},{12,8},{16,20},{20,16},{24,28},{28,24},{1,5},{5... | collective-permute-start | bytes 3145736 | tf_op jit(solution)/shard_map/ppermute | solution.py:1697
  74.9 27.4 %collective-permute-start.3 = (bf16[256,1024]{1,0:T(8,128)(2,1)}, bf16[256,1024]{1,0:T(8,128)(2,1)}, u32[]{:S(2)}, u32[]{:S(2)}) collective-permute-start(bf16[256,1024]{1,0:T(8,128)(2,1)} %slice.56), channel_id=1, source_target_pairs={{0,1},{1,0},{2,3},{3,2},{4,5},{5,4},{6,7},{7,6},{8,9},{9,8},{10,11... | collective-permute-start | bytes 1572872 | tf_op jit(solution)/shard_map/ppermute | solution.py:1720
  75.4 26.9 %collective-permute-start.2 = (bf16[256,1024]{1,0:T(8,128)(2,1)}, bf16[256,1024]{1,0:T(8,128)(2,1)}, u32[]{:S(2)}, u32[]{:S(2)}) collective-permute-start(bf16[256,1024]{1,0:T(8,128)(2,1)} %slice.55), channel_id=1, source_target_pairs={{0,2},{1,3},{2,0},{3,1},{4,6},{5,7},{6,4},{7,5},{8,10},{9,11},{10,... | collective-permute-start | bytes 1572872 | tf_op jit(solution)/shard_map/ppermute | solution.py:1719
  75.9 28.3 %collective-permute-start.4 = (bf16[512,1024]{1,0:T(8,128)(2,1)S(1)}, bf16[512,1024]{1,0:T(8,128)(2,1)}, u32[]{:S(2)}, u32[]{:S(2)}) collective-permute-start(bf16[512,1024]{1,0:T(8,128)(2,1)S(1)} %bitcast.43), channel_id=1, source_target_pairs={{0,4},{4,0},{8,12},{12,8},{16,20},{20,16},{24,28},{28,24},{1,5},{5... | collective-permute-start | bytes 3145736 | tf_op jit(solution)/shard_map/ppermute | solution.py:1697
  76.0 4.2 copy-start.6
  102.3 3.2 collective-permute-start.7
  103.6 2.6 collective-permute-start.8
  203.6 179.4 %reduce-scatter.2.cloned.1.call-start = ((), (), s32[]{:S(2)}) async-start(), calls=%async_computation.4 | async-start | bytes 7077888 | tf_op jit(solution)/shard_map/reduce_scatter | solution.py:1759
  305.5 24.7 %all-to-all-start = ((bf16[8,128,256]{2,1,0:T(8,128)(2,1)}), bf16[8,128,256]{2,1,0:T(8,128)(2,1)S(1)}, u32[]{:S(2)}, u32[]{:S(2)}) async-start(bf16[8,128,256]{2,1,0:T(8,128)(2,1)} %get-tuple-element.98), calls=%async_computation | async-start | bytes 1048576 | tf_op jit(solution)/shard_map/all_to_all | solution.py:1767
  311.0 18.2 %copy-start.3 = (bf16[3,256,512]{2,1,0:T(8,128)(2,1)S(1)}, bf16[3,256,512]{2,1,0:T(8,128)(2,1)}, u32[]{:S(2)}) copy-start(bf16[3,256,512]{2,1,0:T(8,128)(2,1)} %get-tuple-element.104) | copy-start | bytes 2359300
  330.2 0.8 copy-start.4
  386.3 3.3 copy-start.9
  389.5 36.0 %collective-permute-start.9 = (bf16[3,1024,256]{2,1,0:T(8,128)(2,1)}, bf16[3,1024,256]{2,1,0:T(8,128)(2,1)S(1)}, u32[]{:S(2)}, u32[]{:S(2)}) collective-permute-start(bf16[3,1024,256]{2,1,0:T(8,128)(2,1)} %get-tuple-element.125), channel_id=1, source_target_pairs={{0,4},{4,0},{8,12},{12,8},{16,20},{20,16},{24,28},{28,24},{1,5},{5... | collective-permute-start | bytes 4718600 | tf_op jit(solution)/shard_map/ppermute | solution.py:1780
  392.7 11.9 %copy-start.7 = (f32[8,2048]{1,0:T(8,128)S(1)}, f32[8,2048]{1,0:T(8,128)}, u32[]{:S(2)}) copy-start(f32[8,2048]{1,0:T(8,128)} %get-tuple-element.107) | copy-start | bytes 196612
Sparse Core Ops, SparseCore 0:
  11.1 61.5 all-gather.2
  203.8 57.2 all-gather.4
  265.5 78.2 reduce-scatter.1

commit v9 on v7

--- a/solution.py
+++ b/solution.py
@@ -841,22 +841,27 @@
         passing_copy(number, 1 - core).wait_recv()
 
 
-def ffn_rows(n_ctx, own, planes, n_own, chunk=256, wide=512):
+def ffn_rows(n_ctx, own, planes, attended, n_own, chunk=256, wide=512):
     n_fsdp = 4
     size, features = own.shape
     tokens = size // 2
     total = 2 * n_fsdp * tokens
 
     def kernel(
-        own_ref, planes_ref, all_ref, mirror_ref, hidden_a, hidden_b, hidden_c, partial_ref,
+        own_ref, planes_ref, attended_ref, all_ref, mirror_ref, hidden_a, hidden_b, hidden_c, partial_ref, heads_ref,
         rows, weights, hidden, partial, core_in, load, sq_s, sq_r, core_s, core_r, far_s, far_r, mi_s, mi_r, mc_s, mc_r, sum_s, sum_r, out_sem,
+        ri_s, ri_r, le_s, le_r, lc_s, lc_r, heads_sem,
     ):
         chip, core, fsdp, length = place(n_ctx)
         ctx = chip * 2 + core
         sibling = (chip * 2 + 1 - core, fsdp)
         mirror = ((length - 1 - chip) * 2 + core, fsdp)
         first, second, corner = fsdp_neighbours(fsdp)
-        greet([sibling, mirror] + fsdp_peers(n_fsdp, ctx, fsdp))
+        where = (chip, core, fsdp, length)
+        greet([mirror] + line_peers(*where) + fsdp_peers(n_fsdp, ctx, fsdp))
+        line = line_gather(attended_ref, heads_ref, ((ri_s, ri_r), (le_s, le_r), (lc_s, lc_r)), where)
+        heads_own = pltpu.make_async_copy(attended_ref, heads_ref.at[ctx], heads_sem)
+        heads_own.start()
         mine = pltpu.make_async_copy(own_ref, rows.at[core, fsdp], load.at[3])
         mine.start()
         start = pl.multiple_of(core * n_own, n_own)
@@ -957,15 +962,19 @@
         arriving[4].wait_recv()
         group(2, second)
         add_up(1, first)
-        for _ in range(3):
+        next(mirroring)
+        next(line)
+        for _ in range(2):
             next(mirroring)
         arriving[5].wait_recv()
         arriving[6].wait_recv()
         group(3, corner)
+        next(line)
         add_up(2, second)
         next(mirroring)
         add_up(3, corner)
-        run_all(mirroring, gathering)
+        run_all(mirroring, line, gathering)
+        heads_own.wait()
         for each in handed:
             each.wait_send()
         for each in far:
@@ -979,9 +988,17 @@
     all_rows = jax.ShapeDtypeStruct((2, n_fsdp) + own.shape, own.dtype)
     return pl.pallas_call(
         kernel,
-        in_specs=any_specs(2),
-        out_specs=any_specs(6),
-        out_shape=[all_rows, all_rows, act, act, act, jax.ShapeDtypeStruct((n_fsdp,) + own.shape, own.dtype)],
+        in_specs=any_specs(3),
+        out_specs=any_specs(7),
+        out_shape=[
+            all_rows,
+            all_rows,
+            act,
+            act,
+            act,
+            jax.ShapeDtypeStruct((n_fsdp,) + own.shape, own.dtype),
+            jax.ShapeDtypeStruct((n_ctx,) + attended.shape, attended.dtype),
+        ],
         scratch_shapes=[
             pltpu.VMEM((2, n_fsdp) + own.shape, own.dtype),
             pltpu.VMEM((3, n_own, features), own.dtype),
@@ -996,13 +1013,15 @@
         + dma_pair(6)
         + dma_pair(8)
         + dma_pair(4)
-        + [pltpu.SemaphoreType.DMA((2, 9))],
+        + [pltpu.SemaphoreType.DMA((2, 9))]
+        + dma_pair(n_ctx // 2) * 3
+        + [pltpu.SemaphoreType.DMA],
         compiler_params=params(6),
         cost_estimate=pl.CostEstimate(
             flops=12 * total * n_own * features, bytes_accessed=50 * 1024 * 1024, transcendentals=total * n_own
         ),
         name="ffn_rows",
-    )(own, planes)
+    )(own, planes, attended)
 
 
 def ffn_weights(n_ctx, n_fsdp, partial, rows, rows_mirror, hidden, planes, n_own, chunk=256):
@@ -1736,10 +1755,9 @@
     n_own = planes.shape[1] // 2
     blocks = 2 * n_fsdp
     if n_fsdp == 4:
-        ffn_all, mirror_rows, *hidden, sums = ffn_rows(n_ctx, ffn_own, planes, n_own)
+        ffn_all, mirror_rows, *hidden, sums, attended_all = ffn_rows(n_ctx, ffn_own, planes, attended, n_own)
         ffn_all, mirror_rows = (part.reshape(blocks, 2, length, features) for part in (ffn_all, mirror_rows))
         mirror_rows = [mirror_rows]
-        attended_all = gather(attended, "ctx").reshape(n_ctx, rows, own)
         weight_parts, sums, weight_early = ffn_weights(
             n_ctx, n_fsdp, sums, ffn_all, mirror_rows, hidden, planes, n_own
         )

time: 454 us -> 441 us (0.971)
  Pallas kernels: 377 us -> 371 us
    pallas_call x1, Pallas kernels: 74.7 us -> 53.8 us  [ffn_weights(): pl.pallas_call(kernel, grid=(steps,), in_specs=in_specs, out_specs=out_sp...]
    pallas_call x1, Pallas kernels: 83.9 us -> 95.8 us  [ffn_rows(): pl.pallas_call(kernel, in_specs=any_specs(3), out_specs=any_specs(7), out...]
  transfers between devices with their start and end apart: 14 -> 13, of which waited for: 3 -> 2; matrix products, arithmetic and copies ran while one was open for 6% -> 6% of each run, Pallas kernels for 84% -> 48%
where the time goes in v9:
time: 441 us; the launch traced here: 435 us
  Pallas kernels  371 us (84%)
  local copies, waits for them, and re-layouts  27.5 us (6%)
  between operations  14.5 us (3%)
  starting transfers between devices  12.6 us (3%)
  other arithmetic  7.92 us (2%)
    pallas_call x1, Pallas kernels, ffn_rows(): pl.pallas_call(kernel, in_specs=any_specs(3), out_specs=any_specs(7), out...  95.8 us
    pallas_call x1, Pallas kernels, ffn_weights(): pl.pallas_call(kernel, grid=(steps,), in_specs=in_specs, out_specs=out_sp...  53.8 us
    pallas_call x1, Pallas kernels, attention_sums(): pl.pallas_call(kernel, out_shape=[jax.ShapeDtypeStruct(partial.shape[-2:]...  48.9 us
    pallas_call x1, Pallas kernels, line_rows(): pl.pallas_call(kernel, out_shape=jax.ShapeDtypeStruct((n_ctx,) + rows.sha...  42.9 us
    pallas_call x1, Pallas kernels, project_back(): pl.pallas_call(kernel, in_specs=[pl.BlockSpec(memory_space=pltpu.VMEM)] *...  27.6 us
    pallas_call x2, Pallas kernels, connect_back(): pl.pallas_call(kernel, grid=(steps,), in_specs=in_specs, out_specs=out_sp...  24.8 us
    pallas_call x1, Pallas kernels, attention_forward(): pl.pallas_call(kernel, grid=(steps,), in_specs=[pl.BlockSpec((SPAN, featu...  22.1 us
    pallas_call x1, Pallas kernels, attention_backward(): pl.pallas_call(kernel, grid=(steps,), in_specs=[whole_block(a.shape) for...  18.1 us
  transfers between devices with their start and end apart: 13, of which 2 were waited for; matrix products, arithmetic and copies ran while one was open for 6% of the time, Pallas kernels for 48%

profile of v9, /device:TPU:0, one launch (start us, length us, event | category | flops | bytes accessed | tf_op | source)
XLA Modules:
  0.0 435.4 jit_solution(11147093171244079485)
XLA Ops:
  7.2 1.6 constant_dynamic-slice_fusion.2
  8.9 0.9 copy.26
  9.8 1.2 copy.19
  11.1 5.8 %constant_dynamic-slice_fusion.3 = bf16[512,1,1024]{2,1,0:T(2,128)(2,1)S(1)} fusion(bf16[512,4,2048]{2,1,0:T(4,128)(2,1)} %param.8, s32[]{:T(128)S(6)} %add.63, s32[]{:T(128)S(6)} %select_n.36), kind=kLoop, calls=%fused_computation.29 | loop fusion | bytes 2097160 | tf_op jit(solution)/shard_map/slice | solution.py:1705
  16.9 0.4 copy.28
  17.3 0.7 fusion.4
  17.9 0.7 fusion.2
  18.6 6.5 %connect_first.1 = (f32[4,128,8]{2,1,0:T(8,128)}, f32[4,128,8]{2,1,0:T(8,128)}, bf16[128,2048]{1,0:T(8,128)(2,1)}) custom-call(bf16[4,128,2048]{2,1,0:T(8,128)(2,1)} %bitcast.35, f32[8,2048]{1,0:T(8,128)} %get-tuple-element.125.dynamic_ref.refs_6_, f32[4,8]{1,0:T(4,128)} %get-tuple-element.129.static_ref), custom_call_target="tpu_custom_call" | custom-call | tf_op jit(solution)/shard_map/connect_first/pallas_call | solution.py:1411
  25.1 3.0 collective-permute-start.1
  28.1 1.5 collective-permute-start
  29.6 42.9 %line_rows.1 = bf16[8,128,2048]{2,1,0:T(8,128)(2,1)} custom-call(bf16[128,2048]{1,0:T(8,128)(2,1)} %get-tuple-element.59.rows_ref), custom_call_target="tpu_custom_call" | custom-call | tf_op jit(solution)/shard_map/line_rows/pallas_call | solution.py:271
  72.7 0.9 slice.55
  73.6 0.4 collective-permute-start.5
  73.9 0.8 slice.56
  74.8 0.1 collective-permute-start.6
  74.9 0.6 collective-permute-start.3
  75.5 0.5 collective-permute-start.2
  76.0 1.1 copy.20.column_ref
  77.2 3.1 fusion
  80.2 22.1 %attention_forward.1 = (bf16[1024,256]{1,0:T(8,128)(2,1)}, bf16[1024,256]{1,0:T(8,128)(2,1)}, bf16[1024,256]{1,0:T(8,128)(2,1)}, bf16[1024,256]{1,0:T(8,128)(2,1...) custom-call(bf16[1024,2048]{1,0:T(8,128)(2,1)} %bitcast.38, ...), custom_call_target="tpu_custom_call" | custom-call | tf_op jit(solution)/shard_map/attention_forward/pallas_call | solution.py:1287
  102.4 1.3 collective-permute-start.7
  103.8 0.6 pad_add_fusion.1.core_ref
  104.4 1.2 collective-permute-done.7.refs_8_
  105.6 0.7 collective-permute-done.8.refs_9_
  106.3 13.6 %connect_middle.1 = (f32[4,128,2048]{2,1,0:T(8,128)}, f32[128,2048]{1,0:T(8,128)}, f32[4,128,8]{2,1,0:T(8,128)}, f32[4,128,8]{2,1,0:T(8,128)}, bf16[2,128,2048]{2,1,0:T(8,128)(2,1)}) custom-call(s32[2]{0:T(128)} %pad_add_fusion.1.core_ref, bf16[4,128,2048]{2,1,0:T(8,128)(2,1)} %bitcast.36, f32[4,128,8]{2,1,0:T(8,128)} %get-tuple-element.57.coef_ref.refs_8_.refs_1_, ...), custom_call_target="tpu_custom_call" | custom-call | tf_op jit(solution)/shard_map/connect_middle/pallas_call | solution.py:1464
  119.9 95.8 %ffn_rows.1 = (bf16[2,4,256,2048]{3,2,1,0:T(8,128)(2,1)}, bf16[2,4,256,2048]{3,2,1,0:T(8,128)(2,1)}, bf16[1024,1024]{1,0:T(8,128)(2,1)}, bf16[1024,1024]{1,0:T(8...) custom-call(bf16[256,2048]{1,0:T(8,128)(2,1)} %bitcast.60, ...), custom_call_target="tpu_custom_call" | custom-call | flops 25769803776 | bytes 52428800 | tf_op jit(solution)/shard_map/ffn_rows/pallas_call | solution.py:989
  215.7 53.8 %ffn_weights.1 = (bf16[2,3,512,512]{3,2,1,0:T(8,128)(2,1)}, f32[256,2048]{1,0:T(8,128)}, bf16[3,512,512]{2,1,0:T(8,128)(2,1)}) custom-call(bf16[8,2,128,2048]{3,2,1,0:T(8,128)(2,1)} %bitcast.61, bf16[8,2,128,2048]{3,2,1,0:T(8,128)(2,1)} %bitcast.62, bf16[1024,1024]{1,0:T(8,128)(2,1)} %get-tuple-element.76.refs_2_, ...), custom_call_target="tpu_custom_call" | custom-call | flops 25769803776 | bytes 52428800 | tf_op jit(solution)/shard_map/ffn_weights/pallas_call | solution.py:1157
  269.6 0.1 pad_reduce_fusion
  269.7 0.6 fusion.5
  270.3 13.6 %connect_back.2 = (f32[4,128,2048]{2,1,0:T(8,128)}, f32[8,2048]{1,0:T(8,128)}, f32[8,8]{1,0:T(8,128)}, bf16[4,128,2048]{2,1,0:T(8,128)(2,1)}, bf16[128,2048]{1,0:T(8,128)(2,1)}) custom-call(f32[4,128,2048]{2,1,0:T(8,128)} %get-tuple-element.69.refs_0_, f32[4,128,8]{2,1,0:T(8,128)} %get-tuple-element.70.refs_1_, f32[4,128,8]{2,1,0:T(8,128)} %get-tuple-element.71.refs_2_, ...), custom_call_target="tpu_custom_call" | custom-call | tf_op jit(solution)/shard_map/connect_back/pallas_call | solution.py:1670
  283.8 27.6 %project_back.1 = (bf16[8,128,256]{2,1,0:T(8,128)(2,1)}, bf16[8,128,256]{2,1,0:T(8,128)(2,1)}) custom-call(bf16[128,2048]{1,0:T(8,128)(2,1)} %get-tuple-element.88.grad_ref, bf16[512,1024]{1,0:T(8,128)(2,1)} %bitcast.44, bf16[512,1024]{1,0:T(8,128)(2,1)} %copy-done.2, bf16[512,1024]{1,0:T(8,128)(2,1)} %copy-done.1, ...), custom_call_target="tpu_custom_call" | custom-call | tf_op jit(solution)/shard_map/project_back/pallas_call | solution.py:1563
  311.5 5.1 %all-to-all-start = ((bf16[8,128,256]{2,1,0:T(8,128)(2,1)}), bf16[8,128,256]{2,1,0:T(8,128)(2,1)}, u32[]{:S(2)}, u32[]{:S(2)}) async-start(bf16[8,128,256]{2,1,0:T(8,128)(2,1)} %get-tuple-element.96), calls=%async_computation | async-start | bytes 1048576 | tf_op jit(solution)/shard_map/all_to_all | solution.py:1784
  316.6 18.1 %attention_backward.1 = (bf16[1024,768]{1,0:T(8,128)(2,1)}, bf16[1024,2048]{1,0:T(8,128)(2,1)}) custom-call(bf16[1024,256]{1,0:T(8,128)(2,1)} %get-tuple-element.85.query_ref, bf16[1024,256]{1,0:T(8,128)(2,1)} %get-tuple-element.86.key_ref, bf16[1024,256]{1,0:T(8,128)(2,1)} %get-tuple-element.87.value_ref, bf16[1024,256]{1,0:T(8,128)(2,1)} %bitcast.49, ...), custom_call_target="tpu_custom_call" | custom-call | tf_op jit(solution)/shard_map/attention_backward/pallas_call | solution.py:1347
  334.7 1.5 constant_dynamic-update-slice_fusion.1
  336.2 48.9 %attention_sums.1 = (f32[128,2048]{1,0:T(8,128)}, f32[512,1024]{1,0:T(8,128)}) custom-call(bf16[8,128,2048]{2,1,0:T(8,128)(2,1)} %bitcast.58, bf16[1024,2048]{1,0:T(8,128)(2,1)} %bitcast.39, bf16[1024,768]{1,0:T(8,128)(2,1)} %get-tuple-element.94.refs_1_, bf16[8,1024,256]{2,1,0:T(8,128)(2,1)} %get-tuple-element.95.refs_2_, bf16[1024,256]{1,0:T(8,128)(2,1)} %bitcast.21.refs_3_), custom_call_target="tpu_custom_call" | custom-call | flops 4294967296 | bytes 16777216 | tf_op jit(solution)/shard_map/attention_sums/pallas_call | solution.py:665
  385.1 1.5 constant_dynamic-update-slice_fusion
  386.6 1.8 constant_dynamic-slice_fusion.1
  388.6 3.2 reshape.87
  391.7 11.2 %connect_back.3 = (f32[4,128,2048]{2,1,0:T(8,128)}, f32[8,2048]{1,0:T(8,128)}, f32[8,8]{1,0:T(8,128)}) custom-call(bf16[4,128,2048]{2,1,0:T(8,128)(2,1)} %bitcast.37, f32[4,128,8]{2,1,0:T(8,128)} %get-tuple-element.57.coef_ref.refs_8_.refs_1_, f32[4,128,8]{2,1,0:T(8,128)} %get-tuple-element.82.refs_2_, f32[128,2048]{1,0:T(8,128)} %get-tuple-element.83.refs_3_, ...), custom_call_target="tpu_custom_call" | custom-call | tf_op jit(solution)/shard_map/connect_back/pallas_call | solution.py:1670
  403.0 0.7 slice.63
  403.8 0.9 pad_maximum_fusion
  404.6 0.7 reshape.90.values_ref
  405.3 16.6 %sum_everywhere.1 = f32[8,8,512]{2,1,0:T(8,128)} custom-call(f32[8,8,512]{2,1,0:T(8,128)} %reshape.90.values_ref), custom_call_target="tpu_custom_call" | custom-call | tf_op jit(solution)/shard_map/sum_everywhere/pallas_call | solution.py:727
  422.0 0.9 slice.65
  422.9 1.0 reshape.92
  423.9 0.7 reshape.93
  424.6 0.7 copy.22
  425.3 3.0 convert_bitcast_fusion
  (51 shorter events, 0.8 us)
Async XLA Ops:
  7.2 73.1 %all-gather.2.cloned.1.call-start = ((), (), s32[]{:S(2)}) async-start(), calls=%async_computation.2 | async-start | bytes 3932160 | tf_op jit(solution)/shard_map/all_gather | solution.py:53
  7.2 3.8 copy-start.4
  10.9 374.2 %reduce-scatter.2.cloned.1.call-start = ((), (), s32[]{:S(2)}) async-start(), calls=%async_computation.3 | async-start | bytes 4718592 | tf_op jit(solution)/shard_map/reduce_scatter | solution.py:1776
  11.1 6.2 %copy-start.7 = (f32[2,4,6]{2,1,0:T(4,128)S(1)}, f32[2,4,6]{2,1,0:T(4,128)}, u32[]{:S(2)}) copy-start(f32[2,4,6]{2,1,0:T(4,128)} %param.11) | copy-start | bytes 580
  17.3 58.7 %copy-start = (bf16[512,1,1024]{2,0,1:T(8,128)(2,1)}, bf16[512,1,1024]{2,0,1:T(8,128)(2,1)S(1)}, u32[]{:S(2)}) copy-start(bf16[512,1,1024]{2,0,1:T(8,128)(2,1)S(1)} %copy.28) | copy-start | bytes 3145732
  18.6 54.0 %copy-start.9 = (s32[8]{0:T(128)S(1)}, s32[8]{0:T(128)}, u32[]{:S(2)}) copy-start(s32[8]{0:T(128)} %param.13) | copy-start | bytes 100
  25.1 47.5 %collective-permute-start.1 = (bf16[512,1024]{1,0:T(8,128)(2,1)S(1)}, bf16[512,1024]{1,0:T(8,128)(2,1)S(1)}, u32[]{:S(2)}, u32[]{:S(2)}) collective-permute-start(bf16[512,1024]{1,0:T(8,128)(2,1)S(1)} %bitcast.40), channel_id=1, source_target_pairs={{0,2},{1,3},{2,0},{3,1},{4,6},{5,7},{6,4},{7,5},{8,10},{9,11},{10,... | collective-permute-start | bytes 3145736 | tf_op jit(solution)/shard_map/ppermute | solution.py:1711
  28.1 44.5 %collective-permute-start = (bf16[512,1024]{1,0:T(8,128)(2,1)S(1)}, bf16[512,1024]{1,0:T(8,128)(2,1)S(1)}, u32[]{:S(2)}, u32[]{:S(2)}) collective-permute-start(bf16[512,1024]{1,0:T(8,128)(2,1)S(1)} %bitcast.41), channel_id=1, source_target_pairs={{0,1},{1,0},{2,3},{3,2},{4,5},{5,4},{6,7},{7,6},{8,9},{9,8},{10,11... | collective-permute-start | bytes 3145736 | tf_op jit(solution)/shard_map/ppermute | solution.py:1711
  72.7 29.7 %copy-start.1 = (bf16[512,1024]{1,0:T(8,128)(2,1)}, bf16[512,1024]{1,0:T(8,128)(2,1)S(1)}, u32[]{:S(2)}) copy-start(bf16[512,1024]{1,0:T(8,128)(2,1)S(1)} %collective-permute-done.1.refs_2_) | copy-start | bytes 3145732
  72.7 29.7 %copy-start.2 = (bf16[512,1024]{1,0:T(8,128)(2,1)}, bf16[512,1024]{1,0:T(8,128)(2,1)S(1)}, u32[]{:S(2)}) copy-start(bf16[512,1024]{1,0:T(8,128)(2,1)S(1)} %collective-permute-done.refs_1_) | copy-start | bytes 3145732
  73.6 30.8 %collective-permute-start.5 = (bf16[512,1024]{1,0:T(8,128)(2,1)S(1)}, bf16[512,1024]{1,0:T(8,128)(2,1)}, u32[]{:S(2)}, u32[]{:S(2)}) collective-permute-start(bf16[512,1024]{1,0:T(8,128)(2,1)S(1)} %collective-permute-done.refs_1_), channel_id=1, source_target_pairs={{0,4},{4,0},{8,12},{12,8},{16,20},{20,16},{24,28},{28,24},{1,5},{5... | collective-permute-start | bytes 3145736 | tf_op jit(solution)/shard_map/ppermute | solution.py:1716
  74.8 29.6 %collective-permute-start.6 = (bf16[512,1024]{1,0:T(8,128)(2,1)S(1)}, bf16[512,1024]{1,0:T(8,128)(2,1)}, u32[]{:S(2)}, u32[]{:S(2)}) collective-permute-start(bf16[512,1024]{1,0:T(8,128)(2,1)S(1)} %collective-permute-done.1.refs_2_), channel_id=1, source_target_pairs={{0,4},{4,0},{8,12},{12,8},{16,20},{20,16},{24,28},{28,24},{1,5},{5... | collective-permute-start | bytes 3145736 | tf_op jit(solution)/shard_map/ppermute | solution.py:1716
  74.9 27.5 %collective-permute-start.3 = (bf16[256,1024]{1,0:T(8,128)(2,1)}, bf16[256,1024]{1,0:T(8,128)(2,1)}, u32[]{:S(2)}, u32[]{:S(2)}) collective-permute-start(bf16[256,1024]{1,0:T(8,128)(2,1)} %slice.56), channel_id=1, source_target_pairs={{0,1},{1,0},{2,3},{3,2},{4,5},{5,4},{6,7},{7,6},{8,9},{9,8},{10,11... | collective-permute-start | bytes 1572872 | tf_op jit(solution)/shard_map/ppermute | solution.py:1739
  75.5 26.9 %collective-permute-start.2 = (bf16[256,1024]{1,0:T(8,128)(2,1)}, bf16[256,1024]{1,0:T(8,128)(2,1)}, u32[]{:S(2)}, u32[]{:S(2)}) collective-permute-start(bf16[256,1024]{1,0:T(8,128)(2,1)} %slice.55), channel_id=1, source_target_pairs={{0,2},{1,3},{2,0},{3,1},{4,6},{5,7},{6,4},{7,5},{8,10},{9,11},{10,... | collective-permute-start | bytes 1572872 | tf_op jit(solution)/shard_map/ppermute | solution.py:1738
  75.9 28.4 %collective-permute-start.4 = (bf16[512,1024]{1,0:T(8,128)(2,1)S(1)}, bf16[512,1024]{1,0:T(8,128)(2,1)}, u32[]{:S(2)}, u32[]{:S(2)}) collective-permute-start(bf16[512,1024]{1,0:T(8,128)(2,1)S(1)} %bitcast.42), channel_id=1, source_target_pairs={{0,4},{4,0},{8,12},{12,8},{16,20},{20,16},{24,28},{28,24},{1,5},{5... | collective-permute-start | bytes 3145736 | tf_op jit(solution)/shard_map/ppermute | solution.py:1716
  76.0 4.2 copy-start.5
  102.4 3.2 collective-permute-start.7
  103.7 2.6 collective-permute-start.8
  311.5 24.7 %all-to-all-start = ((bf16[8,128,256]{2,1,0:T(8,128)(2,1)}), bf16[8,128,256]{2,1,0:T(8,128)(2,1)}, u32[]{:S(2)}, u32[]{:S(2)}) async-start(bf16[8,128,256]{2,1,0:T(8,128)(2,1)} %get-tuple-element.96), calls=%async_computation | async-start | bytes 1048576 | tf_op jit(solution)/shard_map/all_to_all | solution.py:1784
  386.6 1.9 copy-start.8
  388.5 36.8 %collective-permute-start.9 = (bf16[3,1024,256]{2,1,0:T(8,128)(2,1)}, bf16[3,1024,256]{2,1,0:T(8,128)(2,1)S(1)}, u32[]{:S(2)}, u32[]{:S(2)}) collective-permute-start(bf16[3,1024,256]{2,1,0:T(8,128)(2,1)} %get-tuple-element.123), channel_id=1, source_target_pairs={{0,4},{4,0},{8,12},{12,8},{16,20},{20,16},{24,28},{28,24},{1,5},{5... | collective-permute-start | bytes 4718600 | tf_op jit(solution)/shard_map/ppermute | solution.py:1797
  391.7 12.0 %copy-start.6 = (f32[8,2048]{1,0:T(8,128)S(1)}, f32[8,2048]{1,0:T(8,128)}, u32[]{:S(2)}) copy-start(f32[8,2048]{1,0:T(8,128)} %get-tuple-element.105) | copy-start | bytes 196612
  391.7 33.6 %copy-start.3 = (bf16[3,1024,256]{2,1,0:T(8,128)(2,1)S(1)}, bf16[3,1024,256]{2,1,0:T(8,128)(2,1)}, u32[]{:S(2)}) copy-start(bf16[3,1024,256]{2,1,0:T(8,128)(2,1)} %get-tuple-element.122) | copy-start | bytes 4718596
Sparse Core Ops, SparseCore 0:
  11.1 61.5 all-gather.1
  269.7 53.7 reduce-scatter.1

commit v10 on v9

--- a/solution.py
+++ b/solution.py
@@ -956,6 +956,7 @@
         group(1, first)
         add_up(0, fsdp)
         next(mirroring)
+        next(line)
         for _ in range(2):
             next(gathering)
         arriving[2].wait_recv()
@@ -1055,7 +1056,17 @@
             member = chip % 2
             other = (chip + 1 - 2 * member) * 2 + core
             crossing = [
-                send(give.at[j], take.at[j], (side_s, side_r), j, (other, lax.axis_index("fsdp"))) for j in range(early)
+                [
+                    send(
+                        give.at[j, plane],
+                        take.at[j, plane],
+                        (side_s, side_r),
+                        3 * j + plane,
+                        (other, lax.axis_index("fsdp")),
+                    )
+                    for plane in range(3)
+                ]
+                for j in range(early)
             ]
             starts, *stages = corner_sum_stages(n_ctx, partial_ref, out_ref, held, square_in, load, (sq_s, sq_r))
 
@@ -1111,11 +1122,11 @@
                 def _():
                     weight_ref[z, plane] = low(value)
 
-        for j in range(early):
-
-            @pl.when(step == j)
-            def _():
-                crossing[j].start()
+            for j in range(early):
+
+                @pl.when(step == j)
+                def _():
+                    crossing[j][plane].start()
 
         for at, stage in ((1, 0), (steps - 1, 1)):
             if stage < len(stages):
@@ -1129,8 +1140,8 @@
             @pl.when(step == steps - 1)
             def _():
                 for j in range(early):
-                    crossing[j].wait()
                     for plane in range(3):
+                        crossing[j][plane].wait()
                         early_ref[plane, j * chunk : (j + 1) * chunk] = low(
                             keep[j, plane] + take[j, plane].astype(jnp.float32)
                         )
@@ -1152,7 +1163,7 @@
         out_specs.append(whole_block((3, early * chunk, wide), **once))
         out_shape.append(jax.ShapeDtypeStruct((3, early * chunk, wide), jnp.bfloat16))
         scratch.append(pltpu.VMEM((early, 3, chunk, wide), jnp.float32))
-        scratch += [pltpu.VMEM((early, 3, chunk, wide), jnp.bfloat16)] * 2 + dma_pair(early)
+        scratch += [pltpu.VMEM((early, 3, chunk, wide), jnp.bfloat16)] * 2 + dma_pair(3 * early)
         scratch += corner_sum_scratch(partial)
     return pl.pallas_call(
         kernel,

time: 441 us -> 435 us (0.986)
  Pallas kernels: 371 us -> 365 us
where the time goes in v10:
time: 435 us; the launch traced here: 430 us
  Pallas kernels  365 us (84%)
  local copies, waits for them, and re-layouts  27.5 us (6%)
  between operations  14.5 us (3%)
  starting transfers between devices  12.6 us (3%)
  other arithmetic  7.92 us (2%)
    pallas_call x1, Pallas kernels, ffn_rows(): pl.pallas_call(kernel, in_specs=any_specs(3), out_specs=any_specs(7), out...  93.7 us
    pallas_call x1, Pallas kernels, ffn_weights(): pl.pallas_call(kernel, grid=(steps,), in_specs=in_specs, out_specs=out_sp...  50.8 us
    pallas_call x1, Pallas kernels, attention_sums(): pl.pallas_call(kernel, out_shape=[jax.ShapeDtypeStruct(partial.shape[-2:]...  48.8 us
    pallas_call x1, Pallas kernels, line_rows(): pl.pallas_call(kernel, out_shape=jax.ShapeDtypeStruct((n_ctx,) + rows.sha...  42.9 us
    pallas_call x1, Pallas kernels, project_back(): pl.pallas_call(kernel, in_specs=[pl.BlockSpec(memory_space=pltpu.VMEM)] *...  26.4 us
    pallas_call x2, Pallas kernels, connect_back(): pl.pallas_call(kernel, grid=(steps,), in_specs=in_specs, out_specs=out_sp...  24.8 us
    pallas_call x1, Pallas kernels, attention_forward(): pl.pallas_call(kernel, grid=(steps,), in_specs=[pl.BlockSpec((SPAN, featu...  22.1 us
    pallas_call x1, Pallas kernels, attention_backward(): pl.pallas_call(kernel, grid=(steps,), in_specs=[whole_block(a.shape) for...  18.1 us
  transfers between devices with their start and end apart: 13, of which 2 were waited for; matrix products, arithmetic and copies ran while one was open for 6% of the time, Pallas kernels for 48%

profile of v10, /device:TPU:0, one launch (start us, length us, event | category | flops | bytes accessed | tf_op | source)
XLA Modules:
  0.0 429.6 jit_solution(1754698195075793349)
XLA Ops:
  7.2 1.6 constant_dynamic-slice_fusion.2
  8.9 0.9 copy.26
  9.8 1.2 copy.19
  11.1 5.8 %constant_dynamic-slice_fusion.3 = bf16[512,1,1024]{2,1,0:T(2,128)(2,1)S(1)} fusion(bf16[512,4,2048]{2,1,0:T(4,128)(2,1)} %param.8, s32[]{:T(128)S(6)} %add.63, s32[]{:T(128)S(6)} %select_n.36), kind=kLoop, calls=%fused_computation.29 | loop fusion | bytes 2097160 | tf_op jit(solution)/shard_map/slice | solution.py:1716
  16.9 0.4 copy.28
  17.3 0.7 fusion.4
  17.9 0.7 fusion.2
  18.6 6.5 %connect_first.1 = (f32[4,128,8]{2,1,0:T(8,128)}, f32[4,128,8]{2,1,0:T(8,128)}, bf16[128,2048]{1,0:T(8,128)(2,1)}) custom-call(bf16[4,128,2048]{2,1,0:T(8,128)(2,1)} %bitcast.35, f32[8,2048]{1,0:T(8,128)} %get-tuple-element.125.dynamic_ref.refs_6_, f32[4,8]{1,0:T(4,128)} %get-tuple-element.129.static_ref), custom_call_target="tpu_custom_call" | custom-call | tf_op jit(solution)/shard_map/connect_first/pallas_call | solution.py:1422
  25.1 3.0 collective-permute-start.1
  28.1 1.5 collective-permute-start
  29.6 42.9 %line_rows.1 = bf16[8,128,2048]{2,1,0:T(8,128)(2,1)} custom-call(bf16[128,2048]{1,0:T(8,128)(2,1)} %get-tuple-element.59.rows_ref), custom_call_target="tpu_custom_call" | custom-call | tf_op jit(solution)/shard_map/line_rows/pallas_call | solution.py:271
  72.7 0.9 slice.55
  73.6 0.4 collective-permute-start.5
  73.9 0.8 slice.56
  74.8 0.1 collective-permute-start.6
  74.9 0.6 collective-permute-start.3
  75.5 0.5 collective-permute-start.2
  76.0 1.1 copy.20.column_ref
  77.2 3.1 fusion
  80.2 22.1 %attention_forward.1 = (bf16[1024,256]{1,0:T(8,128)(2,1)}, bf16[1024,256]{1,0:T(8,128)(2,1)}, bf16[1024,256]{1,0:T(8,128)(2,1)}, bf16[1024,256]{1,0:T(8,128)(2,1...) custom-call(bf16[1024,2048]{1,0:T(8,128)(2,1)} %bitcast.38, ...), custom_call_target="tpu_custom_call" | custom-call | tf_op jit(solution)/shard_map/attention_forward/pallas_call | solution.py:1298
  102.4 1.3 collective-permute-start.7
  103.8 0.6 pad_add_fusion.1.core_ref
  104.4 1.2 collective-permute-done.7.refs_8_
  105.6 0.7 collective-permute-done.8.refs_9_
  106.3 13.6 %connect_middle.1 = (f32[4,128,2048]{2,1,0:T(8,128)}, f32[128,2048]{1,0:T(8,128)}, f32[4,128,8]{2,1,0:T(8,128)}, f32[4,128,8]{2,1,0:T(8,128)}, bf16[2,128,2048]{2,1,0:T(8,128)(2,1)}) custom-call(s32[2]{0:T(128)} %pad_add_fusion.1.core_ref, bf16[4,128,2048]{2,1,0:T(8,128)(2,1)} %bitcast.36, f32[4,128,8]{2,1,0:T(8,128)} %get-tuple-element.57.coef_ref.refs_8_.refs_1_, ...), custom_call_target="tpu_custom_call" | custom-call | tf_op jit(solution)/shard_map/connect_middle/pallas_call | solution.py:1475
  119.9 93.7 %ffn_rows.1 = (bf16[2,4,256,2048]{3,2,1,0:T(8,128)(2,1)}, bf16[2,4,256,2048]{3,2,1,0:T(8,128)(2,1)}, bf16[1024,1024]{1,0:T(8,128)(2,1)}, bf16[1024,1024]{1,0:T(8...) custom-call(bf16[256,2048]{1,0:T(8,128)(2,1)} %bitcast.60, ...), custom_call_target="tpu_custom_call" | custom-call | flops 25769803776 | bytes 52428800 | tf_op jit(solution)/shard_map/ffn_rows/pallas_call | solution.py:990
  213.6 50.8 %ffn_weights.1 = (bf16[2,3,512,512]{3,2,1,0:T(8,128)(2,1)}, f32[256,2048]{1,0:T(8,128)}, bf16[3,512,512]{2,1,0:T(8,128)(2,1)}) custom-call(bf16[8,2,128,2048]{3,2,1,0:T(8,128)(2,1)} %bitcast.61, bf16[8,2,128,2048]{3,2,1,0:T(8,128)(2,1)} %bitcast.62, bf16[1024,1024]{1,0:T(8,128)(2,1)} %get-tuple-element.76.refs_2_, ...), custom_call_target="tpu_custom_call" | custom-call | flops 25769803776 | bytes 52428800 | tf_op jit(solution)/shard_map/ffn_weights/pallas_call | solution.py:1168
  264.5 0.1 pad_reduce_fusion
  264.6 0.6 fusion.5
  265.2 13.6 %connect_back.2 = (f32[4,128,2048]{2,1,0:T(8,128)}, f32[8,2048]{1,0:T(8,128)}, f32[8,8]{1,0:T(8,128)}, bf16[4,128,2048]{2,1,0:T(8,128)(2,1)}, bf16[128,2048]{1,0:T(8,128)(2,1)}) custom-call(f32[4,128,2048]{2,1,0:T(8,128)} %get-tuple-element.69.refs_0_, f32[4,128,8]{2,1,0:T(8,128)} %get-tuple-element.70.refs_1_, f32[4,128,8]{2,1,0:T(8,128)} %get-tuple-element.71.refs_2_, ...), custom_call_target="tpu_custom_call" | custom-call | tf_op jit(solution)/shard_map/connect_back/pallas_call | solution.py:1681
  278.7 26.4 %project_back.1 = (bf16[8,128,256]{2,1,0:T(8,128)(2,1)}, bf16[8,128,256]{2,1,0:T(8,128)(2,1)}) custom-call(bf16[128,2048]{1,0:T(8,128)(2,1)} %get-tuple-element.88.grad_ref, bf16[512,1024]{1,0:T(8,128)(2,1)} %bitcast.44, bf16[512,1024]{1,0:T(8,128)(2,1)} %copy-done.2, bf16[512,1024]{1,0:T(8,128)(2,1)} %copy-done.1, ...), custom_call_target="tpu_custom_call" | custom-call | tf_op jit(solution)/shard_map/project_back/pallas_call | solution.py:1574
  305.1 5.1 %all-to-all-start = ((bf16[8,128,256]{2,1,0:T(8,128)(2,1)}), bf16[8,128,256]{2,1,0:T(8,128)(2,1)}, u32[]{:S(2)}, u32[]{:S(2)}) async-start(bf16[8,128,256]{2,1,0:T(8,128)(2,1)} %get-tuple-element.96), calls=%async_computation | async-start | bytes 1048576 | tf_op jit(solution)/shard_map/all_to_all | solution.py:1795
  310.2 18.1 %attention_backward.1 = (bf16[1024,768]{1,0:T(8,128)(2,1)}, bf16[1024,2048]{1,0:T(8,128)(2,1)}) custom-call(bf16[1024,256]{1,0:T(8,128)(2,1)} %get-tuple-element.85.query_ref, bf16[1024,256]{1,0:T(8,128)(2,1)} %get-tuple-element.86.key_ref, bf16[1024,256]{1,0:T(8,128)(2,1)} %get-tuple-element.87.value_ref, bf16[1024,256]{1,0:T(8,128)(2,1)} %bitcast.49, ...), custom_call_target="tpu_custom_call" | custom-call | tf_op jit(solution)/shard_map/attention_backward/pallas_call | solution.py:1358
  328.3 1.5 constant_dynamic-update-slice_fusion.1
  329.9 48.8 %attention_sums.1 = (f32[128,2048]{1,0:T(8,128)}, f32[512,1024]{1,0:T(8,128)}) custom-call(bf16[8,128,2048]{2,1,0:T(8,128)(2,1)} %bitcast.58, bf16[1024,2048]{1,0:T(8,128)(2,1)} %bitcast.39, bf16[1024,768]{1,0:T(8,128)(2,1)} %get-tuple-element.94.refs_1_, bf16[8,1024,256]{2,1,0:T(8,128)(2,1)} %get-tuple-element.95.refs_2_, bf16[1024,256]{1,0:T(8,128)(2,1)} %bitcast.21.refs_3_), custom_call_target="tpu_custom_call" | custom-call | flops 4294967296 | bytes 16777216 | tf_op jit(solution)/shard_map/attention_sums/pallas_call | solution.py:665
  378.8 1.5 constant_dynamic-update-slice_fusion
  380.3 1.8 constant_dynamic-slice_fusion.1
  382.2 3.2 reshape.87
  385.4 11.2 %connect_back.3 = (f32[4,128,2048]{2,1,0:T(8,128)}, f32[8,2048]{1,0:T(8,128)}, f32[8,8]{1,0:T(8,128)}) custom-call(bf16[4,128,2048]{2,1,0:T(8,128)(2,1)} %bitcast.37, f32[4,128,8]{2,1,0:T(8,128)} %get-tuple-element.57.coef_ref.refs_8_.refs_1_, f32[4,128,8]{2,1,0:T(8,128)} %get-tuple-element.82.refs_2_, f32[128,2048]{1,0:T(8,128)} %get-tuple-element.83.refs_3_, ...), custom_call_target="tpu_custom_call" | custom-call | tf_op jit(solution)/shard_map/connect_back/pallas_call | solution.py:1681
  396.6 0.7 slice.63
  397.4 0.9 pad_maximum_fusion
  398.3 0.7 reshape.90.values_ref
  399.0 17.2 %sum_everywhere.1 = f32[8,8,512]{2,1,0:T(8,128)} custom-call(f32[8,8,512]{2,1,0:T(8,128)} %reshape.90.values_ref), custom_call_target="tpu_custom_call" | custom-call | tf_op jit(solution)/shard_map/sum_everywhere/pallas_call | solution.py:727
  416.2 0.9 slice.65
  417.1 1.0 reshape.92
  418.1 0.7 reshape.93
  418.8 0.7 copy.22
  419.5 3.0 convert_bitcast_fusion
  (51 shorter events, 0.8 us)
Async XLA Ops:
  7.2 73.1 %all-gather.2.cloned.1.call-start = ((), (), s32[]{:S(2)}) async-start(), calls=%async_computation.2 | async-start | bytes 3932160 | tf_op jit(solution)/shard_map/all_gather | solution.py:53
  7.2 3.8 copy-start.4
  10.9 367.8 %reduce-scatter.2.cloned.1.call-start = ((), (), s32[]{:S(2)}) async-start(), calls=%async_computation.3 | async-start | bytes 4718592 | tf_op jit(solution)/shard_map/reduce_scatter | solution.py:1787
  11.1 6.2 %copy-start.7 = (f32[2,4,6]{2,1,0:T(4,128)S(1)}, f32[2,4,6]{2,1,0:T(4,128)}, u32[]{:S(2)}) copy-start(f32[2,4,6]{2,1,0:T(4,128)} %param.11) | copy-start | bytes 580
  17.3 58.7 %copy-start = (bf16[512,1,1024]{2,0,1:T(8,128)(2,1)}, bf16[512,1,1024]{2,0,1:T(8,128)(2,1)S(1)}, u32[]{:S(2)}) copy-start(bf16[512,1,1024]{2,0,1:T(8,128)(2,1)S(1)} %copy.28) | copy-start | bytes 3145732
  18.6 54.0 %copy-start.9 = (s32[8]{0:T(128)S(1)}, s32[8]{0:T(128)}, u32[]{:S(2)}) copy-start(s32[8]{0:T(128)} %param.13) | copy-start | bytes 100
  25.1 47.5 %collective-permute-start.1 = (bf16[512,1024]{1,0:T(8,128)(2,1)S(1)}, bf16[512,1024]{1,0:T(8,128)(2,1)S(1)}, u32[]{:S(2)}, u32[]{:S(2)}) collective-permute-start(bf16[512,1024]{1,0:T(8,128)(2,1)S(1)} %bitcast.40), channel_id=1, source_target_pairs={{0,2},{1,3},{2,0},{3,1},{4,6},{5,7},{6,4},{7,5},{8,10},{9,11},{10,... | collective-permute-start | bytes 3145736 | tf_op jit(solution)/shard_map/ppermute | solution.py:1722
  28.1 44.5 %collective-permute-start = (bf16[512,1024]{1,0:T(8,128)(2,1)S(1)}, bf16[512,1024]{1,0:T(8,128)(2,1)S(1)}, u32[]{:S(2)}, u32[]{:S(2)}) collective-permute-start(bf16[512,1024]{1,0:T(8,128)(2,1)S(1)} %bitcast.41), channel_id=1, source_target_pairs={{0,1},{1,0},{2,3},{3,2},{4,5},{5,4},{6,7},{7,6},{8,9},{9,8},{10,11... | collective-permute-start | bytes 3145736 | tf_op jit(solution)/shard_map/ppermute | solution.py:1722
  72.7 29.7 %copy-start.1 = (bf16[512,1024]{1,0:T(8,128)(2,1)}, bf16[512,1024]{1,0:T(8,128)(2,1)S(1)}, u32[]{:S(2)}) copy-start(bf16[512,1024]{1,0:T(8,128)(2,1)S(1)} %collective-permute-done.1.refs_2_) | copy-start | bytes 3145732
  72.7 29.7 %copy-start.2 = (bf16[512,1024]{1,0:T(8,128)(2,1)}, bf16[512,1024]{1,0:T(8,128)(2,1)S(1)}, u32[]{:S(2)}) copy-start(bf16[512,1024]{1,0:T(8,128)(2,1)S(1)} %collective-permute-done.refs_1_) | copy-start | bytes 3145732
  73.6 30.8 %collective-permute-start.5 = (bf16[512,1024]{1,0:T(8,128)(2,1)S(1)}, bf16[512,1024]{1,0:T(8,128)(2,1)}, u32[]{:S(2)}, u32[]{:S(2)}) collective-permute-start(bf16[512,1024]{1,0:T(8,128)(2,1)S(1)} %collective-permute-done.refs_1_), channel_id=1, source_target_pairs={{0,4},{4,0},{8,12},{12,8},{16,20},{20,16},{24,28},{28,24},{1,5},{5... | collective-permute-start | bytes 3145736 | tf_op jit(solution)/shard_map/ppermute | solution.py:1727
  74.8 29.6 %collective-permute-start.6 = (bf16[512,1024]{1,0:T(8,128)(2,1)S(1)}, bf16[512,1024]{1,0:T(8,128)(2,1)}, u32[]{:S(2)}, u32[]{:S(2)}) collective-permute-start(bf16[512,1024]{1,0:T(8,128)(2,1)S(1)} %collective-permute-done.1.refs_2_), channel_id=1, source_target_pairs={{0,4},{4,0},{8,12},{12,8},{16,20},{20,16},{24,28},{28,24},{1,5},{5... | collective-permute-start | bytes 3145736 | tf_op jit(solution)/shard_map/ppermute | solution.py:1727
  74.9 27.5 %collective-permute-start.3 = (bf16[256,1024]{1,0:T(8,128)(2,1)}, bf16[256,1024]{1,0:T(8,128)(2,1)}, u32[]{:S(2)}, u32[]{:S(2)}) collective-permute-start(bf16[256,1024]{1,0:T(8,128)(2,1)} %slice.56), channel_id=1, source_target_pairs={{0,1},{1,0},{2,3},{3,2},{4,5},{5,4},{6,7},{7,6},{8,9},{9,8},{10,11... | collective-permute-start | bytes 1572872 | tf_op jit(solution)/shard_map/ppermute | solution.py:1750
  75.5 26.9 %collective-permute-start.2 = (bf16[256,1024]{1,0:T(8,128)(2,1)}, bf16[256,1024]{1,0:T(8,128)(2,1)}, u32[]{:S(2)}, u32[]{:S(2)}) collective-permute-start(bf16[256,1024]{1,0:T(8,128)(2,1)} %slice.55), channel_id=1, source_target_pairs={{0,2},{1,3},{2,0},{3,1},{4,6},{5,7},{6,4},{7,5},{8,10},{9,11},{10,... | collective-permute-start | bytes 1572872 | tf_op jit(solution)/shard_map/ppermute | solution.py:1749
  75.9 28.4 %collective-permute-start.4 = (bf16[512,1024]{1,0:T(8,128)(2,1)S(1)}, bf16[512,1024]{1,0:T(8,128)(2,1)}, u32[]{:S(2)}, u32[]{:S(2)}) collective-permute-start(bf16[512,1024]{1,0:T(8,128)(2,1)S(1)} %bitcast.42), channel_id=1, source_target_pairs={{0,4},{4,0},{8,12},{12,8},{16,20},{20,16},{24,28},{28,24},{1,5},{5... | collective-permute-start | bytes 3145736 | tf_op jit(solution)/shard_map/ppermute | solution.py:1727
  76.0 4.2 copy-start.5
  102.4 3.2 collective-permute-start.7
  103.7 2.6 collective-permute-start.8
  305.1 24.7 %all-to-all-start = ((bf16[8,128,256]{2,1,0:T(8,128)(2,1)}), bf16[8,128,256]{2,1,0:T(8,128)(2,1)}, u32[]{:S(2)}, u32[]{:S(2)}) async-start(bf16[8,128,256]{2,1,0:T(8,128)(2,1)} %get-tuple-element.96), calls=%async_computation | async-start | bytes 1048576 | tf_op jit(solution)/shard_map/all_to_all | solution.py:1795
  380.3 1.9 copy-start.8
  382.1 37.4 %collective-permute-start.9 = (bf16[3,1024,256]{2,1,0:T(8,128)(2,1)}, bf16[3,1024,256]{2,1,0:T(8,128)(2,1)S(1)}, u32[]{:S(2)}, u32[]{:S(2)}) collective-permute-start(bf16[3,1024,256]{2,1,0:T(8,128)(2,1)} %get-tuple-element.123), channel_id=1, source_target_pairs={{0,4},{4,0},{8,12},{12,8},{16,20},{20,16},{24,28},{28,24},{1,5},{5... | collective-permute-start | bytes 4718600 | tf_op jit(solution)/shard_map/ppermute | solution.py:1808
  385.4 12.0 %copy-start.6 = (f32[8,2048]{1,0:T(8,128)S(1)}, f32[8,2048]{1,0:T(8,128)}, u32[]{:S(2)}) copy-start(f32[8,2048]{1,0:T(8,128)} %get-tuple-element.105) | copy-start | bytes 196612
  385.4 34.1 %copy-start.3 = (bf16[3,1024,256]{2,1,0:T(8,128)(2,1)S(1)}, bf16[3,1024,256]{2,1,0:T(8,128)(2,1)}, u32[]{:S(2)}) copy-start(bf16[3,1024,256]{2,1,0:T(8,128)(2,1)} %get-tuple-element.122) | copy-start | bytes 4718596
Sparse Core Ops, SparseCore 0:
  11.1 61.5 all-gather.1
  264.6 53.9 reduce-scatter.1

commit v11 on v10

--- a/solution.py
+++ b/solution.py
@@ -963,10 +963,9 @@
         arriving[4].wait_recv()
         group(2, second)
         add_up(1, first)
-        next(mirroring)
+        for _ in range(3):
+            next(mirroring)
         next(line)
-        for _ in range(2):
-            next(mirroring)
         arriving[5].wait_recv()
         arriving[6].wait_recv()
         group(3, corner)

time: 435 us -> 435 us (level)
  no operation moved by 1% of the time
where the time goes in v11:
time: 435 us; the launch traced here: 430 us
  Pallas kernels  365 us (84%)
  local copies, waits for them, and re-layouts  27.5 us (6%)
  between operations  14.5 us (3%)
  starting transfers between devices  12.6 us (3%)
  other arithmetic  7.92 us (2%)
    pallas_call x1, Pallas kernels, ffn_rows(): pl.pallas_call(kernel, in_specs=any_specs(3), out_specs=any_specs(7), out...  93.7 us
    pallas_call x1, Pallas kernels, ffn_weights(): pl.pallas_call(kernel, grid=(steps,), in_specs=in_specs, out_specs=out_sp...  50.8 us
    pallas_call x1, Pallas kernels, attention_sums(): pl.pallas_call(kernel, out_shape=[jax.ShapeDtypeStruct(partial.shape[-2:]...  48.8 us
    pallas_call x1, Pallas kernels, line_rows(): pl.pallas_call(kernel, out_shape=jax.ShapeDtypeStruct((n_ctx,) + rows.sha...  42.9 us
    pallas_call x1, Pallas kernels, project_back(): pl.pallas_call(kernel, in_specs=[pl.BlockSpec(memory_space=pltpu.VMEM)] *...  26.4 us
    pallas_call x2, Pallas kernels, connect_back(): pl.pallas_call(kernel, grid=(steps,), in_specs=in_specs, out_specs=out_sp...  24.8 us
    pallas_call x1, Pallas kernels, attention_forward(): pl.pallas_call(kernel, grid=(steps,), in_specs=[pl.BlockSpec((SPAN, featu...  22.1 us
    pallas_call x1, Pallas kernels, attention_backward(): pl.pallas_call(kernel, grid=(steps,), in_specs=[whole_block(a.shape) for...  18.1 us
  transfers between devices with their start and end apart: 13, of which 2 were waited for; matrix products, arithmetic and copies ran while one was open for 6% of the time, Pallas kernels for 48%

profile of v11, /device:TPU:0, one launch (start us, length us, event | category | flops | bytes accessed | tf_op | source)
XLA Modules:
  0.0 429.6 jit_solution(14653809803601601980)
XLA Ops:
  7.2 1.6 constant_dynamic-slice_fusion.2
  8.9 0.9 copy.26
  9.8 1.2 copy.19
  11.1 5.8 %constant_dynamic-slice_fusion.3 = bf16[512,1,1024]{2,1,0:T(2,128)(2,1)S(1)} fusion(bf16[512,4,2048]{2,1,0:T(4,128)(2,1)} %param.8, s32[]{:T(128)S(6)} %add.63, s32[]{:T(128)S(6)} %select_n.36), kind=kLoop, calls=%fused_computation.29 | loop fusion | bytes 2097160 | tf_op jit(solution)/shard_map/slice | solution.py:1715
  16.9 0.4 copy.28
  17.3 0.7 fusion.4
  17.9 0.7 fusion.2
  18.6 6.5 %connect_first.1 = (f32[4,128,8]{2,1,0:T(8,128)}, f32[4,128,8]{2,1,0:T(8,128)}, bf16[128,2048]{1,0:T(8,128)(2,1)}) custom-call(bf16[4,128,2048]{2,1,0:T(8,128)(2,1)} %bitcast.35, f32[8,2048]{1,0:T(8,128)} %get-tuple-element.125.dynamic_ref.refs_6_, f32[4,8]{1,0:T(4,128)} %get-tuple-element.129.static_ref), custom_call_target="tpu_custom_call" | custom-call | tf_op jit(solution)/shard_map/connect_first/pallas_call | solution.py:1421
  25.1 3.0 collective-permute-start.1
  28.1 1.5 collective-permute-start
  29.6 42.9 %line_rows.1 = bf16[8,128,2048]{2,1,0:T(8,128)(2,1)} custom-call(bf16[128,2048]{1,0:T(8,128)(2,1)} %get-tuple-element.59.rows_ref), custom_call_target="tpu_custom_call" | custom-call | tf_op jit(solution)/shard_map/line_rows/pallas_call | solution.py:271
  72.7 0.9 slice.55
  73.6 0.4 collective-permute-start.5
  73.9 0.8 slice.56
  74.8 0.1 collective-permute-start.6
  74.9 0.6 collective-permute-start.3
  75.5 0.5 collective-permute-start.2
  76.0 1.1 copy.20.column_ref
  77.2 3.1 fusion
  80.2 22.1 %attention_forward.1 = (bf16[1024,256]{1,0:T(8,128)(2,1)}, bf16[1024,256]{1,0:T(8,128)(2,1)}, bf16[1024,256]{1,0:T(8,128)(2,1)}, bf16[1024,256]{1,0:T(8,128)(2,1...) custom-call(bf16[1024,2048]{1,0:T(8,128)(2,1)} %bitcast.38, ...), custom_call_target="tpu_custom_call" | custom-call | tf_op jit(solution)/shard_map/attention_forward/pallas_call | solution.py:1297
  102.4 1.3 collective-permute-start.7
  103.8 0.6 pad_add_fusion.1.core_ref
  104.4 1.2 collective-permute-done.7.refs_8_
  105.6 0.7 collective-permute-done.8.refs_9_
  106.3 13.6 %connect_middle.1 = (f32[4,128,2048]{2,1,0:T(8,128)}, f32[128,2048]{1,0:T(8,128)}, f32[4,128,8]{2,1,0:T(8,128)}, f32[4,128,8]{2,1,0:T(8,128)}, bf16[2,128,2048]{2,1,0:T(8,128)(2,1)}) custom-call(s32[2]{0:T(128)} %pad_add_fusion.1.core_ref, bf16[4,128,2048]{2,1,0:T(8,128)(2,1)} %bitcast.36, f32[4,128,8]{2,1,0:T(8,128)} %get-tuple-element.57.coef_ref.refs_8_.refs_1_, ...), custom_call_target="tpu_custom_call" | custom-call | tf_op jit(solution)/shard_map/connect_middle/pallas_call | solution.py:1474
  119.9 93.7 %ffn_rows.1 = (bf16[2,4,256,2048]{3,2,1,0:T(8,128)(2,1)}, bf16[2,4,256,2048]{3,2,1,0:T(8,128)(2,1)}, bf16[1024,1024]{1,0:T(8,128)(2,1)}, bf16[1024,1024]{1,0:T(8...) custom-call(bf16[256,2048]{1,0:T(8,128)(2,1)} %bitcast.60, ...), custom_call_target="tpu_custom_call" | custom-call | flops 25769803776 | bytes 52428800 | tf_op jit(solution)/shard_map/ffn_rows/pallas_call | solution.py:989
  213.6 50.8 %ffn_weights.1 = (bf16[2,3,512,512]{3,2,1,0:T(8,128)(2,1)}, f32[256,2048]{1,0:T(8,128)}, bf16[3,512,512]{2,1,0:T(8,128)(2,1)}) custom-call(bf16[8,2,128,2048]{3,2,1,0:T(8,128)(2,1)} %bitcast.61, bf16[8,2,128,2048]{3,2,1,0:T(8,128)(2,1)} %bitcast.62, bf16[1024,1024]{1,0:T(8,128)(2,1)} %get-tuple-element.76.refs_2_, ...), custom_call_target="tpu_custom_call" | custom-call | flops 25769803776 | bytes 52428800 | tf_op jit(solution)/shard_map/ffn_weights/pallas_call | solution.py:1167
  264.5 0.1 pad_reduce_fusion
  264.6 0.6 fusion.5
  265.2 13.6 %connect_back.2 = (f32[4,128,2048]{2,1,0:T(8,128)}, f32[8,2048]{1,0:T(8,128)}, f32[8,8]{1,0:T(8,128)}, bf16[4,128,2048]{2,1,0:T(8,128)(2,1)}, bf16[128,2048]{1,0:T(8,128)(2,1)}) custom-call(f32[4,128,2048]{2,1,0:T(8,128)} %get-tuple-element.69.refs_0_, f32[4,128,8]{2,1,0:T(8,128)} %get-tuple-element.70.refs_1_, f32[4,128,8]{2,1,0:T(8,128)} %get-tuple-element.71.refs_2_, ...), custom_call_target="tpu_custom_call" | custom-call | tf_op jit(solution)/shard_map/connect_back/pallas_call | solution.py:1680
  278.7 26.4 %project_back.1 = (bf16[8,128,256]{2,1,0:T(8,128)(2,1)}, bf16[8,128,256]{2,1,0:T(8,128)(2,1)}) custom-call(bf16[128,2048]{1,0:T(8,128)(2,1)} %get-tuple-element.88.grad_ref, bf16[512,1024]{1,0:T(8,128)(2,1)} %bitcast.44, bf16[512,1024]{1,0:T(8,128)(2,1)} %copy-done.2, bf16[512,1024]{1,0:T(8,128)(2,1)} %copy-done.1, ...), custom_call_target="tpu_custom_call" | custom-call | tf_op jit(solution)/shard_map/project_back/pallas_call | solution.py:1573
  305.1 5.1 %all-to-all-start = ((bf16[8,128,256]{2,1,0:T(8,128)(2,1)}), bf16[8,128,256]{2,1,0:T(8,128)(2,1)}, u32[]{:S(2)}, u32[]{:S(2)}) async-start(bf16[8,128,256]{2,1,0:T(8,128)(2,1)} %get-tuple-element.96), calls=%async_computation | async-start | bytes 1048576 | tf_op jit(solution)/shard_map/all_to_all | solution.py:1794
  310.2 18.1 %attention_backward.1 = (bf16[1024,768]{1,0:T(8,128)(2,1)}, bf16[1024,2048]{1,0:T(8,128)(2,1)}) custom-call(bf16[1024,256]{1,0:T(8,128)(2,1)} %get-tuple-element.85.query_ref, bf16[1024,256]{1,0:T(8,128)(2,1)} %get-tuple-element.86.key_ref, bf16[1024,256]{1,0:T(8,128)(2,1)} %get-tuple-element.87.value_ref, bf16[1024,256]{1,0:T(8,128)(2,1)} %bitcast.49, ...), custom_call_target="tpu_custom_call" | custom-call | tf_op jit(solution)/shard_map/attention_backward/pallas_call | solution.py:1357
  328.3 1.5 constant_dynamic-update-slice_fusion.1
  329.9 48.8 %attention_sums.1 = (f32[128,2048]{1,0:T(8,128)}, f32[512,1024]{1,0:T(8,128)}) custom-call(bf16[8,128,2048]{2,1,0:T(8,128)(2,1)} %bitcast.58, bf16[1024,2048]{1,0:T(8,128)(2,1)} %bitcast.39, bf16[1024,768]{1,0:T(8,128)(2,1)} %get-tuple-element.94.refs_1_, bf16[8,1024,256]{2,1,0:T(8,128)(2,1)} %get-tuple-element.95.refs_2_, bf16[1024,256]{1,0:T(8,128)(2,1)} %bitcast.21.refs_3_), custom_call_target="tpu_custom_call" | custom-call | flops 4294967296 | bytes 16777216 | tf_op jit(solution)/shard_map/attention_sums/pallas_call | solution.py:665
  378.8 1.5 constant_dynamic-update-slice_fusion
  380.3 1.8 constant_dynamic-slice_fusion.1
  382.2 3.2 reshape.87
  385.4 11.2 %connect_back.3 = (f32[4,128,2048]{2,1,0:T(8,128)}, f32[8,2048]{1,0:T(8,128)}, f32[8,8]{1,0:T(8,128)}) custom-call(bf16[4,128,2048]{2,1,0:T(8,128)(2,1)} %bitcast.37, f32[4,128,8]{2,1,0:T(8,128)} %get-tuple-element.57.coef_ref.refs_8_.refs_1_, f32[4,128,8]{2,1,0:T(8,128)} %get-tuple-element.82.refs_2_, f32[128,2048]{1,0:T(8,128)} %get-tuple-element.83.refs_3_, ...), custom_call_target="tpu_custom_call" | custom-call | tf_op jit(solution)/shard_map/connect_back/pallas_call | solution.py:1680
  396.6 0.7 slice.63
  397.4 0.9 pad_maximum_fusion
  398.3 0.7 reshape.90.values_ref
  399.0 17.2 %sum_everywhere.1 = f32[8,8,512]{2,1,0:T(8,128)} custom-call(f32[8,8,512]{2,1,0:T(8,128)} %reshape.90.values_ref), custom_call_target="tpu_custom_call" | custom-call | tf_op jit(solution)/shard_map/sum_everywhere/pallas_call | solution.py:727
  416.2 0.9 slice.65
  417.1 1.0 reshape.92
  418.1 0.7 reshape.93
  418.8 0.7 copy.22
  419.5 3.0 convert_bitcast_fusion
  (51 shorter events, 0.8 us)
Async XLA Ops:
  7.2 73.1 %all-gather.2.cloned.1.call-start = ((), (), s32[]{:S(2)}) async-start(), calls=%async_computation.2 | async-start | bytes 3932160 | tf_op jit(solution)/shard_map/all_gather | solution.py:53
  7.2 3.8 copy-start.4
  10.9 367.8 %reduce-scatter.2.cloned.1.call-start = ((), (), s32[]{:S(2)}) async-start(), calls=%async_computation.3 | async-start | bytes 4718592 | tf_op jit(solution)/shard_map/reduce_scatter | solution.py:1786
  11.1 6.2 %copy-start.7 = (f32[2,4,6]{2,1,0:T(4,128)S(1)}, f32[2,4,6]{2,1,0:T(4,128)}, u32[]{:S(2)}) copy-start(f32[2,4,6]{2,1,0:T(4,128)} %param.11) | copy-start | bytes 580
  17.3 58.7 %copy-start = (bf16[512,1,1024]{2,0,1:T(8,128)(2,1)}, bf16[512,1,1024]{2,0,1:T(8,128)(2,1)S(1)}, u32[]{:S(2)}) copy-start(bf16[512,1,1024]{2,0,1:T(8,128)(2,1)S(1)} %copy.28) | copy-start | bytes 3145732
  18.6 54.0 %copy-start.9 = (s32[8]{0:T(128)S(1)}, s32[8]{0:T(128)}, u32[]{:S(2)}) copy-start(s32[8]{0:T(128)} %param.13) | copy-start | bytes 100
  25.1 47.5 %collective-permute-start.1 = (bf16[512,1024]{1,0:T(8,128)(2,1)S(1)}, bf16[512,1024]{1,0:T(8,128)(2,1)S(1)}, u32[]{:S(2)}, u32[]{:S(2)}) collective-permute-start(bf16[512,1024]{1,0:T(8,128)(2,1)S(1)} %bitcast.40), channel_id=1, source_target_pairs={{0,2},{1,3},{2,0},{3,1},{4,6},{5,7},{6,4},{7,5},{8,10},{9,11},{10,... | collective-permute-start | bytes 3145736 | tf_op jit(solution)/shard_map/ppermute | solution.py:1721
  28.1 44.5 %collective-permute-start = (bf16[512,1024]{1,0:T(8,128)(2,1)S(1)}, bf16[512,1024]{1,0:T(8,128)(2,1)S(1)}, u32[]{:S(2)}, u32[]{:S(2)}) collective-permute-start(bf16[512,1024]{1,0:T(8,128)(2,1)S(1)} %bitcast.41), channel_id=1, source_target_pairs={{0,1},{1,0},{2,3},{3,2},{4,5},{5,4},{6,7},{7,6},{8,9},{9,8},{10,11... | collective-permute-start | bytes 3145736 | tf_op jit(solution)/shard_map/ppermute | solution.py:1721
  72.7 29.7 %copy-start.1 = (bf16[512,1024]{1,0:T(8,128)(2,1)}, bf16[512,1024]{1,0:T(8,128)(2,1)S(1)}, u32[]{:S(2)}) copy-start(bf16[512,1024]{1,0:T(8,128)(2,1)S(1)} %collective-permute-done.1.refs_2_) | copy-start | bytes 3145732
  72.7 29.7 %copy-start.2 = (bf16[512,1024]{1,0:T(8,128)(2,1)}, bf16[512,1024]{1,0:T(8,128)(2,1)S(1)}, u32[]{:S(2)}) copy-start(bf16[512,1024]{1,0:T(8,128)(2,1)S(1)} %collective-permute-done.refs_1_) | copy-start | bytes 3145732
  73.6 30.8 %collective-permute-start.5 = (bf16[512,1024]{1,0:T(8,128)(2,1)S(1)}, bf16[512,1024]{1,0:T(8,128)(2,1)}, u32[]{:S(2)}, u32[]{:S(2)}) collective-permute-start(bf16[512,1024]{1,0:T(8,128)(2,1)S(1)} %collective-permute-done.refs_1_), channel_id=1, source_target_pairs={{0,4},{4,0},{8,12},{12,8},{16,20},{20,16},{24,28},{28,24},{1,5},{5... | collective-permute-start | bytes 3145736 | tf_op jit(solution)/shard_map/ppermute | solution.py:1726
  74.8 29.6 %collective-permute-start.6 = (bf16[512,1024]{1,0:T(8,128)(2,1)S(1)}, bf16[512,1024]{1,0:T(8,128)(2,1)}, u32[]{:S(2)}, u32[]{:S(2)}) collective-permute-start(bf16[512,1024]{1,0:T(8,128)(2,1)S(1)} %collective-permute-done.1.refs_2_), channel_id=1, source_target_pairs={{0,4},{4,0},{8,12},{12,8},{16,20},{20,16},{24,28},{28,24},{1,5},{5... | collective-permute-start | bytes 3145736 | tf_op jit(solution)/shard_map/ppermute | solution.py:1726
  74.9 27.5 %collective-permute-start.3 = (bf16[256,1024]{1,0:T(8,128)(2,1)}, bf16[256,1024]{1,0:T(8,128)(2,1)}, u32[]{:S(2)}, u32[]{:S(2)}) collective-permute-start(bf16[256,1024]{1,0:T(8,128)(2,1)} %slice.56), channel_id=1, source_target_pairs={{0,1},{1,0},{2,3},{3,2},{4,5},{5,4},{6,7},{7,6},{8,9},{9,8},{10,11... | collective-permute-start | bytes 1572872 | tf_op jit(solution)/shard_map/ppermute | solution.py:1749
  75.5 26.9 %collective-permute-start.2 = (bf16[256,1024]{1,0:T(8,128)(2,1)}, bf16[256,1024]{1,0:T(8,128)(2,1)}, u32[]{:S(2)}, u32[]{:S(2)}) collective-permute-start(bf16[256,1024]{1,0:T(8,128)(2,1)} %slice.55), channel_id=1, source_target_pairs={{0,2},{1,3},{2,0},{3,1},{4,6},{5,7},{6,4},{7,5},{8,10},{9,11},{10,... | collective-permute-start | bytes 1572872 | tf_op jit(solution)/shard_map/ppermute | solution.py:1748
  75.9 28.4 %collective-permute-start.4 = (bf16[512,1024]{1,0:T(8,128)(2,1)S(1)}, bf16[512,1024]{1,0:T(8,128)(2,1)}, u32[]{:S(2)}, u32[]{:S(2)}) collective-permute-start(bf16[512,1024]{1,0:T(8,128)(2,1)S(1)} %bitcast.42), channel_id=1, source_target_pairs={{0,4},{4,0},{8,12},{12,8},{16,20},{20,16},{24,28},{28,24},{1,5},{5... | collective-permute-start | bytes 3145736 | tf_op jit(solution)/shard_map/ppermute | solution.py:1726
  76.0 4.2 copy-start.5
  102.4 3.2 collective-permute-start.7
  103.7 2.6 collective-permute-start.8
  305.1 24.7 %all-to-all-start = ((bf16[8,128,256]{2,1,0:T(8,128)(2,1)}), bf16[8,128,256]{2,1,0:T(8,128)(2,1)}, u32[]{:S(2)}, u32[]{:S(2)}) async-start(bf16[8,128,256]{2,1,0:T(8,128)(2,1)} %get-tuple-element.96), calls=%async_computation | async-start | bytes 1048576 | tf_op jit(solution)/shard_map/all_to_all | solution.py:1794
  380.3 1.9 copy-start.8
  382.1 37.4 %collective-permute-start.9 = (bf16[3,1024,256]{2,1,0:T(8,128)(2,1)}, bf16[3,1024,256]{2,1,0:T(8,128)(2,1)S(1)}, u32[]{:S(2)}, u32[]{:S(2)}) collective-permute-start(bf16[3,1024,256]{2,1,0:T(8,128)(2,1)} %get-tuple-element.123), channel_id=1, source_target_pairs={{0,4},{4,0},{8,12},{12,8},{16,20},{20,16},{24,28},{28,24},{1,5},{5... | collective-permute-start | bytes 4718600 | tf_op jit(solution)/shard_map/ppermute | solution.py:1807
  385.4 12.0 %copy-start.6 = (f32[8,2048]{1,0:T(8,128)S(1)}, f32[8,2048]{1,0:T(8,128)}, u32[]{:S(2)}) copy-start(f32[8,2048]{1,0:T(8,128)} %get-tuple-element.105) | copy-start | bytes 196612
  385.4 34.1 %copy-start.3 = (bf16[3,1024,256]{2,1,0:T(8,128)(2,1)S(1)}, bf16[3,1024,256]{2,1,0:T(8,128)(2,1)}, u32[]{:S(2)}) copy-start(bf16[3,1024,256]{2,1,0:T(8,128)(2,1)} %get-tuple-element.122) | copy-start | bytes 4718596
Sparse Core Ops, SparseCore 0:
  11.1 61.5 all-gather.1
  264.6 53.9 reduce-scatter.1

commit v12 on v11

--- a/solution.py
+++ b/solution.py
@@ -1783,12 +1783,13 @@
         (weight_parts,) = ffn_weights(n_ctx, n_fsdp, None, ffn_all, mirror_rows, hidden, planes, n_own)
     sides = chips // 2
     lines = [[2 * (sides * side + i) + j for i in range(sides)] for side in range(2) for j in range(2)]
-    weight_cols = lax.psum_scatter(weight_parts, "ctx", scatter_dimension=0, axis_index_groups=lines)
 
     grad_first, dynamic_grad_two, static_grad_two, streams_out, grad_attn = connect_back(
         first_out, coef_two, dyn_two, sums, cotangent[0], sums, dynamics[1], means[1:], coef_one, length
     )
     grad_heads, grad_cols = project_back(n_ctx, n_fsdp, grad_attn, w_out_mine, w_out_other, w_out_where, own_rows)
+    grad_heads, weight_parts = lax.optimization_barrier((grad_heads, weight_parts))
+    weight_cols = lax.psum_scatter(weight_parts, "ctx", scatter_dimension=0, axis_index_groups=lines)
     grad_heads = grad_heads.reshape(rows, own)
     grad_heads, grad_cols = lax.optimization_barrier((grad_heads, grad_cols))
     grad_cols = lax.all_to_all(grad_cols, "ctx", 0, 0, tiled=True).reshape(rows, own)

time: 435 us -> 443 us (1.018)
  Pallas kernels: 365 us -> 372 us
    pallas_call x1, Pallas kernels: 48.8 us -> 62.7 us  [attention_sums(): pl.pallas_call(kernel, out_shape=[jax.ShapeDtypeStruct(partial.shape[-2:]...]
    pallas_call x1, Pallas kernels: 26.4 us -> 17.9 us  [project_back(): pl.pallas_call(kernel, in_specs=[pl.BlockSpec(memory_space=pltpu.VMEM)] *...]
  transfers between devices with their start and end apart: 13 -> 13, of which waited for: 2 -> 2; matrix products, arithmetic and copies ran while one was open for 6% -> 6% of each run, Pallas kernels for 48% -> 42%
where the time goes in v12:
time: 443 us; the launch traced here: 438 us
  Pallas kernels  372 us (84%)
  local copies, waits for them, and re-layouts  27.5 us (6%)
  starting transfers between devices  14.8 us (3%)
  between operations  14.5 us (3%)
  other arithmetic  7.92 us (2%)
    pallas_call x1, Pallas kernels, ffn_rows(): pl.pallas_call(kernel, in_specs=any_specs(3), out_specs=any_specs(7), out...  93.7 us
    pallas_call x1, Pallas kernels, attention_sums(): pl.pallas_call(kernel, out_shape=[jax.ShapeDtypeStruct(partial.shape[-2:]...  62.7 us
    pallas_call x1, Pallas kernels, ffn_weights(): pl.pallas_call(kernel, grid=(steps,), in_specs=in_specs, out_specs=out_sp...  50.8 us
    pallas_call x1, Pallas kernels, line_rows(): pl.pallas_call(kernel, out_shape=jax.ShapeDtypeStruct((n_ctx,) + rows.sha...  42.9 us
    pallas_call x2, Pallas kernels, connect_back(): pl.pallas_call(kernel, grid=(steps,), in_specs=in_specs, out_specs=out_sp...  24.8 us
    pallas_call x1, Pallas kernels, attention_forward(): pl.pallas_call(kernel, grid=(steps,), in_specs=[pl.BlockSpec((SPAN, featu...  22.1 us
    pallas_call x1, Pallas kernels, attention_backward(): pl.pallas_call(kernel, grid=(steps,), in_specs=[whole_block(a.shape) for...  19.2 us
    pallas_call x1, Pallas kernels, project_back(): pl.pallas_call(kernel, in_specs=[pl.BlockSpec(memory_space=pltpu.VMEM)] *...  17.9 us
  transfers between devices with their start and end apart: 13, of which 2 were waited for; matrix products, arithmetic and copies ran while one was open for 6% of the time, Pallas kernels for 42%

profile of v12, /device:TPU:0, one launch (start us, length us, event | category | flops | bytes accessed | tf_op | source)
XLA Modules:
  0.0 437.9 jit_solution(9123549967106251164)
XLA Ops:
  7.2 1.6 constant_dynamic-slice_fusion.2
  8.9 0.9 copy.26
  9.8 1.2 copy.19
  11.1 5.8 %constant_dynamic-slice_fusion.3 = bf16[512,1,1024]{2,1,0:T(2,128)(2,1)S(1)} fusion(bf16[512,4,2048]{2,1,0:T(4,128)(2,1)} %param.8, s32[]{:T(128)S(6)} %add.63, s32[]{:T(128)S(6)} %select_n.36), kind=kLoop, calls=%fused_computation.29 | loop fusion | bytes 2097160 | tf_op jit(solution)/shard_map/slice | solution.py:1715
  16.9 0.4 copy.28
  17.3 0.7 fusion.4
  17.9 0.7 fusion.2
  18.6 6.5 %connect_first.1 = (f32[4,128,8]{2,1,0:T(8,128)}, f32[4,128,8]{2,1,0:T(8,128)}, bf16[128,2048]{1,0:T(8,128)(2,1)}) custom-call(bf16[4,128,2048]{2,1,0:T(8,128)(2,1)} %bitcast.35, f32[8,2048]{1,0:T(8,128)} %get-tuple-element.129.dynamic_ref.refs_6_, f32[4,8]{1,0:T(4,128)} %get-tuple-element.133.static_ref), custom_call_target="tpu_custom_call" | custom-call | tf_op jit(solution)/shard_map/connect_first/pallas_call | solution.py:1421
  25.1 3.0 collective-permute-start.1
  28.1 1.5 collective-permute-start
  29.6 42.9 %line_rows.1 = bf16[8,128,2048]{2,1,0:T(8,128)(2,1)} custom-call(bf16[128,2048]{1,0:T(8,128)(2,1)} %get-tuple-element.61.rows_ref), custom_call_target="tpu_custom_call" | custom-call | tf_op jit(solution)/shard_map/line_rows/pallas_call | solution.py:271
  72.7 0.9 slice.55
  73.6 0.4 collective-permute-start.5
  74.0 0.8 slice.56
  74.8 0.1 collective-permute-start.6
  74.9 0.5 collective-permute-start.3
  75.5 0.5 collective-permute-start.2
  76.0 1.0 copy.20.column_ref
  77.1 0.1 pad_reduce_fusion
  77.2 3.1 fusion
  80.3 22.1 %attention_forward.1 = (bf16[1024,256]{1,0:T(8,128)(2,1)}, bf16[1024,256]{1,0:T(8,128)(2,1)}, bf16[1024,256]{1,0:T(8,128)(2,1)}, bf16[1024,256]{1,0:T(8,128)(2,1...) custom-call(bf16[1024,2048]{1,0:T(8,128)(2,1)} %bitcast.38, ...), custom_call_target="tpu_custom_call" | custom-call | tf_op jit(solution)/shard_map/attention_forward/pallas_call | solution.py:1297
  102.5 1.3 collective-permute-start.7
  103.9 0.6 pad_add_fusion.1.core_ref
  104.5 0.5 fusion.5
  105.0 0.5 collective-permute-done.7.refs_8_
  105.5 0.9 collective-permute-done.8.refs_9_
  106.4 13.6 %connect_middle.1 = (f32[4,128,2048]{2,1,0:T(8,128)}, f32[128,2048]{1,0:T(8,128)}, f32[4,128,8]{2,1,0:T(8,128)}, f32[4,128,8]{2,1,0:T(8,128)}, bf16[2,128,2048]{2,1,0:T(8,128)(2,1)}) custom-call(s32[2]{0:T(128)} %pad_add_fusion.1.core_ref, bf16[4,128,2048]{2,1,0:T(8,128)(2,1)} %bitcast.36, f32[4,128,8]{2,1,0:T(8,128)} %get-tuple-element.59.coef_ref.refs_8_.refs_1_, ...), custom_call_target="tpu_custom_call" | custom-call | tf_op jit(solution)/shard_map/connect_middle/pallas_call | solution.py:1474
  120.0 93.7 %ffn_rows.1 = (bf16[2,4,256,2048]{3,2,1,0:T(8,128)(2,1)}, bf16[2,4,256,2048]{3,2,1,0:T(8,128)(2,1)}, bf16[1024,1024]{1,0:T(8,128)(2,1)}, bf16[1024,1024]{1,0:T(8...) custom-call(bf16[256,2048]{1,0:T(8,128)(2,1)} %bitcast.60, ...), custom_call_target="tpu_custom_call" | custom-call | flops 25769803776 | bytes 52428800 | tf_op jit(solution)/shard_map/ffn_rows/pallas_call | solution.py:989
  213.8 50.8 %ffn_weights.1 = (bf16[2,3,512,512]{3,2,1,0:T(8,128)(2,1)}, f32[256,2048]{1,0:T(8,128)}, bf16[3,512,512]{2,1,0:T(8,128)(2,1)}) custom-call(bf16[8,2,128,2048]{3,2,1,0:T(8,128)(2,1)} %bitcast.61, bf16[8,2,128,2048]{3,2,1,0:T(8,128)(2,1)} %bitcast.62, bf16[1024,1024]{1,0:T(8,128)(2,1)} %get-tuple-element.78.refs_2_, ...), custom_call_target="tpu_custom_call" | custom-call | flops 25769803776 | bytes 52428800 | tf_op jit(solution)/shard_map/ffn_weights/pallas_call | solution.py:1167
  264.6 13.6 %connect_back.2 = (f32[4,128,2048]{2,1,0:T(8,128)}, f32[8,2048]{1,0:T(8,128)}, f32[8,8]{1,0:T(8,128)}, bf16[4,128,2048]{2,1,0:T(8,128)(2,1)}, bf16[128,2048]{1,0:T(8,128)(2,1)}) custom-call(f32[4,128,2048]{2,1,0:T(8,128)} %get-tuple-element.71.refs_0_, f32[4,128,8]{2,1,0:T(8,128)} %get-tuple-element.72.refs_1_, f32[4,128,8]{2,1,0:T(8,128)} %get-tuple-element.73.refs_2_, ...), custom_call_target="tpu_custom_call" | custom-call | tf_op jit(solution)/shard_map/connect_back/pallas_call | solution.py:1680
  278.2 17.9 %project_back.1 = (bf16[8,128,256]{2,1,0:T(8,128)(2,1)}, bf16[8,128,256]{2,1,0:T(8,128)(2,1)}) custom-call(bf16[128,2048]{1,0:T(8,128)(2,1)} %get-tuple-element.90.grad_ref, bf16[512,1024]{1,0:T(8,128)(2,1)} %bitcast.44, bf16[512,1024]{1,0:T(8,128)(2,1)} %copy-done.2, bf16[512,1024]{1,0:T(8,128)(2,1)} %copy-done.1, ...), custom_call_target="tpu_custom_call" | custom-call | tf_op jit(solution)/shard_map/project_back/pallas_call | solution.py:1573
  296.1 7.3 %all-to-all-start = ((bf16[8,128,256]{2,1,0:T(8,128)(2,1)}), bf16[8,128,256]{2,1,0:T(8,128)(2,1)}, u32[]{:S(2)}, u32[]{:S(2)}) async-start(bf16[8,128,256]{2,1,0:T(8,128)(2,1)} %get-tuple-element.100), calls=%async_computation | async-start | bytes 1048576 | tf_op jit(solution)/shard_map/all_to_all | solution.py:1795
  303.4 19.2 %attention_backward.1 = (bf16[1024,768]{1,0:T(8,128)(2,1)}, bf16[1024,2048]{1,0:T(8,128)(2,1)}) custom-call(bf16[1024,256]{1,0:T(8,128)(2,1)} %get-tuple-element.87.query_ref, bf16[1024,256]{1,0:T(8,128)(2,1)} %get-tuple-element.88.key_ref, bf16[1024,256]{1,0:T(8,128)(2,1)} %get-tuple-element.89.value_ref, bf16[1024,256]{1,0:T(8,128)(2,1)} %bitcast.49, ...), custom_call_target="tpu_custom_call" | custom-call | tf_op jit(solution)/shard_map/attention_backward/pallas_call | solution.py:1357
  322.6 1.5 constant_dynamic-update-slice_fusion.1
  324.1 62.7 %attention_sums.1 = (f32[128,2048]{1,0:T(8,128)}, f32[512,1024]{1,0:T(8,128)}) custom-call(bf16[8,128,2048]{2,1,0:T(8,128)(2,1)} %bitcast.58, bf16[1024,2048]{1,0:T(8,128)(2,1)} %bitcast.39, bf16[1024,768]{1,0:T(8,128)(2,1)} %get-tuple-element.98.refs_1_, bf16[8,1024,256]{2,1,0:T(8,128)(2,1)} %get-tuple-element.99.refs_2_, bf16[1024,256]{1,0:T(8,128)(2,1)} %bitcast.21.refs_3_), custom_call_target="tpu_custom_call" | custom-call | flops 4294967296 | bytes 16777216 | tf_op jit(solution)/shard_map/attention_sums/pallas_call | solution.py:665
  386.8 1.5 constant_dynamic-update-slice_fusion
  388.3 1.9 constant_dynamic-slice_fusion.1
  390.3 3.2 reshape.87
  393.4 11.2 %connect_back.3 = (f32[4,128,2048]{2,1,0:T(8,128)}, f32[8,2048]{1,0:T(8,128)}, f32[8,8]{1,0:T(8,128)}) custom-call(bf16[4,128,2048]{2,1,0:T(8,128)(2,1)} %bitcast.37, f32[4,128,8]{2,1,0:T(8,128)} %get-tuple-element.59.coef_ref.refs_8_.refs_1_, f32[4,128,8]{2,1,0:T(8,128)} %get-tuple-element.84.refs_2_, f32[128,2048]{1,0:T(8,128)} %get-tuple-element.85.refs_3_, ...), custom_call_target="tpu_custom_call" | custom-call | tf_op jit(solution)/shard_map/connect_back/pallas_call | solution.py:1680
  404.7 0.7 slice.63
  405.5 0.9 pad_maximum_fusion
  406.3 0.7 reshape.90.values_ref
  407.0 17.4 %sum_everywhere.1 = f32[8,8,512]{2,1,0:T(8,128)} custom-call(f32[8,8,512]{2,1,0:T(8,128)} %reshape.90.values_ref), custom_call_target="tpu_custom_call" | custom-call | tf_op jit(solution)/shard_map/sum_everywhere/pallas_call | solution.py:727
  424.5 0.9 slice.65
  425.4 1.0 reshape.92
  426.4 0.7 reshape.93
  427.1 0.7 copy.22
  427.8 3.0 convert_bitcast_fusion
  (53 shorter events, 0.8 us)
Async XLA Ops:
  7.2 73.2 %all-gather.2.cloned.1.call-start = ((), (), s32[]{:S(2)}) async-start(), calls=%async_computation.2 | async-start | bytes 3932160 | tf_op jit(solution)/shard_map/all_gather | solution.py:53
  7.2 3.8 copy-start.5
  10.9 375.8 %reduce-scatter.2.cloned.1.call-start = ((), (), s32[]{:S(2)}) async-start(), calls=%async_computation.3 | async-start | bytes 4718592 | tf_op jit(solution)/shard_map/reduce_scatter | solution.py:1792
  11.1 6.2 %copy-start.8 = (f32[2,4,6]{2,1,0:T(4,128)S(1)}, f32[2,4,6]{2,1,0:T(4,128)}, u32[]{:S(2)}) copy-start(f32[2,4,6]{2,1,0:T(4,128)} %param.11) | copy-start | bytes 580
  17.3 58.7 %copy-start = (bf16[512,1,1024]{2,0,1:T(8,128)(2,1)}, bf16[512,1,1024]{2,0,1:T(8,128)(2,1)S(1)}, u32[]{:S(2)}) copy-start(bf16[512,1,1024]{2,0,1:T(8,128)(2,1)S(1)} %copy.28) | copy-start | bytes 3145732
  18.6 54.0 %copy-start.10 = (s32[8]{0:T(128)S(1)}, s32[8]{0:T(128)}, u32[]{:S(2)}) copy-start(s32[8]{0:T(128)} %param.13) | copy-start | bytes 100
  25.1 47.5 %collective-permute-start.1 = (bf16[512,1024]{1,0:T(8,128)(2,1)S(1)}, bf16[512,1024]{1,0:T(8,128)(2,1)S(1)}, u32[]{:S(2)}, u32[]{:S(2)}) collective-permute-start(bf16[512,1024]{1,0:T(8,128)(2,1)S(1)} %bitcast.40), channel_id=1, source_target_pairs={{0,2},{1,3},{2,0},{3,1},{4,6},{5,7},{6,4},{7,5},{8,10},{9,11},{10,... | collective-permute-start | bytes 3145736 | tf_op jit(solution)/shard_map/ppermute | solution.py:1721
  28.1 44.6 %collective-permute-start = (bf16[512,1024]{1,0:T(8,128)(2,1)S(1)}, bf16[512,1024]{1,0:T(8,128)(2,1)S(1)}, u32[]{:S(2)}, u32[]{:S(2)}) collective-permute-start(bf16[512,1024]{1,0:T(8,128)(2,1)S(1)} %bitcast.41), channel_id=1, source_target_pairs={{0,1},{1,0},{2,3},{3,2},{4,5},{5,4},{6,7},{7,6},{8,9},{9,8},{10,11... | collective-permute-start | bytes 3145736 | tf_op jit(solution)/shard_map/ppermute | solution.py:1721
  72.7 29.8 %copy-start.1 = (bf16[512,1024]{1,0:T(8,128)(2,1)}, bf16[512,1024]{1,0:T(8,128)(2,1)S(1)}, u32[]{:S(2)}) copy-start(bf16[512,1024]{1,0:T(8,128)(2,1)S(1)} %collective-permute-done.1.refs_2_) | copy-start | bytes 3145732
  72.7 29.8 %copy-start.2 = (bf16[512,1024]{1,0:T(8,128)(2,1)}, bf16[512,1024]{1,0:T(8,128)(2,1)S(1)}, u32[]{:S(2)}) copy-start(bf16[512,1024]{1,0:T(8,128)(2,1)S(1)} %collective-permute-done.refs_1_) | copy-start | bytes 3145732
  73.6 31.4 %collective-permute-start.5 = (bf16[512,1024]{1,0:T(8,128)(2,1)S(1)}, bf16[512,1024]{1,0:T(8,128)(2,1)}, u32[]{:S(2)}, u32[]{:S(2)}) collective-permute-start(bf16[512,1024]{1,0:T(8,128)(2,1)S(1)} %collective-permute-done.refs_1_), channel_id=1, source_target_pairs={{0,4},{4,0},{8,12},{12,8},{16,20},{20,16},{24,28},{28,24},{1,5},{5... | collective-permute-start | bytes 3145736 | tf_op jit(solution)/shard_map/ppermute | solution.py:1726
  74.8 30.2 %collective-permute-start.6 = (bf16[512,1024]{1,0:T(8,128)(2,1)S(1)}, bf16[512,1024]{1,0:T(8,128)(2,1)}, u32[]{:S(2)}, u32[]{:S(2)}) collective-permute-start(bf16[512,1024]{1,0:T(8,128)(2,1)S(1)} %collective-permute-done.1.refs_2_), channel_id=1, source_target_pairs={{0,4},{4,0},{8,12},{12,8},{16,20},{20,16},{24,28},{28,24},{1,5},{5... | collective-permute-start | bytes 3145736 | tf_op jit(solution)/shard_map/ppermute | solution.py:1726
  74.9 27.6 %collective-permute-start.3 = (bf16[256,1024]{1,0:T(8,128)(2,1)}, bf16[256,1024]{1,0:T(8,128)(2,1)}, u32[]{:S(2)}, u32[]{:S(2)}) collective-permute-start(bf16[256,1024]{1,0:T(8,128)(2,1)} %slice.56), channel_id=1, source_target_pairs={{0,1},{1,0},{2,3},{3,2},{4,5},{5,4},{6,7},{7,6},{8,9},{9,8},{10,11... | collective-permute-start | bytes 1572872 | tf_op jit(solution)/shard_map/ppermute | solution.py:1749
  75.5 27.0 %collective-permute-start.2 = (bf16[256,1024]{1,0:T(8,128)(2,1)}, bf16[256,1024]{1,0:T(8,128)(2,1)}, u32[]{:S(2)}, u32[]{:S(2)}) collective-permute-start(bf16[256,1024]{1,0:T(8,128)(2,1)} %slice.55), channel_id=1, source_target_pairs={{0,2},{1,3},{2,0},{3,1},{4,6},{5,7},{6,4},{7,5},{8,10},{9,11},{10,... | collective-permute-start | bytes 1572872 | tf_op jit(solution)/shard_map/ppermute | solution.py:1748
  75.9 29.1 %collective-permute-start.4 = (bf16[512,1024]{1,0:T(8,128)(2,1)S(1)}, bf16[512,1024]{1,0:T(8,128)(2,1)}, u32[]{:S(2)}, u32[]{:S(2)}) collective-permute-start(bf16[512,1024]{1,0:T(8,128)(2,1)S(1)} %bitcast.42), channel_id=1, source_target_pairs={{0,4},{4,0},{8,12},{12,8},{16,20},{20,16},{24,28},{28,24},{1,5},{5... | collective-permute-start | bytes 3145736 | tf_op jit(solution)/shard_map/ppermute | solution.py:1726
  76.0 4.3 copy-start.6
  102.5 3.0 collective-permute-start.7
  103.8 2.6 collective-permute-start.8
  105.5 0.9 copy-start.4
  296.1 28.0 %all-to-all-start = ((bf16[8,128,256]{2,1,0:T(8,128)(2,1)}), bf16[8,128,256]{2,1,0:T(8,128)(2,1)}, u32[]{:S(2)}, u32[]{:S(2)}) async-start(bf16[8,128,256]{2,1,0:T(8,128)(2,1)} %get-tuple-element.100), calls=%async_computation | async-start | bytes 1048576 | tf_op jit(solution)/shard_map/all_to_all | solution.py:1795
  388.3 1.9 copy-start.9
  390.2 37.6 %collective-permute-start.9 = (bf16[3,1024,256]{2,1,0:T(8,128)(2,1)}, bf16[3,1024,256]{2,1,0:T(8,128)(2,1)S(1)}, u32[]{:S(2)}, u32[]{:S(2)}) collective-permute-start(bf16[3,1024,256]{2,1,0:T(8,128)(2,1)} %get-tuple-element.127), channel_id=1, source_target_pairs={{0,4},{4,0},{8,12},{12,8},{16,20},{20,16},{24,28},{28,24},{1,5},{5... | collective-permute-start | bytes 4718600 | tf_op jit(solution)/shard_map/ppermute | solution.py:1808
  393.4 12.0 %copy-start.7 = (f32[8,2048]{1,0:T(8,128)S(1)}, f32[8,2048]{1,0:T(8,128)}, u32[]{:S(2)}) copy-start(f32[8,2048]{1,0:T(8,128)} %get-tuple-element.109) | copy-start | bytes 196612
  393.4 34.4 %copy-start.3 = (bf16[3,1024,256]{2,1,0:T(8,128)(2,1)S(1)}, bf16[3,1024,256]{2,1,0:T(8,128)(2,1)}, u32[]{:S(2)}) copy-start(bf16[3,1024,256]{2,1,0:T(8,128)(2,1)} %get-tuple-element.126) | copy-start | bytes 4718596
Sparse Core Ops, SparseCore 0:
  11.1 61.5 all-gather.1
  296.2 64.2 reduce-scatter.1
